TPU v7x, 32 devices: a whole 2x2x4 slice. The times are simulated.
32 devices in a mesh: node: 8 (over z, x), edge: 4 (over y, core).
Axes of the slice: x: 2, y: 2, z: 4, core: 2. Of those that a mesh axis runs over, the one named last changes fastest.
Arguments:
- teleport: float32 [16384, 128], P(('node', 'edge')), may hold values from -6 to 6
- cotangent: float32 [16384, 128], P(('node', 'edge')), may hold values from -6 to 6
- fetch_table: int32 [8, 16], replicated, may hold values from -1 to 7, as said below
- block_row: int32 [8, 192], P('node'), may hold values from 0 to 7
- block_slot: int32 [8, 192], P('node'), may hold values from 0 to 15, as said below
- values: bfloat16 [8, 192, 256, 256], P('node', None, 'edge'), may hold values from -0.078125 to 0.078125
Outputs:
- propagated: float32 [16384, 128], P(('node', 'edge'))
- teleport_grad: float32 [16384, 128], P(('node', 'edge'))
Inputs may be any that keep to these rules, and one draw needn't show every extreme that they name: `fetch_table`: entry n, o * 2 + k names a node block index j of owner group o that group n reads in slot k, or is -1 for an empty slot. Within the 2 slots of one owner the live ones come first and name distinct blocks. One owner group has all 2 slots live in every row. `block_slot`: every entry names a live slot of the group's row of fetch_table, and every live slot of that row is named by at least one adjacency block of the group.
All inputs are finite; a program needn't handle non-finite values.
Results may differ from a plain program's by a relative error of at most 0.004.
Values may be sent and summed in bfloat16 or wider, within the bound.
No kernel may reach another device: no remote copies, remote signals or barrier semaphores. Data moves between devices by JAX's collectives and lax.ppermute only.
A program may use at most 128 MiB of HBM per device.

v0:
```python
import jax
import jax.numpy as jnp
from jax import lax
from jax.sharding import PartitionSpec as P

CAP = 2
STEPS = 2


def per_device(teleport, cotangent, fetch_table, block_row, block_slot, values):
    row_count, hidden = teleport.shape
    quarter = values.shape[2]
    block_count = values.shape[1]
    blocks_dev = row_count // quarter
    slot_total = fetch_table.shape[1]
    owner_count = lax.axis_size("node")
    group_size = 16
    turn_count = block_count // group_size
    owner_index = lax.axis_index("node")
    local_weights = values[0]
    row_ids = block_row[0]
    slot_ids = block_slot[0]
    own_plan = lax.dynamic_index_in_dim(fetch_table, owner_index, 0, keepdims=False)
    local_ids = jnp.take(own_plan, slot_ids, axis=0)
    global_ids = slot_ids // CAP * blocks_dev + local_ids
    requests = lax.dynamic_slice_in_dim(fetch_table, owner_index * CAP, CAP, 1).reshape(slot_total)
    block_range = jnp.arange(blocks_dev, dtype=jnp.int32)
    request_hot = requests[:, None] == block_range[None, :]
    request_float = request_hot.astype(jnp.float32)
    weight_groups = local_weights.reshape(turn_count, group_size, quarter, local_weights.shape[2])
    row_groups = row_ids.reshape(turn_count, group_size)
    slot_groups = slot_ids.reshape(turn_count, group_size)
    current = teleport
    for step_index in range(STEPS):
        propagate_rounded = current.astype(jnp.bfloat16)
        everything = lax.all_gather(propagate_rounded, "node", axis=0, tiled=True)
        feature_table = everything.reshape(owner_count * blocks_dev, quarter, hidden)
        columns = jnp.take(feature_table, global_ids, axis=0)
        column_groups = columns.reshape(turn_count, group_size, quarter, hidden)

        def partial_rows(amount):
            quarters_used = amount // row_count

            def partial_advance(running, inputs):
                weights, sources, targets = inputs
                product = jnp.einsum(
                    "bcr,bch->brh", weights, sources, preferred_element_type=jnp.float32
                )
                product = product.reshape(group_size, quarters_used, quarter, hidden)
                return (running.at[targets].add(product), None)

            start_sum = jnp.zeros((blocks_dev, quarters_used, quarter, hidden), jnp.float32)
            running, _ = lax.scan(
                partial_advance, start_sum, (weight_groups, column_groups, row_groups)
            )
            return running.transpose(1, 0, 2, 3).reshape(amount, hidden)

        current = (
            0.9
            * lax.psum_scatter(
                partial_rows(lax.axis_size("edge") * row_count),
                "edge",
                scatter_dimension=0,
                tiled=True,
            )
            + 0.1 * teleport
        )
    adjoint = cotangent
    gradient = 0.1 * cotangent
    for step_index in range(STEPS):
        rounded = adjoint.astype(jnp.bfloat16).reshape(blocks_dev, quarter, hidden)

        def fold_rows(running, arrived_rows):

            def fold_advance(carried, inputs):
                weights, targets, slot_targets = inputs
                sources = jnp.take(arrived_rows, targets, axis=0)
                product = jnp.einsum(
                    "bcr,brh->bch", weights, sources, preferred_element_type=jnp.float32
                )
                return (carried.at[slot_targets].add(product), None)

            carried, _ = lax.scan(fold_advance, running, (weight_groups, row_groups, slot_groups))
            return carried

        transpose_start_sum = jnp.zeros((slot_total, quarter, hidden), jnp.float32)
        partial_value = fold_rows(
            transpose_start_sum, lax.all_gather(rounded, "edge", axis=1, tiled=True)
        )
        summed = jnp.einsum(
            "sj,sch->jch",
            request_float,
            lax.all_to_all(partial_value, "node", split_axis=0, concat_axis=0, tiled=True),
            precision=lax.Precision.HIGHEST,
        )
        adjoint = 0.9 * summed.reshape(row_count, hidden)
        factor = 0.1 if step_index + 1 < STEPS else 1.0
        gradient = gradient + factor * adjoint
    return (current, gradient)


def solution(mesh):
    placed = (
        P(("node", "edge"), None),
        P(("node", "edge"), None),
        P(),
        P("node", None),
        P("node", None),
        P("node", None, "edge", None),
    )
    return jax.shard_map(
        per_device,
        mesh=mesh,
        in_specs=placed,
        out_specs=(P(("node", "edge"), None), P(("node", "edge"), None)),
        check_vma=False,
    )
```

profile of v0, /device:TPU:0, one launch (start us, length us, event | category | flops | bytes accessed | tf_op | source)
XLA Modules:
  0.0 360.2 jit_solution(17126004902237536595)
XLA Ops:
  11.6 5.0 %compare_select_fusion.8 = (s32[192,1]{0,1:T(1,128)S(1)}, s32[192,1]{0,1:T(1,128)S(1)}) fusion(s32[]{:T(128)} %bitcast.30, s32[]{:T(128)} %bitcast.31, s32[]{:T(128)} %bitcast.32, s32[]{:T(128)} %bitcast.33, s32[]{:T(128)} %bitcast.34, s32[]{:T(128)} %bitcast.36, s32[]{:T(128)} %bitcast.35, s32[1,192]{1,0:T(1,128)} %param.22), kind=kLoop, calls=%fused_computation.88 | loop fusion | flops 2880 | bytes 2332 | tf_op jit(solution)/shard_map/jit(_take)/gather | solution.py:24
  16.6 6.2 %compare_and_fusion.2 = (pred[192]{0:T(512)(128)(4,1)S(1)}, s32[192]{0:T(256)S(1)}) fusion(pred[192]{0:T(512)(128)(4,1)S(1)} %get-tuple-element.152, pred[192]{0:T(512)(128)(4,1)S(1)} %get-tuple-element.151, pred[192]{0:T(512)(128)(4,1)S(1)} %get-tuple-element.150, pred[192]{0:T(512)(128)(4,1)S(1)} %get-tuple-element.149, ...), kind=kLoop, calls=%fused_computation.96 | loop fusion | flops 7296 | bytes 4260 | tf_op jit(solution)/shard_map/jit(_take)/and | solution.py:38
  22.8 30.8 %all-gather.3.cloned.1.call-done = bf16[4096,128]{1,0:T(8,128)(2,1)} async-done(((bf16[512,128]{1,0:T(8,128)(2,1)}), bf16[4096,128]{1,0:T(8,128)(2,1)}) %all-gather.3.cloned.1.call-update) | async-done | bytes 1048592 | tf_op jit(solution)/shard_map/all_gather | solution.py:36
  58.2 46.1 %while.40 = (s32[]{:T(128)}, f32[8,4,64,128]{3,2,1,0:T(8,128)S(1)}, s32[12,16]{1,0:T(8,128)S(1)}, bf16[12,16,64,256]{3,2,1,0:T(8,128)(2,1)}, bf16[12,16,64,128]{3,2,1,0:T(8,128)(2,1)}, /*index=5*/s32[]{:T(128)}) while((s32[]{:T(128)}, f32[8,4,64,128]{3,2,1,0:T(8,128)S(1)}, s32[12,16]{1,0:T(8,128)S(1)}, bf16[12,16,64,256]{3,2,1,0:T(8,128)(2,1)}, ...), condition=%wide.region_2.4_spmd, body=%wide.region_0.0_spmd.sunk | while | flops 67633200 | bytes 9176329 | solution.py:53
  106.2 7.2 %all_gather.14 = bf16[8,256,128]{2,1,0:T(8,128)(2,1)S(1)} all-gather(bf16[8,64,128]{2,1,0:T(8,128)(2,1)S(1)} %bitcast.148), channel_id=1, replica_groups=mesh['node'=8,'edge'=4] {'edge'}, dimensions={1}, use_global_device_ids=true | all-gather | bytes 655360 | tf_op jit(solution)/shard_map/all_gather | solution.py:88
  113.4 15.9 %reduce-scatter.3.cloned.1.call-done = f32[512,128]{1,0:T(8,128)} async-done(((f32[2048,128]{1,0:T(8,128)}), f32[512,128]{1,0:T(8,128)}) %reduce-scatter.3.cloned.1.call-update) | async-done | bytes 262160 | tf_op jit(solution)/shard_map/reduce_scatter | solution.py:60
  131.8 59.3 %while.42 = (s32[]{:T(128)}, f32[16,64,128]{2,1,0:T(8,128)}, s32[12,16]{1,0:T(8,128)S(1)}, bf16[12,16,64,256]{3,2,1,0:T(8,128)(2,1)}, s32[12,16]{1,0:T(8,128)S(1)}, /*index=5*/bf16[8,256,128]{2,1,0:T(8,128)(2,1)S(1)}, s32[]{:T(128)}) while((s32[]{:T(128)}, f32[16,64,128]{2,1,0:T(8,128)}, s32[12,16]{1,0:T(8,128)S(1)}, ...), condition=%wide.region_10.13_spmd, body=%wide.region_8.12_spmd.sunk | while | flops 67765392 | bytes 5772341 | solution.py:83
  134.0 2.7 scatter_fusion.2
  148.8 2.7 scatter_fusion.2
  163.6 2.7 scatter_fusion.2
  168.6 2.7 scatter_fusion.2
  173.5 2.8 scatter_fusion.2
  191.0 5.4 %all-to-all-start = ((f32[16,64,128]{2,1,0:T(8,128)}), f32[16,64,128]{2,1,0:T(8,128)S(1)}, u32[]{:S(2)}, u32[]{:S(2)}) async-start(f32[16,64,128]{2,1,0:T(8,128)} %get-tuple-element.124), calls=%async_computation.2 | async-start | bytes 1048576 | tf_op jit(solution)/shard_map/all_to_all | solution.py:93
  196.7 14.3 %all-to-all-done = f32[16,64,128]{2,1,0:T(8,128)S(1)} async-done(((f32[16,64,128]{2,1,0:T(8,128)}), f32[16,64,128]{2,1,0:T(8,128)S(1)}, u32[]{:S(2)}, u32[]{:S(2)}) %all-to-all-start) | async-done | bytes 524320 | tf_op jit(solution)/shard_map/all_to_all | solution.py:93
  212.3 6.5 %all_gather.15 = bf16[8,256,128]{2,0,1:T(8,128)(2,1)S(1)} all-gather(bf16[8,64,128]{2,0,1:T(8,128)(2,1)S(1)} %get-tuple-element.206), channel_id=1, replica_groups=mesh['node'=8,'edge'=4] {'edge'}, dimensions={1}, use_global_device_ids=true | all-gather | bytes 655360 | tf_op jit(solution)/shard_map/all_gather | solution.py:88
  224.2 46.1 %while.41 = (s32[]{:T(128)}, f32[8,4,64,128]{3,2,1,0:T(8,128)S(1)}, s32[12,16]{1,0:T(8,128)S(1)}, bf16[12,16,64,256]{3,2,1,0:T(8,128)(2,1)}, bf16[12,16,64,128]{3,2,1,0:T(8,128)(2,1)}, /*index=5*/s32[]{:T(128)}) while((s32[]{:T(128)}, f32[8,4,64,128]{3,2,1,0:T(8,128)S(1)}, s32[12,16]{1,0:T(8,128)S(1)}, bf16[12,16,64,256]{3,2,1,0:T(8,128)(2,1)}, ...), condition=%wide.region_6.8_spmd, body=%wide.region_4.7_spmd.sunk | while | flops 67633200 | bytes 9176329 | solution.py:53
  272.3 59.3 %while.43 = (s32[]{:T(128)}, f32[16,64,128]{2,1,0:T(8,128)}, s32[12,16]{1,0:T(8,128)S(1)}, bf16[12,16,64,256]{3,2,1,0:T(8,128)(2,1)}, s32[12,16]{1,0:T(8,128)S(1)}, /*index=5*/bf16[8,256,128]{2,1,0:T(8,128)(2,1)S(1)}, s32[]{:T(128)}) while((s32[]{:T(128)}, f32[16,64,128]{2,1,0:T(8,128)}, s32[12,16]{1,0:T(8,128)S(1)}, ...), condition=%wide.region_13.16_spmd, body=%wide.region_11.15_spmd.sunk | while | flops 67765392 | bytes 5772341 | solution.py:83
  274.5 2.7 scatter_fusion.3
  289.3 2.7 scatter_fusion.3
  304.1 2.7 scatter_fusion.3
  309.1 2.7 scatter_fusion.3
  314.0 2.8 scatter_fusion.3
  331.5 4.0 %all-to-all-start.1 = ((f32[16,64,128]{2,1,0:T(8,128)}), f32[16,64,128]{2,1,0:T(8,128)S(1)}, u32[]{:S(2)}, u32[]{:S(2)}) async-start(f32[16,64,128]{2,1,0:T(8,128)} %get-tuple-element.125), calls=%async_computation.3 | async-start | bytes 1048576 | tf_op jit(solution)/shard_map/all_to_all | solution.py:93
  335.6 14.9 %all-to-all-done.1 = f32[16,64,128]{2,1,0:T(8,128)S(1)} async-done(((f32[16,64,128]{2,1,0:T(8,128)}), f32[16,64,128]{2,1,0:T(8,128)S(1)}, u32[]{:S(2)}, u32[]{:S(2)}) %all-to-all-start.1) | async-done | bytes 524320 | tf_op jit(solution)/shard_map/all_to_all | solution.py:93
  (261 shorter events, 207.1 us)
Async XLA Ops:
  7.2 3.7 %copy-start = (s32[8,16]{1,0:T(8,128)S(1)}, s32[8,16]{1,0:T(8,128)}, u32[]{:S(2)}) copy-start(s32[8,16]{1,0:T(8,128)} %param.20) | copy-start | bytes 1540
  7.2 46.4 %all-gather.3.cloned.1.call-start = ((), (), s32[]{:S(2)}) async-start(), calls=%async_computation.4 | async-start | bytes 1179648 | tf_op jit(solution)/shard_map/all_gather | solution.py:36
  8.9 120.3 %reduce-scatter.3.cloned.1.call-start = ((), (), s32[]{:S(2)}) async-start(), calls=%async_computation.5 | async-start | bytes 1310720 | tf_op jit(solution)/shard_map/reduce_scatter | solution.py:60
  104.2 1.2 copy-start.6
  104.2 1.9 copy-start.4
  104.3 24.9 %copy-start.2 = (f32[512,128]{1,0:T(8,128)S(1)}, f32[512,128]{1,0:T(8,128)}, u32[]{:S(2)}) copy-start(f32[512,128]{1,0:T(8,128)} %param.18) | copy-start | bytes 786436
  105.4 114.3 %all-gather.5.cloned.1.call-start = ((), (), s32[]{:S(2)}) async-start(), calls=%async_computation.6 | async-start | bytes 1179648 | tf_op jit(solution)/shard_map/all_gather | solution.py:36
  191.0 19.9 %all-to-all-start = ((f32[16,64,128]{2,1,0:T(8,128)}), f32[16,64,128]{2,1,0:T(8,128)S(1)}, u32[]{:S(2)}, u32[]{:S(2)}) async-start(f32[16,64,128]{2,1,0:T(8,128)} %get-tuple-element.124), calls=%async_computation.2 | async-start | bytes 1048576 | tf_op jit(solution)/shard_map/all_to_all | solution.py:93
  196.4 155.5 %reduce-scatter.5.cloned.1.call-start = ((), (), s32[]{:S(2)}) async-start(), calls=%async_computation.7 | async-start | bytes 1310720 | tf_op jit(solution)/shard_map/reduce_scatter | solution.py:60
  270.3 2.0 copy-start.1
  272.2 63.3 %copy-start.3 = (f32[8,64,128]{2,0,1:T(8,128)S(1)}, f32[8,64,128]{2,0,1:T(8,128)}, u32[]{:S(2)}) copy-start(f32[8,64,128]{2,0,1:T(8,128)} %get-tuple-element.205) | copy-start | bytes 786436
  272.3 79.0 %copy-start.5 = (f32[512,128]{1,0:T(8,128)S(1)}, f32[512,128]{1,0:T(8,128)}, u32[]{:S(2)}) copy-start(f32[512,128]{1,0:T(8,128)} %param.19) | copy-start | bytes 786436
  331.5 19.0 %all-to-all-start.1 = ((f32[16,64,128]{2,1,0:T(8,128)}), f32[16,64,128]{2,1,0:T(8,128)S(1)}, u32[]{:S(2)}, u32[]{:S(2)}) async-start(f32[16,64,128]{2,1,0:T(8,128)} %get-tuple-element.125), calls=%async_computation.3 | async-start | bytes 1048576 | tf_op jit(solution)/shard_map/all_to_all | solution.py:93
Sparse Core Ops, SparseCore 0:
  10.7 42.8 all-gather.2
  105.5 23.6 reduce-scatter.2
  132.1 40.1 all-gather.4
  271.5 23.6 reduce-scatter.4
where the time goes:
time: 365 us; the launch traced here: 360 us
  other arithmetic  142 us (39%)
  waiting for transfers between devices  76 us (21%)
  matrix products  74.3 us (20%)
  local copies, waits for them, and re-layouts  29.4 us (8%)
  between operations  13.9 us (4%)
  blocking collectives  13.7 us (4%)
  starting transfers between devices  9.61 us (3%)
    scatter-add x24, other arithmetic, fold_advance(): return (carried.at[slot_targets].add(product), None)  64.9 us
    scatter-add x24, other arithmetic, partial_advance(): return (running.at[targets].add(product), None)  52.7 us
    dot_general x24, matrix products, partial_advance(): jnp.einsum('bcr,bch->brh', weights, sources, preferred_element_type=jnp.f...  38.2 us
    dot_general x24, matrix products, fold_advance(): jnp.einsum('bcr,brh->bch', weights, sources, preferred_element_type=jnp.f...  34.2 us
    all_gather x2, waiting for transfers between devices, per_device(): everything = lax.all_gather(propagate_rounded, 'node', axis=0, tiled=True)  30.8 us
    all_to_all x2, waiting for transfers between devices, per_device(): lax.all_to_all(partial_value, 'node', split_axis=0, concat_axis=0, tiled=...  29.2 us
    gather x24, local copies, waits for them, and re-layouts, fold_advance(): sources = jnp.take(arrived_rows, targets, axis=0)  18 us
    reduce_scatter x2, waiting for transfers between devices, per_device(): lax.psum_scatter(partial_rows(lax.axis_size('edge') * row_count), 'edge',...  15.9 us
  transfers between devices with their start and end apart: 6, of which 4 were waited for; matrix products, arithmetic and copies ran while one was open for 38% of the time, Pallas kernels for 0%

commit v1 on v0

--- a/solution.py
+++ b/solution.py
@@ -1,13 +1,292 @@
+import functools
+
 import jax
 import jax.numpy as jnp
 from jax import lax
+from jax.experimental import pallas as pl
+from jax.experimental.pallas import tpu as pltpu
 from jax.sharding import PartitionSpec as P
 
 CAP = 2
 STEPS = 2
-
-
-def per_device(teleport, cotangent, fetch_table, block_row, block_slot, values):
+DENSE_BYTES = 8 * 2**20
+LOW = jnp.bfloat16
+FULL = jnp.float32
+
+VMEM = pl.BlockSpec(memory_space=pltpu.VMEM)
+SMEM = pl.BlockSpec(memory_space=pltpu.SMEM)
+HBM = pl.BlockSpec(memory_space=pltpu.HBM)
+
+
+def params(mebibytes):
+    return pltpu.CompilerParams(vmem_limit_bytes=mebibytes * 2**20)
+
+
+def partner(axis, turn):
+    return lax.axis_index(axis) ^ turn
+
+
+def requested(table, reader, slot):
+    return jnp.maximum(table[reader, lax.axis_index("node") * CAP + slot], 0)
+
+
+def start_kernel(table, teleport, cotangent, *refs):
+    *sends, rounded, plan, state, adjoint, sems = refs
+    copies = [
+        pltpu.make_async_copy(source, target, sems.at[index])
+        for index, (source, target) in enumerate(
+            ((table, plan), (teleport, state), (cotangent, adjoint))
+        )
+    ]
+    for copy in copies:
+        copy.start()
+    copies[0].wait()
+    copies[1].wait()
+    for turn, send in enumerate(sends):
+        for slot in range(CAP):
+            send[slot] = state[requested(plan, partner("node", turn), slot)].astype(LOW)
+    copies[2].wait()
+    rounded[...] = adjoint[...].astype(LOW)
+
+
+def build_kernel(rows, slots, weights, high, low, held, total, sems):
+    parts = sems.shape[0]
+    block_count, quarter, width = held.shape
+    chunk = block_count // parts
+    copies = [
+        pltpu.make_async_copy(
+            weights.at[0, pl.ds(part * chunk, chunk)],
+            held.at[pl.ds(part * chunk, chunk)],
+            sems.at[part],
+        )
+        for part in range(parts)
+    ]
+    for copy in copies:
+        copy.start()
+    total[...] = jnp.zeros_like(total)
+    for part, copy in enumerate(copies):
+        copy.wait()
+        for block in range(part * chunk, (part + 1) * chunk):
+            total[slots[0, block], rows[0, block]] += held[block].astype(FULL)
+    for slot in range(total.shape[0]):
+        for row in range(total.shape[1]):
+            place = (pl.ds(slot * quarter, quarter), pl.ds(row * width, width))
+            value = total[slot, row]
+            rounded = value.astype(LOW)
+            high[place] = rounded
+            low[place] = (value - rounded.astype(FULL)).astype(LOW)
+
+
+def forward_kernel(owners, operators, *refs):
+    columns = refs[:owners]
+    dense = refs[owners : owners + operators]
+    *partials, source, product = refs[owners + operators :]
+    quarters, quarter, hidden = product.shape
+    width = quarters * quarter
+    for turn in range(owners):
+        source[partner("node", turn)] = columns[turn][...]
+    vectors = source[...].reshape(-1, hidden)
+    for row in range(partials[0].shape[0]):
+        summed = sum(
+            lax.dot_general(
+                vectors,
+                part[:, row * width : (row + 1) * width],
+                (((0,), (0,)), ((), ())),
+                preferred_element_type=FULL,
+            )
+            for part in dense
+        )
+        product[...] = summed.T.reshape(product.shape)
+        for turn, partial in enumerate(partials):
+            partial[row] = product[partner("edge", turn)].astype(partial.dtype)
+
+
+def adjoint_kernel(owners, operators, *refs):
+    quarters = len(refs) - operators - owners - 2
+    arrived = refs[:quarters]
+    dense = refs[quarters : quarters + operators]
+    *sends, source, product = refs[quarters + operators :]
+    for turn in range(quarters):
+        source[:, partner("edge", turn)] = arrived[turn][...]
+    vectors = source[...].reshape(-1, source.shape[-1])
+    product[...] = sum(
+        jnp.dot(part[...], vectors, preferred_element_type=FULL) for part in dense
+    ).reshape(product.shape)
+    for turn, send in enumerate(sends):
+        send[...] = product[partner("node", turn)].astype(send.dtype)
+
+
+def state_of(arrived, teleport):
+    summed = arrived[0][...]
+    for part in arrived[1:]:
+        summed += part[...].astype(FULL)
+    return 0.9 * summed + 0.1 * teleport[...]
+
+
+def next_state_kernel(quarters, table, teleport, *refs):
+    arrived = refs[:quarters]
+    *sends, state = refs[quarters:]
+    state[...] = state_of(arrived, teleport)
+    for turn, send in enumerate(sends):
+        for slot in range(CAP):
+            send[slot] = state[requested(table, partner("node", turn), slot)].astype(LOW)
+
+
+def last_state_kernel(teleport, *refs):
+    *arrived, state = refs
+    state[...] = state_of(arrived, teleport)
+
+
+def gather_adjoint(table, arrived, summed):
+    summed[...] = jnp.zeros_like(summed)
+    for turn, part in enumerate(arrived):
+        for slot in range(CAP):
+            own = requested(table, partner("node", turn), slot)
+            summed[own] += part[slot].astype(FULL)
+
+
+def next_adjoint_kernel(table, cotangent, *refs):
+    *arrived, gradient, rounded, summed = refs
+    gather_adjoint(table, arrived, summed)
+    adjoint = 0.9 * summed[...]
+    gradient[...] = 0.1 * cotangent[...] + 0.1 * adjoint
+    rounded[...] = adjoint.astype(LOW)
+
+
+def last_adjoint_kernel(table, gradient_in, *refs):
+    *arrived, gradient, summed = refs
+    gather_adjoint(table, arrived, summed)
+    gradient[...] = gradient_in[...] + 0.9 * summed[...]
+
+
+def per_device_dense(teleport, cotangent, fetch_table, block_row, block_slot, values):
+    row_count, hidden = teleport.shape
+    _, block_count, quarter, width = values.shape
+    count = row_count // quarter
+    quarters = lax.axis_size("edge")
+    owners = lax.axis_size("node")
+    shape = (count, quarter, hidden)
+    pair_shape = (CAP, quarter, hidden)
+    slot_total = owners * CAP
+    teleport = teleport.reshape(shape)
+    cotangent = cotangent.reshape(shape)
+
+    def call(kernel, operands, places, outs, scratch, mebibytes=8, cost=None):
+        return pl.pallas_call(
+            kernel,
+            out_shape=[jax.ShapeDtypeStruct(*out) for out in outs],
+            in_specs=places,
+            out_specs=[VMEM] * len(outs),
+            scratch_shapes=scratch,
+            compiler_params=params(mebibytes),
+            cost_estimate=cost,
+        )(*operands)
+
+    def exchange(arrays, axis):
+        size = lax.axis_size(axis)
+        return [arrays[0]] + [
+            lax.ppermute(arrays[turn], axis, [(place, place ^ turn) for place in range(size)])
+            for turn in range(1, size)
+        ]
+
+    *sends, rounded = call(
+        start_kernel,
+        (fetch_table, teleport, cotangent),
+        [HBM] * 3,
+        [(pair_shape, LOW)] * owners + [(shape, LOW)],
+        [
+            pltpu.SMEM(fetch_table.shape, fetch_table.dtype),
+            pltpu.VMEM(shape, FULL),
+            pltpu.VMEM(shape, FULL),
+            pltpu.SemaphoreType.DMA((3,)),
+        ],
+    )
+    dense_shape = (slot_total * quarter, count * width)
+    parts = next(size for size in (12, 8, 4, 2, 1) if block_count % size == 0)
+    high, low = call(
+        build_kernel,
+        (block_row, block_slot, values),
+        [SMEM, SMEM, HBM],
+        [(dense_shape, LOW)] * 2,
+        [
+            pltpu.VMEM((block_count, quarter, width), LOW),
+            pltpu.VMEM((slot_total, count, quarter, width), FULL),
+            pltpu.SemaphoreType.DMA((parts,)),
+        ],
+        28,
+        pl.CostEstimate(flops=0, bytes_accessed=values.size * 2, transcendentals=0),
+    )
+
+    gradient = cotangent
+    for step in range(STEPS):
+        last = step + 1 == STEPS
+        dense = (high,) if last else (high, low)
+        cost = pl.CostEstimate(
+            flops=2 * len(dense) * high.size * hidden,
+            bytes_accessed=len(dense) * high.size * 2,
+            transcendentals=0,
+        )
+        columns = exchange(sends, "node")
+        arrived = exchange([rounded] * quarters, "edge")
+        partials = call(
+            functools.partial(forward_kernel, owners, len(dense)),
+            (*columns, *dense),
+            [VMEM] * (owners + len(dense)),
+            [(shape, FULL)] + [(shape, LOW)] * (quarters - 1),
+            [
+                pltpu.VMEM((owners,) + pair_shape, LOW),
+                pltpu.VMEM((quarters, quarter, hidden), FULL),
+            ],
+            cost=cost,
+        )
+        transposed = call(
+            functools.partial(adjoint_kernel, owners, len(dense)),
+            (*arrived, *dense),
+            [VMEM] * (quarters + len(dense)),
+            [(pair_shape, FULL)] + [(pair_shape, LOW)] * (owners - 1),
+            [
+                pltpu.VMEM((count, quarters, quarter, hidden), LOW),
+                pltpu.VMEM((owners,) + pair_shape, FULL),
+            ],
+            cost=cost,
+        )
+        partials = exchange(partials, "edge")
+        transposed = exchange(transposed, "node")
+        total = [pltpu.VMEM(shape, FULL)]
+        if not last:
+            sends = call(
+                functools.partial(next_state_kernel, quarters),
+                (fetch_table, teleport, *partials),
+                [SMEM] + [VMEM] * (1 + quarters),
+                [(pair_shape, LOW)] * owners,
+                total,
+            )
+            gradient, rounded = call(
+                next_adjoint_kernel,
+                (fetch_table, gradient, *transposed),
+                [SMEM] + [VMEM] * (1 + owners),
+                [(shape, FULL), (shape, LOW)],
+                total,
+            )
+        else:
+            (state,) = call(
+                last_state_kernel,
+                (teleport, *partials),
+                [VMEM] * (1 + quarters),
+                [(shape, FULL)],
+                [],
+            )
+            (gradient,) = call(
+                last_adjoint_kernel,
+                (fetch_table, gradient, *transposed),
+                [SMEM] + [VMEM] * (1 + owners),
+                [(shape, FULL)],
+                total,
+            )
+    return state.reshape(row_count, hidden), gradient.reshape(row_count, hidden)
+
+
+def per_device_blocks(teleport, cotangent, fetch_table, block_row, block_slot, values):
     row_count, hidden = teleport.shape
     quarter = values.shape[2]
     block_count = values.shape[1]
@@ -99,6 +378,15 @@
     return (current, gradient)
 
 
+def per_device(teleport, cotangent, fetch_table, block_row, block_slot, values):
+    arguments = (teleport, cotangent, fetch_table, block_row, block_slot, values)
+    row_count = teleport.shape[0]
+    dense_bytes = fetch_table.shape[1] * row_count * values.shape[3] * 2
+    if dense_bytes <= DENSE_BYTES:
+        return per_device_dense(*arguments)
+    return per_device_blocks(*arguments)
+
+
 def solution(mesh):
     placed = (
         P(("node", "edge"), None),

time: 365 us -> 93.9 us (0.26); the launches traced: 360 us -> 93.6 us
  other arithmetic: 142 us -> 0 us
  matrix products: 74.3 us -> 0 us
  waiting for transfers between devices: 76 us -> 15.9 us
  starting transfers between devices: 9.61 us -> 55.2 us
  local copies, waits for them, and re-layouts: 29.4 us -> 6.74 us
  Pallas kernels: 0 us -> 15 us
  blocking collectives: 13.7 us -> 0 us
  between operations: 13.9 us -> 0.83 us
    scatter-add x48 -> x0, other arithmetic: 118 us -> none  [the longest x24 64.9 us: fold_advance(): return (carried.at[slot_targets].add(product), None)]
    dot_general x50 -> x0, matrix products: 74.3 us -> none  [the longest x24 38.2 us: partial_advance(): jnp.einsum('bcr,bch->brh', weights, sources, preferred_element_type=jnp.f...]
    ppermute x0 -> x40, starting transfers between devices: none -> 55.2 us  [exchange(): lax.ppermute(arrays[turn], axis, [(place, place ^ turn) for place in rang...]
    all_gather x2 -> x0, waiting for transfers between devices: 30.8 us -> none  [per_device(): everything = lax.all_gather(propagate_rounded, 'node', axis=0, tiled=True)]
    all_to_all x2 -> x0, waiting for transfers between devices: 29.2 us -> none  [per_device(): lax.all_to_all(partial_value, 'node', split_axis=0, concat_axis=0, tiled=...]
    gather x27 -> x0, local copies, waits for them, and re-layouts: 23.4 us -> none  [the longest x24 18 us: fold_advance(): sources = jnp.take(arrived_rows, targets, axis=0)]
    ppermute x0 -> x40, waiting for transfers between devices: none -> 15.9 us  [exchange(): lax.ppermute(arrays[turn], axis, [(place, place ^ turn) for place in rang...]
    reduce_scatter x2 -> x0, waiting for transfers between devices: 15.9 us -> none  [per_device(): lax.psum_scatter(partial_rows(lax.axis_size('edge') * row_count), 'edge',...]
  transfers between devices with their start and end apart: 6 -> 40, of which waited for: 4 -> 9; matrix products, arithmetic and copies ran while one was open for 38% -> 0% of each run, Pallas kernels for 0% -> 14%
where the time goes in v1:
time: 93.9 us; the launch traced here: 93.6 us
  starting transfers between devices  55.2 us (59%)
  waiting for transfers between devices  15.9 us (17%)
  Pallas kernels  15 us (16%)
  local copies, waits for them, and re-layouts  6.74 us (7%)
    ppermute x40, starting transfers between devices, exchange(): lax.ppermute(arrays[turn], axis, [(place, place ^ turn) for place in rang...  55.2 us
    ppermute x40, waiting for transfers between devices, exchange(): lax.ppermute(arrays[turn], axis, [(place, place ^ turn) for place in rang...  15.9 us
    pallas_call x10, Pallas kernels, call(): pl.pallas_call(kernel, out_shape=[jax.ShapeDtypeStruct(*out) for out in o...  15 us
    unnamed x18, local copies, waits for them, and re-layouts  6.74 us
  transfers between devices with their start and end apart: 40, of which 9 were waited for; matrix products, arithmetic and copies ran while one was open for 0% of the time, Pallas kernels for 14%

profile of v1, /device:TPU:0, one launch (start us, length us, event | category | flops | bytes accessed | tf_op | source)
XLA Modules:
  0.0 93.6 jit_solution(17234314212936040778)
XLA Ops:
  3.9 3.0 %collective-permute-start = (bf16[2,64,128]{2,1,0:T(8,128)(2,1)S(1)}, bf16[2,64,128]{2,1,0:T(8,128)(2,1)S(1)}, u32[]{:S(2)}, u32[]{:S(2)}) collective-permute-start(bf16[2,64,128]{2,1,0:T(8,128)(2,1)S(1)} %get-tuple-element.48), channel_id=1, source_target_pairs={{0,4},{4,0},{8,12},{12,8},{16,20},{20,16},{24,28},{28,24},{1,5},{5... | collective-permute-start | bytes 98312 | tf_op jit(solution)/shard_map/ppermute | solution.py:188
  6.9 1.6 %collective-permute-start.1 = (bf16[2,64,128]{2,1,0:T(8,128)(2,1)S(1)}, bf16[2,64,128]{2,1,0:T(8,128)(2,1)S(1)}, u32[]{:S(2)}, u32[]{:S(2)}) collective-permute-start(bf16[2,64,128]{2,1,0:T(8,128)(2,1)S(1)} %get-tuple-element.49), channel_id=1, source_target_pairs={{0,8},{4,12},{8,0},{12,4},{16,24},{20,28},{24,16},{28,20},{1,9},{5... | collective-permute-start | bytes 98312 | tf_op jit(solution)/shard_map/ppermute | solution.py:188
  8.5 3.0 %collective-permute-start.3 = (bf16[2,64,128]{2,1,0:T(8,128)(2,1)S(1)}, bf16[2,64,128]{2,1,0:T(8,128)(2,1)S(1)}, u32[]{:S(2)}, u32[]{:S(2)}) collective-permute-start(bf16[2,64,128]{2,1,0:T(8,128)(2,1)S(1)} %get-tuple-element.51), channel_id=1, source_target_pairs={{0,16},{4,20},{8,24},{12,28},{16,0},{20,4},{24,8},{28,12},{1,17},{... | collective-permute-start | bytes 98312 | tf_op jit(solution)/shard_map/ppermute | solution.py:188
  12.8 3.6 %collective-permute-start.5 = (bf16[2,64,128]{2,1,0:T(8,128)(2,1)S(1)}, bf16[2,64,128]{2,1,0:T(8,128)(2,1)S(1)}, u32[]{:S(2)}, u32[]{:S(2)}) collective-permute-start(bf16[2,64,128]{2,1,0:T(8,128)(2,1)S(1)} %get-tuple-element.53), channel_id=1, source_target_pairs={{0,24},{4,28},{8,16},{12,20},{16,8},{20,12},{24,0},{28,4},{1,25},{... | collective-permute-start | bytes 98312 | tf_op jit(solution)/shard_map/ppermute | solution.py:188
  16.5 1.7 %collective-permute-start.21 = (bf16[8,64,128]{2,1,0:T(8,128)(2,1)S(1)}, bf16[8,64,128]{2,1,0:T(8,128)(2,1)S(1)}, u32[]{:S(2)}, u32[]{:S(2)}) collective-permute-start(bf16[8,64,128]{2,1,0:T(8,128)(2,1)S(1)} %get-tuple-element.73.refs_0_), channel_id=1, source_target_pairs={{0,2},{1,3},{2,0},{3,1},{4,6},{5,7},{6,4},{7,5},{8,10},{9,11},{10,... | collective-permute-start | bytes 393224 | tf_op jit(solution)/shard_map/ppermute | solution.py:188
  18.3 2.8 %copy-done = bf16[1,192,64,256]{3,2,1,0:T(8,128)(2,1)S(1)} copy-done((bf16[1,192,64,256]{3,2,1,0:T(8,128)(2,1)S(1)}, bf16[1,192,64,256]{3,2,1,0:T(8,128)(2,1)}, u32[]{:S(2)}) %copy-start) | copy-done | bytes 6291480
  22.5 4.3 %shard_map.78 = (bf16[1024,2048]{1,0:T(8,128)(2,1)S(1)}, bf16[1024,2048]{1,0:T(8,128)(2,1)S(1)}) custom-call(s32[1,192]{1,0:T(1,128)S(1)} %copy-done.7, s32[1,192]{1,0:T(1,128)S(1)} %copy-done.8, bf16[1,192,64,256]{3,2,1,0:T(8,128)(2,1)S(1)} %copy-done), custom_call_target="tpu_custom_call" | custom-call | bytes 6291456 | tf_op jit(solution)/shard_map/pallas_call | solution.py:175
  26.8 1.5 %shard_map.79 = (f32[8,64,128]{2,1,0:T(8,128)S(1)}, bf16[8,64,128]{2,1,0:T(8,128)(2,1)S(1)}, bf16[8,64,128]{2,1,0:T(8,128)(2,1)S(1)}, bf16[8,64,128]{2,1,0:T(8,128)(2,1)S(1)}) custom-call(bf16[2,64,128]{2,1,0:T(8,128)(2,1)S(1)} %get-tuple-element.47.refs_0_, bf16[2,64,128]{2,1,0:T(8,128)(2,1)S(1)} %collective-permute-done.refs_1_, ...), custom_call_target="tpu_custom_call" | custom-call | flops 1073741824 | bytes 8388608 | tf_op jit(solution)/shard_map/pallas_call | solution.py:175
  29.2 2.4 %shard_map.83 = (f32[2,64,128]{2,1,0:T(8,128)S(1)}, bf16[2,64,128]{2,1,0:T(8,128)(2,1)S(1)}, bf16[2,64,128]{2,1,0:T(8,128)(2,1)S(1)}, bf16[2,64,128]{2,1,0:T(8,1...) custom-call(bf16[8,64,128]{2,1,0:T(8,128)(2,1)S(1)} %get-tuple-eleme, ...), custom_call_target="tpu_custom_call" | custom-call | flops 1073741824 | bytes 8388608 | tf_op jit(solution)/shard_map/pallas_call | solution.py:175
  33.0 1.6 %collective-permute-start.24 = (bf16[2,64,128]{2,1,0:T(8,128)(2,1)S(1)}, bf16[2,64,128]{2,1,0:T(8,128)(2,1)S(1)}, u32[]{:S(2)}, u32[]{:S(2)}) collective-permute-start(bf16[2,64,128]{2,1,0:T(8,128)(2,1)S(1)} %get-tuple-element.76), channel_id=1, source_target_pairs={{0,8},{4,12},{8,0},{12,4},{16,24},{20,28},{24,16},{28,20},{1,9},{5... | collective-permute-start | bytes 98312 | tf_op jit(solution)/shard_map/ppermute | solution.py:188
  35.2 1.9 %collective-permute-start.26 = (bf16[2,64,128]{2,1,0:T(8,128)(2,1)S(1)}, bf16[2,64,128]{2,1,0:T(8,128)(2,1)S(1)}, u32[]{:S(2)}, u32[]{:S(2)}) collective-permute-start(bf16[2,64,128]{2,1,0:T(8,128)(2,1)S(1)} %get-tuple-element.78), channel_id=1, source_target_pairs={{0,16},{4,20},{8,24},{12,28},{16,0},{20,4},{24,8},{28,12},{1,17},{... | collective-permute-start | bytes 98312 | tf_op jit(solution)/shard_map/ppermute | solution.py:188
  37.1 1.7 %collective-permute-start.27 = (bf16[2,64,128]{2,1,0:T(8,128)(2,1)S(1)}, bf16[2,64,128]{2,1,0:T(8,128)(2,1)S(1)}, u32[]{:S(2)}, u32[]{:S(2)}) collective-permute-start(bf16[2,64,128]{2,1,0:T(8,128)(2,1)S(1)} %get-tuple-element.79), channel_id=1, source_target_pairs={{0,20},{4,16},{8,28},{12,24},{16,4},{20,0},{24,12},{28,8},{1,21},{... | collective-permute-start | bytes 98312 | tf_op jit(solution)/shard_map/ppermute | solution.py:188
  40.3 3.7 %collective-permute-start.28 = (bf16[2,64,128]{2,1,0:T(8,128)(2,1)S(1)}, bf16[2,64,128]{2,1,0:T(8,128)(2,1)S(1)}, u32[]{:S(2)}, u32[]{:S(2)}) collective-permute-start(bf16[2,64,128]{2,1,0:T(8,128)(2,1)S(1)} %get-tuple-element.80), channel_id=1, source_target_pairs={{0,24},{4,28},{8,16},{12,20},{16,8},{20,12},{24,0},{28,4},{1,25},{... | collective-permute-start | bytes 98312 | tf_op jit(solution)/shard_map/ppermute | solution.py:188
  44.0 1.8 %collective-permute-start.29 = (bf16[2,64,128]{2,1,0:T(8,128)(2,1)S(1)}, bf16[2,64,128]{2,1,0:T(8,128)(2,1)S(1)}, u32[]{:S(2)}, u32[]{:S(2)}) collective-permute-start(bf16[2,64,128]{2,1,0:T(8,128)(2,1)S(1)} %get-tuple-element.81), channel_id=1, source_target_pairs={{0,28},{4,24},{8,20},{12,16},{16,12},{20,8},{24,4},{28,0},{1,29},{... | collective-permute-start | bytes 98312 | tf_op jit(solution)/shard_map/ppermute | solution.py:188
  46.1 4.5 %collective-permute-done.29.refs_7_ = bf16[2,64,128]{2,1,0:T(8,128)(2,1)S(1)} collective-permute-done((bf16[2,64,128]{2,1,0:T(8,128)(2,1)S(1)}, bf16[2,64,128]{2,1,0:T(8,128)(2,1)S(1)}, u32[]{:S(2)}, u32[]{:S(2)}) %collective-permute-start.29) | collective-permute-done | bytes 32800 | tf_op jit(solution)/shard_map/ppermute | solution.py:188
  55.2 2.9 %collective-permute-done.10.refs_1_ = bf16[2,64,128]{2,1,0:T(8,128)(2,1)S(1)} collective-permute-done((bf16[2,64,128]{2,1,0:T(8,128)(2,1)S(1)}, bf16[2,64,128]{2,1,0:T(8,128)(2,1)S(1)}, u32[]{:S(2)}, u32[]{:S(2)}) %collective-permute-start.10) | collective-permute-done | bytes 32800 | tf_op jit(solution)/shard_map/ppermute | solution.py:188
  60.5 2.0 %collective-permute-start.14 = (bf16[2,64,128]{2,1,0:T(8,128)(2,1)S(1)}, bf16[2,64,128]{2,1,0:T(8,128)(2,1)S(1)}, u32[]{:S(2)}, u32[]{:S(2)}) collective-permute-start(bf16[2,64,128]{2,1,0:T(8,128)(2,1)S(1)} %get-tuple-element.66), channel_id=1, source_target_pairs={{0,20},{4,16},{8,28},{12,24},{16,4},{20,0},{24,12},{28,8},{1,21},{... | collective-permute-start | bytes 98312 | tf_op jit(solution)/shard_map/ppermute | solution.py:188
  63.5 3.2 %collective-permute-start.16 = (bf16[2,64,128]{2,1,0:T(8,128)(2,1)S(1)}, bf16[2,64,128]{2,1,0:T(8,128)(2,1)S(1)}, u32[]{:S(2)}, u32[]{:S(2)}) collective-permute-start(bf16[2,64,128]{2,1,0:T(8,128)(2,1)S(1)} %get-tuple-element.68), channel_id=1, source_target_pairs={{0,28},{4,24},{8,20},{12,16},{16,12},{20,8},{24,4},{28,0},{1,29},{... | collective-permute-start | bytes 98312 | tf_op jit(solution)/shard_map/ppermute | solution.py:188
  71.2 1.5 %collective-permute-start.18 = (bf16[8,64,128]{2,1,0:T(8,128)(2,1)S(1)}, bf16[8,64,128]{2,1,0:T(8,128)(2,1)S(1)}, u32[]{:S(2)}, u32[]{:S(2)}) collective-permute-start(bf16[8,64,128]{2,1,0:T(8,128)(2,1)S(1)} %get-tuple-element.71), channel_id=1, source_target_pairs={{0,2},{1,3},{2,0},{3,1},{4,6},{5,7},{6,4},{7,5},{8,10},{9,11},{10,... | collective-permute-start | bytes 393224 | tf_op jit(solution)/shard_map/ppermute | solution.py:188
  73.0 2.8 %collective-permute-start.35 = (bf16[2,64,128]{2,1,0:T(8,128)(2,1)S(1)}, bf16[2,64,128]{2,1,0:T(8,128)(2,1)S(1)}, u32[]{:S(2)}, u32[]{:S(2)}) collective-permute-start(bf16[2,64,128]{2,1,0:T(8,128)(2,1)S(1)} %get-tuple-element.87), channel_id=1, source_target_pairs={{0,12},{4,8},{8,4},{12,0},{16,28},{20,24},{24,20},{28,16},{1,13},{... | collective-permute-start | bytes 98312 | tf_op jit(solution)/shard_map/ppermute | solution.py:188
  78.3 3.7 %collective-permute-start.37 = (bf16[2,64,128]{2,1,0:T(8,128)(2,1)S(1)}, bf16[2,64,128]{2,1,0:T(8,128)(2,1)S(1)}, u32[]{:S(2)}, u32[]{:S(2)}) collective-permute-start(bf16[2,64,128]{2,1,0:T(8,128)(2,1)S(1)} %get-tuple-element.89), channel_id=1, source_target_pairs={{0,20},{4,16},{8,28},{12,24},{16,4},{20,0},{24,12},{28,8},{1,21},{... | collective-permute-start | bytes 98312 | tf_op jit(solution)/shard_map/ppermute | solution.py:188
  82.5 2.2 %collective-permute-start.38 = (bf16[2,64,128]{2,1,0:T(8,128)(2,1)S(1)}, bf16[2,64,128]{2,1,0:T(8,128)(2,1)S(1)}, u32[]{:S(2)}, u32[]{:S(2)}) collective-permute-start(bf16[2,64,128]{2,1,0:T(8,128)(2,1)S(1)} %get-tuple-element.90), channel_id=1, source_target_pairs={{0,24},{4,28},{8,16},{12,20},{16,8},{20,12},{24,0},{28,4},{1,25},{... | collective-permute-start | bytes 98312 | tf_op jit(solution)/shard_map/ppermute | solution.py:188
  84.7 2.2 %collective-permute-start.39 = (bf16[2,64,128]{2,1,0:T(8,128)(2,1)S(1)}, bf16[2,64,128]{2,1,0:T(8,128)(2,1)S(1)}, u32[]{:S(2)}, u32[]{:S(2)}) collective-permute-start(bf16[2,64,128]{2,1,0:T(8,128)(2,1)S(1)} %get-tuple-element.91), channel_id=1, source_target_pairs={{0,28},{4,24},{8,20},{12,16},{16,12},{20,8},{24,4},{28,0},{1,29},{... | collective-permute-start | bytes 98312 | tf_op jit(solution)/shard_map/ppermute | solution.py:188
  88.3 3.0 %collective-permute-done.39.refs_7_ = bf16[2,64,128]{2,1,0:T(8,128)(2,1)S(1)} collective-permute-done((bf16[2,64,128]{2,1,0:T(8,128)(2,1)S(1)}, bf16[2,64,128]{2,1,0:T(8,128)(2,1)S(1)}, u32[]{:S(2)}, u32[]{:S(2)}) %collective-permute-start.39) | collective-permute-done | bytes 32800 | tf_op jit(solution)/shard_map/ppermute | solution.py:188
  (84 shorter events, 30.1 us)
Async XLA Ops:
  3.9 8.9 %collective-permute-start = (bf16[2,64,128]{2,1,0:T(8,128)(2,1)S(1)}, bf16[2,64,128]{2,1,0:T(8,128)(2,1)S(1)}, u32[]{:S(2)}, u32[]{:S(2)}) collective-permute-start(bf16[2,64,128]{2,1,0:T(8,128)(2,1)S(1)} %get-tuple-element.48), channel_id=1, source_target_pairs={{0,4},{4,0},{8,12},{12,8},{16,20},{20,16},{24,28},{28,24},{1,5},{5... | collective-permute-start | bytes 98312 | tf_op jit(solution)/shard_map/ppermute | solution.py:188
  6.9 9.5 %collective-permute-start.1 = (bf16[2,64,128]{2,1,0:T(8,128)(2,1)S(1)}, bf16[2,64,128]{2,1,0:T(8,128)(2,1)S(1)}, u32[]{:S(2)}, u32[]{:S(2)}) collective-permute-start(bf16[2,64,128]{2,1,0:T(8,128)(2,1)S(1)} %get-tuple-element.49), channel_id=1, source_target_pairs={{0,8},{4,12},{8,0},{12,4},{16,24},{20,28},{24,16},{28,20},{1,9},{5... | collective-permute-start | bytes 98312 | tf_op jit(solution)/shard_map/ppermute | solution.py:188
  8.5 7.9 %collective-permute-start.2 = (bf16[2,64,128]{2,1,0:T(8,128)(2,1)S(1)}, bf16[2,64,128]{2,1,0:T(8,128)(2,1)S(1)}, u32[]{:S(2)}, u32[]{:S(2)}) collective-permute-start(bf16[2,64,128]{2,1,0:T(8,128)(2,1)S(1)} %get-tuple-element.50), channel_id=1, source_target_pairs={{0,12},{4,8},{8,4},{12,0},{16,28},{20,24},{24,20},{28,16},{1,13},{... | collective-permute-start | bytes 98312 | tf_op jit(solution)/shard_map/ppermute | solution.py:188
  8.5 8.0 %collective-permute-start.3 = (bf16[2,64,128]{2,1,0:T(8,128)(2,1)S(1)}, bf16[2,64,128]{2,1,0:T(8,128)(2,1)S(1)}, u32[]{:S(2)}, u32[]{:S(2)}) collective-permute-start(bf16[2,64,128]{2,1,0:T(8,128)(2,1)S(1)} %get-tuple-element.51), channel_id=1, source_target_pairs={{0,16},{4,20},{8,24},{12,28},{16,0},{20,4},{24,8},{28,12},{1,17},{... | collective-permute-start | bytes 98312 | tf_op jit(solution)/shard_map/ppermute | solution.py:188
  11.5 6.7 %collective-permute-start.4 = (bf16[2,64,128]{2,1,0:T(8,128)(2,1)S(1)}, bf16[2,64,128]{2,1,0:T(8,128)(2,1)S(1)}, u32[]{:S(2)}, u32[]{:S(2)}) collective-permute-start(bf16[2,64,128]{2,1,0:T(8,128)(2,1)S(1)} %get-tuple-element.52), channel_id=1, source_target_pairs={{0,20},{4,16},{8,28},{12,24},{16,4},{20,0},{24,12},{28,8},{1,21},{... | collective-permute-start | bytes 98312 | tf_op jit(solution)/shard_map/ppermute | solution.py:188
  12.8 14.0 %collective-permute-start.5 = (bf16[2,64,128]{2,1,0:T(8,128)(2,1)S(1)}, bf16[2,64,128]{2,1,0:T(8,128)(2,1)S(1)}, u32[]{:S(2)}, u32[]{:S(2)}) collective-permute-start(bf16[2,64,128]{2,1,0:T(8,128)(2,1)S(1)} %get-tuple-element.53), channel_id=1, source_target_pairs={{0,24},{4,28},{8,16},{12,20},{16,8},{20,12},{24,0},{28,4},{1,25},{... | collective-permute-start | bytes 98312 | tf_op jit(solution)/shard_map/ppermute | solution.py:188
  16.4 10.4 %collective-permute-start.6 = (bf16[2,64,128]{2,1,0:T(8,128)(2,1)S(1)}, bf16[2,64,128]{2,1,0:T(8,128)(2,1)S(1)}, u32[]{:S(2)}, u32[]{:S(2)}) collective-permute-start(bf16[2,64,128]{2,1,0:T(8,128)(2,1)S(1)} %get-tuple-element.54), channel_id=1, source_target_pairs={{0,28},{4,24},{8,20},{12,16},{16,12},{20,8},{24,4},{28,0},{1,29},{... | collective-permute-start | bytes 98312 | tf_op jit(solution)/shard_map/ppermute | solution.py:188
  16.4 12.8 %collective-permute-start.20 = (bf16[8,64,128]{2,1,0:T(8,128)(2,1)S(1)}, bf16[8,64,128]{2,1,0:T(8,128)(2,1)S(1)}, u32[]{:S(2)}, u32[]{:S(2)}) collective-permute-start(bf16[8,64,128]{2,1,0:T(8,128)(2,1)S(1)} %get-tuple-element.73.refs_0_), channel_id=1, source_target_pairs={{0,1},{1,0},{2,3},{3,2},{4,5},{5,4},{6,7},{7,6},{8,9},{9,8},{10,11... | collective-permute-start | bytes 393224 | tf_op jit(solution)/shard_map/ppermute | solution.py:188
  16.5 12.7 %collective-permute-start.21 = (bf16[8,64,128]{2,1,0:T(8,128)(2,1)S(1)}, bf16[8,64,128]{2,1,0:T(8,128)(2,1)S(1)}, u32[]{:S(2)}, u32[]{:S(2)}) collective-permute-start(bf16[8,64,128]{2,1,0:T(8,128)(2,1)S(1)} %get-tuple-element.73.refs_0_), channel_id=1, source_target_pairs={{0,2},{1,3},{2,0},{3,1},{4,6},{5,7},{6,4},{7,5},{8,10},{9,11},{10,... | collective-permute-start | bytes 393224 | tf_op jit(solution)/shard_map/ppermute | solution.py:188
  18.2 11.0 %collective-permute-start.22 = (bf16[8,64,128]{2,1,0:T(8,128)(2,1)S(1)}, bf16[8,64,128]{2,1,0:T(8,128)(2,1)S(1)}, u32[]{:S(2)}, u32[]{:S(2)}) collective-permute-start(bf16[8,64,128]{2,1,0:T(8,128)(2,1)S(1)} %get-tuple-element.73.refs_0_), channel_id=1, source_target_pairs={{0,3},{1,2},{2,1},{3,0},{4,7},{5,6},{6,5},{7,4},{8,11},{9,10},{10,... | collective-permute-start | bytes 393224 | tf_op jit(solution)/shard_map/ppermute | solution.py:188
  28.4 24.3 %collective-permute-start.7 = (bf16[8,64,128]{2,1,0:T(8,128)(2,1)S(1)}, bf16[8,64,128]{2,1,0:T(8,128)(2,1)S(1)}, u32[]{:S(2)}, u32[]{:S(2)}) collective-permute-start(bf16[8,64,128]{2,1,0:T(8,128)(2,1)S(1)} %get-tuple-element.58), channel_id=1, source_target_pairs={{0,1},{1,0},{2,3},{3,2},{4,5},{5,4},{6,7},{7,6},{8,9},{9,8},{10,11... | collective-permute-start | bytes 393224 | tf_op jit(solution)/shard_map/ppermute | solution.py:188
  37.1 6.9 %collective-permute-start.27 = (bf16[2,64,128]{2,1,0:T(8,128)(2,1)S(1)}, bf16[2,64,128]{2,1,0:T(8,128)(2,1)S(1)}, u32[]{:S(2)}, u32[]{:S(2)}) collective-permute-start(bf16[2,64,128]{2,1,0:T(8,128)(2,1)S(1)} %get-tuple-element.79), channel_id=1, source_target_pairs={{0,20},{4,16},{8,28},{12,24},{16,4},{20,0},{24,12},{28,8},{1,21},{... | collective-permute-start | bytes 98312 | tf_op jit(solution)/shard_map/ppermute | solution.py:188
  38.8 14.5 %collective-permute-start.8 = (bf16[8,64,128]{2,1,0:T(8,128)(2,1)S(1)}, bf16[8,64,128]{2,1,0:T(8,128)(2,1)S(1)}, u32[]{:S(2)}, u32[]{:S(2)}) collective-permute-start(bf16[8,64,128]{2,1,0:T(8,128)(2,1)S(1)} %get-tuple-element.59), channel_id=1, source_target_pairs={{0,2},{1,3},{2,0},{3,1},{4,6},{5,7},{6,4},{7,5},{8,10},{9,11},{10,... | collective-permute-start | bytes 393224 | tf_op jit(solution)/shard_map/ppermute | solution.py:188
  40.3 13.1 %collective-permute-start.9 = (bf16[8,64,128]{2,1,0:T(8,128)(2,1)S(1)}, bf16[8,64,128]{2,1,0:T(8,128)(2,1)S(1)}, u32[]{:S(2)}, u32[]{:S(2)}) collective-permute-start(bf16[8,64,128]{2,1,0:T(8,128)(2,1)S(1)} %get-tuple-element.60), channel_id=1, source_target_pairs={{0,3},{1,2},{2,1},{3,0},{4,7},{5,6},{6,5},{7,4},{8,11},{9,10},{10,... | collective-permute-start | bytes 393224 | tf_op jit(solution)/shard_map/ppermute | solution.py:188
  51.4 9.1 %collective-permute-start.30 = (bf16[8,64,128]{2,1,0:T(8,128)(2,1)S(1)}, bf16[8,64,128]{2,1,0:T(8,128)(2,1)S(1)}, u32[]{:S(2)}, u32[]{:S(2)}) collective-permute-start(bf16[8,64,128]{2,1,0:T(8,128)(2,1)S(1)} %get-tuple-element.83.refs_0_), channel_id=1, source_target_pairs={{0,1},{1,0},{2,3},{3,2},{4,5},{5,4},{6,7},{7,6},{8,9},{9,8},{10,11... | collective-permute-start | bytes 393224 | tf_op jit(solution)/shard_map/ppermute | solution.py:188
  51.5 11.0 %collective-permute-start.31 = (bf16[8,64,128]{2,1,0:T(8,128)(2,1)S(1)}, bf16[8,64,128]{2,1,0:T(8,128)(2,1)S(1)}, u32[]{:S(2)}, u32[]{:S(2)}) collective-permute-start(bf16[8,64,128]{2,1,0:T(8,128)(2,1)S(1)} %get-tuple-element.83.refs_0_), channel_id=1, source_target_pairs={{0,2},{1,3},{2,0},{3,1},{4,6},{5,7},{6,4},{7,5},{8,10},{9,11},{10,... | collective-permute-start | bytes 393224 | tf_op jit(solution)/shard_map/ppermute | solution.py:188
  52.7 10.8 %collective-permute-start.32 = (bf16[8,64,128]{2,1,0:T(8,128)(2,1)S(1)}, bf16[8,64,128]{2,1,0:T(8,128)(2,1)S(1)}, u32[]{:S(2)}, u32[]{:S(2)}) collective-permute-start(bf16[8,64,128]{2,1,0:T(8,128)(2,1)S(1)} %get-tuple-element.83.refs_0_), channel_id=1, source_target_pairs={{0,3},{1,2},{2,1},{3,0},{4,7},{5,6},{6,5},{7,4},{8,11},{9,10},{10,... | collective-permute-start | bytes 393224 | tf_op jit(solution)/shard_map/ppermute | solution.py:188
  58.1 10.0 %collective-permute-start.12 = (bf16[2,64,128]{2,1,0:T(8,128)(2,1)S(1)}, bf16[2,64,128]{2,1,0:T(8,128)(2,1)S(1)}, u32[]{:S(2)}, u32[]{:S(2)}) collective-permute-start(bf16[2,64,128]{2,1,0:T(8,128)(2,1)S(1)} %get-tuple-element.64), channel_id=1, source_target_pairs={{0,12},{4,8},{8,4},{12,0},{16,28},{20,24},{24,20},{28,16},{1,13},{... | collective-permute-start | bytes 98312 | tf_op jit(solution)/shard_map/ppermute | solution.py:188
  59.1 10.1 %collective-permute-start.13 = (bf16[2,64,128]{2,1,0:T(8,128)(2,1)S(1)}, bf16[2,64,128]{2,1,0:T(8,128)(2,1)S(1)}, u32[]{:S(2)}, u32[]{:S(2)}) collective-permute-start(bf16[2,64,128]{2,1,0:T(8,128)(2,1)S(1)} %get-tuple-element.65), channel_id=1, source_target_pairs={{0,16},{4,20},{8,24},{12,28},{16,0},{20,4},{24,8},{28,12},{1,17},{... | collective-permute-start | bytes 98312 | tf_op jit(solution)/shard_map/ppermute | solution.py:188
  60.5 8.7 %collective-permute-start.14 = (bf16[2,64,128]{2,1,0:T(8,128)(2,1)S(1)}, bf16[2,64,128]{2,1,0:T(8,128)(2,1)S(1)}, u32[]{:S(2)}, u32[]{:S(2)}) collective-permute-start(bf16[2,64,128]{2,1,0:T(8,128)(2,1)S(1)} %get-tuple-element.66), channel_id=1, source_target_pairs={{0,20},{4,16},{8,28},{12,24},{16,4},{20,0},{24,12},{28,8},{1,21},{... | collective-permute-start | bytes 98312 | tf_op jit(solution)/shard_map/ppermute | solution.py:188
  62.5 6.7 %collective-permute-start.15 = (bf16[2,64,128]{2,1,0:T(8,128)(2,1)S(1)}, bf16[2,64,128]{2,1,0:T(8,128)(2,1)S(1)}, u32[]{:S(2)}, u32[]{:S(2)}) collective-permute-start(bf16[2,64,128]{2,1,0:T(8,128)(2,1)S(1)} %get-tuple-element.67), channel_id=1, source_target_pairs={{0,24},{4,28},{8,16},{12,20},{16,8},{20,12},{24,0},{28,4},{1,25},{... | collective-permute-start | bytes 98312 | tf_op jit(solution)/shard_map/ppermute | solution.py:188
  71.1 21.7 %collective-permute-start.17 = (bf16[8,64,128]{2,1,0:T(8,128)(2,1)S(1)}, bf16[8,64,128]{2,1,0:T(8,128)(2,1)S(1)}, u32[]{:S(2)}, u32[]{:S(2)}) collective-permute-start(bf16[8,64,128]{2,1,0:T(8,128)(2,1)S(1)} %get-tuple-element.70), channel_id=1, source_target_pairs={{0,1},{1,0},{2,3},{3,2},{4,5},{5,4},{6,7},{7,6},{8,9},{9,8},{10,11... | collective-permute-start | bytes 393224 | tf_op jit(solution)/shard_map/ppermute | solution.py:188
  71.2 21.7 %collective-permute-start.18 = (bf16[8,64,128]{2,1,0:T(8,128)(2,1)S(1)}, bf16[8,64,128]{2,1,0:T(8,128)(2,1)S(1)}, u32[]{:S(2)}, u32[]{:S(2)}) collective-permute-start(bf16[8,64,128]{2,1,0:T(8,128)(2,1)S(1)} %get-tuple-element.71), channel_id=1, source_target_pairs={{0,2},{1,3},{2,0},{3,1},{4,6},{5,7},{6,4},{7,5},{8,10},{9,11},{10,... | collective-permute-start | bytes 393224 | tf_op jit(solution)/shard_map/ppermute | solution.py:188
  72.7 20.1 %collective-permute-start.19 = (bf16[8,64,128]{2,1,0:T(8,128)(2,1)S(1)}, bf16[8,64,128]{2,1,0:T(8,128)(2,1)S(1)}, u32[]{:S(2)}, u32[]{:S(2)}) collective-permute-start(bf16[8,64,128]{2,1,0:T(8,128)(2,1)S(1)} %get-tuple-element.72), channel_id=1, source_target_pairs={{0,3},{1,2},{2,1},{3,0},{4,7},{5,6},{6,5},{7,4},{8,11},{9,10},{10,... | collective-permute-start | bytes 393224 | tf_op jit(solution)/shard_map/ppermute | solution.py:188
  (25 other events, 163.9 us)

commit v2 on v1

--- a/solution.py
+++ b/solution.py
@@ -10,6 +10,8 @@
 CAP = 2
 STEPS = 2
 DENSE_BYTES = 8 * 2**20
+START_MEBIBYTES = 60
+BUILD_MEBIBYTES = 40
 LOW = jnp.bfloat16
 FULL = jnp.float32
 
@@ -26,12 +28,13 @@
     return lax.axis_index(axis) ^ turn
 
 
-def requested(table, reader, slot):
-    return jnp.maximum(table[reader, lax.axis_index("node") * CAP + slot], 0)
+def requested(table, slot):
+    column = lax.axis_index("node") * CAP + slot % CAP
+    return jnp.maximum(table[slot // CAP, column], 0)
 
 
 def start_kernel(table, teleport, cotangent, *refs):
-    *sends, rounded, plan, state, adjoint, sems = refs
+    send, rounded, plan, state, adjoint, sems = refs
     copies = [
         pltpu.make_async_copy(source, target, sems.at[index])
         for index, (source, target) in enumerate(
@@ -42,9 +45,8 @@
         copy.start()
     copies[0].wait()
     copies[1].wait()
-    for turn, send in enumerate(sends):
-        for slot in range(CAP):
-            send[slot] = state[requested(plan, partner("node", turn), slot)].astype(LOW)
+    for slot in range(send.shape[0]):
+        send[slot] = state[requested(plan, slot)].astype(LOW)
     copies[2].wait()
     rounded[...] = adjoint[...].astype(LOW)
 
@@ -77,15 +79,12 @@
             low[place] = (value - rounded.astype(FULL)).astype(LOW)
 
 
-def forward_kernel(owners, operators, *refs):
-    columns = refs[:owners]
-    dense = refs[owners : owners + operators]
-    *partials, source, product = refs[owners + operators :]
+def forward_kernel(operators, columns, *refs):
+    dense = refs[:operators]
+    *partials, product = refs[operators:]
     quarters, quarter, hidden = product.shape
     width = quarters * quarter
-    for turn in range(owners):
-        source[partner("node", turn)] = columns[turn][...]
-    vectors = source[...].reshape(-1, hidden)
+    vectors = columns[...].reshape(-1, hidden)
     for row in range(partials[0].shape[0]):
         summed = sum(
             lax.dot_general(
@@ -101,19 +100,13 @@
             partial[row] = product[partner("edge", turn)].astype(partial.dtype)
 
 
-def adjoint_kernel(owners, operators, *refs):
-    quarters = len(refs) - operators - owners - 2
-    arrived = refs[:quarters]
-    dense = refs[quarters : quarters + operators]
-    *sends, source, product = refs[quarters + operators :]
-    for turn in range(quarters):
-        source[:, partner("edge", turn)] = arrived[turn][...]
+def adjoint_kernel(operators, *refs):
+    *arrived, send, source = refs[operators:]
+    for turn, part in enumerate(arrived):
+        source[:, partner("edge", turn)] = part[...]
     vectors = source[...].reshape(-1, source.shape[-1])
-    product[...] = sum(
-        jnp.dot(part[...], vectors, preferred_element_type=FULL) for part in dense
-    ).reshape(product.shape)
-    for turn, send in enumerate(sends):
-        send[...] = product[partner("node", turn)].astype(send.dtype)
+    product = sum(jnp.dot(part[...], vectors, preferred_element_type=FULL) for part in refs[:operators])
+    send[...] = product.reshape(send.shape).astype(LOW)
 
 
 def state_of(arrived, teleport):
@@ -123,13 +116,11 @@
     return 0.9 * summed + 0.1 * teleport[...]
 
 
-def next_state_kernel(quarters, table, teleport, *refs):
-    arrived = refs[:quarters]
-    *sends, state = refs[quarters:]
+def next_state_kernel(table, teleport, *refs):
+    *arrived, send, state = refs
     state[...] = state_of(arrived, teleport)
-    for turn, send in enumerate(sends):
-        for slot in range(CAP):
-            send[slot] = state[requested(table, partner("node", turn), slot)].astype(LOW)
+    for slot in range(send.shape[0]):
+        send[slot] = state[requested(table, slot)].astype(LOW)
 
 
 def last_state_kernel(teleport, *refs):
@@ -139,22 +130,18 @@
 
 def gather_adjoint(table, arrived, summed):
     summed[...] = jnp.zeros_like(summed)
-    for turn, part in enumerate(arrived):
-        for slot in range(CAP):
-            own = requested(table, partner("node", turn), slot)
-            summed[own] += part[slot].astype(FULL)
-
-
-def next_adjoint_kernel(table, cotangent, *refs):
-    *arrived, gradient, rounded, summed = refs
+    for slot in range(arrived.shape[0]):
+        summed[requested(table, slot)] += arrived[slot].astype(FULL)
+
+
+def next_adjoint_kernel(table, cotangent, arrived, gradient, rounded, summed):
     gather_adjoint(table, arrived, summed)
     adjoint = 0.9 * summed[...]
     gradient[...] = 0.1 * cotangent[...] + 0.1 * adjoint
     rounded[...] = adjoint.astype(LOW)
 
 
-def last_adjoint_kernel(table, gradient_in, *refs):
-    *arrived, gradient, summed = refs
+def last_adjoint_kernel(table, gradient_in, arrived, gradient, summed):
     gather_adjoint(table, arrived, summed)
     gradient[...] = gradient_in[...] + 0.9 * summed[...]
 
@@ -164,10 +151,9 @@
     _, block_count, quarter, width = values.shape
     count = row_count // quarter
     quarters = lax.axis_size("edge")
-    owners = lax.axis_size("node")
+    slot_total = fetch_table.shape[1]
     shape = (count, quarter, hidden)
-    pair_shape = (CAP, quarter, hidden)
-    slot_total = owners * CAP
+    slot_shape = (slot_total, quarter, hidden)
     teleport = teleport.reshape(shape)
     cotangent = cotangent.reshape(shape)
 
@@ -182,24 +168,27 @@
             cost_estimate=cost,
         )(*operands)
 
-    def exchange(arrays, axis):
-        size = lax.axis_size(axis)
+    def over_node(array):
+        return lax.all_to_all(array, "node", 0, 0, tiled=True)
+
+    def over_edge(arrays):
         return [arrays[0]] + [
-            lax.ppermute(arrays[turn], axis, [(place, place ^ turn) for place in range(size)])
-            for turn in range(1, size)
+            lax.ppermute(arrays[turn], "edge", [(place, place ^ turn) for place in range(quarters)])
+            for turn in range(1, quarters)
         ]
 
-    *sends, rounded = call(
+    send, rounded = call(
         start_kernel,
         (fetch_table, teleport, cotangent),
         [HBM] * 3,
-        [(pair_shape, LOW)] * owners + [(shape, LOW)],
+        [(slot_shape, LOW), (shape, LOW)],
         [
             pltpu.SMEM(fetch_table.shape, fetch_table.dtype),
             pltpu.VMEM(shape, FULL),
             pltpu.VMEM(shape, FULL),
             pltpu.SemaphoreType.DMA((3,)),
         ],
+        START_MEBIBYTES,
     )
     dense_shape = (slot_total * quarter, count * width)
     parts = next(size for size in (12, 8, 4, 2, 1) if block_count % size == 0)
@@ -213,7 +202,7 @@
             pltpu.VMEM((slot_total, count, quarter, width), FULL),
             pltpu.SemaphoreType.DMA((parts,)),
         ],
-        28,
+        BUILD_MEBIBYTES,
         pl.CostEstimate(flops=0, bytes_accessed=values.size * 2, transcendentals=0),
     )
 
@@ -226,45 +215,41 @@
             bytes_accessed=len(dense) * high.size * 2,
             transcendentals=0,
         )
-        columns = exchange(sends, "node")
-        arrived = exchange([rounded] * quarters, "edge")
+        columns = over_node(send)
+        arrived = over_edge([rounded] * quarters)
+        (transposed,) = call(
+            functools.partial(adjoint_kernel, len(dense)),
+            (*dense, *arrived),
+            [VMEM] * (quarters + len(dense)),
+            [(slot_shape, LOW)],
+            [pltpu.VMEM((count, quarters, quarter, hidden), LOW)],
+            cost=cost,
+        )
+        transposed, columns = lax.optimization_barrier((transposed, columns))
         partials = call(
-            functools.partial(forward_kernel, owners, len(dense)),
-            (*columns, *dense),
-            [VMEM] * (owners + len(dense)),
+            functools.partial(forward_kernel, len(dense)),
+            (columns, *dense),
+            [VMEM] * (1 + len(dense)),
             [(shape, FULL)] + [(shape, LOW)] * (quarters - 1),
-            [
-                pltpu.VMEM((owners,) + pair_shape, LOW),
-                pltpu.VMEM((quarters, quarter, hidden), FULL),
-            ],
+            [pltpu.VMEM((quarters, quarter, hidden), FULL)],
             cost=cost,
         )
-        transposed = call(
-            functools.partial(adjoint_kernel, owners, len(dense)),
-            (*arrived, *dense),
-            [VMEM] * (quarters + len(dense)),
-            [(pair_shape, FULL)] + [(pair_shape, LOW)] * (owners - 1),
-            [
-                pltpu.VMEM((count, quarters, quarter, hidden), LOW),
-                pltpu.VMEM((owners,) + pair_shape, FULL),
-            ],
-            cost=cost,
-        )
-        partials = exchange(partials, "edge")
-        transposed = exchange(transposed, "node")
+        transposed = over_node(transposed)
+        partials = over_edge(partials)
         total = [pltpu.VMEM(shape, FULL)]
         if not last:
-            sends = call(
-                functools.partial(next_state_kernel, quarters),
+            (send,) = call(
+                next_state_kernel,
                 (fetch_table, teleport, *partials),
                 [SMEM] + [VMEM] * (1 + quarters),
-                [(pair_shape, LOW)] * owners,
+                [(slot_shape, LOW)],
                 total,
             )
+            send, transposed = lax.optimization_barrier((send, transposed))
             gradient, rounded = call(
                 next_adjoint_kernel,
-                (fetch_table, gradient, *transposed),
-                [SMEM] + [VMEM] * (1 + owners),
+                (fetch_table, gradient, transposed),
+                [SMEM, VMEM, VMEM],
                 [(shape, FULL), (shape, LOW)],
                 total,
             )
@@ -276,10 +261,11 @@
                 [(shape, FULL)],
                 [],
             )
+            state, transposed = lax.optimization_barrier((state, transposed))
             (gradient,) = call(
                 last_adjoint_kernel,
-                (fetch_table, gradient, *transposed),
-                [SMEM] + [VMEM] * (1 + owners),
+                (fetch_table, gradient, transposed),
+                [SMEM, VMEM, VMEM],
                 [(shape, FULL)],
                 total,
             )

time: 93.9 us -> 87.3 us (0.930)
  starting transfers between devices: 55.2 us -> 32.8 us
  local copies, waits for them, and re-layouts: 6.74 us -> 14.1 us
  waiting for transfers between devices: 15.9 us -> 20.4 us
  Pallas kernels: 15 us -> 18.5 us
    ppermute x40 -> x12, starting transfers between devices: 55.2 us -> 7.65 us  [over_edge(): lax.ppermute(arrays[turn], 'edge', [(place, place ^ turn) for place in ra...]
    all_to_all x0 -> x4, starting transfers between devices: none -> 25.2 us  [over_node(): return lax.all_to_all(array, 'node', 0, 0, tiled=True)]
    unnamed x18 -> x24, local copies, waits for them, and re-layouts: 6.74 us -> 14.1 us
    ppermute x40 -> x12, waiting for transfers between devices: 15.9 us -> 20.4 us  [over_edge(): lax.ppermute(arrays[turn], 'edge', [(place, place ^ turn) for place in ra...]
    pallas_call x10, Pallas kernels: 15 us -> 18.5 us  [call(): pl.pallas_call(kernel, out_shape=[jax.ShapeDtypeStruct(*out) for out in o...]
  transfers between devices with their start and end apart: 40 -> 16, of which waited for: 9 -> 7; matrix products, arithmetic and copies ran while one was open for 0% -> 0% of each run, Pallas kernels for 14% -> 18%
where the time goes in v2:
time: 87.3 us; the launch traced here: 86.6 us
  starting transfers between devices  32.8 us (38%)
  waiting for transfers between devices  20.4 us (23%)
  Pallas kernels  18.5 us (21%)
  local copies, waits for them, and re-layouts  14.1 us (16%)
    all_to_all x4, starting transfers between devices, over_node(): return lax.all_to_all(array, 'node', 0, 0, tiled=True)  25.2 us
    ppermute x12, waiting for transfers between devices, over_edge(): lax.ppermute(arrays[turn], 'edge', [(place, place ^ turn) for place in ra...  20.4 us
    pallas_call x10, Pallas kernels, call(): pl.pallas_call(kernel, out_shape=[jax.ShapeDtypeStruct(*out) for out in o...  18.5 us
    unnamed x24, local copies, waits for them, and re-layouts  14.1 us
    ppermute x12, starting transfers between devices, over_edge(): lax.ppermute(arrays[turn], 'edge', [(place, place ^ turn) for place in ra...  7.65 us
  transfers between devices with their start and end apart: 16, of which 7 were waited for; matrix products, arithmetic and copies ran while one was open for 0% of the time, Pallas kernels for 18%

profile of v2, /device:TPU:0, one launch (start us, length us, event | category | flops | bytes accessed | tf_op | source)
XLA Modules:
  0.0 86.6 jit_solution(10011736772626039762)
XLA Ops:
  0.6 1.8 %shard_map.78 = (bf16[16,64,128]{2,1,0:T(8,128)(2,1)}, bf16[8,64,128]{2,1,0:T(8,128)(2,1)}) custom-call(s32[8,16]{1,0:T(8,128)} %table.7, f32[8,64,128]{2,1,0:T(8,128)} %bitcast.4, f32[8,64,128]{2,1,0:T(8,128)} %bitcast.7), custom_call_target="tpu_custom_call" | custom-call | tf_op jit(solution)/shard_map/pallas_call | solution.py:161
  2.4 7.4 %all-to-all-start = ((bf16[16,64,128]{2,1,0:T(8,128)(2,1)}), bf16[16,64,128]{2,1,0:T(8,128)(2,1)S(1)}, u32[]{:S(2)}, u32[]{:S(2)}) async-start(bf16[16,64,128]{2,1,0:T(8,128)(2,1)} %get-tuple-element.27), calls=%async_computation | async-start | bytes 524288 | tf_op jit(solution)/shard_map/all_to_all | solution.py:172
  13.1 4.7 %shard_map.77 = (bf16[1024,2048]{1,0:T(8,128)(2,1)S(1)}, bf16[1024,2048]{1,0:T(8,128)(2,1)S(1)}) custom-call(s32[1,192]{1,0:T(1,128)S(1)} %copy-done.10, s32[1,192]{1,0:T(1,128)S(1)} %copy-done.11, bf16[1,192,64,256]{3,2,1,0:T(8,128)(2,1)} %weights.1), custom_call_target="tpu_custom_call" | custom-call | bytes 6291456 | tf_op jit(solution)/shard_map/pallas_call | solution.py:161
  18.7 3.1 %shard_map.79 = bf16[16,64,128]{2,1,0:T(8,128)(2,1)} custom-call(bf16[1024,2048]{1,0:T(8,128)(2,1)S(1)} %get-tuple-element.24.refs_0_, bf16[1024,2048]{1,0:T(8,128)(2,1)S(1)} %get-tuple-element.25.refs_1_, bf16[8,64,128]{2,1,0:T(8,128)(2,1)S(1)} %copy-done.8, bf16[8,64,128]{2,1,0:T(8,128)(2,1)S(1)} %collective-permute-done.refs_3_, ...), custom_call_target="tpu_custom_call" | custom-call | flops 1073741824 | bytes 8388608 | tf_op jit(solution)/shard_map/pallas_call | solution.py:161
  21.8 2.0 %copy-done = bf16[1024,2048]{1,0:T(8,128)(2,1)} copy-done((bf16[1024,2048]{1,0:T(8,128)(2,1)}, bf16[1024,2048]{1,0:T(8,128)(2,1)S(1)}, u32[]{:S(2)}) %copy-start) | copy-done | bytes 4194328
  23.7 2.0 %copy-done.4 = bf16[1024,2048]{1,0:T(8,128)(2,1)} copy-done((bf16[1024,2048]{1,0:T(8,128)(2,1)}, bf16[1024,2048]{1,0:T(8,128)(2,1)S(1)}, u32[]{:S(2)}) %copy-start.4) | copy-done | bytes 4194328
  25.8 6.0 %all-to-all-start.1 = ((bf16[16,64,128]{2,1,0:T(8,128)(2,1)}), bf16[16,64,128]{2,1,0:T(8,128)(2,1)S(1)}, u32[]{:S(2)}, u32[]{:S(2)}) async-start(bf16[16,64,128]{2,1,0:T(8,128)(2,1)} %shard_map.79), calls=%async_computation.1 | async-start | bytes 524288 | tf_op jit(solution)/shard_map/all_to_all | solution.py:172
  31.8 2.2 %copy-done.1 = bf16[1024,2048]{1,0:T(8,128)(2,1)S(1)} copy-done((bf16[1024,2048]{1,0:T(8,128)(2,1)S(1)}, bf16[1024,2048]{1,0:T(8,128)(2,1)}, u32[]{:S(2)}) %copy-start.1) | copy-done | bytes 4194328
  33.9 2.2 %copy-done.5 = bf16[1024,2048]{1,0:T(8,128)(2,1)S(1)} copy-done((bf16[1024,2048]{1,0:T(8,128)(2,1)S(1)}, bf16[1024,2048]{1,0:T(8,128)(2,1)}, u32[]{:S(2)}) %copy-start.5) | copy-done | bytes 4194328
  36.1 1.5 %shard_map.80 = (f32[8,64,128]{2,1,0:T(8,128)S(1)}, bf16[8,64,128]{2,1,0:T(8,128)(2,1)S(1)}, bf16[8,64,128]{2,1,0:T(8,128)(2,1)S(1)}, bf16[8,64,128]{2,1,0:T(8,128)(2,1)S(1)}) custom-call(bf16[16,64,128]{2,1,0:T(8,128)(2,1)S(1)} %all-to-all-done.columns, bf16[1024,2048]{1,0:T(8,128)(2,1)S(1)} %copy-done.1, bf16[1024,2048]{1,0:T(8,128)(2,1)S(1)} %copy-done.5), custom_call_target="tpu_custom_call" | custom-call | flops 1073741824 | bytes 8388608 | tf_op jit(solution)/shard_map/pallas_call | solution.py:161
  39.6 4.5 %collective-permute-done.4.refs_2_ = bf16[8,64,128]{2,1,0:T(8,128)(2,1)S(1)} collective-permute-done((bf16[8,64,128]{2,1,0:T(8,128)(2,1)S(1)}, bf16[8,64,128]{2,1,0:T(8,128)(2,1)S(1)}, u32[]{:S(2)}, u32[]{:S(2)}) %collective-permute-start.4) | collective-permute-done | bytes 131104 | tf_op jit(solution)/shard_map/ppermute | solution.py:176
  44.1 1.9 %collective-permute-done.5.refs_3_ = bf16[8,64,128]{2,1,0:T(8,128)(2,1)S(1)} collective-permute-done((bf16[8,64,128]{2,1,0:T(8,128)(2,1)S(1)}, bf16[8,64,128]{2,1,0:T(8,128)(2,1)S(1)}, u32[]{:S(2)}, u32[]{:S(2)}) %collective-permute-start.5) | collective-permute-done | bytes 131104 | tf_op jit(solution)/shard_map/ppermute | solution.py:176
  46.0 1.4 %shard_map.81 = bf16[16,64,128]{2,1,0:T(8,128)(2,1)} custom-call(s32[8,16]{1,0:T(8,128)S(1)} %copy-done.9, f32[8,64,128]{2,1,0:T(8,128)S(1)} %bitcast.5, f32[8,64,128]{2,1,0:T(8,128)S(1)} %get-tuple-element.29.refs_0_, bf16[8,64,128]{2,1,0:T(8,128)(2,1)S(1)} %collective-permute-done.3.refs_1_, bf16[8,64,128]{2,1,0:T(8,128)(2,1)S(1)} %collective-permute-done.4.refs_2_, ...), custom_call_target="tpu_custom_call" | custom-call | tf_op jit(solution)/shard_map/pallas_call | solution.py:161
  47.4 6.0 %all-to-all-start.2 = ((bf16[16,64,128]{2,1,0:T(8,128)(2,1)}), bf16[16,64,128]{2,1,0:T(8,128)(2,1)S(1)}, u32[]{:S(2)}, u32[]{:S(2)}) async-start(bf16[16,64,128]{2,1,0:T(8,128)(2,1)} %shard_map.81), calls=%async_computation.2 | async-start | bytes 524288 | tf_op jit(solution)/shard_map/all_to_all | solution.py:172
  54.6 1.3 %collective-permute-start.7 = (bf16[8,64,128]{2,1,0:T(8,128)(2,1)S(1)}, bf16[8,64,128]{2,1,0:T(8,128)(2,1)S(1)}, u32[]{:S(2)}, u32[]{:S(2)}) collective-permute-start(bf16[8,64,128]{2,1,0:T(8,128)(2,1)S(1)} %get-tuple-element.35.refs_1_), channel_id=1, source_target_pairs={{0,2},{1,3},{2,0},{3,1},{4,6},{5,7},{6,4},{7,5},{8,10},{9,11},{10,... | collective-permute-start | bytes 393224 | tf_op jit(solution)/shard_map/ppermute | solution.py:176
  56.1 3.8 %collective-permute-done.8.refs_4_ = bf16[8,64,128]{2,1,0:T(8,128)(2,1)S(1)} collective-permute-done((bf16[8,64,128]{2,1,0:T(8,128)(2,1)S(1)}, bf16[8,64,128]{2,1,0:T(8,128)(2,1)S(1)}, u32[]{:S(2)}, u32[]{:S(2)}) %collective-permute-start.8) | collective-permute-done | bytes 131104 | tf_op jit(solution)/shard_map/ppermute | solution.py:176
  59.9 3.0 %collective-permute-done.7.refs_3_ = bf16[8,64,128]{2,1,0:T(8,128)(2,1)S(1)} collective-permute-done((bf16[8,64,128]{2,1,0:T(8,128)(2,1)S(1)}, bf16[8,64,128]{2,1,0:T(8,128)(2,1)S(1)}, u32[]{:S(2)}, u32[]{:S(2)}) %collective-permute-start.7) | collective-permute-done | bytes 131104 | tf_op jit(solution)/shard_map/ppermute | solution.py:176
  62.9 2.2 %copy-done.2 = bf16[1024,2048]{1,0:T(8,128)(2,1)S(1)} copy-done((bf16[1024,2048]{1,0:T(8,128)(2,1)S(1)}, bf16[1024,2048]{1,0:T(8,128)(2,1)}, u32[]{:S(2)}) %copy-start.2) | copy-done | bytes 4194328
  65.1 2.0 %shard_map.83 = bf16[16,64,128]{2,1,0:T(8,128)(2,1)} custom-call(bf16[1024,2048]{1,0:T(8,128)(2,1)S(1)} %copy-done.2, bf16[8,64,128]{2,1,0:T(8,128)(2,1)S(1)} %get-tuple-element.35.refs_1_, bf16[8,64,128]{2,1,0:T(8,128)(2,1)S(1)} %collective-permute-done.6.refs_2_, bf16[8,64,128]{2,1,0:T(8,128)(2,1)S(1)} %collective-permute-done.7.refs_3_, ...), custom_call_target="tpu_custom_call" | custom-call | flops 536870912 | bytes 4194304 | tf_op jit(solution)/shard_map/pallas_call | solution.py:161
  67.1 5.8 %all-to-all-start.3 = ((bf16[16,64,128]{2,1,0:T(8,128)(2,1)}), bf16[16,64,128]{2,1,0:T(8,128)(2,1)S(1)}, u32[]{:S(2)}, u32[]{:S(2)}) async-start(bf16[16,64,128]{2,1,0:T(8,128)(2,1)} %shard_map.83), calls=%async_computation.3 | async-start | bytes 524288 | tf_op jit(solution)/shard_map/all_to_all | solution.py:172
  72.9 2.2 %copy-done.3 = bf16[1024,2048]{1,0:T(8,128)(2,1)S(1)} copy-done((bf16[1024,2048]{1,0:T(8,128)(2,1)S(1)}, bf16[1024,2048]{1,0:T(8,128)(2,1)}, u32[]{:S(2)}) %copy-start.3) | copy-done | bytes 4194328
  77.9 4.5 %collective-permute-done.10.refs_2_ = bf16[8,64,128]{2,1,0:T(8,128)(2,1)S(1)} collective-permute-done((bf16[8,64,128]{2,1,0:T(8,128)(2,1)S(1)}, bf16[8,64,128]{2,1,0:T(8,128)(2,1)S(1)}, u32[]{:S(2)}, u32[]{:S(2)}) %collective-permute-start.10) | collective-permute-done | bytes 131104 | tf_op jit(solution)/shard_map/ppermute | solution.py:176
  82.4 1.9 %collective-permute-done.11.refs_3_ = bf16[8,64,128]{2,1,0:T(8,128)(2,1)S(1)} collective-permute-done((bf16[8,64,128]{2,1,0:T(8,128)(2,1)S(1)}, bf16[8,64,128]{2,1,0:T(8,128)(2,1)S(1)}, u32[]{:S(2)}, u32[]{:S(2)}) %collective-permute-start.11) | collective-permute-done | bytes 131104 | tf_op jit(solution)/shard_map/ppermute | solution.py:176
  85.1 1.4 %shard_map.86 = f32[8,64,128]{2,1,0:T(8,128)} custom-call(s32[8,16]{1,0:T(8,128)S(1)} %copy-done.9, f32[8,64,128]{2,1,0:T(8,128)S(1)} %get-tuple-element.44.gradient_in, bf16[16,64,128]{2,1,0:T(8,128)(2,1)S(1)} %all-to-all-done.3.arrived), custom_call_target="tpu_custom_call" | custom-call | tf_op jit(solution)/shard_map/pallas_call | solution.py:161
  (42 shorter events, 11.0 us)
Async XLA Ops:
  2.4 16.2 %copy-start.8 = (bf16[8,64,128]{2,1,0:T(8,128)(2,1)S(1)}, bf16[8,64,128]{2,1,0:T(8,128)(2,1)}, u32[]{:S(2)}) copy-start(bf16[8,64,128]{2,1,0:T(8,128)(2,1)} %get-tuple-element.26.refs_2_) | copy-start | bytes 393220
  2.4 23.3 %all-to-all-start = ((bf16[16,64,128]{2,1,0:T(8,128)(2,1)}), bf16[16,64,128]{2,1,0:T(8,128)(2,1)S(1)}, u32[]{:S(2)}, u32[]{:S(2)}) async-start(bf16[16,64,128]{2,1,0:T(8,128)(2,1)} %get-tuple-element.27), calls=%async_computation | async-start | bytes 524288 | tf_op jit(solution)/shard_map/all_to_all | solution.py:172
  9.8 8.0 %collective-permute-start.2 = (bf16[8,64,128]{2,1,0:T(8,128)(2,1)}, bf16[8,64,128]{2,1,0:T(8,128)(2,1)S(1)}, u32[]{:S(2)}, u32[]{:S(2)}) collective-permute-start(bf16[8,64,128]{2,1,0:T(8,128)(2,1)} %get-tuple-element.26.refs_2_), channel_id=1, source_target_pairs={{0,3},{1,2},{2,1},{3,0},{4,7},{5,6},{6,5},{7,4},{8,11},{9,10},{10,... | collective-permute-start | bytes 393224 | tf_op jit(solution)/shard_map/ppermute | solution.py:176
  10.5 8.1 %collective-permute-start.1 = (bf16[8,64,128]{2,1,0:T(8,128)(2,1)}, bf16[8,64,128]{2,1,0:T(8,128)(2,1)S(1)}, u32[]{:S(2)}, u32[]{:S(2)}) collective-permute-start(bf16[8,64,128]{2,1,0:T(8,128)(2,1)} %get-tuple-element.26.refs_2_), channel_id=1, source_target_pairs={{0,2},{1,3},{2,0},{3,1},{4,6},{5,7},{6,4},{7,5},{8,10},{9,11},{10,... | collective-permute-start | bytes 393224 | tf_op jit(solution)/shard_map/ppermute | solution.py:176
  11.4 7.2 %collective-permute-start = (bf16[8,64,128]{2,1,0:T(8,128)(2,1)}, bf16[8,64,128]{2,1,0:T(8,128)(2,1)S(1)}, u32[]{:S(2)}, u32[]{:S(2)}) collective-permute-start(bf16[8,64,128]{2,1,0:T(8,128)(2,1)} %get-tuple-element.26.refs_2_), channel_id=1, source_target_pairs={{0,1},{1,0},{2,3},{3,2},{4,5},{5,4},{6,7},{7,6},{8,9},{9,8},{10,11... | collective-permute-start | bytes 393224 | tf_op jit(solution)/shard_map/ppermute | solution.py:176
  25.8 21.7 %all-to-all-start.1 = ((bf16[16,64,128]{2,1,0:T(8,128)(2,1)}), bf16[16,64,128]{2,1,0:T(8,128)(2,1)S(1)}, u32[]{:S(2)}, u32[]{:S(2)}) async-start(bf16[16,64,128]{2,1,0:T(8,128)(2,1)} %shard_map.79), calls=%async_computation.1 | async-start | bytes 524288 | tf_op jit(solution)/shard_map/all_to_all | solution.py:172
  31.8 2.2 %copy-start.1 = (bf16[1024,2048]{1,0:T(8,128)(2,1)S(1)}, bf16[1024,2048]{1,0:T(8,128)(2,1)}, u32[]{:S(2)}) copy-start(bf16[1024,2048]{1,0:T(8,128)(2,1)} %copy-done) | copy-start | bytes 12582916
  33.9 2.2 %copy-start.5 = (bf16[1024,2048]{1,0:T(8,128)(2,1)S(1)}, bf16[1024,2048]{1,0:T(8,128)(2,1)}, u32[]{:S(2)}) copy-start(bf16[1024,2048]{1,0:T(8,128)(2,1)} %copy-done.4) | copy-start | bytes 12582916
  36.1 9.8 %copy-start.6 = (f32[512,128]{1,0:T(8,128)S(1)}, f32[512,128]{1,0:T(8,128)}, u32[]{:S(2)}) copy-start(f32[512,128]{1,0:T(8,128)} %param.6) | copy-start | bytes 786436
  36.1 9.8 %copy-start.9 = (s32[8,16]{1,0:T(8,128)S(1)}, s32[8,16]{1,0:T(8,128)}, u32[]{:S(2)}) copy-start(s32[8,16]{1,0:T(8,128)} %table.7) | copy-start | bytes 1540
  36.1 17.3 %copy-start.7 = (f32[512,128]{1,0:T(8,128)S(1)}, f32[512,128]{1,0:T(8,128)}, u32[]{:S(2)}) copy-start(f32[512,128]{1,0:T(8,128)} %param.7) | copy-start | bytes 786436
  37.6 1.9 %collective-permute-start.3 = (bf16[8,64,128]{2,1,0:T(8,128)(2,1)S(1)}, bf16[8,64,128]{2,1,0:T(8,128)(2,1)S(1)}, u32[]{:S(2)}, u32[]{:S(2)}) collective-permute-start(bf16[8,64,128]{2,1,0:T(8,128)(2,1)S(1)} %get-tuple-element.30), channel_id=1, source_target_pairs={{0,1},{1,0},{2,3},{3,2},{4,5},{5,4},{6,7},{7,6},{8,9},{9,8},{10,11... | collective-permute-start | bytes 393224 | tf_op jit(solution)/shard_map/ppermute | solution.py:176
  37.7 6.4 %collective-permute-start.4 = (bf16[8,64,128]{2,1,0:T(8,128)(2,1)S(1)}, bf16[8,64,128]{2,1,0:T(8,128)(2,1)S(1)}, u32[]{:S(2)}, u32[]{:S(2)}) collective-permute-start(bf16[8,64,128]{2,1,0:T(8,128)(2,1)S(1)} %get-tuple-element.31), channel_id=1, source_target_pairs={{0,2},{1,3},{2,0},{3,1},{4,6},{5,7},{6,4},{7,5},{8,10},{9,11},{10,... | collective-permute-start | bytes 393224 | tf_op jit(solution)/shard_map/ppermute | solution.py:176
  38.4 7.5 %collective-permute-start.5 = (bf16[8,64,128]{2,1,0:T(8,128)(2,1)S(1)}, bf16[8,64,128]{2,1,0:T(8,128)(2,1)S(1)}, u32[]{:S(2)}, u32[]{:S(2)}) collective-permute-start(bf16[8,64,128]{2,1,0:T(8,128)(2,1)S(1)} %get-tuple-element.32), channel_id=1, source_target_pairs={{0,3},{1,2},{2,1},{3,0},{4,7},{5,6},{6,5},{7,4},{8,11},{9,10},{10,... | collective-permute-start | bytes 393224 | tf_op jit(solution)/shard_map/ppermute | solution.py:176
  47.4 19.7 %all-to-all-start.2 = ((bf16[16,64,128]{2,1,0:T(8,128)(2,1)}), bf16[16,64,128]{2,1,0:T(8,128)(2,1)S(1)}, u32[]{:S(2)}, u32[]{:S(2)}) async-start(bf16[16,64,128]{2,1,0:T(8,128)(2,1)} %shard_map.81), calls=%async_computation.2 | async-start | bytes 524288 | tf_op jit(solution)/shard_map/all_to_all | solution.py:172
  54.2 5.7 %collective-permute-start.8 = (bf16[8,64,128]{2,1,0:T(8,128)(2,1)S(1)}, bf16[8,64,128]{2,1,0:T(8,128)(2,1)S(1)}, u32[]{:S(2)}, u32[]{:S(2)}) collective-permute-start(bf16[8,64,128]{2,1,0:T(8,128)(2,1)S(1)} %get-tuple-element.35.refs_1_), channel_id=1, source_target_pairs={{0,3},{1,2},{2,1},{3,0},{4,7},{5,6},{6,5},{7,4},{8,11},{9,10},{10,... | collective-permute-start | bytes 393224 | tf_op jit(solution)/shard_map/ppermute | solution.py:176
  54.6 8.3 %collective-permute-start.7 = (bf16[8,64,128]{2,1,0:T(8,128)(2,1)S(1)}, bf16[8,64,128]{2,1,0:T(8,128)(2,1)S(1)}, u32[]{:S(2)}, u32[]{:S(2)}) collective-permute-start(bf16[8,64,128]{2,1,0:T(8,128)(2,1)S(1)} %get-tuple-element.35.refs_1_), channel_id=1, source_target_pairs={{0,2},{1,3},{2,0},{3,1},{4,6},{5,7},{6,4},{7,5},{8,10},{9,11},{10,... | collective-permute-start | bytes 393224 | tf_op jit(solution)/shard_map/ppermute | solution.py:176
  55.9 7.0 %collective-permute-start.6 = (bf16[8,64,128]{2,1,0:T(8,128)(2,1)S(1)}, bf16[8,64,128]{2,1,0:T(8,128)(2,1)S(1)}, u32[]{:S(2)}, u32[]{:S(2)}) collective-permute-start(bf16[8,64,128]{2,1,0:T(8,128)(2,1)S(1)} %get-tuple-element.35.refs_1_), channel_id=1, source_target_pairs={{0,1},{1,0},{2,3},{3,2},{4,5},{5,4},{6,7},{7,6},{8,9},{9,8},{10,11... | collective-permute-start | bytes 393224 | tf_op jit(solution)/shard_map/ppermute | solution.py:176
  62.9 2.2 %copy-start.2 = (bf16[1024,2048]{1,0:T(8,128)(2,1)S(1)}, bf16[1024,2048]{1,0:T(8,128)(2,1)}, u32[]{:S(2)}) copy-start(bf16[1024,2048]{1,0:T(8,128)(2,1)} %copy-done) | copy-start | bytes 12582916
  67.1 18.0 %all-to-all-start.3 = ((bf16[16,64,128]{2,1,0:T(8,128)(2,1)}), bf16[16,64,128]{2,1,0:T(8,128)(2,1)S(1)}, u32[]{:S(2)}, u32[]{:S(2)}) async-start(bf16[16,64,128]{2,1,0:T(8,128)(2,1)} %shard_map.83), calls=%async_computation.3 | async-start | bytes 524288 | tf_op jit(solution)/shard_map/all_to_all | solution.py:172
  72.9 2.2 %copy-start.3 = (bf16[1024,2048]{1,0:T(8,128)(2,1)S(1)}, bf16[1024,2048]{1,0:T(8,128)(2,1)}, u32[]{:S(2)}) copy-start(bf16[1024,2048]{1,0:T(8,128)(2,1)} %copy-done) | copy-start | bytes 12582916
  76.0 1.9 %collective-permute-start.9 = (bf16[8,64,128]{2,1,0:T(8,128)(2,1)S(1)}, bf16[8,64,128]{2,1,0:T(8,128)(2,1)S(1)}, u32[]{:S(2)}, u32[]{:S(2)}) collective-permute-start(bf16[8,64,128]{2,1,0:T(8,128)(2,1)S(1)} %get-tuple-element.39), channel_id=1, source_target_pairs={{0,1},{1,0},{2,3},{3,2},{4,5},{5,4},{6,7},{7,6},{8,9},{9,8},{10,11... | collective-permute-start | bytes 393224 | tf_op jit(solution)/shard_map/ppermute | solution.py:176
  76.1 6.4 %collective-permute-start.10 = (bf16[8,64,128]{2,1,0:T(8,128)(2,1)S(1)}, bf16[8,64,128]{2,1,0:T(8,128)(2,1)S(1)}, u32[]{:S(2)}, u32[]{:S(2)}) collective-permute-start(bf16[8,64,128]{2,1,0:T(8,128)(2,1)S(1)} %get-tuple-element.40), channel_id=1, source_target_pairs={{0,2},{1,3},{2,0},{3,1},{4,6},{5,7},{6,4},{7,5},{8,10},{9,11},{10,... | collective-permute-start | bytes 393224 | tf_op jit(solution)/shard_map/ppermute | solution.py:176
  76.8 7.5 %collective-permute-start.11 = (bf16[8,64,128]{2,1,0:T(8,128)(2,1)S(1)}, bf16[8,64,128]{2,1,0:T(8,128)(2,1)S(1)}, u32[]{:S(2)}, u32[]{:S(2)}) collective-permute-start(bf16[8,64,128]{2,1,0:T(8,128)(2,1)S(1)} %get-tuple-element.41), channel_id=1, source_target_pairs={{0,3},{1,2},{2,1},{3,0},{4,7},{5,6},{6,5},{7,4},{8,11},{9,10},{10,... | collective-permute-start | bytes 393224 | tf_op jit(solution)/shard_map/ppermute | solution.py:176
  (4 other events, 5.3 us)

commit v3 on v2

--- a/solution.py
+++ b/solution.py
@@ -11,7 +11,7 @@
 STEPS = 2
 DENSE_BYTES = 8 * 2**20
 START_MEBIBYTES = 60
-BUILD_MEBIBYTES = 40
+BUILD_MEBIBYTES = 32
 LOW = jnp.bfloat16
 FULL = jnp.float32
 
@@ -96,17 +96,24 @@
             for part in dense
         )
         product[...] = summed.T.reshape(product.shape)
-        for turn, partial in enumerate(partials):
+        for turn, partial in zip((0, *range(quarters - 1, 0, -1)), partials):
             partial[row] = product[partner("edge", turn)].astype(partial.dtype)
+
+
+def apply_adjoint(dense, vectors, send):
+    product = sum(jnp.dot(part[...], vectors, preferred_element_type=FULL) for part in dense)
+    send[...] = product.reshape(send.shape).astype(LOW)
 
 
 def adjoint_kernel(operators, *refs):
     *arrived, send, source = refs[operators:]
     for turn, part in enumerate(arrived):
         source[:, partner("edge", turn)] = part[...]
-    vectors = source[...].reshape(-1, source.shape[-1])
-    product = sum(jnp.dot(part[...], vectors, preferred_element_type=FULL) for part in refs[:operators])
-    send[...] = product.reshape(send.shape).astype(LOW)
+    apply_adjoint(refs[:operators], source[...].reshape(-1, source.shape[-1]), send)
+
+
+def gathered_adjoint_kernel(dense, arrived, send):
+    apply_adjoint((dense,), arrived[...].reshape(-1, arrived.shape[-1]), send)
 
 
 def state_of(arrived, teleport):
@@ -169,12 +176,13 @@
         )(*operands)
 
     def over_node(array):
-        return lax.all_to_all(array, "node", 0, 0, tiled=True)
-
-    def over_edge(arrays):
+        merged = array.reshape(lax.axis_size("node"), CAP * quarter, hidden)
+        return lax.all_to_all(merged, "node", 0, 0, tiled=True).reshape(slot_shape)
+
+    def over_edge(arrays, turns):
         return [arrays[0]] + [
-            lax.ppermute(arrays[turn], "edge", [(place, place ^ turn) for place in range(quarters)])
-            for turn in range(1, quarters)
+            lax.ppermute(array, "edge", [(place, place ^ turn) for place in range(quarters)])
+            for turn, array in zip(turns, arrays[1:])
         ]
 
     send, rounded = call(
@@ -216,15 +224,25 @@
             transcendentals=0,
         )
         columns = over_node(send)
-        arrived = over_edge([rounded] * quarters)
-        (transposed,) = call(
-            functools.partial(adjoint_kernel, len(dense)),
-            (*dense, *arrived),
-            [VMEM] * (quarters + len(dense)),
-            [(slot_shape, LOW)],
-            [pltpu.VMEM((count, quarters, quarter, hidden), LOW)],
-            cost=cost,
-        )
+        if not last:
+            arrived = over_edge([rounded] * quarters, range(1, quarters))
+            (transposed,) = call(
+                functools.partial(adjoint_kernel, len(dense)),
+                (*dense, *arrived),
+                [VMEM] * (quarters + len(dense)),
+                [(slot_shape, LOW)],
+                [pltpu.VMEM((count, quarters, quarter, hidden), LOW)],
+                cost=cost,
+            )
+        else:
+            (transposed,) = call(
+                gathered_adjoint_kernel,
+                (high, lax.all_gather(rounded, "edge", axis=1, tiled=True)),
+                [VMEM] * 2,
+                [(slot_shape, LOW)],
+                [],
+                cost=cost,
+            )
         transposed, columns = lax.optimization_barrier((transposed, columns))
         partials = call(
             functools.partial(forward_kernel, len(dense)),
@@ -235,7 +253,7 @@
             cost=cost,
         )
         transposed = over_node(transposed)
-        partials = over_edge(partials)
+        partials = over_edge(partials, range(quarters - 1, 0, -1))
         total = [pltpu.VMEM(shape, FULL)]
         if not last:
             (send,) = call(

time: 87.3 us -> 87.6 us (level)
  waiting for transfers between devices: 20.4 us -> 13.5 us
  blocking collectives: 0 us -> 6.7 us
  local copies, waits for them, and re-layouts: 14.1 us -> 16.9 us
  starting transfers between devices: 32.8 us -> 31 us
    ppermute x12 -> x9, waiting for transfers between devices: 20.4 us -> 13.5 us  [over_edge(): lax.ppermute(array, 'edge', [(place, place ^ turn) for place in range(qua...]
    all_gather x0 -> x1, blocking collectives: none -> 6.7 us  [per_device_dense(): lax.all_gather(rounded, 'edge', axis=1, tiled=True)]
    unnamed x24 -> x26, local copies, waits for them, and re-layouts: 14.1 us -> 16.9 us
    ppermute x12 -> x9, starting transfers between devices: 7.65 us -> 5.73 us  [over_edge(): lax.ppermute(array, 'edge', [(place, place ^ turn) for place in range(qua...]
  transfers between devices with their start and end apart: 16 -> 13, of which waited for: 7 -> 4; matrix products, arithmetic and copies ran while one was open for 0% -> 0% of each run, Pallas kernels for 18% -> 17%
where the time goes in v3:
time: 87.6 us; the launch traced here: 86.8 us
  starting transfers between devices  31 us (35%)
  Pallas kernels  18 us (21%)
  local copies, waits for them, and re-layouts  16.9 us (19%)
  waiting for transfers between devices  13.5 us (15%)
  blocking collectives  6.7 us (8%)
    all_to_all x4, starting transfers between devices, over_node(): return lax.all_to_all(merged, 'node', 0, 0, tiled=True).reshape(slot_shape)  25.3 us
    pallas_call x10, Pallas kernels, call(): pl.pallas_call(kernel, out_shape=[jax.ShapeDtypeStruct(*out) for out in o...  18 us
    unnamed x26, local copies, waits for them, and re-layouts  16.9 us
    ppermute x9, waiting for transfers between devices, over_edge(): lax.ppermute(array, 'edge', [(place, place ^ turn) for place in range(qua...  13.5 us
    all_gather x1, blocking collectives, per_device_dense(): lax.all_gather(rounded, 'edge', axis=1, tiled=True)  6.7 us
    ppermute x9, starting transfers between devices, over_edge(): lax.ppermute(array, 'edge', [(place, place ^ turn) for place in range(qua...  5.73 us
  transfers between devices with their start and end apart: 13, of which 4 were waited for; matrix products, arithmetic and copies ran while one was open for 0% of the time, Pallas kernels for 17%

profile of v3, /device:TPU:0, one launch (start us, length us, event | category | flops | bytes accessed | tf_op | source)
XLA Modules:
  0.0 86.8 jit_solution(2100504683313408715)
XLA Ops:
  0.6 1.8 %shard_map.78 = (bf16[16,64,128]{2,1,0:T(8,128)(2,1)}, bf16[8,64,128]{2,1,0:T(8,128)(2,1)}) custom-call(s32[8,16]{1,0:T(8,128)} %table.7, f32[8,64,128]{2,1,0:T(8,128)} %bitcast.12, f32[8,64,128]{2,1,0:T(8,128)} %bitcast.18), custom_call_target="tpu_custom_call" | custom-call | tf_op jit(solution)/shard_map/pallas_call | solution.py:168
  2.4 7.4 %all-to-all-start = ((bf16[8,128,128]{2,1,0:T(8,128)(2,1)}), bf16[8,128,128]{2,1,0:T(8,128)(2,1)S(1)}, u32[]{:S(2)}, u32[]{:S(2)}) async-start(bf16[8,128,128]{2,1,0:T(8,128)(2,1)} %bitcast.22), calls=%async_computation | async-start | bytes 524288 | tf_op jit(solution)/shard_map/all_to_all | solution.py:180
  11.7 2.8 %copy-done.6 = bf16[1,192,64,256]{3,2,1,0:T(8,128)(2,1)S(1)} copy-done((bf16[1,192,64,256]{3,2,1,0:T(8,128)(2,1)S(1)}, bf16[1,192,64,256]{3,2,1,0:T(8,128)(2,1)}, u32[]{:S(2)}) %copy-start.6) | copy-done | bytes 6291480
  15.9 4.3 %shard_map.77 = (bf16[1024,2048]{1,0:T(8,128)(2,1)S(1)}, bf16[1024,2048]{1,0:T(8,128)(2,1)S(1)}) custom-call(s32[1,192]{1,0:T(1,128)S(1)} %copy-done.11, s32[1,192]{1,0:T(1,128)S(1)} %copy-done.12, bf16[1,192,64,256]{3,2,1,0:T(8,128)(2,1)S(1)} %copy-done.6), custom_call_target="tpu_custom_call" | custom-call | bytes 6291456 | tf_op jit(solution)/shard_map/pallas_call | solution.py:168
  20.2 3.1 %shard_map.79 = bf16[16,64,128]{2,1,0:T(8,128)(2,1)} custom-call(bf16[1024,2048]{1,0:T(8,128)(2,1)S(1)} %get-tuple-element.24.refs_0_.dense, bf16[1024,2048]{1,0:T(8,128)(2,1)S(1)} %get-tuple-element.25.refs_1_, bf16[8,64,128]{2,1,0:T(8,128)(2,1)S(1)} %copy-done.9, bf16[8,64,128]{2,1,0:T(8,128)(2,1)S(1)} %collective-permute-done.refs_3_, ...), custom_call_target="tpu_custom_call" | custom-call | flops 1073741824 | bytes 8388608 | tf_op jit(solution)/shard_map/pallas_call | solution.py:168
  23.3 2.0 %copy-done = bf16[1024,2048]{1,0:T(8,128)(2,1)} copy-done((bf16[1024,2048]{1,0:T(8,128)(2,1)}, bf16[1024,2048]{1,0:T(8,128)(2,1)S(1)}, u32[]{:S(2)}) %copy-start) | copy-done | bytes 4194328
  25.3 2.0 %copy-done.4 = bf16[1024,2048]{1,0:T(8,128)(2,1)} copy-done((bf16[1024,2048]{1,0:T(8,128)(2,1)}, bf16[1024,2048]{1,0:T(8,128)(2,1)S(1)}, u32[]{:S(2)}) %copy-start.4) | copy-done | bytes 4194328
  27.3 6.0 %all-to-all-start.1 = ((bf16[8,128,128]{2,1,0:T(8,128)(2,1)}), bf16[8,128,128]{2,1,0:T(8,128)(2,1)S(1)}, u32[]{:S(2)}, u32[]{:S(2)}) async-start(bf16[8,128,128]{2,1,0:T(8,128)(2,1)} %bitcast.4), calls=%async_computation.1 | async-start | bytes 524288 | tf_op jit(solution)/shard_map/all_to_all | solution.py:180
  33.3 2.2 %copy-done.1 = bf16[1024,2048]{1,0:T(8,128)(2,1)S(1)} copy-done((bf16[1024,2048]{1,0:T(8,128)(2,1)S(1)}, bf16[1024,2048]{1,0:T(8,128)(2,1)}, u32[]{:S(2)}) %copy-start.1) | copy-done | bytes 4194328
  35.5 2.2 %copy-done.5 = bf16[1024,2048]{1,0:T(8,128)(2,1)S(1)} copy-done((bf16[1024,2048]{1,0:T(8,128)(2,1)S(1)}, bf16[1024,2048]{1,0:T(8,128)(2,1)}, u32[]{:S(2)}) %copy-start.5) | copy-done | bytes 4194328
  37.7 1.5 %shard_map.80 = (f32[8,64,128]{2,1,0:T(8,128)S(1)}, bf16[8,64,128]{2,1,0:T(8,128)(2,1)S(1)}, bf16[8,64,128]{2,1,0:T(8,128)(2,1)S(1)}, bf16[8,64,128]{2,1,0:T(8,128)(2,1)S(1)}) custom-call(bf16[16,64,128]{2,1,0:T(8,128)(2,1)S(1)} %bitcast.15, bf16[1024,2048]{1,0:T(8,128)(2,1)S(1)} %copy-done.1, bf16[1024,2048]{1,0:T(8,128)(2,1)S(1)} %copy-done.5), custom_call_target="tpu_custom_call" | custom-call | flops 1073741824 | bytes 8388608 | tf_op jit(solution)/shard_map/pallas_call | solution.py:168
  39.1 0.9 %collective-permute-start.3 = (bf16[8,64,128]{2,1,0:T(8,128)(2,1)S(1)}, bf16[8,64,128]{2,1,0:T(8,128)(2,1)S(1)}, u32[]{:S(2)}, u32[]{:S(2)}) collective-permute-start(bf16[8,64,128]{2,1,0:T(8,128)(2,1)S(1)} %get-tuple-element.30), channel_id=1, source_target_pairs={{0,3},{1,2},{2,1},{3,0},{4,7},{5,6},{6,5},{7,4},{8,11},{9,10},{10,... | collective-permute-start | bytes 393224 | tf_op jit(solution)/shard_map/ppermute | solution.py:184
  41.1 3.8 %collective-permute-done.3.refs_1_ = bf16[8,64,128]{2,1,0:T(8,128)(2,1)S(1)} collective-permute-done((bf16[8,64,128]{2,1,0:T(8,128)(2,1)S(1)}, bf16[8,64,128]{2,1,0:T(8,128)(2,1)S(1)}, u32[]{:S(2)}, u32[]{:S(2)}) %collective-permute-start.3) | collective-permute-done | bytes 131104 | tf_op jit(solution)/shard_map/ppermute | solution.py:184
  44.9 2.9 %collective-permute-done.4.refs_2_ = bf16[8,64,128]{2,1,0:T(8,128)(2,1)S(1)} collective-permute-done((bf16[8,64,128]{2,1,0:T(8,128)(2,1)S(1)}, bf16[8,64,128]{2,1,0:T(8,128)(2,1)S(1)}, u32[]{:S(2)}, u32[]{:S(2)}) %collective-permute-start.4) | collective-permute-done | bytes 131104 | tf_op jit(solution)/shard_map/ppermute | solution.py:184
  47.8 1.4 %shard_map.81 = bf16[16,64,128]{2,1,0:T(8,128)(2,1)} custom-call(s32[8,16]{1,0:T(8,128)S(1)} %copy-done.10, f32[8,64,128]{2,1,0:T(8,128)S(1)} %bitcast.13, f32[8,64,128]{2,1,0:T(8,128)S(1)} %get-tuple-element.29.refs_0_, bf16[8,64,128]{2,1,0:T(8,128)(2,1)S(1)} %collective-permute-done.3.refs_1_, bf16[8,64,128]{2,1,0:T(8,128)(2,1)S(1)} %collective-permute-done.4.refs_2_, ...), custom_call_target="tpu_custom_call" | custom-call | tf_op jit(solution)/shard_map/pallas_call | solution.py:168
  49.3 6.0 %all-to-all-start.2 = ((bf16[8,128,128]{2,1,0:T(8,128)(2,1)}), bf16[8,128,128]{2,1,0:T(8,128)(2,1)S(1)}, u32[]{:S(2)}, u32[]{:S(2)}) async-start(bf16[8,128,128]{2,1,0:T(8,128)(2,1)} %bitcast.6), calls=%async_computation.2 | async-start | bytes 524288 | tf_op jit(solution)/shard_map/all_to_all | solution.py:180
  56.1 6.7 %all_gather.3.arrived = bf16[8,256,128]{2,1,0:T(8,128)(2,1)S(1)} all-gather(bf16[8,64,128]{2,1,0:T(8,128)(2,1)S(1)} %get-tuple-element.35), channel_id=1, replica_groups=mesh['node'=8,'edge'=4] {'edge'}, dimensions={1}, use_global_device_ids=true | all-gather | bytes 655360 | tf_op jit(solution)/shard_map/all_gather | solution.py:240
  62.8 2.2 %copy-done.2 = bf16[1024,2048]{1,0:T(8,128)(2,1)S(1)} copy-done((bf16[1024,2048]{1,0:T(8,128)(2,1)S(1)}, bf16[1024,2048]{1,0:T(8,128)(2,1)}, u32[]{:S(2)}) %copy-start.2) | copy-done | bytes 4194328
  65.0 1.9 %shard_map.83 = bf16[16,64,128]{2,1,0:T(8,128)(2,1)} custom-call(bf16[1024,2048]{1,0:T(8,128)(2,1)S(1)} %copy-done.2, bf16[8,256,128]{2,1,0:T(8,128)(2,1)S(1)} %all_gather.3.arrived), custom_call_target="tpu_custom_call" | custom-call | flops 536870912 | bytes 4194304 | tf_op jit(solution)/shard_map/pallas_call | solution.py:168
  66.9 5.9 %all-to-all-start.3 = ((bf16[8,128,128]{2,1,0:T(8,128)(2,1)}), bf16[8,128,128]{2,1,0:T(8,128)(2,1)S(1)}, u32[]{:S(2)}, u32[]{:S(2)}) async-start(bf16[8,128,128]{2,1,0:T(8,128)(2,1)} %bitcast.8), calls=%async_computation.3 | async-start | bytes 524288 | tf_op jit(solution)/shard_map/all_to_all | solution.py:180
  72.8 2.2 %copy-done.3 = bf16[1024,2048]{1,0:T(8,128)(2,1)S(1)} copy-done((bf16[1024,2048]{1,0:T(8,128)(2,1)S(1)}, bf16[1024,2048]{1,0:T(8,128)(2,1)}, u32[]{:S(2)}) %copy-start.3) | copy-done | bytes 4194328
  77.8 3.7 %collective-permute-done.6.refs_1_ = bf16[8,64,128]{2,1,0:T(8,128)(2,1)S(1)} collective-permute-done((bf16[8,64,128]{2,1,0:T(8,128)(2,1)S(1)}, bf16[8,64,128]{2,1,0:T(8,128)(2,1)S(1)}, u32[]{:S(2)}, u32[]{:S(2)}) %collective-permute-start.6) | collective-permute-done | bytes 131104 | tf_op jit(solution)/shard_map/ppermute | solution.py:184
  81.5 3.1 %collective-permute-done.7.refs_2_ = bf16[8,64,128]{2,1,0:T(8,128)(2,1)S(1)} collective-permute-done((bf16[8,64,128]{2,1,0:T(8,128)(2,1)S(1)}, bf16[8,64,128]{2,1,0:T(8,128)(2,1)S(1)}, u32[]{:S(2)}, u32[]{:S(2)}) %collective-permute-start.7) | collective-permute-done | bytes 131104 | tf_op jit(solution)/shard_map/ppermute | solution.py:184
  85.4 1.4 %shard_map.86 = f32[8,64,128]{2,1,0:T(8,128)} custom-call(s32[8,16]{1,0:T(8,128)S(1)} %copy-done.10, f32[8,64,128]{2,1,0:T(8,128)S(1)} %get-tuple-element.44.gradient_in, bf16[16,64,128]{2,1,0:T(8,128)(2,1)S(1)} %bitcast.16), custom_call_target="tpu_custom_call" | custom-call | tf_op jit(solution)/shard_map/pallas_call | solution.py:168
  (39 shorter events, 8.7 us)
Async XLA Ops:
  2.4 17.8 %copy-start.9 = (bf16[8,64,128]{2,1,0:T(8,128)(2,1)S(1)}, bf16[8,64,128]{2,1,0:T(8,128)(2,1)}, u32[]{:S(2)}) copy-start(bf16[8,64,128]{2,1,0:T(8,128)(2,1)} %get-tuple-element.26.refs_2_) | copy-start | bytes 393220
  2.4 24.8 %all-to-all-start = ((bf16[8,128,128]{2,1,0:T(8,128)(2,1)}), bf16[8,128,128]{2,1,0:T(8,128)(2,1)S(1)}, u32[]{:S(2)}, u32[]{:S(2)}) async-start(bf16[8,128,128]{2,1,0:T(8,128)(2,1)} %bitcast.22), calls=%async_computation | async-start | bytes 524288 | tf_op jit(solution)/shard_map/all_to_all | solution.py:180
  9.8 10.3 %collective-permute-start.2 = (bf16[8,64,128]{2,1,0:T(8,128)(2,1)}, bf16[8,64,128]{2,1,0:T(8,128)(2,1)S(1)}, u32[]{:S(2)}, u32[]{:S(2)}) collective-permute-start(bf16[8,64,128]{2,1,0:T(8,128)(2,1)} %get-tuple-element.26.refs_2_), channel_id=1, source_target_pairs={{0,3},{1,2},{2,1},{3,0},{4,7},{5,6},{6,5},{7,4},{8,11},{9,10},{10,... | collective-permute-start | bytes 393224 | tf_op jit(solution)/shard_map/ppermute | solution.py:184
  10.5 9.7 %collective-permute-start.1 = (bf16[8,64,128]{2,1,0:T(8,128)(2,1)}, bf16[8,64,128]{2,1,0:T(8,128)(2,1)S(1)}, u32[]{:S(2)}, u32[]{:S(2)}) collective-permute-start(bf16[8,64,128]{2,1,0:T(8,128)(2,1)} %get-tuple-element.26.refs_2_), channel_id=1, source_target_pairs={{0,2},{1,3},{2,0},{3,1},{4,6},{5,7},{6,4},{7,5},{8,10},{9,11},{10,... | collective-permute-start | bytes 393224 | tf_op jit(solution)/shard_map/ppermute | solution.py:184
  11.4 8.8 %collective-permute-start = (bf16[8,64,128]{2,1,0:T(8,128)(2,1)}, bf16[8,64,128]{2,1,0:T(8,128)(2,1)S(1)}, u32[]{:S(2)}, u32[]{:S(2)}) collective-permute-start(bf16[8,64,128]{2,1,0:T(8,128)(2,1)} %get-tuple-element.26.refs_2_), channel_id=1, source_target_pairs={{0,1},{1,0},{2,3},{3,2},{4,5},{5,4},{6,7},{7,6},{8,9},{9,8},{10,11... | collective-permute-start | bytes 393224 | tf_op jit(solution)/shard_map/ppermute | solution.py:184
  11.7 2.8 %copy-start.6 = (bf16[1,192,64,256]{3,2,1,0:T(8,128)(2,1)S(1)}, bf16[1,192,64,256]{3,2,1,0:T(8,128)(2,1)}, u32[]{:S(2)}) copy-start(bf16[1,192,64,256]{3,2,1,0:T(8,128)(2,1)} %weights.1) | copy-start | bytes 18874372
  23.3 2.0 %copy-start = (bf16[1024,2048]{1,0:T(8,128)(2,1)}, bf16[1024,2048]{1,0:T(8,128)(2,1)S(1)}, u32[]{:S(2)}) copy-start(bf16[1024,2048]{1,0:T(8,128)(2,1)S(1)} %get-tuple-element.24.refs_0_.dense) | copy-start | bytes 12582916
  25.3 2.0 %copy-start.4 = (bf16[1024,2048]{1,0:T(8,128)(2,1)}, bf16[1024,2048]{1,0:T(8,128)(2,1)S(1)}, u32[]{:S(2)}) copy-start(bf16[1024,2048]{1,0:T(8,128)(2,1)S(1)} %get-tuple-element.25.refs_1_) | copy-start | bytes 12582916
  27.3 22.0 %all-to-all-start.1 = ((bf16[8,128,128]{2,1,0:T(8,128)(2,1)}), bf16[8,128,128]{2,1,0:T(8,128)(2,1)S(1)}, u32[]{:S(2)}, u32[]{:S(2)}) async-start(bf16[8,128,128]{2,1,0:T(8,128)(2,1)} %bitcast.4), calls=%async_computation.1 | async-start | bytes 524288 | tf_op jit(solution)/shard_map/all_to_all | solution.py:180
  33.3 2.2 %copy-start.1 = (bf16[1024,2048]{1,0:T(8,128)(2,1)S(1)}, bf16[1024,2048]{1,0:T(8,128)(2,1)}, u32[]{:S(2)}) copy-start(bf16[1024,2048]{1,0:T(8,128)(2,1)} %copy-done) | copy-start | bytes 12582916
  35.5 2.2 %copy-start.5 = (bf16[1024,2048]{1,0:T(8,128)(2,1)S(1)}, bf16[1024,2048]{1,0:T(8,128)(2,1)}, u32[]{:S(2)}) copy-start(bf16[1024,2048]{1,0:T(8,128)(2,1)} %copy-done.4) | copy-start | bytes 12582916
  37.7 10.2 %copy-start.7 = (f32[512,128]{1,0:T(8,128)S(1)}, f32[512,128]{1,0:T(8,128)}, u32[]{:S(2)}) copy-start(f32[512,128]{1,0:T(8,128)} %param.6) | copy-start | bytes 786436
  37.7 10.2 %copy-start.10 = (s32[8,16]{1,0:T(8,128)S(1)}, s32[8,16]{1,0:T(8,128)}, u32[]{:S(2)}) copy-start(s32[8,16]{1,0:T(8,128)} %table.7) | copy-start | bytes 1540
  37.7 17.6 %copy-start.8 = (f32[512,128]{1,0:T(8,128)S(1)}, f32[512,128]{1,0:T(8,128)}, u32[]{:S(2)}) copy-start(f32[512,128]{1,0:T(8,128)} %param.7) | copy-start | bytes 786436
  39.1 5.7 %collective-permute-start.3 = (bf16[8,64,128]{2,1,0:T(8,128)(2,1)S(1)}, bf16[8,64,128]{2,1,0:T(8,128)(2,1)S(1)}, u32[]{:S(2)}, u32[]{:S(2)}) collective-permute-start(bf16[8,64,128]{2,1,0:T(8,128)(2,1)S(1)} %get-tuple-element.30), channel_id=1, source_target_pairs={{0,3},{1,2},{2,1},{3,0},{4,7},{5,6},{6,5},{7,4},{8,11},{9,10},{10,... | collective-permute-start | bytes 393224 | tf_op jit(solution)/shard_map/ppermute | solution.py:184
  40.1 7.7 %collective-permute-start.4 = (bf16[8,64,128]{2,1,0:T(8,128)(2,1)S(1)}, bf16[8,64,128]{2,1,0:T(8,128)(2,1)S(1)}, u32[]{:S(2)}, u32[]{:S(2)}) collective-permute-start(bf16[8,64,128]{2,1,0:T(8,128)(2,1)S(1)} %get-tuple-element.31), channel_id=1, source_target_pairs={{0,2},{1,3},{2,0},{3,1},{4,6},{5,7},{6,4},{7,5},{8,10},{9,11},{10,... | collective-permute-start | bytes 393224 | tf_op jit(solution)/shard_map/ppermute | solution.py:184
  40.8 7.0 %collective-permute-start.5 = (bf16[8,64,128]{2,1,0:T(8,128)(2,1)S(1)}, bf16[8,64,128]{2,1,0:T(8,128)(2,1)S(1)}, u32[]{:S(2)}, u32[]{:S(2)}) collective-permute-start(bf16[8,64,128]{2,1,0:T(8,128)(2,1)S(1)} %get-tuple-element.32), channel_id=1, source_target_pairs={{0,1},{1,0},{2,3},{3,2},{4,5},{5,4},{6,7},{7,6},{8,9},{9,8},{10,11... | collective-permute-start | bytes 393224 | tf_op jit(solution)/shard_map/ppermute | solution.py:184
  49.3 17.6 %all-to-all-start.2 = ((bf16[8,128,128]{2,1,0:T(8,128)(2,1)}), bf16[8,128,128]{2,1,0:T(8,128)(2,1)S(1)}, u32[]{:S(2)}, u32[]{:S(2)}) async-start(bf16[8,128,128]{2,1,0:T(8,128)(2,1)} %bitcast.6), calls=%async_computation.2 | async-start | bytes 524288 | tf_op jit(solution)/shard_map/all_to_all | solution.py:180
  62.8 2.2 %copy-start.2 = (bf16[1024,2048]{1,0:T(8,128)(2,1)S(1)}, bf16[1024,2048]{1,0:T(8,128)(2,1)}, u32[]{:S(2)}) copy-start(bf16[1024,2048]{1,0:T(8,128)(2,1)} %copy-done) | copy-start | bytes 12582916
  66.9 18.4 %all-to-all-start.3 = ((bf16[8,128,128]{2,1,0:T(8,128)(2,1)}), bf16[8,128,128]{2,1,0:T(8,128)(2,1)S(1)}, u32[]{:S(2)}, u32[]{:S(2)}) async-start(bf16[8,128,128]{2,1,0:T(8,128)(2,1)} %bitcast.8), calls=%async_computation.3 | async-start | bytes 524288 | tf_op jit(solution)/shard_map/all_to_all | solution.py:180
  72.8 2.2 %copy-start.3 = (bf16[1024,2048]{1,0:T(8,128)(2,1)S(1)}, bf16[1024,2048]{1,0:T(8,128)(2,1)}, u32[]{:S(2)}) copy-start(bf16[1024,2048]{1,0:T(8,128)(2,1)} %copy-done) | copy-start | bytes 12582916
  75.9 5.6 %collective-permute-start.6 = (bf16[8,64,128]{2,1,0:T(8,128)(2,1)S(1)}, bf16[8,64,128]{2,1,0:T(8,128)(2,1)S(1)}, u32[]{:S(2)}, u32[]{:S(2)}) collective-permute-start(bf16[8,64,128]{2,1,0:T(8,128)(2,1)S(1)} %get-tuple-element.39), channel_id=1, source_target_pairs={{0,3},{1,2},{2,1},{3,0},{4,7},{5,6},{6,5},{7,4},{8,11},{9,10},{10,... | collective-permute-start | bytes 393224 | tf_op jit(solution)/shard_map/ppermute | solution.py:184
  76.8 7.8 %collective-permute-start.7 = (bf16[8,64,128]{2,1,0:T(8,128)(2,1)S(1)}, bf16[8,64,128]{2,1,0:T(8,128)(2,1)S(1)}, u32[]{:S(2)}, u32[]{:S(2)}) collective-permute-start(bf16[8,64,128]{2,1,0:T(8,128)(2,1)S(1)} %get-tuple-element.40), channel_id=1, source_target_pairs={{0,2},{1,3},{2,0},{3,1},{4,6},{5,7},{6,4},{7,5},{8,10},{9,11},{10,... | collective-permute-start | bytes 393224 | tf_op jit(solution)/shard_map/ppermute | solution.py:184
  77.7 6.9 %collective-permute-start.8 = (bf16[8,64,128]{2,1,0:T(8,128)(2,1)S(1)}, bf16[8,64,128]{2,1,0:T(8,128)(2,1)S(1)}, u32[]{:S(2)}, u32[]{:S(2)}) collective-permute-start(bf16[8,64,128]{2,1,0:T(8,128)(2,1)S(1)} %get-tuple-element.41), channel_id=1, source_target_pairs={{0,1},{1,0},{2,3},{3,2},{4,5},{5,4},{6,7},{7,6},{8,9},{9,8},{10,11... | collective-permute-start | bytes 393224 | tf_op jit(solution)/shard_map/ppermute | solution.py:184
  (2 other events, 1.4 us)

commit v4 on v2

--- a/solution.py
+++ b/solution.py
@@ -11,7 +11,8 @@
 STEPS = 2
 DENSE_BYTES = 8 * 2**20
 START_MEBIBYTES = 60
-BUILD_MEBIBYTES = 40
+BUILD_MEBIBYTES = 60
+APPLY_MEBIBYTES = 57
 LOW = jnp.bfloat16
 FULL = jnp.float32
 
@@ -51,10 +52,16 @@
     rounded[...] = adjoint[...].astype(LOW)
 
 
-def build_kernel(rows, slots, weights, high, low, held, total, sems):
-    parts = sems.shape[0]
+def build_kernel(rows, slots, weights, *refs):
+    outs = refs[:2]
+    row_of, slot_of, held, total, high, low, sems, out_sems = refs[2:]
+    parts = sems.shape[0] - 2
     block_count, quarter, width = held.shape
     chunk = block_count // parts
+    indices = [
+        pltpu.make_async_copy(source, target, sems.at[parts + index])
+        for index, (source, target) in enumerate(((rows, row_of), (slots, slot_of)))
+    ]
     copies = [
         pltpu.make_async_copy(
             weights.at[0, pl.ds(part * chunk, chunk)],
@@ -63,50 +70,83 @@
         )
         for part in range(parts)
     ]
-    for copy in copies:
+    for copy in indices + copies:
         copy.start()
     total[...] = jnp.zeros_like(total)
+    for copy in indices:
+        copy.wait()
     for part, copy in enumerate(copies):
         copy.wait()
         for block in range(part * chunk, (part + 1) * chunk):
-            total[slots[0, block], rows[0, block]] += held[block].astype(FULL)
-    for slot in range(total.shape[0]):
-        for row in range(total.shape[1]):
-            place = (pl.ds(slot * quarter, quarter), pl.ds(row * width, width))
-            value = total[slot, row]
-            rounded = value.astype(LOW)
-            high[place] = rounded
-            low[place] = (value - rounded.astype(FULL)).astype(LOW)
-
-
-def forward_kernel(operators, columns, *refs):
-    dense = refs[:operators]
-    *partials, product = refs[operators:]
+            total[row_of[0, block], slot_of[0, block]] += held[block].astype(FULL)
+    stores = []
+    for row in range(total.shape[0]):
+        value = total[row].reshape(-1, width)
+        rounded = value.astype(LOW)
+        high[row] = rounded
+        low[row] = (value - rounded.astype(FULL)).astype(LOW)
+        for index, part in enumerate((high, low)):
+            store = pltpu.make_async_copy(
+                part.at[row], outs[index].at[row], out_sems.at[index, row]
+            )
+            store.start()
+            stores.append(store)
+    for store in stores:
+        store.wait()
+
+
+def fetch(dense, held, sems):
+    copies = [
+        [
+            pltpu.make_async_copy(part.at[row], held.at[index, row], sems.at[index, row])
+            for index, part in enumerate(dense)
+        ]
+        for row in range(held.shape[1])
+    ]
+    for row_copies in copies:
+        for copy in row_copies:
+            copy.start()
+    return copies
+
+
+def forward_kernel(operators, *refs):
+    columns, *partials, product, held, sems = refs[operators:]
+    copies = fetch(refs[:operators], held, sems)
     quarters, quarter, hidden = product.shape
-    width = quarters * quarter
     vectors = columns[...].reshape(-1, hidden)
-    for row in range(partials[0].shape[0]):
+    for row, row_copies in enumerate(copies):
+        for copy in row_copies:
+            copy.wait()
         summed = sum(
             lax.dot_general(
                 vectors,
-                part[:, row * width : (row + 1) * width],
+                held[index, row],
                 (((0,), (0,)), ((), ())),
                 preferred_element_type=FULL,
             )
-            for part in dense
+            for index in range(operators)
         )
         product[...] = summed.T.reshape(product.shape)
-        for turn, partial in enumerate(partials):
+        for turn, partial in zip((0, *range(quarters - 1, 0, -1)), partials):
             partial[row] = product[partner("edge", turn)].astype(partial.dtype)
 
 
 def adjoint_kernel(operators, *refs):
-    *arrived, send, source = refs[operators:]
-    for turn, part in enumerate(arrived):
-        source[:, partner("edge", turn)] = part[...]
-    vectors = source[...].reshape(-1, source.shape[-1])
-    product = sum(jnp.dot(part[...], vectors, preferred_element_type=FULL) for part in refs[:operators])
-    send[...] = product.reshape(send.shape).astype(LOW)
+    *arrived, send, source, held, sems = refs[operators:]
+    copies = fetch(refs[:operators], held, sems)
+    if len(arrived) == 1:
+        source = arrived[0]
+    else:
+        for turn, part in enumerate(arrived):
+            source[:, partner("edge", turn)] = part[...]
+    total = 0
+    for row, row_copies in enumerate(copies):
+        for copy in row_copies:
+            copy.wait()
+        vectors = source[row].reshape(-1, source.shape[-1])
+        for index in range(operators):
+            total += jnp.dot(held[index, row], vectors, preferred_element_type=FULL)
+    send[...] = total.reshape(send.shape).astype(LOW)
 
 
 def state_of(arrived, teleport):
@@ -157,24 +197,25 @@
     teleport = teleport.reshape(shape)
     cotangent = cotangent.reshape(shape)
 
-    def call(kernel, operands, places, outs, scratch, mebibytes=8, cost=None):
+    def call(kernel, operands, places, outs, scratch, mebibytes=8, cost=None, place=VMEM):
         return pl.pallas_call(
             kernel,
             out_shape=[jax.ShapeDtypeStruct(*out) for out in outs],
             in_specs=places,
-            out_specs=[VMEM] * len(outs),
+            out_specs=[place] * len(outs),
             scratch_shapes=scratch,
             compiler_params=params(mebibytes),
             cost_estimate=cost,
         )(*operands)
 
     def over_node(array):
-        return lax.all_to_all(array, "node", 0, 0, tiled=True)
-
-    def over_edge(arrays):
+        merged = array.reshape(lax.axis_size("node"), CAP * quarter, hidden)
+        return lax.all_to_all(merged, "node", 0, 0, tiled=True).reshape(slot_shape)
+
+    def over_edge(arrays, turns):
         return [arrays[0]] + [
-            lax.ppermute(arrays[turn], "edge", [(place, place ^ turn) for place in range(quarters)])
-            for turn in range(1, quarters)
+            lax.ppermute(array, "edge", [(place, place ^ turn) for place in range(quarters)])
+            for turn, array in zip(turns, arrays[1:])
         ]
 
     send, rounded = call(
@@ -190,20 +231,26 @@
         ],
         START_MEBIBYTES,
     )
-    dense_shape = (slot_total * quarter, count * width)
+    dense_shape = (count, slot_total * quarter, width)
     parts = next(size for size in (12, 8, 4, 2, 1) if block_count % size == 0)
     high, low = call(
         build_kernel,
         (block_row, block_slot, values),
-        [SMEM, SMEM, HBM],
+        [HBM] * 3,
         [(dense_shape, LOW)] * 2,
         [
+            pltpu.SMEM(block_row.shape, block_row.dtype),
+            pltpu.SMEM(block_slot.shape, block_slot.dtype),
             pltpu.VMEM((block_count, quarter, width), LOW),
-            pltpu.VMEM((slot_total, count, quarter, width), FULL),
-            pltpu.SemaphoreType.DMA((parts,)),
+            pltpu.VMEM((count, slot_total, quarter, width), FULL),
+            pltpu.VMEM(dense_shape, LOW),
+            pltpu.VMEM(dense_shape, LOW),
+            pltpu.SemaphoreType.DMA((parts + 2,)),
+            pltpu.SemaphoreType.DMA((2, count)),
         ],
         BUILD_MEBIBYTES,
         pl.CostEstimate(flops=0, bytes_accessed=values.size * 2, transcendentals=0),
+        HBM,
     )
 
     gradient = cotangent
@@ -215,27 +262,36 @@
             bytes_accessed=len(dense) * high.size * 2,
             transcendentals=0,
         )
+        fetched = [
+            pltpu.VMEM((len(dense),) + dense_shape, LOW),
+            pltpu.SemaphoreType.DMA((len(dense), count)),
+        ]
         columns = over_node(send)
-        arrived = over_edge([rounded] * quarters)
+        if not last:
+            arrived = over_edge([rounded] * quarters, range(1, quarters))
+        else:
+            arrived = [lax.all_gather(rounded, "edge", axis=1, tiled=True)]
         (transposed,) = call(
             functools.partial(adjoint_kernel, len(dense)),
             (*dense, *arrived),
-            [VMEM] * (quarters + len(dense)),
+            [HBM] * len(dense) + [VMEM] * len(arrived),
             [(slot_shape, LOW)],
-            [pltpu.VMEM((count, quarters, quarter, hidden), LOW)],
-            cost=cost,
+            [pltpu.VMEM((count, quarters, quarter, hidden), LOW), *fetched],
+            APPLY_MEBIBYTES,
+            cost,
         )
         transposed, columns = lax.optimization_barrier((transposed, columns))
         partials = call(
             functools.partial(forward_kernel, len(dense)),
-            (columns, *dense),
-            [VMEM] * (1 + len(dense)),
+            (*dense, columns),
+            [HBM] * len(dense) + [VMEM],
             [(shape, FULL)] + [(shape, LOW)] * (quarters - 1),
-            [pltpu.VMEM((quarters, quarter, hidden), FULL)],
-            cost=cost,
+            [pltpu.VMEM((quarters, quarter, hidden), FULL), *fetched],
+            APPLY_MEBIBYTES,
+            cost,
         )
         transposed = over_node(transposed)
-        partials = over_edge(partials)
+        partials = over_edge(partials, range(quarters - 1, 0, -1))
         total = [pltpu.VMEM(shape, FULL)]
         if not last:
             (send,) = call(

time: 87.3 us -> 95.6 us (1.095)
  Pallas kernels: 18.5 us -> 39.5 us
  local copies, waits for them, and re-layouts: 14.1 us -> 2.65 us
  blocking collectives: 0 us -> 7.24 us
  waiting for transfers between devices: 20.4 us -> 14.2 us
  starting transfers between devices: 32.8 us -> 30.5 us
    pallas_call x10, Pallas kernels: 18.5 us -> 39.5 us  [call(): pl.pallas_call(kernel, out_shape=[jax.ShapeDtypeStruct(*out) for out in o...]
    unnamed x24 -> x20, local copies, waits for them, and re-layouts: 14.1 us -> 2.65 us
    all_gather x0 -> x1, blocking collectives: none -> 7.24 us  [per_device_dense(): arrived = [lax.all_gather(rounded, 'edge', axis=1, tiled=True)]]
    ppermute x12 -> x9, waiting for transfers between devices: 20.4 us -> 14.2 us  [over_edge(): lax.ppermute(array, 'edge', [(place, place ^ turn) for place in range(qua...]
    ppermute x12 -> x9, starting transfers between devices: 7.65 us -> 5.73 us  [over_edge(): lax.ppermute(array, 'edge', [(place, place ^ turn) for place in range(qua...]
  transfers between devices with their start and end apart: 16 -> 13, of which waited for: 7 -> 5; matrix products, arithmetic and copies ran while one was open for 0% -> 0% of each run, Pallas kernels for 18% -> 38%
where the time goes in v4:
time: 95.6 us; the launch traced here: 94.9 us
  Pallas kernels  39.5 us (41%)
  starting transfers between devices  30.5 us (32%)
  waiting for transfers between devices  14.2 us (15%)
  blocking collectives  7.24 us (8%)
  local copies, waits for them, and re-layouts  2.65 us (3%)
    pallas_call x10, Pallas kernels, call(): pl.pallas_call(kernel, out_shape=[jax.ShapeDtypeStruct(*out) for out in o...  39.5 us
    all_to_all x4, starting transfers between devices, over_node(): return lax.all_to_all(merged, 'node', 0, 0, tiled=True).reshape(slot_shape)  24.8 us
    ppermute x9, waiting for transfers between devices, over_edge(): lax.ppermute(array, 'edge', [(place, place ^ turn) for place in range(qua...  14.2 us
    all_gather x1, blocking collectives, per_device_dense(): arrived = [lax.all_gather(rounded, 'edge', axis=1, tiled=True)]  7.24 us
    ppermute x9, starting transfers between devices, over_edge(): lax.ppermute(array, 'edge', [(place, place ^ turn) for place in range(qua...  5.73 us
    unnamed x20, local copies, waits for them, and re-layouts  2.65 us
  transfers between devices with their start and end apart: 13, of which 5 were waited for; matrix products, arithmetic and copies ran while one was open for 0% of the time, Pallas kernels for 38%

profile of v4, /device:TPU:0, one launch (start us, length us, event | category | flops | bytes accessed | tf_op | source)
XLA Modules:
  0.0 94.9 jit_solution(16667941885930199298)
XLA Ops:
  0.6 1.8 %shard_map.78 = (bf16[16,64,128]{2,1,0:T(8,128)(2,1)}, bf16[8,64,128]{2,1,0:T(8,128)(2,1)}) custom-call(s32[8,16]{1,0:T(8,128)} %table.7, f32[8,64,128]{2,1,0:T(8,128)} %bitcast.12, f32[8,64,128]{2,1,0:T(8,128)} %bitcast.16), custom_call_target="tpu_custom_call" | custom-call | tf_op jit(solution)/shard_map/pallas_call | solution.py:201
  2.4 7.3 %all-to-all-start = ((bf16[8,128,128]{2,1,0:T(8,128)(2,1)}), bf16[8,128,128]{2,1,0:T(8,128)(2,1)S(1)}, u32[]{:S(2)}, u32[]{:S(2)}) async-start(bf16[8,128,128]{2,1,0:T(8,128)(2,1)} %bitcast.24), calls=%async_computation | async-start | bytes 524288 | tf_op jit(solution)/shard_map/all_to_all | solution.py:213
  10.4 0.9 collective-permute-start.1
  11.6 6.5 %shard_map.77 = (bf16[8,1024,256]{2,1,0:T(8,128)(2,1)}, bf16[8,1024,256]{2,1,0:T(8,128)(2,1)}) custom-call(s32[1,192]{1,0:T(1,128)} %rows.1, s32[1,192]{1,0:T(1,128)} %slots.1, bf16[1,192,64,256]{3,2,1,0:T(8,128)(2,1)} %weights.1), custom_call_target="tpu_custom_call" | custom-call | bytes 6291456 | tf_op jit(solution)/shard_map/pallas_call | solution.py:201
  19.2 8.0 %shard_map.79 = bf16[16,64,128]{2,1,0:T(8,128)(2,1)} custom-call(bf16[8,1024,256]{2,1,0:T(8,128)(2,1)} %get-tuple-element.24.refs_0_, bf16[8,1024,256]{2,1,0:T(8,128)(2,1)} %get-tuple-element.25.refs_1_, bf16[8,64,128]{2,1,0:T(8,128)(2,1)} %get-tuple-element.26.refs_2_, bf16[8,64,128]{2,1,0:T(8,128)(2,1)} %copy-done.9, bf16[8,64,128]{2,1,0:T(8,128)(2,1)} %copy-done.8, ...), custom_call_target="tpu_custom_call" | custom-call | flops 1073741824 | bytes 8388608 | tf_op jit(solution)/shard_map/pallas_call | solution.py:201
  27.3 6.0 %all-to-all-start.1 = ((bf16[8,128,128]{2,1,0:T(8,128)(2,1)}), bf16[8,128,128]{2,1,0:T(8,128)(2,1)S(1)}, u32[]{:S(2)}, u32[]{:S(2)}) async-start(bf16[8,128,128]{2,1,0:T(8,128)(2,1)} %bitcast.19), calls=%async_computation.1 | async-start | bytes 524288 | tf_op jit(solution)/shard_map/all_to_all | solution.py:213
  33.3 7.2 %shard_map.80 = (f32[8,64,128]{2,1,0:T(8,128)}, bf16[8,64,128]{2,1,0:T(8,128)(2,1)}, bf16[8,64,128]{2,1,0:T(8,128)(2,1)}, bf16[8,64,128]{2,1,0:T(8,128)(2,1)}) custom-call(bf16[8,1024,256]{2,1,0:T(8,128)(2,1)} %get-tuple-element.24.refs_0_, bf16[8,1024,256]{2,1,0:T(8,128)(2,1)} %get-tuple-element.25.refs_1_, bf16[16,64,128]{2,1,0:T(8,128)(2,1)} %bitcast.20), custom_call_target="tpu_custom_call" | custom-call | flops 1073741824 | bytes 8388608 | tf_op jit(solution)/shard_map/pallas_call | solution.py:201
  41.2 0.9 collective-permute-start.4
  42.5 4.1 %collective-permute-done.3.refs_1_ = bf16[8,64,128]{2,1,0:T(8,128)(2,1)S(1)} collective-permute-done((bf16[8,64,128]{2,1,0:T(8,128)(2,1)}, bf16[8,64,128]{2,1,0:T(8,128)(2,1)S(1)}, u32[]{:S(2)}, u32[]{:S(2)}) %collective-permute-start.3) | collective-permute-done | bytes 131104 | tf_op jit(solution)/shard_map/ppermute | solution.py:217
  46.6 2.8 %collective-permute-done.4.refs_2_ = bf16[8,64,128]{2,1,0:T(8,128)(2,1)S(1)} collective-permute-done((bf16[8,64,128]{2,1,0:T(8,128)(2,1)}, bf16[8,64,128]{2,1,0:T(8,128)(2,1)S(1)}, u32[]{:S(2)}, u32[]{:S(2)}) %collective-permute-start.4) | collective-permute-done | bytes 131104 | tf_op jit(solution)/shard_map/ppermute | solution.py:217
  49.4 0.9 copy-done.2
  50.3 1.4 %shard_map.81 = bf16[16,64,128]{2,1,0:T(8,128)(2,1)} custom-call(s32[8,16]{1,0:T(8,128)S(1)} %copy-done.4, f32[8,64,128]{2,1,0:T(8,128)S(1)} %bitcast.13, f32[8,64,128]{2,1,0:T(8,128)S(1)} %copy-done.2, bf16[8,64,128]{2,1,0:T(8,128)(2,1)S(1)} %collective-permute-done.3.refs_1_, bf16[8,64,128]{2,1,0:T(8,128)(2,1)S(1)} %collective-permute-done.4.refs_2_, ...), custom_call_target="tpu_custom_call" | custom-call | tf_op jit(solution)/shard_map/pallas_call | solution.py:201
  51.8 5.5 %all-to-all-start.2 = ((bf16[8,128,128]{2,1,0:T(8,128)(2,1)}), bf16[8,128,128]{2,1,0:T(8,128)(2,1)S(1)}, u32[]{:S(2)}, u32[]{:S(2)}) async-start(bf16[8,128,128]{2,1,0:T(8,128)(2,1)} %bitcast.6), calls=%async_computation.2 | async-start | bytes 524288 | tf_op jit(solution)/shard_map/all_to_all | solution.py:213
  57.3 0.8 shard_map.82
  58.1 7.2 %all_gather.3.refs_1_ = bf16[8,256,128]{2,1,0:T(8,128)(2,1)} all-gather(bf16[8,64,128]{2,1,0:T(8,128)(2,1)S(1)} %get-tuple-element.35), channel_id=1, replica_groups=mesh['node'=8,'edge'=4] {'edge'}, dimensions={1}, use_global_device_ids=true | all-gather | bytes 655360 | tf_op jit(solution)/shard_map/all_gather | solution.py:273
  65.3 5.6 %shard_map.83 = bf16[16,64,128]{2,1,0:T(8,128)(2,1)} custom-call(bf16[8,1024,256]{2,1,0:T(8,128)(2,1)} %get-tuple-element.24.refs_0_, bf16[8,256,128]{2,1,0:T(8,128)(2,1)} %all_gather.3.refs_1_), custom_call_target="tpu_custom_call" | custom-call | flops 536870912 | bytes 4194304 | tf_op jit(solution)/shard_map/pallas_call | solution.py:201
  71.0 6.0 %all-to-all-start.3 = ((bf16[8,128,128]{2,1,0:T(8,128)(2,1)}), bf16[8,128,128]{2,1,0:T(8,128)(2,1)S(1)}, u32[]{:S(2)}, u32[]{:S(2)}) async-start(bf16[8,128,128]{2,1,0:T(8,128)(2,1)} %bitcast.21), calls=%async_computation.3 | async-start | bytes 524288 | tf_op jit(solution)/shard_map/all_to_all | solution.py:213
  77.0 5.8 %shard_map.84 = (f32[8,64,128]{2,1,0:T(8,128)}, bf16[8,64,128]{2,1,0:T(8,128)(2,1)}, bf16[8,64,128]{2,1,0:T(8,128)(2,1)}, bf16[8,64,128]{2,1,0:T(8,128)(2,1)}) custom-call(bf16[8,1024,256]{2,1,0:T(8,128)(2,1)} %get-tuple-element.24.refs_0_, bf16[16,64,128]{2,1,0:T(8,128)(2,1)} %bitcast.22), custom_call_target="tpu_custom_call" | custom-call | flops 536870912 | bytes 4194304 | tf_op jit(solution)/shard_map/pallas_call | solution.py:201
  83.6 1.1 %collective-permute-start.7 = (bf16[8,64,128]{2,1,0:T(8,128)(2,1)}, bf16[8,64,128]{2,1,0:T(8,128)(2,1)S(1)}, u32[]{:S(2)}, u32[]{:S(2)}) collective-permute-start(bf16[8,64,128]{2,1,0:T(8,128)(2,1)} %get-tuple-element.40), channel_id=1, source_target_pairs={{0,2},{1,3},{2,0},{3,1},{4,6},{5,7},{6,4},{7,5},{8,10},{9,11},{10,... | collective-permute-start | bytes 393224 | tf_op jit(solution)/shard_map/ppermute | solution.py:217
  84.8 3.8 %collective-permute-done.6.refs_1_ = bf16[8,64,128]{2,1,0:T(8,128)(2,1)S(1)} collective-permute-done((bf16[8,64,128]{2,1,0:T(8,128)(2,1)}, bf16[8,64,128]{2,1,0:T(8,128)(2,1)S(1)}, u32[]{:S(2)}, u32[]{:S(2)}) %collective-permute-start.6) | collective-permute-done | bytes 131104 | tf_op jit(solution)/shard_map/ppermute | solution.py:217
  88.6 3.1 %collective-permute-done.7.refs_2_ = bf16[8,64,128]{2,1,0:T(8,128)(2,1)S(1)} collective-permute-done((bf16[8,64,128]{2,1,0:T(8,128)(2,1)}, bf16[8,64,128]{2,1,0:T(8,128)(2,1)S(1)}, u32[]{:S(2)}, u32[]{:S(2)}) %collective-permute-start.7) | collective-permute-done | bytes 131104 | tf_op jit(solution)/shard_map/ppermute | solution.py:217
  91.7 0.9 %copy-done.3 = f32[8,64,128]{2,1,0:T(8,128)S(1)} copy-done((f32[8,64,128]{2,1,0:T(8,128)S(1)}, f32[8,64,128]{2,1,0:T(8,128)}, u32[]{:S(2)}) %copy-start.3) | copy-done | bytes 262168
  92.7 0.8 shard_map.85
  93.5 1.4 %shard_map.86 = f32[8,64,128]{2,1,0:T(8,128)} custom-call(s32[8,16]{1,0:T(8,128)S(1)} %copy-done.4, f32[8,64,128]{2,1,0:T(8,128)S(1)} %get-tuple-element.44.gradient_in, bf16[16,64,128]{2,1,0:T(8,128)(2,1)S(1)} %bitcast.15), custom_call_target="tpu_custom_call" | custom-call | tf_op jit(solution)/shard_map/pallas_call | solution.py:201
  (33 shorter events, 4.0 us)
Async XLA Ops:
  2.4 24.8 %all-to-all-start = ((bf16[8,128,128]{2,1,0:T(8,128)(2,1)}), bf16[8,128,128]{2,1,0:T(8,128)(2,1)S(1)}, u32[]{:S(2)}, u32[]{:S(2)}) async-start(bf16[8,128,128]{2,1,0:T(8,128)(2,1)} %bitcast.24), calls=%async_computation | async-start | bytes 524288 | tf_op jit(solution)/shard_map/all_to_all | solution.py:213
  9.7 8.4 %collective-permute-start.2 = (bf16[8,64,128]{2,1,0:T(8,128)(2,1)}, bf16[8,64,128]{2,1,0:T(8,128)(2,1)S(1)}, u32[]{:S(2)}, u32[]{:S(2)}) collective-permute-start(bf16[8,64,128]{2,1,0:T(8,128)(2,1)} %get-tuple-element.26.refs_2_), channel_id=1, source_target_pairs={{0,3},{1,2},{2,1},{3,0},{4,7},{5,6},{6,5},{7,4},{8,11},{9,10},{10,... | collective-permute-start | bytes 393224 | tf_op jit(solution)/shard_map/ppermute | solution.py:217
  10.4 8.1 %collective-permute-start.1 = (bf16[8,64,128]{2,1,0:T(8,128)(2,1)}, bf16[8,64,128]{2,1,0:T(8,128)(2,1)S(1)}, u32[]{:S(2)}, u32[]{:S(2)}) collective-permute-start(bf16[8,64,128]{2,1,0:T(8,128)(2,1)} %get-tuple-element.26.refs_2_), channel_id=1, source_target_pairs={{0,2},{1,3},{2,0},{3,1},{4,6},{5,7},{6,4},{7,5},{8,10},{9,11},{10,... | collective-permute-start | bytes 393224 | tf_op jit(solution)/shard_map/ppermute | solution.py:217
  11.3 7.2 %collective-permute-start = (bf16[8,64,128]{2,1,0:T(8,128)(2,1)}, bf16[8,64,128]{2,1,0:T(8,128)(2,1)S(1)}, u32[]{:S(2)}, u32[]{:S(2)}) collective-permute-start(bf16[8,64,128]{2,1,0:T(8,128)(2,1)} %get-tuple-element.26.refs_2_), channel_id=1, source_target_pairs={{0,1},{1,0},{2,3},{3,2},{4,5},{5,4},{6,7},{7,6},{8,9},{9,8},{10,11... | collective-permute-start | bytes 393224 | tf_op jit(solution)/shard_map/ppermute | solution.py:217
  18.1 0.7 copy-start.7
  18.5 0.7 copy-start.8
  18.5 0.7 copy-start.9
  27.2 6.0 %copy-start.5 = (bf16[8,128,128]{2,1,0:T(8,128)(2,1)}, bf16[8,128,128]{2,1,0:T(8,128)(2,1)S(1)}, u32[]{:S(2)}) copy-start(bf16[8,128,128]{2,1,0:T(8,128)(2,1)S(1)} %all-to-all-done) | copy-start | bytes 786436
  27.3 24.5 %all-to-all-start.1 = ((bf16[8,128,128]{2,1,0:T(8,128)(2,1)}), bf16[8,128,128]{2,1,0:T(8,128)(2,1)S(1)}, u32[]{:S(2)}, u32[]{:S(2)}) async-start(bf16[8,128,128]{2,1,0:T(8,128)(2,1)} %bitcast.19), calls=%async_computation.1 | async-start | bytes 524288 | tf_op jit(solution)/shard_map/all_to_all | solution.py:213
  33.3 16.1 %copy-start = (f32[512,128]{1,0:T(8,128)S(1)}, f32[512,128]{1,0:T(8,128)}, u32[]{:S(2)}) copy-start(f32[512,128]{1,0:T(8,128)} %param.6) | copy-start | bytes 786436
  33.3 16.1 %copy-start.4 = (s32[8,16]{1,0:T(8,128)S(1)}, s32[8,16]{1,0:T(8,128)}, u32[]{:S(2)}) copy-start(s32[8,16]{1,0:T(8,128)} %table.7) | copy-start | bytes 1540
  33.3 24.0 %copy-start.1 = (f32[512,128]{1,0:T(8,128)S(1)}, f32[512,128]{1,0:T(8,128)}, u32[]{:S(2)}) copy-start(f32[512,128]{1,0:T(8,128)} %param.7) | copy-start | bytes 786436
  40.5 6.1 %collective-permute-start.3 = (bf16[8,64,128]{2,1,0:T(8,128)(2,1)}, bf16[8,64,128]{2,1,0:T(8,128)(2,1)S(1)}, u32[]{:S(2)}, u32[]{:S(2)}) collective-permute-start(bf16[8,64,128]{2,1,0:T(8,128)(2,1)} %get-tuple-element.30), channel_id=1, source_target_pairs={{0,3},{1,2},{2,1},{3,0},{4,7},{5,6},{6,5},{7,4},{8,11},{9,10},{10,... | collective-permute-start | bytes 393224 | tf_op jit(solution)/shard_map/ppermute | solution.py:217
  41.2 8.2 %collective-permute-start.4 = (bf16[8,64,128]{2,1,0:T(8,128)(2,1)}, bf16[8,64,128]{2,1,0:T(8,128)(2,1)S(1)}, u32[]{:S(2)}, u32[]{:S(2)}) collective-permute-start(bf16[8,64,128]{2,1,0:T(8,128)(2,1)} %get-tuple-element.31), channel_id=1, source_target_pairs={{0,2},{1,3},{2,0},{3,1},{4,6},{5,7},{6,4},{7,5},{8,10},{9,11},{10,... | collective-permute-start | bytes 393224 | tf_op jit(solution)/shard_map/ppermute | solution.py:217
  42.0 7.3 %collective-permute-start.5 = (bf16[8,64,128]{2,1,0:T(8,128)(2,1)}, bf16[8,64,128]{2,1,0:T(8,128)(2,1)S(1)}, u32[]{:S(2)}, u32[]{:S(2)}) collective-permute-start(bf16[8,64,128]{2,1,0:T(8,128)(2,1)} %get-tuple-element.32), channel_id=1, source_target_pairs={{0,1},{1,0},{2,3},{3,2},{4,5},{5,4},{6,7},{7,6},{8,9},{9,8},{10,11... | collective-permute-start | bytes 393224 | tf_op jit(solution)/shard_map/ppermute | solution.py:217
  49.4 1.0 %copy-start.2 = (f32[8,64,128]{2,1,0:T(8,128)S(1)}, f32[8,64,128]{2,1,0:T(8,128)}, u32[]{:S(2)}) copy-start(f32[8,64,128]{2,1,0:T(8,128)} %get-tuple-element.29.refs_0_) | copy-start | bytes 786436
  51.8 19.2 %all-to-all-start.2 = ((bf16[8,128,128]{2,1,0:T(8,128)(2,1)}), bf16[8,128,128]{2,1,0:T(8,128)(2,1)S(1)}, u32[]{:S(2)}, u32[]{:S(2)}) async-start(bf16[8,128,128]{2,1,0:T(8,128)(2,1)} %bitcast.6), calls=%async_computation.2 | async-start | bytes 524288 | tf_op jit(solution)/shard_map/all_to_all | solution.py:213
  71.0 6.0 %copy-start.6 = (bf16[8,128,128]{2,1,0:T(8,128)(2,1)}, bf16[8,128,128]{2,1,0:T(8,128)(2,1)S(1)}, u32[]{:S(2)}) copy-start(bf16[8,128,128]{2,1,0:T(8,128)(2,1)S(1)} %all-to-all-done.2) | copy-start | bytes 786436
  71.0 22.5 %all-to-all-start.3 = ((bf16[8,128,128]{2,1,0:T(8,128)(2,1)}), bf16[8,128,128]{2,1,0:T(8,128)(2,1)S(1)}, u32[]{:S(2)}, u32[]{:S(2)}) async-start(bf16[8,128,128]{2,1,0:T(8,128)(2,1)} %bitcast.21), calls=%async_computation.3 | async-start | bytes 524288 | tf_op jit(solution)/shard_map/all_to_all | solution.py:213
  82.8 5.8 %collective-permute-start.6 = (bf16[8,64,128]{2,1,0:T(8,128)(2,1)}, bf16[8,64,128]{2,1,0:T(8,128)(2,1)S(1)}, u32[]{:S(2)}, u32[]{:S(2)}) collective-permute-start(bf16[8,64,128]{2,1,0:T(8,128)(2,1)} %get-tuple-element.39), channel_id=1, source_target_pairs={{0,3},{1,2},{2,1},{3,0},{4,7},{5,6},{6,5},{7,4},{8,11},{9,10},{10,... | collective-permute-start | bytes 393224 | tf_op jit(solution)/shard_map/ppermute | solution.py:217
  83.6 8.1 %collective-permute-start.7 = (bf16[8,64,128]{2,1,0:T(8,128)(2,1)}, bf16[8,64,128]{2,1,0:T(8,128)(2,1)S(1)}, u32[]{:S(2)}, u32[]{:S(2)}) collective-permute-start(bf16[8,64,128]{2,1,0:T(8,128)(2,1)} %get-tuple-element.40), channel_id=1, source_target_pairs={{0,2},{1,3},{2,0},{3,1},{4,6},{5,7},{6,4},{7,5},{8,10},{9,11},{10,... | collective-permute-start | bytes 393224 | tf_op jit(solution)/shard_map/ppermute | solution.py:217
  84.6 7.1 %collective-permute-start.8 = (bf16[8,64,128]{2,1,0:T(8,128)(2,1)}, bf16[8,64,128]{2,1,0:T(8,128)(2,1)S(1)}, u32[]{:S(2)}, u32[]{:S(2)}) collective-permute-start(bf16[8,64,128]{2,1,0:T(8,128)(2,1)} %get-tuple-element.41), channel_id=1, source_target_pairs={{0,1},{1,0},{2,3},{3,2},{4,5},{5,4},{6,7},{7,6},{8,9},{9,8},{10,11... | collective-permute-start | bytes 393224 | tf_op jit(solution)/shard_map/ppermute | solution.py:217
  91.7 1.0 %copy-start.3 = (f32[8,64,128]{2,1,0:T(8,128)S(1)}, f32[8,64,128]{2,1,0:T(8,128)}, u32[]{:S(2)}) copy-start(f32[8,64,128]{2,1,0:T(8,128)} %get-tuple-element.38.refs_0_) | copy-start | bytes 786436

commit v5 on v2

--- a/solution.py
+++ b/solution.py
@@ -28,13 +28,20 @@
     return lax.axis_index(axis) ^ turn
 
 
-def requested(table, slot):
-    column = lax.axis_index("node") * CAP + slot % CAP
-    return jnp.maximum(table[slot // CAP, column], 0)
+def requested(table, turn, slot):
+    column = lax.axis_index("node") * CAP + slot
+    return jnp.maximum(table[partner("node", turn), column], 0)
+
+
+def fill(sends, block):
+    for low, send in enumerate(sends):
+        for turn in range(send.shape[0]):
+            for slot in range(CAP):
+                send[turn, slot] = block(2 * turn + low, slot).astype(send.dtype)
 
 
 def start_kernel(table, teleport, cotangent, *refs):
-    send, rounded, plan, state, adjoint, sems = refs
+    *sends, rounded, plan, state, adjoint, sems = refs
     copies = [
         pltpu.make_async_copy(source, target, sems.at[index])
         for index, (source, target) in enumerate(
@@ -45,8 +52,7 @@
         copy.start()
     copies[0].wait()
     copies[1].wait()
-    for slot in range(send.shape[0]):
-        send[slot] = state[requested(plan, slot)].astype(LOW)
+    fill(sends, lambda turn, slot: state[requested(plan, turn, slot)])
     copies[2].wait()
     rounded[...] = adjoint[...].astype(LOW)
 
@@ -79,12 +85,30 @@
             low[place] = (value - rounded.astype(FULL)).astype(LOW)
 
 
-def forward_kernel(operators, columns, *refs):
+def pair_kernel(kept, got, *pairs):
+    for turn, pair in enumerate(pairs, 1):
+        pair[0] = kept[turn]
+        pair[1] = got[turn]
+
+
+def by_turn(parts):
+    kept, got, *pairs = parts
+    yield 0, kept.at[0]
+    yield 1, got.at[0]
+    for turn, pair in enumerate(pairs, 1):
+        yield 2 * turn, pair.at[0]
+        yield 2 * turn + 1, pair.at[1]
+
+
+def forward_kernel(operators, *refs):
     dense = refs[:operators]
-    *partials, product = refs[operators:]
+    parts = refs[operators : operators + 1 + refs[operators].shape[0]]
+    *partials, source, product = refs[operators + len(parts) :]
     quarters, quarter, hidden = product.shape
     width = quarters * quarter
-    vectors = columns[...].reshape(-1, hidden)
+    for turn, part in by_turn(parts):
+        source[partner("node", turn)] = part[...]
+    vectors = source[...].reshape(-1, hidden)
     for row in range(partials[0].shape[0]):
         summed = sum(
             lax.dot_general(
@@ -96,17 +120,19 @@
             for part in dense
         )
         product[...] = summed.T.reshape(product.shape)
-        for turn, partial in enumerate(partials):
+        for turn, partial in zip((0, *range(quarters - 1, 0, -1)), partials):
             partial[row] = product[partner("edge", turn)].astype(partial.dtype)
 
 
 def adjoint_kernel(operators, *refs):
-    *arrived, send, source = refs[operators:]
+    *arrived, kept, away, source, product = refs[operators:]
     for turn, part in enumerate(arrived):
         source[:, partner("edge", turn)] = part[...]
     vectors = source[...].reshape(-1, source.shape[-1])
-    product = sum(jnp.dot(part[...], vectors, preferred_element_type=FULL) for part in refs[:operators])
-    send[...] = product.reshape(send.shape).astype(LOW)
+    product[...] = sum(
+        jnp.dot(part[...], vectors, preferred_element_type=FULL) for part in refs[:operators]
+    ).reshape(product.shape)
+    fill((kept, away), lambda turn, slot: product[partner("node", turn), slot])
 
 
 def state_of(arrived, teleport):
@@ -117,10 +143,9 @@
 
 
 def next_state_kernel(table, teleport, *refs):
-    *arrived, send, state = refs
+    *arrived, kept, away, state = refs
     state[...] = state_of(arrived, teleport)
-    for slot in range(send.shape[0]):
-        send[slot] = state[requested(table, slot)].astype(LOW)
+    fill((kept, away), lambda turn, slot: state[requested(table, turn, slot)])
 
 
 def last_state_kernel(teleport, *refs):
@@ -128,21 +153,24 @@
     state[...] = state_of(arrived, teleport)
 
 
-def gather_adjoint(table, arrived, summed):
+def gather_adjoint(table, parts, summed):
     summed[...] = jnp.zeros_like(summed)
-    for slot in range(arrived.shape[0]):
-        summed[requested(table, slot)] += arrived[slot].astype(FULL)
-
-
-def next_adjoint_kernel(table, cotangent, arrived, gradient, rounded, summed):
-    gather_adjoint(table, arrived, summed)
+    for turn, part in by_turn(parts):
+        for slot in range(CAP):
+            summed[requested(table, turn, slot)] += part[slot].astype(FULL)
+
+
+def next_adjoint_kernel(table, cotangent, *refs):
+    *parts, gradient, rounded, summed = refs
+    gather_adjoint(table, parts, summed)
     adjoint = 0.9 * summed[...]
     gradient[...] = 0.1 * cotangent[...] + 0.1 * adjoint
     rounded[...] = adjoint.astype(LOW)
 
 
-def last_adjoint_kernel(table, gradient_in, arrived, gradient, summed):
-    gather_adjoint(table, arrived, summed)
+def last_adjoint_kernel(table, gradient_in, *refs):
+    *parts, gradient, summed = refs
+    gather_adjoint(table, parts, summed)
     gradient[...] = gradient_in[...] + 0.9 * summed[...]
 
 
@@ -152,8 +180,10 @@
     count = row_count // quarter
     quarters = lax.axis_size("edge")
     slot_total = fetch_table.shape[1]
+    owners = lax.axis_size("node")
     shape = (count, quarter, hidden)
-    slot_shape = (slot_total, quarter, hidden)
+    half_shape = (owners // 2, CAP, quarter, hidden)
+    pair_shape = (2, CAP, quarter, hidden)
     teleport = teleport.reshape(shape)
     cotangent = cotangent.reshape(shape)
 
@@ -168,20 +198,34 @@
             cost_estimate=cost,
         )(*operands)
 
-    def over_node(array):
-        return lax.all_to_all(array, "node", 0, 0, tiled=True)
-
-    def over_edge(arrays):
+    def after(arrays, others):
+        return lax.optimization_barrier((tuple(arrays), tuple(others)))[0]
+
+    def to_node(array, turn):
+        return lax.ppermute(array, "node", [(place, place ^ turn) for place in range(owners)])
+
+    def over_node(kept, got):
+        pairs = call(
+            pair_kernel,
+            (kept, got),
+            [VMEM] * 2,
+            [(pair_shape, LOW)] * (owners // 2 - 1),
+            [],
+        )
+        moved = [to_node(pair, 2 * turn) for turn, pair in enumerate(pairs, 1)]
+        return (kept, got, *moved), pairs
+
+    def over_edge(arrays, turns):
         return [arrays[0]] + [
-            lax.ppermute(arrays[turn], "edge", [(place, place ^ turn) for place in range(quarters)])
-            for turn in range(1, quarters)
+            lax.ppermute(array, "edge", [(place, place ^ turn) for place in range(quarters)])
+            for turn, array in zip(turns, arrays[1:])
         ]
 
-    send, rounded = call(
+    kept, away, rounded = call(
         start_kernel,
         (fetch_table, teleport, cotangent),
         [HBM] * 3,
-        [(slot_shape, LOW), (shape, LOW)],
+        [(half_shape, LOW)] * 2 + [(shape, LOW)],
         [
             pltpu.SMEM(fetch_table.shape, fetch_table.dtype),
             pltpu.VMEM(shape, FULL),
@@ -190,6 +234,9 @@
         ],
         START_MEBIBYTES,
     )
+    got = to_node(away, 1)
+    columns, pairs = over_node(kept, got)
+    block_row, block_slot = after((block_row, block_slot), pairs)
     dense_shape = (slot_total * quarter, count * width)
     parts = next(size for size in (12, 8, 4, 2, 1) if block_count % size == 0)
     high, low = call(
@@ -215,41 +262,52 @@
             bytes_accessed=len(dense) * high.size * 2,
             transcendentals=0,
         )
-        columns = over_node(send)
-        arrived = over_edge([rounded] * quarters)
-        (transposed,) = call(
+        arrived = over_edge([rounded] * quarters, range(1, quarters))
+        if step > 0:
+            got = to_node(away, 1)
+            (got,) = after((got,), (rounded,))
+            columns, _ = over_node(kept, got)
+        kept_sums, away_sums = call(
             functools.partial(adjoint_kernel, len(dense)),
             (*dense, *arrived),
             [VMEM] * (quarters + len(dense)),
-            [(slot_shape, LOW)],
-            [pltpu.VMEM((count, quarters, quarter, hidden), LOW)],
+            [(half_shape, LOW)] * 2,
+            [
+                pltpu.VMEM((count, quarters, quarter, hidden), LOW),
+                pltpu.VMEM((owners, CAP, quarter, hidden), FULL),
+            ],
             cost=cost,
         )
-        transposed, columns = lax.optimization_barrier((transposed, columns))
+        got_sums = to_node(away_sums, 1)
+        columns = after(columns, (away_sums,))
         partials = call(
             functools.partial(forward_kernel, len(dense)),
-            (columns, *dense),
-            [VMEM] * (1 + len(dense)),
+            (*dense, *columns),
+            [VMEM] * (len(columns) + len(dense)),
             [(shape, FULL)] + [(shape, LOW)] * (quarters - 1),
-            [pltpu.VMEM((quarters, quarter, hidden), FULL)],
+            [
+                pltpu.VMEM((owners, CAP, quarter, hidden), LOW),
+                pltpu.VMEM((quarters, quarter, hidden), FULL),
+            ],
             cost=cost,
         )
-        transposed = over_node(transposed)
-        partials = over_edge(partials)
+        (got_sums,) = after((got_sums,), partials[1:])
+        transposed, _ = over_node(kept_sums, got_sums)
+        partials = over_edge(partials, range(quarters - 1, 0, -1))
         total = [pltpu.VMEM(shape, FULL)]
         if not last:
-            (send,) = call(
+            kept, away = call(
                 next_state_kernel,
                 (fetch_table, teleport, *partials),
                 [SMEM] + [VMEM] * (1 + quarters),
-                [(slot_shape, LOW)],
+                [(half_shape, LOW)] * 2,
                 total,
             )
-            send, transposed = lax.optimization_barrier((send, transposed))
+            transposed = after(transposed, (away,))
             gradient, rounded = call(
                 next_adjoint_kernel,
-                (fetch_table, gradient, transposed),
-                [SMEM, VMEM, VMEM],
+                (fetch_table, gradient, *transposed),
+                [SMEM] + [VMEM] * (1 + len(transposed)),
                 [(shape, FULL), (shape, LOW)],
                 total,
             )
@@ -261,11 +319,11 @@
                 [(shape, FULL)],
                 [],
             )
-            state, transposed = lax.optimization_barrier((state, transposed))
+            transposed = after(transposed, (state,))
             (gradient,) = call(
                 last_adjoint_kernel,
-                (fetch_table, gradient, transposed),
-                [SMEM, VMEM, VMEM],
+                (fetch_table, gradient, *transposed),
+                [SMEM] + [VMEM] * (1 + len(transposed)),
                 [(shape, FULL)],
                 total,
             )

time: 87.3 us -> 67.1 us (0.77)
  local copies, waits for them, and re-layouts: 14.1 us -> 2.29 us
  waiting for transfers between devices: 20.4 us -> 14.5 us
  Pallas kernels: 18.5 us -> 16.5 us
    all_to_all x4 -> x0, starting transfers between devices: 25.2 us -> none  [over_node(): return lax.all_to_all(array, 'node', 0, 0, tiled=True)]
    ppermute x12 -> x28, starting transfers between devices: 7.65 us -> 32.7 us  [the longest x16 25.1 us: to_node(): lax.ppermute(array, 'node', [(place, place ^ turn) for place in range(own...]
    unnamed x24 -> x16, local copies, waits for them, and re-layouts: 14.1 us -> 2.29 us
    ppermute x12 -> x28, waiting for transfers between devices: 20.4 us -> 14.5 us  [the longest x16 8.12 us: to_node(): lax.ppermute(array, 'node', [(place, place ^ turn) for place in range(own...]
    pallas_call x10 -> x14, Pallas kernels: 18.5 us -> 16.5 us  [call(): pl.pallas_call(kernel, out_shape=[jax.ShapeDtypeStruct(*out) for out in o...]
  transfers between devices with their start and end apart: 16 -> 28, of which waited for: 7 -> 13; matrix products, arithmetic and copies ran while one was open for 0% -> 0% of each run, Pallas kernels for 18% -> 20%
where the time goes in v5:
time: 67.1 us; the launch traced here: 66.9 us
  starting transfers between devices  32.7 us (49%)
  Pallas kernels  16.5 us (25%)
  waiting for transfers between devices  14.5 us (22%)
  local copies, waits for them, and re-layouts  2.29 us (3%)
  between operations  0.85 us (1%)
    ppermute x16, starting transfers between devices, to_node(): lax.ppermute(array, 'node', [(place, place ^ turn) for place in range(own...  25.1 us
    pallas_call x14, Pallas kernels, call(): pl.pallas_call(kernel, out_shape=[jax.ShapeDtypeStruct(*out) for out in o...  16.5 us
    ppermute x16, waiting for transfers between devices, to_node(): lax.ppermute(array, 'node', [(place, place ^ turn) for place in range(own...  8.12 us
    ppermute x12, starting transfers between devices, over_edge(): lax.ppermute(array, 'edge', [(place, place ^ turn) for place in range(qua...  7.64 us
    ppermute x12, waiting for transfers between devices, over_edge(): lax.ppermute(array, 'edge', [(place, place ^ turn) for place in range(qua...  6.4 us
    unnamed x16, local copies, waits for them, and re-layouts  2.29 us
  transfers between devices with their start and end apart: 28, of which 13 were waited for; matrix products, arithmetic and copies ran while one was open for 0% of the time, Pallas kernels for 20%

profile of v5, /device:TPU:0, one launch (start us, length us, event | category | flops | bytes accessed | tf_op | source)
XLA Modules:
  0.0 66.9 jit_solution(752654676442112583)
XLA Ops:
  0.6 1.8 %shard_map.77 = (bf16[4,2,64,128]{3,2,1,0:T(8,128)(2,1)}, bf16[4,2,64,128]{3,2,1,0:T(8,128)(2,1)}, bf16[8,64,128]{2,1,0:T(8,128)(2,1)}) custom-call(s32[8,16]{1,0:T(8,128)} %table.7, f32[8,64,128]{2,1,0:T(8,128)} %bitcast.4, f32[8,64,128]{2,1,0:T(8,128)} %bitcast.7), custom_call_target="tpu_custom_call" | custom-call | tf_op jit(solution)/shard_map/pallas_call | solution.py:191
  2.4 3.0 %collective-permute-start = (bf16[4,2,64,128]{3,2,1,0:T(8,128)(2,1)}, bf16[4,2,64,128]{3,2,1,0:T(8,128)(2,1)S(1)}, u32[]{:S(2)}, u32[]{:S(2)}) collective-permute-start(bf16[4,2,64,128]{3,2,1,0:T(8,128)(2,1)} %get-tuple-element.61), channel_id=1, source_target_pairs={{0,4},{4,0},{8,12},{12,8},{16,20},{20,16},{24,28},{28,24},{1,5},{5... | collective-permute-start | bytes 393224 | tf_op jit(solution)/shard_map/ppermute | solution.py:205
  7.3 1.8 %collective-permute-done.got.refs_3_ = bf16[4,2,64,128]{3,2,1,0:T(8,128)(2,1)S(1)} collective-permute-done((bf16[4,2,64,128]{3,2,1,0:T(8,128)(2,1)}, bf16[4,2,64,128]{3,2,1,0:T(8,128)(2,1)S(1)}, u32[]{:S(2)}, u32[]{:S(2)}) %collective-permute-start) | collective-permute-done | bytes 131104 | tf_op jit(solution)/shard_map/ppermute | solution.py:205
  10.1 1.9 %collective-permute-start.1 = (bf16[2,2,64,128]{3,2,1,0:T(8,128)(2,1)S(1)}, bf16[2,2,64,128]{3,2,1,0:T(8,128)(2,1)S(1)}, u32[]{:S(2)}, u32[]{:S(2)}) collective-permute-start(bf16[2,2,64,128]{3,2,1,0:T(8,128)(2,1)S(1)} %get-tuple-element.62), channel_id=1, source_target_pairs={{0,8},{4,12},{8,0},{12,4},{16,24},{20,28},{24,16},{28,20},{1,9},{5... | collective-permute-start | bytes 196616 | tf_op jit(solution)/shard_map/ppermute | solution.py:205
  12.0 2.6 %collective-permute-start.2 = (bf16[2,2,64,128]{3,2,1,0:T(8,128)(2,1)S(1)}, bf16[2,2,64,128]{3,2,1,0:T(8,128)(2,1)S(1)}, u32[]{:S(2)}, u32[]{:S(2)}) collective-permute-start(bf16[2,2,64,128]{3,2,1,0:T(8,128)(2,1)S(1)} %get-tuple-element.63), channel_id=1, source_target_pairs={{0,16},{4,20},{8,24},{12,28},{16,0},{20,4},{24,8},{28,12},{1,17},{... | collective-permute-start | bytes 196616 | tf_op jit(solution)/shard_map/ppermute | solution.py:205
  15.9 4.7 %shard_map.79 = (bf16[1024,2048]{1,0:T(8,128)(2,1)S(1)}, bf16[1024,2048]{1,0:T(8,128)(2,1)S(1)}) custom-call(s32[1,192]{1,0:T(1,128)S(1)} %copy-done.6, s32[1,192]{1,0:T(1,128)S(1)} %copy-done.7, bf16[1,192,64,256]{3,2,1,0:T(8,128)(2,1)} %weights.1), custom_call_target="tpu_custom_call" | custom-call | bytes 6291456 | tf_op jit(solution)/shard_map/pallas_call | solution.py:191
  20.8 2.4 %shard_map.80 = (bf16[4,2,64,128]{3,2,1,0:T(8,128)(2,1)S(1)}, bf16[4,2,64,128]{3,2,1,0:T(8,128)(2,1)S(1)}) custom-call(bf16[1024,2048]{1,0:T(8,128)(2,1)S(1)} %get-tuple-element.67.refs_0_, bf16[1024,2048]{1,0:T(8,128)(2,1)S(1)} %get-tuple-element.68.refs_1_, bf16[8,64,128]{2,1,0:T(8,128)(2,1)S(1)} %copy-done.4, ...), custom_call_target="tpu_custom_call" | custom-call | flops 1073741824 | bytes 8388608 | tf_op jit(solution)/shard_map/pallas_call | solution.py:191
  23.2 1.7 %collective-permute-start.11 = (bf16[4,2,64,128]{3,2,1,0:T(8,128)(2,1)S(1)}, bf16[4,2,64,128]{3,2,1,0:T(8,128)(2,1)S(1)}, u32[]{:S(2)}, u32[]{:S(2)}) collective-permute-start(bf16[4,2,64,128]{3,2,1,0:T(8,128)(2,1)S(1)} %get-tuple-element.70), channel_id=1, source_target_pairs={{0,4},{4,0},{8,12},{12,8},{16,20},{20,16},{24,28},{28,24},{1,5},{5... | collective-permute-start | bytes 393224 | tf_op jit(solution)/shard_map/ppermute | solution.py:205
  25.0 1.8 %collective-permute-done.3.refs_6_ = bf16[2,2,64,128]{3,2,1,0:T(8,128)(2,1)S(1)} collective-permute-done((bf16[2,2,64,128]{3,2,1,0:T(8,128)(2,1)S(1)}, bf16[2,2,64,128]{3,2,1,0:T(8,128)(2,1)S(1)}, u32[]{:S(2)}, u32[]{:S(2)}) %collective-permute-start.3) | collective-permute-done | bytes 65568 | tf_op jit(solution)/shard_map/ppermute | solution.py:205
  26.8 1.5 %shard_map.81 = (f32[8,64,128]{2,1,0:T(8,128)S(1)}, bf16[8,64,128]{2,1,0:T(8,128)(2,1)S(1)}, bf16[8,64,128]{2,1,0:T(8,128)(2,1)S(1)}, bf16[8,64,128]{2,1,0:T(8,128)(2,1)S(1)}) custom-call(bf16[1024,2048]{1,0:T(8,128)(2,1)S(1)} %get-tuple-element.67.refs_0_, bf16[1024,2048]{1,0:T(8,128)(2,1)S(1)} %get-tuple-element.68.refs_1_, ...), custom_call_target="tpu_custom_call" | custom-call | flops 1073741824 | bytes 8388608 | tf_op jit(solution)/shard_map/pallas_call | solution.py:191
  28.4 1.6 %collective-permute-start.8 = (bf16[8,64,128]{2,1,0:T(8,128)(2,1)S(1)}, bf16[8,64,128]{2,1,0:T(8,128)(2,1)S(1)}, u32[]{:S(2)}, u32[]{:S(2)}) collective-permute-start(bf16[8,64,128]{2,1,0:T(8,128)(2,1)S(1)} %get-tuple-element.78), channel_id=1, source_target_pairs={{0,2},{1,3},{2,0},{3,1},{4,6},{5,7},{6,4},{7,5},{8,10},{9,11},{10,... | collective-permute-start | bytes 393224 | tf_op jit(solution)/shard_map/ppermute | solution.py:220
  30.3 2.4 %collective-permute-start.13 = (bf16[2,2,64,128]{3,2,1,0:T(8,128)(2,1)S(1)}, bf16[2,2,64,128]{3,2,1,0:T(8,128)(2,1)S(1)}, u32[]{:S(2)}, u32[]{:S(2)}) collective-permute-start(bf16[2,2,64,128]{3,2,1,0:T(8,128)(2,1)S(1)} %get-tuple-element.85), channel_id=1, source_target_pairs={{0,16},{4,20},{8,24},{12,28},{16,0},{20,4},{24,8},{28,12},{1,17},{... | collective-permute-start | bytes 196616 | tf_op jit(solution)/shard_map/ppermute | solution.py:205
  32.7 1.4 %collective-permute-done.7.refs_1_ = bf16[8,64,128]{2,1,0:T(8,128)(2,1)S(1)} collective-permute-done((bf16[8,64,128]{2,1,0:T(8,128)(2,1)S(1)}, bf16[8,64,128]{2,1,0:T(8,128)(2,1)S(1)}, u32[]{:S(2)}, u32[]{:S(2)}) %collective-permute-start.7) | collective-permute-done | bytes 131104 | tf_op jit(solution)/shard_map/ppermute | solution.py:220
  34.1 1.8 %collective-permute-start.14 = (bf16[2,2,64,128]{3,2,1,0:T(8,128)(2,1)S(1)}, bf16[2,2,64,128]{3,2,1,0:T(8,128)(2,1)S(1)}, u32[]{:S(2)}, u32[]{:S(2)}) collective-permute-start(bf16[2,2,64,128]{3,2,1,0:T(8,128)(2,1)S(1)} %get-tuple-element.86), channel_id=1, source_target_pairs={{0,24},{4,28},{8,16},{12,20},{16,8},{20,12},{24,0},{28,4},{1,25},{... | collective-permute-start | bytes 196616 | tf_op jit(solution)/shard_map/ppermute | solution.py:205
  37.7 1.6 %collective-permute-start.10 = (bf16[4,2,64,128]{3,2,1,0:T(8,128)(2,1)S(1)}, bf16[4,2,64,128]{3,2,1,0:T(8,128)(2,1)S(1)}, u32[]{:S(2)}, u32[]{:S(2)}) collective-permute-start(bf16[4,2,64,128]{3,2,1,0:T(8,128)(2,1)S(1)} %get-tuple-element.81), channel_id=1, source_target_pairs={{0,4},{4,0},{8,12},{12,8},{16,20},{20,16},{24,28},{28,24},{1,5},{5... | collective-permute-start | bytes 393224 | tf_op jit(solution)/shard_map/ppermute | solution.py:205
  41.0 1.6 %collective-permute-start.19 = (bf16[8,64,128]{2,1,0:T(8,128)(2,1)S(1)}, bf16[8,64,128]{2,1,0:T(8,128)(2,1)S(1)}, u32[]{:S(2)}, u32[]{:S(2)}) collective-permute-start(bf16[8,64,128]{2,1,0:T(8,128)(2,1)S(1)} %get-tuple-element.92.refs_1_), channel_id=1, source_target_pairs={{0,2},{1,3},{2,0},{3,1},{4,6},{5,7},{6,4},{7,5},{8,10},{9,11},{10,... | collective-permute-start | bytes 393224 | tf_op jit(solution)/shard_map/ppermute | solution.py:220
  43.3 2.4 %collective-permute-start.16 = (bf16[2,2,64,128]{3,2,1,0:T(8,128)(2,1)S(1)}, bf16[2,2,64,128]{3,2,1,0:T(8,128)(2,1)S(1)}, u32[]{:S(2)}, u32[]{:S(2)}) collective-permute-start(bf16[2,2,64,128]{3,2,1,0:T(8,128)(2,1)S(1)} %get-tuple-element.95), channel_id=1, source_target_pairs={{0,16},{4,20},{8,24},{12,28},{16,0},{20,4},{24,8},{28,12},{1,17},{... | collective-permute-start | bytes 196616 | tf_op jit(solution)/shard_map/ppermute | solution.py:205
  46.7 1.8 %collective-permute-start.17 = (bf16[2,2,64,128]{3,2,1,0:T(8,128)(2,1)S(1)}, bf16[2,2,64,128]{3,2,1,0:T(8,128)(2,1)S(1)}, u32[]{:S(2)}, u32[]{:S(2)}) collective-permute-start(bf16[2,2,64,128]{3,2,1,0:T(8,128)(2,1)S(1)} %get-tuple-element.96), channel_id=1, source_target_pairs={{0,24},{4,28},{8,16},{12,20},{16,8},{20,12},{24,0},{28,4},{1,25},{... | collective-permute-start | bytes 196616 | tf_op jit(solution)/shard_map/ppermute | solution.py:205
  50.9 1.5 %collective-permute-start.24 = (bf16[4,2,64,128]{3,2,1,0:T(8,128)(2,1)S(1)}, bf16[4,2,64,128]{3,2,1,0:T(8,128)(2,1)S(1)}, u32[]{:S(2)}, u32[]{:S(2)}) collective-permute-start(bf16[4,2,64,128]{3,2,1,0:T(8,128)(2,1)S(1)} %get-tuple-element.97), channel_id=1, source_target_pairs={{0,4},{4,0},{8,12},{12,8},{16,20},{20,16},{24,28},{28,24},{1,5},{5... | collective-permute-start | bytes 393224 | tf_op jit(solution)/shard_map/ppermute | solution.py:205
  53.8 1.7 %collective-permute-start.22 = (bf16[8,64,128]{2,1,0:T(8,128)(2,1)S(1)}, bf16[8,64,128]{2,1,0:T(8,128)(2,1)S(1)}, u32[]{:S(2)}, u32[]{:S(2)}) collective-permute-start(bf16[8,64,128]{2,1,0:T(8,128)(2,1)S(1)} %get-tuple-element.105), channel_id=1, source_target_pairs={{0,2},{1,3},{2,0},{3,1},{4,6},{5,7},{6,4},{7,5},{8,10},{9,11},{10,... | collective-permute-start | bytes 393224 | tf_op jit(solution)/shard_map/ppermute | solution.py:220
  56.5 2.3 %collective-permute-start.26 = (bf16[2,2,64,128]{3,2,1,0:T(8,128)(2,1)S(1)}, bf16[2,2,64,128]{3,2,1,0:T(8,128)(2,1)S(1)}, u32[]{:S(2)}, u32[]{:S(2)}) collective-permute-start(bf16[2,2,64,128]{3,2,1,0:T(8,128)(2,1)S(1)} %get-tuple-element.111), channel_id=1, source_target_pairs={{0,16},{4,20},{8,24},{12,28},{16,0},{20,4},{24,8},{28,12},{1,17},{... | collective-permute-start | bytes 196616 | tf_op jit(solution)/shard_map/ppermute | solution.py:205
  59.4 1.8 %collective-permute-start.27 = (bf16[2,2,64,128]{3,2,1,0:T(8,128)(2,1)S(1)}, bf16[2,2,64,128]{3,2,1,0:T(8,128)(2,1)S(1)}, u32[]{:S(2)}, u32[]{:S(2)}) collective-permute-start(bf16[2,2,64,128]{3,2,1,0:T(8,128)(2,1)S(1)} %get-tuple-element.112), channel_id=1, source_target_pairs={{0,24},{4,28},{8,16},{12,20},{16,8},{20,12},{24,0},{28,4},{1,25},{... | collective-permute-start | bytes 196616 | tf_op jit(solution)/shard_map/ppermute | solution.py:205
  63.2 2.2 %collective-permute-done.27.refs_4_ = bf16[2,2,64,128]{3,2,1,0:T(8,128)(2,1)S(1)} collective-permute-done((bf16[2,2,64,128]{3,2,1,0:T(8,128)(2,1)S(1)}, bf16[2,2,64,128]{3,2,1,0:T(8,128)(2,1)S(1)}, u32[]{:S(2)}, u32[]{:S(2)}) %collective-permute-start.27) | collective-permute-done | bytes 65568 | tf_op jit(solution)/shard_map/ppermute | solution.py:205
  65.5 1.4 %shard_map.90 = f32[8,64,128]{2,1,0:T(8,128)} custom-call(s32[8,16]{1,0:T(8,128)S(1)} %copy-done.5, f32[8,64,128]{2,1,0:T(8,128)S(1)} %get-tuple-element.107.gradient_in, bf16[4,2,64,128]{3,2,1,0:T(8,128)(2,1)S(1)} %get-tuple-element.113.kept.refs_0_, bf16[4,2,64,128]{3,2,1,0:T(8,128)(2,1)S(1)} %collective-permute-done.24.got.refs_1_, ...), custom_call_target="tpu_custom_call" | custom-call | tf_op jit(solution)/shard_map/pallas_call | solution.py:191
  (62 shorter events, 17.2 us)
Async XLA Ops:
  2.4 6.7 %collective-permute-start = (bf16[4,2,64,128]{3,2,1,0:T(8,128)(2,1)}, bf16[4,2,64,128]{3,2,1,0:T(8,128)(2,1)S(1)}, u32[]{:S(2)}, u32[]{:S(2)}) collective-permute-start(bf16[4,2,64,128]{3,2,1,0:T(8,128)(2,1)} %get-tuple-element.61), channel_id=1, source_target_pairs={{0,4},{4,0},{8,12},{12,8},{16,20},{20,16},{24,28},{28,24},{1,5},{5... | collective-permute-start | bytes 393224 | tf_op jit(solution)/shard_map/ppermute | solution.py:205
  5.4 15.2 %collective-permute-start.6 = (bf16[8,64,128]{2,1,0:T(8,128)(2,1)}, bf16[8,64,128]{2,1,0:T(8,128)(2,1)S(1)}, u32[]{:S(2)}, u32[]{:S(2)}) collective-permute-start(bf16[8,64,128]{2,1,0:T(8,128)(2,1)} %get-tuple-element.69.refs_2_), channel_id=1, source_target_pairs={{0,3},{1,2},{2,1},{3,0},{4,7},{5,6},{6,5},{7,4},{8,11},{9,10},{10,... | collective-permute-start | bytes 393224 | tf_op jit(solution)/shard_map/ppermute | solution.py:220
  6.1 14.6 %collective-permute-start.5 = (bf16[8,64,128]{2,1,0:T(8,128)(2,1)}, bf16[8,64,128]{2,1,0:T(8,128)(2,1)S(1)}, u32[]{:S(2)}, u32[]{:S(2)}) collective-permute-start(bf16[8,64,128]{2,1,0:T(8,128)(2,1)} %get-tuple-element.69.refs_2_), channel_id=1, source_target_pairs={{0,2},{1,3},{2,0},{3,1},{4,6},{5,7},{6,4},{7,5},{8,10},{9,11},{10,... | collective-permute-start | bytes 393224 | tf_op jit(solution)/shard_map/ppermute | solution.py:220
  7.0 13.7 %collective-permute-start.4 = (bf16[8,64,128]{2,1,0:T(8,128)(2,1)}, bf16[8,64,128]{2,1,0:T(8,128)(2,1)S(1)}, u32[]{:S(2)}, u32[]{:S(2)}) collective-permute-start(bf16[8,64,128]{2,1,0:T(8,128)(2,1)} %get-tuple-element.69.refs_2_), channel_id=1, source_target_pairs={{0,1},{1,0},{2,3},{3,2},{4,5},{5,4},{6,7},{7,6},{8,9},{9,8},{10,11... | collective-permute-start | bytes 393224 | tf_op jit(solution)/shard_map/ppermute | solution.py:220
  10.1 14.9 %collective-permute-start.1 = (bf16[2,2,64,128]{3,2,1,0:T(8,128)(2,1)S(1)}, bf16[2,2,64,128]{3,2,1,0:T(8,128)(2,1)S(1)}, u32[]{:S(2)}, u32[]{:S(2)}) collective-permute-start(bf16[2,2,64,128]{3,2,1,0:T(8,128)(2,1)S(1)} %get-tuple-element.62), channel_id=1, source_target_pairs={{0,8},{4,12},{8,0},{12,4},{16,24},{20,28},{24,16},{28,20},{1,9},{5... | collective-permute-start | bytes 196616 | tf_op jit(solution)/shard_map/ppermute | solution.py:205
  12.0 13.0 %collective-permute-start.2 = (bf16[2,2,64,128]{3,2,1,0:T(8,128)(2,1)S(1)}, bf16[2,2,64,128]{3,2,1,0:T(8,128)(2,1)S(1)}, u32[]{:S(2)}, u32[]{:S(2)}) collective-permute-start(bf16[2,2,64,128]{3,2,1,0:T(8,128)(2,1)S(1)} %get-tuple-element.63), channel_id=1, source_target_pairs={{0,16},{4,20},{8,24},{12,28},{16,0},{20,4},{24,8},{28,12},{1,17},{... | collective-permute-start | bytes 196616 | tf_op jit(solution)/shard_map/ppermute | solution.py:205
  20.6 6.1 %collective-permute-start.3 = (bf16[2,2,64,128]{3,2,1,0:T(8,128)(2,1)S(1)}, bf16[2,2,64,128]{3,2,1,0:T(8,128)(2,1)S(1)}, u32[]{:S(2)}, u32[]{:S(2)}) collective-permute-start(bf16[2,2,64,128]{3,2,1,0:T(8,128)(2,1)S(1)} %get-tuple-element.64), channel_id=1, source_target_pairs={{0,24},{4,28},{8,16},{12,20},{16,8},{20,12},{24,0},{28,4},{1,25},{... | collective-permute-start | bytes 196616 | tf_op jit(solution)/shard_map/ppermute | solution.py:205
  23.2 7.0 %collective-permute-start.11 = (bf16[4,2,64,128]{3,2,1,0:T(8,128)(2,1)S(1)}, bf16[4,2,64,128]{3,2,1,0:T(8,128)(2,1)S(1)}, u32[]{:S(2)}, u32[]{:S(2)}) collective-permute-start(bf16[4,2,64,128]{3,2,1,0:T(8,128)(2,1)S(1)} %get-tuple-element.70), channel_id=1, source_target_pairs={{0,4},{4,0},{8,12},{12,8},{16,20},{20,16},{24,28},{28,24},{1,5},{5... | collective-permute-start | bytes 393224 | tf_op jit(solution)/shard_map/ppermute | solution.py:205
  28.3 5.8 %collective-permute-start.7 = (bf16[8,64,128]{2,1,0:T(8,128)(2,1)S(1)}, bf16[8,64,128]{2,1,0:T(8,128)(2,1)S(1)}, u32[]{:S(2)}, u32[]{:S(2)}) collective-permute-start(bf16[8,64,128]{2,1,0:T(8,128)(2,1)S(1)} %get-tuple-element.77), channel_id=1, source_target_pairs={{0,3},{1,2},{2,1},{3,0},{4,7},{5,6},{6,5},{7,4},{8,11},{9,10},{10,... | collective-permute-start | bytes 393224 | tf_op jit(solution)/shard_map/ppermute | solution.py:220
  28.4 8.6 %collective-permute-start.8 = (bf16[8,64,128]{2,1,0:T(8,128)(2,1)S(1)}, bf16[8,64,128]{2,1,0:T(8,128)(2,1)S(1)}, u32[]{:S(2)}, u32[]{:S(2)}) collective-permute-start(bf16[8,64,128]{2,1,0:T(8,128)(2,1)S(1)} %get-tuple-element.78), channel_id=1, source_target_pairs={{0,2},{1,3},{2,0},{3,1},{4,6},{5,7},{6,4},{7,5},{8,10},{9,11},{10,... | collective-permute-start | bytes 393224 | tf_op jit(solution)/shard_map/ppermute | solution.py:220
  30.0 7.0 %collective-permute-start.9 = (bf16[8,64,128]{2,1,0:T(8,128)(2,1)S(1)}, bf16[8,64,128]{2,1,0:T(8,128)(2,1)S(1)}, u32[]{:S(2)}, u32[]{:S(2)}) collective-permute-start(bf16[8,64,128]{2,1,0:T(8,128)(2,1)S(1)} %get-tuple-element.79), channel_id=1, source_target_pairs={{0,1},{1,0},{2,3},{3,2},{4,5},{5,4},{6,7},{7,6},{8,9},{9,8},{10,11... | collective-permute-start | bytes 393224 | tf_op jit(solution)/shard_map/ppermute | solution.py:220
  30.2 9.0 %collective-permute-start.12 = (bf16[2,2,64,128]{3,2,1,0:T(8,128)(2,1)S(1)}, bf16[2,2,64,128]{3,2,1,0:T(8,128)(2,1)S(1)}, u32[]{:S(2)}, u32[]{:S(2)}) collective-permute-start(bf16[2,2,64,128]{3,2,1,0:T(8,128)(2,1)S(1)} %get-tuple-element.84), channel_id=1, source_target_pairs={{0,8},{4,12},{8,0},{12,4},{16,24},{20,28},{24,16},{28,20},{1,9},{5... | collective-permute-start | bytes 196616 | tf_op jit(solution)/shard_map/ppermute | solution.py:205
  30.3 9.0 %collective-permute-start.13 = (bf16[2,2,64,128]{3,2,1,0:T(8,128)(2,1)S(1)}, bf16[2,2,64,128]{3,2,1,0:T(8,128)(2,1)S(1)}, u32[]{:S(2)}, u32[]{:S(2)}) collective-permute-start(bf16[2,2,64,128]{3,2,1,0:T(8,128)(2,1)S(1)} %get-tuple-element.85), channel_id=1, source_target_pairs={{0,16},{4,20},{8,24},{12,28},{16,0},{20,4},{24,8},{28,12},{1,17},{... | collective-permute-start | bytes 196616 | tf_op jit(solution)/shard_map/ppermute | solution.py:205
  34.1 6.1 %collective-permute-start.14 = (bf16[2,2,64,128]{3,2,1,0:T(8,128)(2,1)S(1)}, bf16[2,2,64,128]{3,2,1,0:T(8,128)(2,1)S(1)}, u32[]{:S(2)}, u32[]{:S(2)}) collective-permute-start(bf16[2,2,64,128]{3,2,1,0:T(8,128)(2,1)S(1)} %get-tuple-element.86), channel_id=1, source_target_pairs={{0,24},{4,28},{8,16},{12,20},{16,8},{20,12},{24,0},{28,4},{1,25},{... | collective-permute-start | bytes 196616 | tf_op jit(solution)/shard_map/ppermute | solution.py:205
  41.0 8.6 %collective-permute-start.19 = (bf16[8,64,128]{2,1,0:T(8,128)(2,1)S(1)}, bf16[8,64,128]{2,1,0:T(8,128)(2,1)S(1)}, u32[]{:S(2)}, u32[]{:S(2)}) collective-permute-start(bf16[8,64,128]{2,1,0:T(8,128)(2,1)S(1)} %get-tuple-element.92.refs_1_), channel_id=1, source_target_pairs={{0,2},{1,3},{2,0},{3,1},{4,6},{5,7},{6,4},{7,5},{8,10},{9,11},{10,... | collective-permute-start | bytes 393224 | tf_op jit(solution)/shard_map/ppermute | solution.py:220
  42.7 7.0 %collective-permute-start.18 = (bf16[8,64,128]{2,1,0:T(8,128)(2,1)S(1)}, bf16[8,64,128]{2,1,0:T(8,128)(2,1)S(1)}, u32[]{:S(2)}, u32[]{:S(2)}) collective-permute-start(bf16[8,64,128]{2,1,0:T(8,128)(2,1)S(1)} %get-tuple-element.92.refs_1_), channel_id=1, source_target_pairs={{0,1},{1,0},{2,3},{3,2},{4,5},{5,4},{6,7},{7,6},{8,9},{9,8},{10,11... | collective-permute-start | bytes 393224 | tf_op jit(solution)/shard_map/ppermute | solution.py:220
  43.3 9.2 %collective-permute-start.15 = (bf16[2,2,64,128]{3,2,1,0:T(8,128)(2,1)S(1)}, bf16[2,2,64,128]{3,2,1,0:T(8,128)(2,1)S(1)}, u32[]{:S(2)}, u32[]{:S(2)}) collective-permute-start(bf16[2,2,64,128]{3,2,1,0:T(8,128)(2,1)S(1)} %get-tuple-element.94), channel_id=1, source_target_pairs={{0,8},{4,12},{8,0},{12,4},{16,24},{20,28},{24,16},{28,20},{1,9},{5... | collective-permute-start | bytes 196616 | tf_op jit(solution)/shard_map/ppermute | solution.py:205
  43.3 9.2 %collective-permute-start.16 = (bf16[2,2,64,128]{3,2,1,0:T(8,128)(2,1)S(1)}, bf16[2,2,64,128]{3,2,1,0:T(8,128)(2,1)S(1)}, u32[]{:S(2)}, u32[]{:S(2)}) collective-permute-start(bf16[2,2,64,128]{3,2,1,0:T(8,128)(2,1)S(1)} %get-tuple-element.95), channel_id=1, source_target_pairs={{0,16},{4,20},{8,24},{12,28},{16,0},{20,4},{24,8},{28,12},{1,17},{... | collective-permute-start | bytes 196616 | tf_op jit(solution)/shard_map/ppermute | solution.py:205
  46.7 6.1 %collective-permute-start.17 = (bf16[2,2,64,128]{3,2,1,0:T(8,128)(2,1)S(1)}, bf16[2,2,64,128]{3,2,1,0:T(8,128)(2,1)S(1)}, u32[]{:S(2)}, u32[]{:S(2)}) collective-permute-start(bf16[2,2,64,128]{3,2,1,0:T(8,128)(2,1)S(1)} %get-tuple-element.96), channel_id=1, source_target_pairs={{0,24},{4,28},{8,16},{12,20},{16,8},{20,12},{24,0},{28,4},{1,25},{... | collective-permute-start | bytes 196616 | tf_op jit(solution)/shard_map/ppermute | solution.py:205
  53.8 8.6 %collective-permute-start.22 = (bf16[8,64,128]{2,1,0:T(8,128)(2,1)S(1)}, bf16[8,64,128]{2,1,0:T(8,128)(2,1)S(1)}, u32[]{:S(2)}, u32[]{:S(2)}) collective-permute-start(bf16[8,64,128]{2,1,0:T(8,128)(2,1)S(1)} %get-tuple-element.105), channel_id=1, source_target_pairs={{0,2},{1,3},{2,0},{3,1},{4,6},{5,7},{6,4},{7,5},{8,10},{9,11},{10,... | collective-permute-start | bytes 393224 | tf_op jit(solution)/shard_map/ppermute | solution.py:220
  55.5 6.9 %collective-permute-start.23 = (bf16[8,64,128]{2,1,0:T(8,128)(2,1)S(1)}, bf16[8,64,128]{2,1,0:T(8,128)(2,1)S(1)}, u32[]{:S(2)}, u32[]{:S(2)}) collective-permute-start(bf16[8,64,128]{2,1,0:T(8,128)(2,1)S(1)} %get-tuple-element.106), channel_id=1, source_target_pairs={{0,1},{1,0},{2,3},{3,2},{4,5},{5,4},{6,7},{7,6},{8,9},{9,8},{10,11... | collective-permute-start | bytes 393224 | tf_op jit(solution)/shard_map/ppermute | solution.py:220
  56.4 6.8 %collective-permute-start.25 = (bf16[2,2,64,128]{3,2,1,0:T(8,128)(2,1)S(1)}, bf16[2,2,64,128]{3,2,1,0:T(8,128)(2,1)S(1)}, u32[]{:S(2)}, u32[]{:S(2)}) collective-permute-start(bf16[2,2,64,128]{3,2,1,0:T(8,128)(2,1)S(1)} %get-tuple-element.110), channel_id=1, source_target_pairs={{0,8},{4,12},{8,0},{12,4},{16,24},{20,28},{24,16},{28,20},{1,9},{5... | collective-permute-start | bytes 196616 | tf_op jit(solution)/shard_map/ppermute | solution.py:205
  56.5 6.7 %collective-permute-start.26 = (bf16[2,2,64,128]{3,2,1,0:T(8,128)(2,1)S(1)}, bf16[2,2,64,128]{3,2,1,0:T(8,128)(2,1)S(1)}, u32[]{:S(2)}, u32[]{:S(2)}) collective-permute-start(bf16[2,2,64,128]{3,2,1,0:T(8,128)(2,1)S(1)} %get-tuple-element.111), channel_id=1, source_target_pairs={{0,16},{4,20},{8,24},{12,28},{16,0},{20,4},{24,8},{28,12},{1,17},{... | collective-permute-start | bytes 196616 | tf_op jit(solution)/shard_map/ppermute | solution.py:205
  59.4 6.1 %collective-permute-start.27 = (bf16[2,2,64,128]{3,2,1,0:T(8,128)(2,1)S(1)}, bf16[2,2,64,128]{3,2,1,0:T(8,128)(2,1)S(1)}, u32[]{:S(2)}, u32[]{:S(2)}) collective-permute-start(bf16[2,2,64,128]{3,2,1,0:T(8,128)(2,1)S(1)} %get-tuple-element.112), channel_id=1, source_target_pairs={{0,24},{4,28},{8,16},{12,20},{16,8},{20,12},{24,0},{28,4},{1,25},{... | collective-permute-start | bytes 196616 | tf_op jit(solution)/shard_map/ppermute | solution.py:205
  (12 other events, 85.9 us)

commit v6 on v5

--- a/solution.py
+++ b/solution.py
@@ -85,8 +85,12 @@
             low[place] = (value - rounded.astype(FULL)).astype(LOW)
 
 
+def far_first(pairs):
+    return zip(range(len(pairs), 0, -1), pairs)
+
+
 def pair_kernel(kept, got, *pairs):
-    for turn, pair in enumerate(pairs, 1):
+    for turn, pair in far_first(pairs):
         pair[0] = kept[turn]
         pair[1] = got[turn]
 
@@ -95,7 +99,7 @@
     kept, got, *pairs = parts
     yield 0, kept.at[0]
     yield 1, got.at[0]
-    for turn, pair in enumerate(pairs, 1):
+    for turn, pair in far_first(pairs):
         yield 2 * turn, pair.at[0]
         yield 2 * turn + 1, pair.at[1]
 
@@ -212,8 +216,7 @@
             [(pair_shape, LOW)] * (owners // 2 - 1),
             [],
         )
-        moved = [to_node(pair, 2 * turn) for turn, pair in enumerate(pairs, 1)]
-        return (kept, got, *moved), pairs
+        return (kept, got, *(to_node(pair, 2 * turn) for turn, pair in far_first(pairs)))
 
     def over_edge(arrays, turns):
         return [arrays[0]] + [
@@ -234,9 +237,6 @@
         ],
         START_MEBIBYTES,
     )
-    got = to_node(away, 1)
-    columns, pairs = over_node(kept, got)
-    block_row, block_slot = after((block_row, block_slot), pairs)
     dense_shape = (slot_total * quarter, count * width)
     parts = next(size for size in (12, 8, 4, 2, 1) if block_count % size == 0)
     high, low = call(
@@ -263,10 +263,9 @@
             transcendentals=0,
         )
         arrived = over_edge([rounded] * quarters, range(1, quarters))
-        if step > 0:
-            got = to_node(away, 1)
-            (got,) = after((got,), (rounded,))
-            columns, _ = over_node(kept, got)
+        got = to_node(away, 1)
+        (got,) = after((got,), (rounded, high) if step else (high,))
+        columns = over_node(kept, got)
         kept_sums, away_sums = call(
             functools.partial(adjoint_kernel, len(dense)),
             (*dense, *arrived),
@@ -292,7 +291,7 @@
             cost=cost,
         )
         (got_sums,) = after((got_sums,), partials[1:])
-        transposed, _ = over_node(kept_sums, got_sums)
+        transposed = over_node(kept_sums, got_sums)
         partials = over_edge(partials, range(quarters - 1, 0, -1))
         total = [pltpu.VMEM(shape, FULL)]
         if not last:

time: 67.1 us -> 62.6 us (0.933)
  starting transfers between devices: 32.7 us -> 28.5 us
  local copies, waits for them, and re-layouts: 2.29 us -> 1.39 us
  waiting for transfers between devices: 14.5 us -> 15.2 us
    ppermute x16, starting transfers between devices: 25.1 us -> 20.8 us  [to_node(): lax.ppermute(array, 'node', [(place, place ^ turn) for place in range(own...]
    ppermute x16, waiting for transfers between devices: 8.12 us -> 9.24 us  [to_node(): lax.ppermute(array, 'node', [(place, place ^ turn) for place in range(own...]
    unnamed x16 -> x14, local copies, waits for them, and re-layouts: 2.29 us -> 1.39 us
  transfers between devices with their start and end apart: 28 -> 28, of which waited for: 13 -> 16; matrix products, arithmetic and copies ran while one was open for 0% -> 0% of each run, Pallas kernels for 20% -> 21%
where the time goes in v6:
time: 62.6 us; the launch traced here: 62.4 us
  starting transfers between devices  28.5 us (46%)
  Pallas kernels  16.5 us (26%)
  waiting for transfers between devices  15.2 us (24%)
  local copies, waits for them, and re-layouts  1.39 us (2%)
  between operations  0.79 us (1%)
    ppermute x16, starting transfers between devices, to_node(): lax.ppermute(array, 'node', [(place, place ^ turn) for place in range(own...  20.8 us
    pallas_call x14, Pallas kernels, call(): pl.pallas_call(kernel, out_shape=[jax.ShapeDtypeStruct(*out) for out in o...  16.5 us
    ppermute x16, waiting for transfers between devices, to_node(): lax.ppermute(array, 'node', [(place, place ^ turn) for place in range(own...  9.24 us
    ppermute x12, starting transfers between devices, over_edge(): lax.ppermute(array, 'edge', [(place, place ^ turn) for place in range(qua...  7.64 us
    ppermute x12, waiting for transfers between devices, over_edge(): lax.ppermute(array, 'edge', [(place, place ^ turn) for place in range(qua...  5.95 us
    unnamed x14, local copies, waits for them, and re-layouts  1.39 us
  transfers between devices with their start and end apart: 28, of which 16 were waited for; matrix products, arithmetic and copies ran while one was open for 0% of the time, Pallas kernels for 21%

profile of v6, /device:TPU:0, one launch (start us, length us, event | category | flops | bytes accessed | tf_op | source)
XLA Modules:
  0.0 62.4 jit_solution(6033637602615581619)
XLA Ops:
  0.6 1.8 %shard_map.78 = (bf16[4,2,64,128]{3,2,1,0:T(8,128)(2,1)}, bf16[4,2,64,128]{3,2,1,0:T(8,128)(2,1)}, bf16[8,64,128]{2,1,0:T(8,128)(2,1)}) custom-call(s32[8,16]{1,0:T(8,128)} %table.7, f32[8,64,128]{2,1,0:T(8,128)} %bitcast.4, f32[8,64,128]{2,1,0:T(8,128)} %bitcast.7), custom_call_target="tpu_custom_call" | custom-call | tf_op jit(solution)/shard_map/pallas_call | solution.py:195
  2.5 3.0 %collective-permute-start = (bf16[4,2,64,128]{3,2,1,0:T(8,128)(2,1)}, bf16[4,2,64,128]{3,2,1,0:T(8,128)(2,1)S(1)}, u32[]{:S(2)}, u32[]{:S(2)}) collective-permute-start(bf16[4,2,64,128]{3,2,1,0:T(8,128)(2,1)} %get-tuple-element.62), channel_id=1, source_target_pairs={{0,4},{4,0},{8,12},{12,8},{16,20},{20,16},{24,28},{28,24},{1,5},{5... | collective-permute-start | bytes 393224 | tf_op jit(solution)/shard_map/ppermute | solution.py:209
  8.7 4.7 %shard_map.77 = (bf16[1024,2048]{1,0:T(8,128)(2,1)S(1)}, bf16[1024,2048]{1,0:T(8,128)(2,1)S(1)}) custom-call(s32[1,192]{1,0:T(1,128)S(1)} %copy-done.5, s32[1,192]{1,0:T(1,128)S(1)} %copy-done.6, bf16[1,192,64,256]{3,2,1,0:T(8,128)(2,1)} %weights.1), custom_call_target="tpu_custom_call" | custom-call | bytes 6291456 | tf_op jit(solution)/shard_map/pallas_call | solution.py:195
  13.4 3.7 %collective-permute-start.1 = (bf16[2,2,64,128]{3,2,1,0:T(8,128)(2,1)S(1)}, bf16[2,2,64,128]{3,2,1,0:T(8,128)(2,1)S(1)}, u32[]{:S(2)}, u32[]{:S(2)}) collective-permute-start(bf16[2,2,64,128]{3,2,1,0:T(8,128)(2,1)S(1)} %get-tuple-element.64), channel_id=1, source_target_pairs={{0,24},{4,28},{8,16},{12,20},{16,8},{20,12},{24,0},{28,4},{1,25},{... | collective-permute-start | bytes 196616 | tf_op jit(solution)/shard_map/ppermute | solution.py:209
  17.9 2.4 %shard_map.80 = (bf16[4,2,64,128]{3,2,1,0:T(8,128)(2,1)S(1)}, bf16[4,2,64,128]{3,2,1,0:T(8,128)(2,1)S(1)}) custom-call(bf16[1024,2048]{1,0:T(8,128)(2,1)S(1)} %get-tuple-element.59.refs_0_, bf16[1024,2048]{1,0:T(8,128)(2,1)S(1)} %get-tuple-element.60.refs_1_, bf16[8,64,128]{2,1,0:T(8,128)(2,1)S(1)} %copy-done.3, ...), custom_call_target="tpu_custom_call" | custom-call | flops 1073741824 | bytes 8388608 | tf_op jit(solution)/shard_map/pallas_call | solution.py:195
  20.8 2.2 %collective-permute-done.2.refs_5_ = bf16[2,2,64,128]{3,2,1,0:T(8,128)(2,1)S(1)} collective-permute-done((bf16[2,2,64,128]{3,2,1,0:T(8,128)(2,1)S(1)}, bf16[2,2,64,128]{3,2,1,0:T(8,128)(2,1)S(1)}, u32[]{:S(2)}, u32[]{:S(2)}) %collective-permute-start.2) | collective-permute-done | bytes 65568 | tf_op jit(solution)/shard_map/ppermute | solution.py:209
  23.0 1.5 %shard_map.81 = (f32[8,64,128]{2,1,0:T(8,128)S(1)}, bf16[8,64,128]{2,1,0:T(8,128)(2,1)S(1)}, bf16[8,64,128]{2,1,0:T(8,128)(2,1)S(1)}, bf16[8,64,128]{2,1,0:T(8,128)(2,1)S(1)}) custom-call(bf16[1024,2048]{1,0:T(8,128)(2,1)S(1)} %get-tuple-element.59.refs_0_, bf16[1024,2048]{1,0:T(8,128)(2,1)S(1)} %get-tuple-element.60.refs_1_, ...), custom_call_target="tpu_custom_call" | custom-call | flops 1073741824 | bytes 8388608 | tf_op jit(solution)/shard_map/pallas_call | solution.py:195
  26.5 2.6 %collective-permute-start.12 = (bf16[2,2,64,128]{3,2,1,0:T(8,128)(2,1)S(1)}, bf16[2,2,64,128]{3,2,1,0:T(8,128)(2,1)S(1)}, u32[]{:S(2)}, u32[]{:S(2)}) collective-permute-start(bf16[2,2,64,128]{3,2,1,0:T(8,128)(2,1)S(1)} %get-tuple-element.82), channel_id=1, source_target_pairs={{0,24},{4,28},{8,16},{12,20},{16,8},{20,12},{24,0},{28,4},{1,25},{... | collective-permute-start | bytes 196616 | tf_op jit(solution)/shard_map/ppermute | solution.py:209
  29.2 1.2 %collective-permute-done.7.refs_1_ = bf16[8,64,128]{2,1,0:T(8,128)(2,1)S(1)} collective-permute-done((bf16[8,64,128]{2,1,0:T(8,128)(2,1)S(1)}, bf16[8,64,128]{2,1,0:T(8,128)(2,1)S(1)}, u32[]{:S(2)}, u32[]{:S(2)}) %collective-permute-start.7) | collective-permute-done | bytes 131104 | tf_op jit(solution)/shard_map/ppermute | solution.py:223
  30.4 1.2 %collective-permute-start.14 = (bf16[2,2,64,128]{3,2,1,0:T(8,128)(2,1)S(1)}, bf16[2,2,64,128]{3,2,1,0:T(8,128)(2,1)S(1)}, u32[]{:S(2)}, u32[]{:S(2)}) collective-permute-start(bf16[2,2,64,128]{3,2,1,0:T(8,128)(2,1)S(1)} %get-tuple-element.84), channel_id=1, source_target_pairs={{0,8},{4,12},{8,0},{12,4},{16,24},{20,28},{24,16},{28,20},{1,9},{5... | collective-permute-start | bytes 196616 | tf_op jit(solution)/shard_map/ppermute | solution.py:209
  31.6 1.6 %collective-permute-done.8.refs_2_ = bf16[8,64,128]{2,1,0:T(8,128)(2,1)S(1)} collective-permute-done((bf16[8,64,128]{2,1,0:T(8,128)(2,1)S(1)}, bf16[8,64,128]{2,1,0:T(8,128)(2,1)S(1)}, u32[]{:S(2)}, u32[]{:S(2)}) %collective-permute-start.8) | collective-permute-done | bytes 131104 | tf_op jit(solution)/shard_map/ppermute | solution.py:223
  34.5 1.2 %collective-permute-done.13.refs_3_ = bf16[2,2,64,128]{3,2,1,0:T(8,128)(2,1)S(1)} collective-permute-done((bf16[2,2,64,128]{3,2,1,0:T(8,128)(2,1)S(1)}, bf16[2,2,64,128]{3,2,1,0:T(8,128)(2,1)S(1)}, u32[]{:S(2)}, u32[]{:S(2)}) %collective-permute-start.13) | collective-permute-done | bytes 65568 | tf_op jit(solution)/shard_map/ppermute | solution.py:209
  37.3 1.1 %collective-permute-start.19 = (bf16[8,64,128]{2,1,0:T(8,128)(2,1)S(1)}, bf16[8,64,128]{2,1,0:T(8,128)(2,1)S(1)}, u32[]{:S(2)}, u32[]{:S(2)}) collective-permute-start(bf16[8,64,128]{2,1,0:T(8,128)(2,1)S(1)} %get-tuple-element.90.refs_1_), channel_id=1, source_target_pairs={{0,2},{1,3},{2,0},{3,1},{4,6},{5,7},{6,4},{7,5},{8,10},{9,11},{10,... | collective-permute-start | bytes 393224 | tf_op jit(solution)/shard_map/ppermute | solution.py:223
  39.5 2.5 %collective-permute-start.15 = (bf16[2,2,64,128]{3,2,1,0:T(8,128)(2,1)S(1)}, bf16[2,2,64,128]{3,2,1,0:T(8,128)(2,1)S(1)}, u32[]{:S(2)}, u32[]{:S(2)}) collective-permute-start(bf16[2,2,64,128]{3,2,1,0:T(8,128)(2,1)S(1)} %get-tuple-element.92), channel_id=1, source_target_pairs={{0,24},{4,28},{8,16},{12,20},{16,8},{20,12},{24,0},{28,4},{1,25},{... | collective-permute-start | bytes 196616 | tf_op jit(solution)/shard_map/ppermute | solution.py:209
  42.7 1.3 %collective-permute-start.17 = (bf16[2,2,64,128]{3,2,1,0:T(8,128)(2,1)S(1)}, bf16[2,2,64,128]{3,2,1,0:T(8,128)(2,1)S(1)}, u32[]{:S(2)}, u32[]{:S(2)}) collective-permute-start(bf16[2,2,64,128]{3,2,1,0:T(8,128)(2,1)S(1)} %get-tuple-element.94), channel_id=1, source_target_pairs={{0,8},{4,12},{8,0},{12,4},{16,24},{20,28},{24,16},{28,20},{1,9},{5... | collective-permute-start | bytes 196616 | tf_op jit(solution)/shard_map/ppermute | solution.py:209
  44.0 1.4 %collective-permute-done.19.refs_3_ = bf16[8,64,128]{2,1,0:T(8,128)(2,1)S(1)} collective-permute-done((bf16[8,64,128]{2,1,0:T(8,128)(2,1)S(1)}, bf16[8,64,128]{2,1,0:T(8,128)(2,1)S(1)}, u32[]{:S(2)}, u32[]{:S(2)}) %collective-permute-start.19) | collective-permute-done | bytes 131104 | tf_op jit(solution)/shard_map/ppermute | solution.py:223
  45.4 1.3 %shard_map.86 = (bf16[4,2,64,128]{3,2,1,0:T(8,128)(2,1)S(1)}, bf16[4,2,64,128]{3,2,1,0:T(8,128)(2,1)S(1)}) custom-call(bf16[1024,2048]{1,0:T(8,128)(2,1)S(1)} %get-tuple-element.59.refs_0_, bf16[8,64,128]{2,1,0:T(8,128)(2,1)S(1)} %get-tuple-element.90.refs_1_, bf16[8,64,128]{2,1,0:T(8,128)(2,1)S(1)} %collective-permute-done.18.refs_2_, ...), custom_call_target="tpu_custom_call" | custom-call | flops 536870912 | bytes 4194304 | tf_op jit(solution)/shard_map/pallas_call | solution.py:195
  47.3 1.0 %collective-permute-done.16.refs_4_ = bf16[2,2,64,128]{3,2,1,0:T(8,128)(2,1)S(1)} collective-permute-done((bf16[2,2,64,128]{3,2,1,0:T(8,128)(2,1)S(1)}, bf16[2,2,64,128]{3,2,1,0:T(8,128)(2,1)S(1)}, u32[]{:S(2)}, u32[]{:S(2)}) %collective-permute-start.16) | collective-permute-done | bytes 65568 | tf_op jit(solution)/shard_map/ppermute | solution.py:209
  48.4 1.0 %shard_map.87 = (f32[8,64,128]{2,1,0:T(8,128)S(1)}, bf16[8,64,128]{2,1,0:T(8,128)(2,1)S(1)}, bf16[8,64,128]{2,1,0:T(8,128)(2,1)S(1)}, bf16[8,64,128]{2,1,0:T(8,128)(2,1)S(1)}) custom-call(bf16[1024,2048]{1,0:T(8,128)(2,1)S(1)} %get-tuple-element.59.refs_0_, bf16[4,2,64,128]{3,2,1,0:T(8,128)(2,1)S(1)} %get-tuple-element.96.kept.refs_1_, ...), custom_call_target="tpu_custom_call" | custom-call | flops 536870912 | bytes 4194304 | tf_op jit(solution)/shard_map/pallas_call | solution.py:195
  51.3 1.1 %collective-permute-done.24.got.refs_1_ = bf16[4,2,64,128]{3,2,1,0:T(8,128)(2,1)S(1)} collective-permute-done((bf16[4,2,64,128]{3,2,1,0:T(8,128)(2,1)S(1)}, bf16[4,2,64,128]{3,2,1,0:T(8,128)(2,1)S(1)}, u32[]{:S(2)}, u32[]{:S(2)}) %collective-permute-start.24) | collective-permute-done | bytes 131104 | tf_op jit(solution)/shard_map/ppermute | solution.py:209
  52.4 2.3 %collective-permute-start.25 = (bf16[2,2,64,128]{3,2,1,0:T(8,128)(2,1)S(1)}, bf16[2,2,64,128]{3,2,1,0:T(8,128)(2,1)S(1)}, u32[]{:S(2)}, u32[]{:S(2)}) collective-permute-start(bf16[2,2,64,128]{3,2,1,0:T(8,128)(2,1)S(1)} %get-tuple-element.108), channel_id=1, source_target_pairs={{0,24},{4,28},{8,16},{12,20},{16,8},{20,12},{24,0},{28,4},{1,25},{... | collective-permute-start | bytes 196616 | tf_op jit(solution)/shard_map/ppermute | solution.py:209
  55.2 1.6 %collective-permute-start.27 = (bf16[2,2,64,128]{3,2,1,0:T(8,128)(2,1)S(1)}, bf16[2,2,64,128]{3,2,1,0:T(8,128)(2,1)S(1)}, u32[]{:S(2)}, u32[]{:S(2)}) collective-permute-start(bf16[2,2,64,128]{3,2,1,0:T(8,128)(2,1)S(1)} %get-tuple-element.110), channel_id=1, source_target_pairs={{0,8},{4,12},{8,0},{12,4},{16,24},{20,28},{24,16},{28,20},{1,9},{5... | collective-permute-start | bytes 196616 | tf_op jit(solution)/shard_map/ppermute | solution.py:209
  58.6 1.9 %collective-permute-done.26.refs_3_ = bf16[2,2,64,128]{3,2,1,0:T(8,128)(2,1)S(1)} collective-permute-done((bf16[2,2,64,128]{3,2,1,0:T(8,128)(2,1)S(1)}, bf16[2,2,64,128]{3,2,1,0:T(8,128)(2,1)S(1)}, u32[]{:S(2)}, u32[]{:S(2)}) %collective-permute-start.26) | collective-permute-done | bytes 65568 | tf_op jit(solution)/shard_map/ppermute | solution.py:209
  60.9 1.4 %shard_map.90 = f32[8,64,128]{2,1,0:T(8,128)} custom-call(s32[8,16]{1,0:T(8,128)S(1)} %copy-done.4, f32[8,64,128]{2,1,0:T(8,128)S(1)} %get-tuple-element.105.gradient_in, bf16[4,2,64,128]{3,2,1,0:T(8,128)(2,1)S(1)} %get-tuple-element.111.kept.refs_0_, bf16[4,2,64,128]{3,2,1,0:T(8,128)(2,1)S(1)} %collective-permute-done.24.got.refs_1_, ...), custom_call_target="tpu_custom_call" | custom-call | tf_op jit(solution)/shard_map/pallas_call | solution.py:195
  (60 shorter events, 16.7 us)
Async XLA Ops:
  2.5 11.0 %collective-permute-start = (bf16[4,2,64,128]{3,2,1,0:T(8,128)(2,1)}, bf16[4,2,64,128]{3,2,1,0:T(8,128)(2,1)S(1)}, u32[]{:S(2)}, u32[]{:S(2)}) collective-permute-start(bf16[4,2,64,128]{3,2,1,0:T(8,128)(2,1)} %get-tuple-element.62), channel_id=1, source_target_pairs={{0,4},{4,0},{8,12},{12,8},{16,20},{20,16},{24,28},{28,24},{1,5},{5... | collective-permute-start | bytes 393224 | tf_op jit(solution)/shard_map/ppermute | solution.py:209
  5.5 11.7 %collective-permute-start.6 = (bf16[8,64,128]{2,1,0:T(8,128)(2,1)}, bf16[8,64,128]{2,1,0:T(8,128)(2,1)S(1)}, u32[]{:S(2)}, u32[]{:S(2)}) collective-permute-start(bf16[8,64,128]{2,1,0:T(8,128)(2,1)} %get-tuple-element.67.refs_2_), channel_id=1, source_target_pairs={{0,3},{1,2},{2,1},{3,0},{4,7},{5,6},{6,5},{7,4},{8,11},{9,10},{10,... | collective-permute-start | bytes 393224 | tf_op jit(solution)/shard_map/ppermute | solution.py:223
  6.1 11.8 %collective-permute-start.5 = (bf16[8,64,128]{2,1,0:T(8,128)(2,1)}, bf16[8,64,128]{2,1,0:T(8,128)(2,1)S(1)}, u32[]{:S(2)}, u32[]{:S(2)}) collective-permute-start(bf16[8,64,128]{2,1,0:T(8,128)(2,1)} %get-tuple-element.67.refs_2_), channel_id=1, source_target_pairs={{0,2},{1,3},{2,0},{3,1},{4,6},{5,7},{6,4},{7,5},{8,10},{9,11},{10,... | collective-permute-start | bytes 393224 | tf_op jit(solution)/shard_map/ppermute | solution.py:223
  7.0 10.9 %collective-permute-start.4 = (bf16[8,64,128]{2,1,0:T(8,128)(2,1)}, bf16[8,64,128]{2,1,0:T(8,128)(2,1)S(1)}, u32[]{:S(2)}, u32[]{:S(2)}) collective-permute-start(bf16[8,64,128]{2,1,0:T(8,128)(2,1)} %get-tuple-element.67.refs_2_), channel_id=1, source_target_pairs={{0,1},{1,0},{2,3},{3,2},{4,5},{5,4},{6,7},{7,6},{8,9},{9,8},{10,11... | collective-permute-start | bytes 393224 | tf_op jit(solution)/shard_map/ppermute | solution.py:223
  13.4 7.4 %collective-permute-start.1 = (bf16[2,2,64,128]{3,2,1,0:T(8,128)(2,1)S(1)}, bf16[2,2,64,128]{3,2,1,0:T(8,128)(2,1)S(1)}, u32[]{:S(2)}, u32[]{:S(2)}) collective-permute-start(bf16[2,2,64,128]{3,2,1,0:T(8,128)(2,1)S(1)} %get-tuple-element.64), channel_id=1, source_target_pairs={{0,24},{4,28},{8,16},{12,20},{16,8},{20,12},{24,0},{28,4},{1,25},{... | collective-permute-start | bytes 196616 | tf_op jit(solution)/shard_map/ppermute | solution.py:209
  17.1 5.9 %collective-permute-start.2 = (bf16[2,2,64,128]{3,2,1,0:T(8,128)(2,1)S(1)}, bf16[2,2,64,128]{3,2,1,0:T(8,128)(2,1)S(1)}, u32[]{:S(2)}, u32[]{:S(2)}) collective-permute-start(bf16[2,2,64,128]{3,2,1,0:T(8,128)(2,1)S(1)} %get-tuple-element.65), channel_id=1, source_target_pairs={{0,16},{4,20},{8,24},{12,28},{16,0},{20,4},{24,8},{28,12},{1,17},{... | collective-permute-start | bytes 196616 | tf_op jit(solution)/shard_map/ppermute | solution.py:209
  17.1 5.9 %collective-permute-start.3 = (bf16[2,2,64,128]{3,2,1,0:T(8,128)(2,1)S(1)}, bf16[2,2,64,128]{3,2,1,0:T(8,128)(2,1)S(1)}, u32[]{:S(2)}, u32[]{:S(2)}) collective-permute-start(bf16[2,2,64,128]{3,2,1,0:T(8,128)(2,1)S(1)} %get-tuple-element.66), channel_id=1, source_target_pairs={{0,8},{4,12},{8,0},{12,4},{16,24},{20,28},{24,16},{28,20},{1,9},{5... | collective-permute-start | bytes 196616 | tf_op jit(solution)/shard_map/ppermute | solution.py:209
  20.4 6.1 %collective-permute-start.11 = (bf16[4,2,64,128]{3,2,1,0:T(8,128)(2,1)S(1)}, bf16[4,2,64,128]{3,2,1,0:T(8,128)(2,1)S(1)}, u32[]{:S(2)}, u32[]{:S(2)}) collective-permute-start(bf16[4,2,64,128]{3,2,1,0:T(8,128)(2,1)S(1)} %get-tuple-element.68), channel_id=1, source_target_pairs={{0,4},{4,0},{8,12},{12,8},{16,20},{20,16},{24,28},{28,24},{1,5},{5... | collective-permute-start | bytes 393224 | tf_op jit(solution)/shard_map/ppermute | solution.py:209
  24.5 5.9 %collective-permute-start.7 = (bf16[8,64,128]{2,1,0:T(8,128)(2,1)S(1)}, bf16[8,64,128]{2,1,0:T(8,128)(2,1)S(1)}, u32[]{:S(2)}, u32[]{:S(2)}) collective-permute-start(bf16[8,64,128]{2,1,0:T(8,128)(2,1)S(1)} %get-tuple-element.75), channel_id=1, source_target_pairs={{0,3},{1,2},{2,1},{3,0},{4,7},{5,6},{6,5},{7,4},{8,11},{9,10},{10,... | collective-permute-start | bytes 393224 | tf_op jit(solution)/shard_map/ppermute | solution.py:223
  25.3 7.8 %collective-permute-start.8 = (bf16[8,64,128]{2,1,0:T(8,128)(2,1)S(1)}, bf16[8,64,128]{2,1,0:T(8,128)(2,1)S(1)}, u32[]{:S(2)}, u32[]{:S(2)}) collective-permute-start(bf16[8,64,128]{2,1,0:T(8,128)(2,1)S(1)} %get-tuple-element.76), channel_id=1, source_target_pairs={{0,2},{1,3},{2,0},{3,1},{4,6},{5,7},{6,4},{7,5},{8,10},{9,11},{10,... | collective-permute-start | bytes 393224 | tf_op jit(solution)/shard_map/ppermute | solution.py:223
  26.1 7.0 %collective-permute-start.9 = (bf16[8,64,128]{2,1,0:T(8,128)(2,1)S(1)}, bf16[8,64,128]{2,1,0:T(8,128)(2,1)S(1)}, u32[]{:S(2)}, u32[]{:S(2)}) collective-permute-start(bf16[8,64,128]{2,1,0:T(8,128)(2,1)S(1)} %get-tuple-element.77), channel_id=1, source_target_pairs={{0,1},{1,0},{2,3},{3,2},{4,5},{5,4},{6,7},{7,6},{8,9},{9,8},{10,11... | collective-permute-start | bytes 393224 | tf_op jit(solution)/shard_map/ppermute | solution.py:223
  26.5 8.0 %collective-permute-start.12 = (bf16[2,2,64,128]{3,2,1,0:T(8,128)(2,1)S(1)}, bf16[2,2,64,128]{3,2,1,0:T(8,128)(2,1)S(1)}, u32[]{:S(2)}, u32[]{:S(2)}) collective-permute-start(bf16[2,2,64,128]{3,2,1,0:T(8,128)(2,1)S(1)} %get-tuple-element.82), channel_id=1, source_target_pairs={{0,24},{4,28},{8,16},{12,20},{16,8},{20,12},{24,0},{28,4},{1,25},{... | collective-permute-start | bytes 196616 | tf_op jit(solution)/shard_map/ppermute | solution.py:209
  29.1 6.7 %collective-permute-start.13 = (bf16[2,2,64,128]{3,2,1,0:T(8,128)(2,1)S(1)}, bf16[2,2,64,128]{3,2,1,0:T(8,128)(2,1)S(1)}, u32[]{:S(2)}, u32[]{:S(2)}) collective-permute-start(bf16[2,2,64,128]{3,2,1,0:T(8,128)(2,1)S(1)} %get-tuple-element.83), channel_id=1, source_target_pairs={{0,16},{4,20},{8,24},{12,28},{16,0},{20,4},{24,8},{28,12},{1,17},{... | collective-permute-start | bytes 196616 | tf_op jit(solution)/shard_map/ppermute | solution.py:209
  36.9 5.9 %collective-permute-start.20 = (bf16[8,64,128]{2,1,0:T(8,128)(2,1)S(1)}, bf16[8,64,128]{2,1,0:T(8,128)(2,1)S(1)}, u32[]{:S(2)}, u32[]{:S(2)}) collective-permute-start(bf16[8,64,128]{2,1,0:T(8,128)(2,1)S(1)} %get-tuple-element.90.refs_1_), channel_id=1, source_target_pairs={{0,3},{1,2},{2,1},{3,0},{4,7},{5,6},{6,5},{7,4},{8,11},{9,10},{10,... | collective-permute-start | bytes 393224 | tf_op jit(solution)/shard_map/ppermute | solution.py:223
  37.3 8.1 %collective-permute-start.19 = (bf16[8,64,128]{2,1,0:T(8,128)(2,1)S(1)}, bf16[8,64,128]{2,1,0:T(8,128)(2,1)S(1)}, u32[]{:S(2)}, u32[]{:S(2)}) collective-permute-start(bf16[8,64,128]{2,1,0:T(8,128)(2,1)S(1)} %get-tuple-element.90.refs_1_), channel_id=1, source_target_pairs={{0,2},{1,3},{2,0},{3,1},{4,6},{5,7},{6,4},{7,5},{8,10},{9,11},{10,... | collective-permute-start | bytes 393224 | tf_op jit(solution)/shard_map/ppermute | solution.py:223
  38.4 7.0 %collective-permute-start.18 = (bf16[8,64,128]{2,1,0:T(8,128)(2,1)S(1)}, bf16[8,64,128]{2,1,0:T(8,128)(2,1)S(1)}, u32[]{:S(2)}, u32[]{:S(2)}) collective-permute-start(bf16[8,64,128]{2,1,0:T(8,128)(2,1)S(1)} %get-tuple-element.90.refs_1_), channel_id=1, source_target_pairs={{0,1},{1,0},{2,3},{3,2},{4,5},{5,4},{6,7},{7,6},{8,9},{9,8},{10,11... | collective-permute-start | bytes 393224 | tf_op jit(solution)/shard_map/ppermute | solution.py:223
  39.5 7.8 %collective-permute-start.15 = (bf16[2,2,64,128]{3,2,1,0:T(8,128)(2,1)S(1)}, bf16[2,2,64,128]{3,2,1,0:T(8,128)(2,1)S(1)}, u32[]{:S(2)}, u32[]{:S(2)}) collective-permute-start(bf16[2,2,64,128]{3,2,1,0:T(8,128)(2,1)S(1)} %get-tuple-element.92), channel_id=1, source_target_pairs={{0,24},{4,28},{8,16},{12,20},{16,8},{20,12},{24,0},{28,4},{1,25},{... | collective-permute-start | bytes 196616 | tf_op jit(solution)/shard_map/ppermute | solution.py:209
  42.0 6.3 %collective-permute-start.16 = (bf16[2,2,64,128]{3,2,1,0:T(8,128)(2,1)S(1)}, bf16[2,2,64,128]{3,2,1,0:T(8,128)(2,1)S(1)}, u32[]{:S(2)}, u32[]{:S(2)}) collective-permute-start(bf16[2,2,64,128]{3,2,1,0:T(8,128)(2,1)S(1)} %get-tuple-element.93), channel_id=1, source_target_pairs={{0,16},{4,20},{8,24},{12,28},{16,0},{20,4},{24,8},{28,12},{1,17},{... | collective-permute-start | bytes 196616 | tf_op jit(solution)/shard_map/ppermute | solution.py:209
  49.4 5.9 %collective-permute-start.21 = (bf16[8,64,128]{2,1,0:T(8,128)(2,1)S(1)}, bf16[8,64,128]{2,1,0:T(8,128)(2,1)S(1)}, u32[]{:S(2)}, u32[]{:S(2)}) collective-permute-start(bf16[8,64,128]{2,1,0:T(8,128)(2,1)S(1)} %get-tuple-element.102), channel_id=1, source_target_pairs={{0,3},{1,2},{2,1},{3,0},{4,7},{5,6},{6,5},{7,4},{8,11},{9,10},{10,... | collective-permute-start | bytes 393224 | tf_op jit(solution)/shard_map/ppermute | solution.py:223
  49.9 7.7 %collective-permute-start.22 = (bf16[8,64,128]{2,1,0:T(8,128)(2,1)S(1)}, bf16[8,64,128]{2,1,0:T(8,128)(2,1)S(1)}, u32[]{:S(2)}, u32[]{:S(2)}) collective-permute-start(bf16[8,64,128]{2,1,0:T(8,128)(2,1)S(1)} %get-tuple-element.103), channel_id=1, source_target_pairs={{0,2},{1,3},{2,0},{3,1},{4,6},{5,7},{6,4},{7,5},{8,10},{9,11},{10,... | collective-permute-start | bytes 393224 | tf_op jit(solution)/shard_map/ppermute | solution.py:223
  50.7 6.8 %collective-permute-start.23 = (bf16[8,64,128]{2,1,0:T(8,128)(2,1)S(1)}, bf16[8,64,128]{2,1,0:T(8,128)(2,1)S(1)}, u32[]{:S(2)}, u32[]{:S(2)}) collective-permute-start(bf16[8,64,128]{2,1,0:T(8,128)(2,1)S(1)} %get-tuple-element.104), channel_id=1, source_target_pairs={{0,1},{1,0},{2,3},{3,2},{4,5},{5,4},{6,7},{7,6},{8,9},{9,8},{10,11... | collective-permute-start | bytes 393224 | tf_op jit(solution)/shard_map/ppermute | solution.py:223
  52.4 6.2 %collective-permute-start.25 = (bf16[2,2,64,128]{3,2,1,0:T(8,128)(2,1)S(1)}, bf16[2,2,64,128]{3,2,1,0:T(8,128)(2,1)S(1)}, u32[]{:S(2)}, u32[]{:S(2)}) collective-permute-start(bf16[2,2,64,128]{3,2,1,0:T(8,128)(2,1)S(1)} %get-tuple-element.108), channel_id=1, source_target_pairs={{0,24},{4,28},{8,16},{12,20},{16,8},{20,12},{24,0},{28,4},{1,25},{... | collective-permute-start | bytes 196616 | tf_op jit(solution)/shard_map/ppermute | solution.py:209
  54.7 5.7 %collective-permute-start.26 = (bf16[2,2,64,128]{3,2,1,0:T(8,128)(2,1)S(1)}, bf16[2,2,64,128]{3,2,1,0:T(8,128)(2,1)S(1)}, u32[]{:S(2)}, u32[]{:S(2)}) collective-permute-start(bf16[2,2,64,128]{3,2,1,0:T(8,128)(2,1)S(1)} %get-tuple-element.109), channel_id=1, source_target_pairs={{0,16},{4,20},{8,24},{12,28},{16,0},{20,4},{24,8},{28,12},{1,17},{... | collective-permute-start | bytes 196616 | tf_op jit(solution)/shard_map/ppermute | solution.py:209
  55.2 5.7 %collective-permute-start.27 = (bf16[2,2,64,128]{3,2,1,0:T(8,128)(2,1)S(1)}, bf16[2,2,64,128]{3,2,1,0:T(8,128)(2,1)S(1)}, u32[]{:S(2)}, u32[]{:S(2)}) collective-permute-start(bf16[2,2,64,128]{3,2,1,0:T(8,128)(2,1)S(1)} %get-tuple-element.110), channel_id=1, source_target_pairs={{0,8},{4,12},{8,0},{12,4},{16,24},{20,28},{24,16},{28,20},{1,9},{5... | collective-permute-start | bytes 196616 | tf_op jit(solution)/shard_map/ppermute | solution.py:209
  (11 other events, 91.7 us)

commit v7 on v6

--- a/solution.py
+++ b/solution.py
@@ -107,13 +107,13 @@
 def forward_kernel(operators, *refs):
     dense = refs[:operators]
     parts = refs[operators : operators + 1 + refs[operators].shape[0]]
-    *partials, source, product = refs[operators + len(parts) :]
+    *owns, away, source, product = refs[operators + len(parts) :]
     quarters, quarter, hidden = product.shape
     width = quarters * quarter
     for turn, part in by_turn(parts):
         source[partner("node", turn)] = part[...]
     vectors = source[...].reshape(-1, hidden)
-    for row in range(partials[0].shape[0]):
+    for row in range(away.shape[1]):
         summed = sum(
             lax.dot_general(
                 vectors,
@@ -124,8 +124,13 @@
             for part in dense
         )
         product[...] = summed.T.reshape(product.shape)
-        for turn, partial in zip((0, *range(quarters - 1, 0, -1)), partials):
-            partial[row] = product[partner("edge", turn)].astype(partial.dtype)
+        for turn, own in enumerate(owns):
+            own[row] = product[partner("edge", 2 * turn)]
+            away[turn, row] = product[partner("edge", 2 * turn + 1)].astype(LOW)
+
+
+def half_sum_kernel(turn, own, got, send):
+    send[...] = (own[...] + got[turn].astype(FULL)).astype(LOW)
 
 
 def adjoint_kernel(operators, *refs):
@@ -139,22 +144,22 @@
     fill((kept, away), lambda turn, slot: product[partner("node", turn), slot])
 
 
-def state_of(arrived, teleport):
-    summed = arrived[0][...]
-    for part in arrived[1:]:
+def state_of(own, got, arrived, teleport):
+    summed = own[...] + got[0].astype(FULL)
+    for part in arrived:
         summed += part[...].astype(FULL)
     return 0.9 * summed + 0.1 * teleport[...]
 
 
-def next_state_kernel(table, teleport, *refs):
+def next_state_kernel(table, teleport, own, got, *refs):
     *arrived, kept, away, state = refs
-    state[...] = state_of(arrived, teleport)
+    state[...] = state_of(own, got, arrived, teleport)
     fill((kept, away), lambda turn, slot: state[requested(table, turn, slot)])
 
 
-def last_state_kernel(teleport, *refs):
+def last_state_kernel(teleport, own, got, *refs):
     *arrived, state = refs
-    state[...] = state_of(arrived, teleport)
+    state[...] = state_of(own, got, arrived, teleport)
 
 
 def gather_adjoint(table, parts, summed):
@@ -208,20 +213,37 @@
     def to_node(array, turn):
         return lax.ppermute(array, "node", [(place, place ^ turn) for place in range(owners)])
 
-    def over_node(kept, got):
-        pairs = call(
+    def pair_up(kept, got):
+        return call(
             pair_kernel,
             (kept, got),
             [VMEM] * 2,
             [(pair_shape, LOW)] * (owners // 2 - 1),
             [],
         )
-        return (kept, got, *(to_node(pair, 2 * turn) for turn, pair in far_first(pairs)))
-
-    def over_edge(arrays, turns):
-        return [arrays[0]] + [
-            lax.ppermute(array, "edge", [(place, place ^ turn) for place in range(quarters)])
-            for turn, array in zip(turns, arrays[1:])
+
+    def second_hop(pairs):
+        return [to_node(pair, 2 * turn) for turn, pair in far_first(pairs)]
+
+    def to_edge(array, turn):
+        return lax.ppermute(array, "edge", [(place, place ^ turn) for place in range(quarters)])
+
+    def gather_edge(array, others):
+        moved = [to_edge(array, turn) for turn in range(2, quarters, 2)]
+        near = to_edge(array, 1)
+        moved = after(moved, others)
+        return [array, near] + [part for high in moved for part in (high, to_edge(high, 1))]
+
+    def half_sums(owns, got):
+        return [
+            call(
+                functools.partial(half_sum_kernel, turn),
+                (own, got),
+                [VMEM] * 2,
+                [(shape, LOW)],
+                [],
+            )[0]
+            for turn, own in enumerate(owns[1:], 1)
         ]
 
     kept, away, rounded = call(
@@ -258,14 +280,15 @@
         last = step + 1 == STEPS
         dense = (high,) if last else (high, low)
         cost = pl.CostEstimate(
-            flops=2 * len(dense) * high.size * hidden,
-            bytes_accessed=len(dense) * high.size * 2,
+            flops=4 * high.size * hidden,
+            bytes_accessed=2 * high.size * 2,
             transcendentals=0,
         )
-        arrived = over_edge([rounded] * quarters, range(1, quarters))
         got = to_node(away, 1)
         (got,) = after((got,), (rounded, high) if step else (high,))
-        columns = over_node(kept, got)
+        pairs = pair_up(kept, got)
+        columns = (kept, got, *second_hop(pairs))
+        arrived = gather_edge(rounded, pairs if step else (high,))
         kept_sums, away_sums = call(
             functools.partial(adjoint_kernel, len(dense)),
             (*dense, *arrived),
@@ -279,26 +302,32 @@
         )
         got_sums = to_node(away_sums, 1)
         columns = after(columns, (away_sums,))
-        partials = call(
+        *owns, away_rows = call(
             functools.partial(forward_kernel, len(dense)),
             (*dense, *columns),
             [VMEM] * (len(columns) + len(dense)),
-            [(shape, FULL)] + [(shape, LOW)] * (quarters - 1),
+            [(shape, FULL)] * (quarters // 2) + [((quarters // 2, *shape), LOW)],
             [
                 pltpu.VMEM((owners, CAP, quarter, hidden), LOW),
                 pltpu.VMEM((quarters, quarter, hidden), FULL),
             ],
             cost=cost,
         )
-        (got_sums,) = after((got_sums,), partials[1:])
-        transposed = over_node(kept_sums, got_sums)
-        partials = over_edge(partials, range(quarters - 1, 0, -1))
+        (waiting_rows,) = after((away_rows,), (got_sums,))
+        (got_sums,) = after((got_sums,), (away_rows,))
+        got_rows = to_edge(waiting_rows, 1)
+        *far, near = pair_up(kept_sums, got_sums)
+        halves = half_sums(after(owns, (far[0],)), got_rows)
+        moved_rows = [to_edge(half, 2 * turn) for turn, half in enumerate(halves, 1)]
+        pairs = (*far, *after((near,), halves))
+        transposed = (kept_sums, got_sums, *second_hop(pairs))
+        partials = (owns[0], got_rows, *moved_rows)
         total = [pltpu.VMEM(shape, FULL)]
         if not last:
             kept, away = call(
                 next_state_kernel,
                 (fetch_table, teleport, *partials),
-                [SMEM] + [VMEM] * (1 + quarters),
+                [SMEM] + [VMEM] * (1 + len(partials)),
                 [(half_shape, LOW)] * 2,
                 total,
             )
@@ -314,7 +343,7 @@
             (state,) = call(
                 last_state_kernel,
                 (teleport, *partials),
-                [VMEM] * (1 + quarters),
+                [VMEM] * (1 + len(partials)),
                 [(shape, FULL)],
                 [],
             )

time: 62.6 us -> 67.1 us (1.072)
  waiting for transfers between devices: 15.2 us -> 19.9 us
    ppermute x16, waiting for transfers between devices: 9.24 us -> 12.7 us  [to_node(): lax.ppermute(array, 'node', [(place, place ^ turn) for place in range(own...]
    ppermute x12 -> x10, waiting for transfers between devices: 5.95 us -> 7.18 us  [to_edge(): lax.ppermute(array, 'edge', [(place, place ^ turn) for place in range(qua...]
    ppermute x12 -> x10, starting transfers between devices: 7.64 us -> 7.35 us  [to_edge(): lax.ppermute(array, 'edge', [(place, place ^ turn) for place in range(qua...]
    pallas_call x14 -> x16, Pallas kernels: 16.5 us -> 16.5 us  [call(): pl.pallas_call(kernel, out_shape=[jax.ShapeDtypeStruct(*out) for out in o...]
  transfers between devices with their start and end apart: 28 -> 26, of which waited for: 16 -> 11; matrix products, arithmetic and copies ran while one was open for 0% -> 0% of each run, Pallas kernels for 21% -> 20%
where the time goes in v7:
time: 67.1 us; the launch traced here: 66.9 us
  starting transfers between devices  28.2 us (42%)
  waiting for transfers between devices  19.9 us (30%)
  Pallas kernels  16.5 us (25%)
  local copies, waits for them, and re-layouts  1.39 us (2%)
  between operations  0.79 us (1%)
    ppermute x16, starting transfers between devices, to_node(): lax.ppermute(array, 'node', [(place, place ^ turn) for place in range(own...  20.9 us
    pallas_call x16, Pallas kernels, call(): pl.pallas_call(kernel, out_shape=[jax.ShapeDtypeStruct(*out) for out in o...  16.5 us
    ppermute x16, waiting for transfers between devices, to_node(): lax.ppermute(array, 'node', [(place, place ^ turn) for place in range(own...  12.7 us
    ppermute x10, starting transfers between devices, to_edge(): lax.ppermute(array, 'edge', [(place, place ^ turn) for place in range(qua...  7.35 us
    ppermute x10, waiting for transfers between devices, to_edge(): lax.ppermute(array, 'edge', [(place, place ^ turn) for place in range(qua...  7.18 us
    unnamed x14, local copies, waits for them, and re-layouts  1.39 us
  transfers between devices with their start and end apart: 26, of which 11 were waited for; matrix products, arithmetic and copies ran while one was open for 0% of the time, Pallas kernels for 20%

profile of v7, /device:TPU:0, one launch (start us, length us, event | category | flops | bytes accessed | tf_op | source)
XLA Modules:
  0.0 66.9 jit_solution(541044972432904202)
XLA Ops:
  0.6 1.8 %shard_map.78 = (bf16[4,2,64,128]{3,2,1,0:T(8,128)(2,1)}, bf16[4,2,64,128]{3,2,1,0:T(8,128)(2,1)}, bf16[8,64,128]{2,1,0:T(8,128)(2,1)}) custom-call(s32[8,16]{1,0:T(8,128)} %table.7, f32[8,64,128]{2,1,0:T(8,128)} %bitcast.4, f32[8,64,128]{2,1,0:T(8,128)} %bitcast.7), custom_call_target="tpu_custom_call" | custom-call | tf_op jit(solution)/shard_map/pallas_call | solution.py:200
  2.5 3.0 %collective-permute-start.5 = (bf16[8,64,128]{2,1,0:T(8,128)(2,1)}, bf16[8,64,128]{2,1,0:T(8,128)(2,1)S(1)}, u32[]{:S(2)}, u32[]{:S(2)}) collective-permute-start(bf16[8,64,128]{2,1,0:T(8,128)(2,1)} %get-tuple-element.73.refs_2_), channel_id=1, source_target_pairs={{0,2},{1,3},{2,0},{3,1},{4,6},{5,7},{6,4},{7,5},{8,10},{9,11},{10,... | collective-permute-start | bytes 393224 | tf_op jit(solution)/shard_map/ppermute | solution.py:229
  5.5 1.5 %collective-permute-start = (bf16[4,2,64,128]{3,2,1,0:T(8,128)(2,1)}, bf16[4,2,64,128]{3,2,1,0:T(8,128)(2,1)S(1)}, u32[]{:S(2)}, u32[]{:S(2)}) collective-permute-start(bf16[4,2,64,128]{3,2,1,0:T(8,128)(2,1)} %get-tuple-element.68), channel_id=1, source_target_pairs={{0,4},{4,0},{8,12},{12,8},{16,20},{20,16},{24,28},{28,24},{1,5},{5... | collective-permute-start | bytes 393224 | tf_op jit(solution)/shard_map/ppermute | solution.py:214
  8.3 4.7 %shard_map.77 = (bf16[1024,2048]{1,0:T(8,128)(2,1)S(1)}, bf16[1024,2048]{1,0:T(8,128)(2,1)S(1)}) custom-call(s32[1,192]{1,0:T(1,128)S(1)} %copy-done.5, s32[1,192]{1,0:T(1,128)S(1)} %copy-done.6, bf16[1,192,64,256]{3,2,1,0:T(8,128)(2,1)} %weights.1), custom_call_target="tpu_custom_call" | custom-call | bytes 6291456 | tf_op jit(solution)/shard_map/pallas_call | solution.py:200
  13.7 3.7 %collective-permute-start.1 = (bf16[2,2,64,128]{3,2,1,0:T(8,128)(2,1)S(1)}, bf16[2,2,64,128]{3,2,1,0:T(8,128)(2,1)S(1)}, u32[]{:S(2)}, u32[]{:S(2)}) collective-permute-start(bf16[2,2,64,128]{3,2,1,0:T(8,128)(2,1)S(1)} %get-tuple-element.70), channel_id=1, source_target_pairs={{0,24},{4,28},{8,16},{12,20},{16,8},{20,12},{24,0},{28,4},{1,25},{... | collective-permute-start | bytes 196616 | tf_op jit(solution)/shard_map/ppermute | solution.py:214
  18.1 2.4 %shard_map.80 = (bf16[4,2,64,128]{3,2,1,0:T(8,128)(2,1)S(1)}, bf16[4,2,64,128]{3,2,1,0:T(8,128)(2,1)S(1)}) custom-call(bf16[1024,2048]{1,0:T(8,128)(2,1)S(1)} %get-tuple-element.65.refs_0_, bf16[1024,2048]{1,0:T(8,128)(2,1)S(1)} %get-tuple-element.66.refs_1_, bf16[8,64,128]{2,1,0:T(8,128)(2,1)S(1)} %copy-done.3, ...), custom_call_target="tpu_custom_call" | custom-call | flops 1073741824 | bytes 8388608 | tf_op jit(solution)/shard_map/pallas_call | solution.py:200
  21.2 2.0 %collective-permute-done.2.refs_5_ = bf16[2,2,64,128]{3,2,1,0:T(8,128)(2,1)S(1)} collective-permute-done((bf16[2,2,64,128]{3,2,1,0:T(8,128)(2,1)S(1)}, bf16[2,2,64,128]{3,2,1,0:T(8,128)(2,1)S(1)}, u32[]{:S(2)}, u32[]{:S(2)}) %collective-permute-start.2) | collective-permute-done | bytes 65568 | tf_op jit(solution)/shard_map/ppermute | solution.py:214
  23.1 1.5 %shard_map.81 = (f32[8,64,128]{2,1,0:T(8,128)S(1)}, f32[8,64,128]{2,1,0:T(8,128)S(1)}, bf16[2,8,64,128]{3,2,1,0:T(8,128)(2,1)S(1)}) custom-call(bf16[1024,2048]{1,0:T(8,128)(2,1)S(1)} %get-tuple-element.65.refs_0_, bf16[1024,2048]{1,0:T(8,128)(2,1)S(1)} %get-tuple-element.66.refs_1_, bf16[4,2,64,128]{3,2,1,0:T(8,128)(2,1)S(1)} %copy-done.2, ...), custom_call_target="tpu_custom_call" | custom-call | flops 1073741824 | bytes 8388608 | tf_op jit(solution)/shard_map/pallas_call | solution.py:200
  25.6 1.5 %collective-permute-done.8.got = bf16[2,8,64,128]{3,2,1,0:T(8,128)(2,1)S(1)} collective-permute-done((bf16[2,8,64,128]{3,2,1,0:T(8,128)(2,1)S(1)}, bf16[2,8,64,128]{3,2,1,0:T(8,128)(2,1)S(1)}, u32[]{:S(2)}, u32[]{:S(2)}) %collective-permute-start.8) | collective-permute-done | bytes 262176 | tf_op jit(solution)/shard_map/ppermute | solution.py:229
  27.8 3.6 %collective-permute-start.11 = (bf16[2,2,64,128]{3,2,1,0:T(8,128)(2,1)S(1)}, bf16[2,2,64,128]{3,2,1,0:T(8,128)(2,1)S(1)}, u32[]{:S(2)}, u32[]{:S(2)}) collective-permute-start(bf16[2,2,64,128]{3,2,1,0:T(8,128)(2,1)S(1)} %get-tuple-element.87), channel_id=1, source_target_pairs={{0,24},{4,28},{8,16},{12,20},{16,8},{20,12},{24,0},{28,4},{1,25},{... | collective-permute-start | bytes 196616 | tf_op jit(solution)/shard_map/ppermute | solution.py:214
  34.1 2.9 %collective-permute-done.12.refs_3_ = bf16[2,2,64,128]{3,2,1,0:T(8,128)(2,1)S(1)} collective-permute-done((bf16[2,2,64,128]{3,2,1,0:T(8,128)(2,1)S(1)}, bf16[2,2,64,128]{3,2,1,0:T(8,128)(2,1)S(1)}, u32[]{:S(2)}, u32[]{:S(2)}) %collective-permute-start.12) | collective-permute-done | bytes 65568 | tf_op jit(solution)/shard_map/ppermute | solution.py:214
  37.8 1.6 %collective-permute-start.18 = (bf16[8,64,128]{2,1,0:T(8,128)(2,1)S(1)}, bf16[8,64,128]{2,1,0:T(8,128)(2,1)S(1)}, u32[]{:S(2)}, u32[]{:S(2)}) collective-permute-start(bf16[8,64,128]{2,1,0:T(8,128)(2,1)S(1)} %get-tuple-element.99.refs_1_), channel_id=1, source_target_pairs={{0,2},{1,3},{2,0},{3,1},{4,6},{5,7},{6,4},{7,5},{8,10},{9,11},{10,... | collective-permute-start | bytes 393224 | tf_op jit(solution)/shard_map/ppermute | solution.py:229
  39.4 3.5 %collective-permute-done.18.refs_3_ = bf16[8,64,128]{2,1,0:T(8,128)(2,1)S(1)} collective-permute-done((bf16[8,64,128]{2,1,0:T(8,128)(2,1)S(1)}, bf16[8,64,128]{2,1,0:T(8,128)(2,1)S(1)}, u32[]{:S(2)}, u32[]{:S(2)}) %collective-permute-start.18) | collective-permute-done | bytes 131104 | tf_op jit(solution)/shard_map/ppermute | solution.py:229
  42.9 2.2 %collective-permute-start.14 = (bf16[2,2,64,128]{3,2,1,0:T(8,128)(2,1)S(1)}, bf16[2,2,64,128]{3,2,1,0:T(8,128)(2,1)S(1)}, u32[]{:S(2)}, u32[]{:S(2)}) collective-permute-start(bf16[2,2,64,128]{3,2,1,0:T(8,128)(2,1)S(1)} %get-tuple-element.101), channel_id=1, source_target_pairs={{0,24},{4,28},{8,16},{12,20},{16,8},{20,12},{24,0},{28,4},{1,25},{... | collective-permute-start | bytes 196616 | tf_op jit(solution)/shard_map/ppermute | solution.py:214
  45.4 2.0 %collective-permute-start.16 = (bf16[2,2,64,128]{3,2,1,0:T(8,128)(2,1)S(1)}, bf16[2,2,64,128]{3,2,1,0:T(8,128)(2,1)S(1)}, u32[]{:S(2)}, u32[]{:S(2)}) collective-permute-start(bf16[2,2,64,128]{3,2,1,0:T(8,128)(2,1)S(1)} %get-tuple-element.103), channel_id=1, source_target_pairs={{0,8},{4,12},{8,0},{12,4},{16,24},{20,28},{24,16},{28,20},{1,9},{5... | collective-permute-start | bytes 196616 | tf_op jit(solution)/shard_map/ppermute | solution.py:214
  47.3 1.3 %shard_map.87 = (bf16[4,2,64,128]{3,2,1,0:T(8,128)(2,1)S(1)}, bf16[4,2,64,128]{3,2,1,0:T(8,128)(2,1)S(1)}) custom-call(bf16[1024,2048]{1,0:T(8,128)(2,1)S(1)} %get-tuple-element.65.refs_0_, bf16[8,64,128]{2,1,0:T(8,128)(2,1)S(1)} %get-tuple-element.99.refs_1_, bf16[8,64,128]{2,1,0:T(8,128)(2,1)S(1)} %collective-permute-done.17.refs_2_, ...), custom_call_target="tpu_custom_call" | custom-call | flops 1073741824 | bytes 8388608 | tf_op jit(solution)/shard_map/pallas_call | solution.py:200
  49.7 2.3 %collective-permute-done.15.refs_4_ = bf16[2,2,64,128]{3,2,1,0:T(8,128)(2,1)S(1)} collective-permute-done((bf16[2,2,64,128]{3,2,1,0:T(8,128)(2,1)S(1)}, bf16[2,2,64,128]{3,2,1,0:T(8,128)(2,1)S(1)}, u32[]{:S(2)}, u32[]{:S(2)}) %collective-permute-start.15) | collective-permute-done | bytes 65568 | tf_op jit(solution)/shard_map/ppermute | solution.py:214
  52.1 1.0 %shard_map.88 = (f32[8,64,128]{2,1,0:T(8,128)S(1)}, f32[8,64,128]{2,1,0:T(8,128)S(1)}, bf16[2,8,64,128]{3,2,1,0:T(8,128)(2,1)S(1)}) custom-call(bf16[1024,2048]{1,0:T(8,128)(2,1)S(1)} %get-tuple-element.65.refs_0_, bf16[4,2,64,128]{3,2,1,0:T(8,128)(2,1)S(1)} %get-tuple-element.106.kept.refs_1_, ...), custom_call_target="tpu_custom_call" | custom-call | flops 1073741824 | bytes 8388608 | tf_op jit(solution)/shard_map/pallas_call | solution.py:200
  53.8 1.5 %collective-permute-done.21.got = bf16[2,8,64,128]{3,2,1,0:T(8,128)(2,1)S(1)} collective-permute-done((bf16[2,8,64,128]{3,2,1,0:T(8,128)(2,1)S(1)}, bf16[2,8,64,128]{3,2,1,0:T(8,128)(2,1)S(1)}, u32[]{:S(2)}, u32[]{:S(2)}) %collective-permute-start.21) | collective-permute-done | bytes 262176 | tf_op jit(solution)/shard_map/ppermute | solution.py:229
  55.4 1.6 %collective-permute-start.22 = (bf16[8,64,128]{2,1,0:T(8,128)(2,1)S(1)}, bf16[8,64,128]{2,1,0:T(8,128)(2,1)S(1)}, u32[]{:S(2)}, u32[]{:S(2)}) collective-permute-start(bf16[8,64,128]{2,1,0:T(8,128)(2,1)S(1)} %shard_map.90), channel_id=1, source_target_pairs={{0,2},{1,3},{2,0},{3,1},{4,6},{5,7},{6,4},{7,5},{8,10},{9,11},{10,... | collective-permute-start | bytes 393224 | tf_op jit(solution)/shard_map/ppermute | solution.py:229
  56.9 2.2 %collective-permute-start.23 = (bf16[2,2,64,128]{3,2,1,0:T(8,128)(2,1)S(1)}, bf16[2,2,64,128]{3,2,1,0:T(8,128)(2,1)S(1)}, u32[]{:S(2)}, u32[]{:S(2)}) collective-permute-start(bf16[2,2,64,128]{3,2,1,0:T(8,128)(2,1)S(1)} %get-tuple-element.117), channel_id=1, source_target_pairs={{0,24},{4,28},{8,16},{12,20},{16,8},{20,12},{24,0},{28,4},{1,25},{... | collective-permute-start | bytes 196616 | tf_op jit(solution)/shard_map/ppermute | solution.py:214
  59.1 2.2 %collective-permute-start.25 = (bf16[2,2,64,128]{3,2,1,0:T(8,128)(2,1)S(1)}, bf16[2,2,64,128]{3,2,1,0:T(8,128)(2,1)S(1)}, u32[]{:S(2)}, u32[]{:S(2)}) collective-permute-start(bf16[2,2,64,128]{3,2,1,0:T(8,128)(2,1)S(1)} %get-tuple-element.122), channel_id=1, source_target_pairs={{0,8},{4,12},{8,0},{12,4},{16,24},{20,28},{24,16},{28,20},{1,9},{5... | collective-permute-start | bytes 196616 | tf_op jit(solution)/shard_map/ppermute | solution.py:214
  62.1 3.3 %collective-permute-done.24.refs_3_ = bf16[2,2,64,128]{3,2,1,0:T(8,128)(2,1)S(1)} collective-permute-done((bf16[2,2,64,128]{3,2,1,0:T(8,128)(2,1)S(1)}, bf16[2,2,64,128]{3,2,1,0:T(8,128)(2,1)S(1)}, u32[]{:S(2)}, u32[]{:S(2)}) %collective-permute-start.24) | collective-permute-done | bytes 65568 | tf_op jit(solution)/shard_map/ppermute | solution.py:214
  65.4 1.4 %shard_map.92 = f32[8,64,128]{2,1,0:T(8,128)} custom-call(s32[8,16]{1,0:T(8,128)S(1)} %copy-done.4, f32[8,64,128]{2,1,0:T(8,128)S(1)} %get-tuple-element.119.gradient_in, bf16[4,2,64,128]{3,2,1,0:T(8,128)(2,1)S(1)} %get-tuple-element.123.kept.refs_0_, bf16[4,2,64,128]{3,2,1,0:T(8,128)(2,1)S(1)} %collective-permute-done.20.got.refs_1_, ...), custom_call_target="tpu_custom_call" | custom-call | tf_op jit(solution)/shard_map/pallas_call | solution.py:200
  (58 shorter events, 11.4 us)
Async XLA Ops:
  2.5 10.6 %collective-permute-start.5 = (bf16[8,64,128]{2,1,0:T(8,128)(2,1)}, bf16[8,64,128]{2,1,0:T(8,128)(2,1)S(1)}, u32[]{:S(2)}, u32[]{:S(2)}) collective-permute-start(bf16[8,64,128]{2,1,0:T(8,128)(2,1)} %get-tuple-element.73.refs_2_), channel_id=1, source_target_pairs={{0,2},{1,3},{2,0},{3,1},{4,6},{5,7},{6,4},{7,5},{8,10},{9,11},{10,... | collective-permute-start | bytes 393224 | tf_op jit(solution)/shard_map/ppermute | solution.py:229
  5.5 8.2 %collective-permute-start = (bf16[4,2,64,128]{3,2,1,0:T(8,128)(2,1)}, bf16[4,2,64,128]{3,2,1,0:T(8,128)(2,1)S(1)}, u32[]{:S(2)}, u32[]{:S(2)}) collective-permute-start(bf16[4,2,64,128]{3,2,1,0:T(8,128)(2,1)} %get-tuple-element.68), channel_id=1, source_target_pairs={{0,4},{4,0},{8,12},{12,8},{16,20},{20,16},{24,28},{28,24},{1,5},{5... | collective-permute-start | bytes 393224 | tf_op jit(solution)/shard_map/ppermute | solution.py:214
  7.0 11.2 %collective-permute-start.4 = (bf16[8,64,128]{2,1,0:T(8,128)(2,1)}, bf16[8,64,128]{2,1,0:T(8,128)(2,1)S(1)}, u32[]{:S(2)}, u32[]{:S(2)}) collective-permute-start(bf16[8,64,128]{2,1,0:T(8,128)(2,1)} %get-tuple-element.73.refs_2_), channel_id=1, source_target_pairs={{0,1},{1,0},{2,3},{3,2},{4,5},{5,4},{6,7},{7,6},{8,9},{9,8},{10,11... | collective-permute-start | bytes 393224 | tf_op jit(solution)/shard_map/ppermute | solution.py:229
  13.1 5.1 %collective-permute-start.6 = (bf16[8,64,128]{2,1,0:T(8,128)(2,1)S(1)}, bf16[8,64,128]{2,1,0:T(8,128)(2,1)S(1)}, u32[]{:S(2)}, u32[]{:S(2)}) collective-permute-start(bf16[8,64,128]{2,1,0:T(8,128)(2,1)S(1)} %collective-permute-done.5.refs_4_), channel_id=1, source_target_pairs={{0,1},{1,0},{2,3},{3,2},{4,5},{5,4},{6,7},{7,6},{8,9},{9,8},{10,11... | collective-permute-start | bytes 393224 | tf_op jit(solution)/shard_map/ppermute | solution.py:229
  13.7 7.5 %collective-permute-start.1 = (bf16[2,2,64,128]{3,2,1,0:T(8,128)(2,1)S(1)}, bf16[2,2,64,128]{3,2,1,0:T(8,128)(2,1)S(1)}, u32[]{:S(2)}, u32[]{:S(2)}) collective-permute-start(bf16[2,2,64,128]{3,2,1,0:T(8,128)(2,1)S(1)} %get-tuple-element.70), channel_id=1, source_target_pairs={{0,24},{4,28},{8,16},{12,20},{16,8},{20,12},{24,0},{28,4},{1,25},{... | collective-permute-start | bytes 196616 | tf_op jit(solution)/shard_map/ppermute | solution.py:214
  17.3 5.8 %collective-permute-start.2 = (bf16[2,2,64,128]{3,2,1,0:T(8,128)(2,1)S(1)}, bf16[2,2,64,128]{3,2,1,0:T(8,128)(2,1)S(1)}, u32[]{:S(2)}, u32[]{:S(2)}) collective-permute-start(bf16[2,2,64,128]{3,2,1,0:T(8,128)(2,1)S(1)} %get-tuple-element.71), channel_id=1, source_target_pairs={{0,16},{4,20},{8,24},{12,28},{16,0},{20,4},{24,8},{28,12},{1,17},{... | collective-permute-start | bytes 196616 | tf_op jit(solution)/shard_map/ppermute | solution.py:214
  17.3 5.8 %collective-permute-start.3 = (bf16[2,2,64,128]{3,2,1,0:T(8,128)(2,1)S(1)}, bf16[2,2,64,128]{3,2,1,0:T(8,128)(2,1)S(1)}, u32[]{:S(2)}, u32[]{:S(2)}) collective-permute-start(bf16[2,2,64,128]{3,2,1,0:T(8,128)(2,1)S(1)} %get-tuple-element.72), channel_id=1, source_target_pairs={{0,8},{4,12},{8,0},{12,4},{16,24},{20,28},{24,16},{28,20},{1,9},{5... | collective-permute-start | bytes 196616 | tf_op jit(solution)/shard_map/ppermute | solution.py:214
  20.6 5.0 %collective-permute-start.7 = (bf16[4,2,64,128]{3,2,1,0:T(8,128)(2,1)S(1)}, bf16[4,2,64,128]{3,2,1,0:T(8,128)(2,1)S(1)}, u32[]{:S(2)}, u32[]{:S(2)}) collective-permute-start(bf16[4,2,64,128]{3,2,1,0:T(8,128)(2,1)S(1)} %get-tuple-element.75), channel_id=1, source_target_pairs={{0,4},{4,0},{8,12},{12,8},{16,20},{20,16},{24,28},{28,24},{1,5},{5... | collective-permute-start | bytes 393224 | tf_op jit(solution)/shard_map/ppermute | solution.py:214
  27.2 5.6 %collective-permute-start.9 = (bf16[8,64,128]{2,1,0:T(8,128)(2,1)S(1)}, bf16[8,64,128]{2,1,0:T(8,128)(2,1)S(1)}, u32[]{:S(2)}, u32[]{:S(2)}) collective-permute-start(bf16[8,64,128]{2,1,0:T(8,128)(2,1)S(1)} %shard_map.83), channel_id=1, source_target_pairs={{0,2},{1,3},{2,0},{3,1},{4,6},{5,7},{6,4},{7,5},{8,10},{9,11},{10,... | collective-permute-start | bytes 393224 | tf_op jit(solution)/shard_map/ppermute | solution.py:229
  27.8 9.3 %collective-permute-start.11 = (bf16[2,2,64,128]{3,2,1,0:T(8,128)(2,1)S(1)}, bf16[2,2,64,128]{3,2,1,0:T(8,128)(2,1)S(1)}, u32[]{:S(2)}, u32[]{:S(2)}) collective-permute-start(bf16[2,2,64,128]{3,2,1,0:T(8,128)(2,1)S(1)} %get-tuple-element.87), channel_id=1, source_target_pairs={{0,24},{4,28},{8,16},{12,20},{16,8},{20,12},{24,0},{28,4},{1,25},{... | collective-permute-start | bytes 196616 | tf_op jit(solution)/shard_map/ppermute | solution.py:214
  31.4 5.7 %collective-permute-start.12 = (bf16[2,2,64,128]{3,2,1,0:T(8,128)(2,1)S(1)}, bf16[2,2,64,128]{3,2,1,0:T(8,128)(2,1)S(1)}, u32[]{:S(2)}, u32[]{:S(2)}) collective-permute-start(bf16[2,2,64,128]{3,2,1,0:T(8,128)(2,1)S(1)} %get-tuple-element.91), channel_id=1, source_target_pairs={{0,16},{4,20},{8,24},{12,28},{16,0},{20,4},{24,8},{28,12},{1,17},{... | collective-permute-start | bytes 196616 | tf_op jit(solution)/shard_map/ppermute | solution.py:214
  31.4 5.7 %collective-permute-start.13 = (bf16[2,2,64,128]{3,2,1,0:T(8,128)(2,1)S(1)}, bf16[2,2,64,128]{3,2,1,0:T(8,128)(2,1)S(1)}, u32[]{:S(2)}, u32[]{:S(2)}) collective-permute-start(bf16[2,2,64,128]{3,2,1,0:T(8,128)(2,1)S(1)} %get-tuple-element.93), channel_id=1, source_target_pairs={{0,8},{4,12},{8,0},{12,4},{16,24},{20,28},{24,16},{28,20},{1,9},{5... | collective-permute-start | bytes 196616 | tf_op jit(solution)/shard_map/ppermute | solution.py:214
  33.5 5.9 %collective-permute-start.10 = (bf16[4,2,64,128]{3,2,1,0:T(8,128)(2,1)S(1)}, bf16[4,2,64,128]{3,2,1,0:T(8,128)(2,1)S(1)}, u32[]{:S(2)}, u32[]{:S(2)}) collective-permute-start(bf16[4,2,64,128]{3,2,1,0:T(8,128)(2,1)S(1)} %get-tuple-element.90), channel_id=1, source_target_pairs={{0,4},{4,0},{8,12},{12,8},{16,20},{20,16},{24,28},{28,24},{1,5},{5... | collective-permute-start | bytes 393224 | tf_op jit(solution)/shard_map/ppermute | solution.py:214
  37.8 5.1 %collective-permute-start.18 = (bf16[8,64,128]{2,1,0:T(8,128)(2,1)S(1)}, bf16[8,64,128]{2,1,0:T(8,128)(2,1)S(1)}, u32[]{:S(2)}, u32[]{:S(2)}) collective-permute-start(bf16[8,64,128]{2,1,0:T(8,128)(2,1)S(1)} %get-tuple-element.99.refs_1_), channel_id=1, source_target_pairs={{0,2},{1,3},{2,0},{3,1},{4,6},{5,7},{6,4},{7,5},{8,10},{9,11},{10,... | collective-permute-start | bytes 393224 | tf_op jit(solution)/shard_map/ppermute | solution.py:229
  39.4 7.9 %collective-permute-start.17 = (bf16[8,64,128]{2,1,0:T(8,128)(2,1)S(1)}, bf16[8,64,128]{2,1,0:T(8,128)(2,1)S(1)}, u32[]{:S(2)}, u32[]{:S(2)}) collective-permute-start(bf16[8,64,128]{2,1,0:T(8,128)(2,1)S(1)} %get-tuple-element.99.refs_1_), channel_id=1, source_target_pairs={{0,1},{1,0},{2,3},{3,2},{4,5},{5,4},{6,7},{7,6},{8,9},{9,8},{10,11... | collective-permute-start | bytes 393224 | tf_op jit(solution)/shard_map/ppermute | solution.py:229
  42.9 4.4 %collective-permute-start.19 = (bf16[8,64,128]{2,1,0:T(8,128)(2,1)S(1)}, bf16[8,64,128]{2,1,0:T(8,128)(2,1)S(1)}, u32[]{:S(2)}, u32[]{:S(2)}) collective-permute-start(bf16[8,64,128]{2,1,0:T(8,128)(2,1)S(1)} %collective-permute-done.18.refs_3_), channel_id=1, source_target_pairs={{0,1},{1,0},{2,3},{3,2},{4,5},{5,4},{6,7},{7,6},{8,9},{9,8},{10,11... | collective-permute-start | bytes 393224 | tf_op jit(solution)/shard_map/ppermute | solution.py:229
  42.9 6.8 %collective-permute-start.14 = (bf16[2,2,64,128]{3,2,1,0:T(8,128)(2,1)S(1)}, bf16[2,2,64,128]{3,2,1,0:T(8,128)(2,1)S(1)}, u32[]{:S(2)}, u32[]{:S(2)}) collective-permute-start(bf16[2,2,64,128]{3,2,1,0:T(8,128)(2,1)S(1)} %get-tuple-element.101), channel_id=1, source_target_pairs={{0,24},{4,28},{8,16},{12,20},{16,8},{20,12},{24,0},{28,4},{1,25},{... | collective-permute-start | bytes 196616 | tf_op jit(solution)/shard_map/ppermute | solution.py:214
  45.1 6.9 %collective-permute-start.15 = (bf16[2,2,64,128]{3,2,1,0:T(8,128)(2,1)S(1)}, bf16[2,2,64,128]{3,2,1,0:T(8,128)(2,1)S(1)}, u32[]{:S(2)}, u32[]{:S(2)}) collective-permute-start(bf16[2,2,64,128]{3,2,1,0:T(8,128)(2,1)S(1)} %get-tuple-element.102), channel_id=1, source_target_pairs={{0,16},{4,20},{8,24},{12,28},{16,0},{20,4},{24,8},{28,12},{1,17},{... | collective-permute-start | bytes 196616 | tf_op jit(solution)/shard_map/ppermute | solution.py:214
  45.4 6.7 %collective-permute-start.16 = (bf16[2,2,64,128]{3,2,1,0:T(8,128)(2,1)S(1)}, bf16[2,2,64,128]{3,2,1,0:T(8,128)(2,1)S(1)}, u32[]{:S(2)}, u32[]{:S(2)}) collective-permute-start(bf16[2,2,64,128]{3,2,1,0:T(8,128)(2,1)S(1)} %get-tuple-element.103), channel_id=1, source_target_pairs={{0,8},{4,12},{8,0},{12,4},{16,24},{20,28},{24,16},{28,20},{1,9},{5... | collective-permute-start | bytes 196616 | tf_op jit(solution)/shard_map/ppermute | solution.py:214
  48.7 5.1 %collective-permute-start.20 = (bf16[4,2,64,128]{3,2,1,0:T(8,128)(2,1)S(1)}, bf16[4,2,64,128]{3,2,1,0:T(8,128)(2,1)S(1)}, u32[]{:S(2)}, u32[]{:S(2)}) collective-permute-start(bf16[4,2,64,128]{3,2,1,0:T(8,128)(2,1)S(1)} %get-tuple-element.105), channel_id=1, source_target_pairs={{0,4},{4,0},{8,12},{12,8},{16,20},{20,16},{24,28},{28,24},{1,5},{5... | collective-permute-start | bytes 393224 | tf_op jit(solution)/shard_map/ppermute | solution.py:214
  55.4 6.0 %collective-permute-start.22 = (bf16[8,64,128]{2,1,0:T(8,128)(2,1)S(1)}, bf16[8,64,128]{2,1,0:T(8,128)(2,1)S(1)}, u32[]{:S(2)}, u32[]{:S(2)}) collective-permute-start(bf16[8,64,128]{2,1,0:T(8,128)(2,1)S(1)} %shard_map.90), channel_id=1, source_target_pairs={{0,2},{1,3},{2,0},{3,1},{4,6},{5,7},{6,4},{7,5},{8,10},{9,11},{10,... | collective-permute-start | bytes 393224 | tf_op jit(solution)/shard_map/ppermute | solution.py:229
  56.9 8.5 %collective-permute-start.23 = (bf16[2,2,64,128]{3,2,1,0:T(8,128)(2,1)S(1)}, bf16[2,2,64,128]{3,2,1,0:T(8,128)(2,1)S(1)}, u32[]{:S(2)}, u32[]{:S(2)}) collective-permute-start(bf16[2,2,64,128]{3,2,1,0:T(8,128)(2,1)S(1)} %get-tuple-element.117), channel_id=1, source_target_pairs={{0,24},{4,28},{8,16},{12,20},{16,8},{20,12},{24,0},{28,4},{1,25},{... | collective-permute-start | bytes 196616 | tf_op jit(solution)/shard_map/ppermute | solution.py:214
  59.1 6.3 %collective-permute-start.24 = (bf16[2,2,64,128]{3,2,1,0:T(8,128)(2,1)S(1)}, bf16[2,2,64,128]{3,2,1,0:T(8,128)(2,1)S(1)}, u32[]{:S(2)}, u32[]{:S(2)}) collective-permute-start(bf16[2,2,64,128]{3,2,1,0:T(8,128)(2,1)S(1)} %get-tuple-element.120), channel_id=1, source_target_pairs={{0,16},{4,20},{8,24},{12,28},{16,0},{20,4},{24,8},{28,12},{1,17},{... | collective-permute-start | bytes 196616 | tf_op jit(solution)/shard_map/ppermute | solution.py:214
  59.1 6.3 %collective-permute-start.25 = (bf16[2,2,64,128]{3,2,1,0:T(8,128)(2,1)S(1)}, bf16[2,2,64,128]{3,2,1,0:T(8,128)(2,1)S(1)}, u32[]{:S(2)}, u32[]{:S(2)}) collective-permute-start(bf16[2,2,64,128]{3,2,1,0:T(8,128)(2,1)S(1)} %get-tuple-element.122), channel_id=1, source_target_pairs={{0,8},{4,12},{8,0},{12,4},{16,24},{20,28},{24,16},{28,20},{1,9},{5... | collective-permute-start | bytes 196616 | tf_op jit(solution)/shard_map/ppermute | solution.py:214
  (9 other events, 72.3 us)

commit v8 on v6

--- a/solution.py
+++ b/solution.py
@@ -12,6 +12,7 @@
 DENSE_BYTES = 8 * 2**20
 START_MEBIBYTES = 60
 BUILD_MEBIBYTES = 40
+IDS_ROOM = 24576
 LOW = jnp.bfloat16
 FULL = jnp.float32
 
@@ -40,12 +41,18 @@
                 send[turn, slot] = block(2 * turn + low, slot).astype(send.dtype)
 
 
-def start_kernel(table, teleport, cotangent, *refs):
-    *sends, rounded, plan, state, adjoint, sems = refs
+def start_kernel(table, teleport, cotangent, rows, slots, *refs):
+    *sends, rounded, ids, plan, state, adjoint, sems = refs
     copies = [
         pltpu.make_async_copy(source, target, sems.at[index])
         for index, (source, target) in enumerate(
-            ((table, plan), (teleport, state), (cotangent, adjoint))
+            (
+                (table, plan),
+                (teleport, state),
+                (cotangent, adjoint),
+                (rows, ids.at[0]),
+                (slots, ids.at[1]),
+            )
         )
     ]
     for copy in copies:
@@ -55,10 +62,12 @@
     fill(sends, lambda turn, slot: state[requested(plan, turn, slot)])
     copies[2].wait()
     rounded[...] = adjoint[...].astype(LOW)
-
-
-def build_kernel(rows, slots, weights, high, low, held, total, sems):
-    parts = sems.shape[0]
+    copies[3].wait()
+    copies[4].wait()
+
+
+def build_kernel(ids, weights, high, low, held, total, own_ids, sems):
+    parts = sems.shape[0] - 1
     block_count, quarter, width = held.shape
     chunk = block_count // parts
     copies = [
@@ -69,13 +78,16 @@
         )
         for part in range(parts)
     ]
+    ids_copy = pltpu.make_async_copy(ids.at[pl.ds(0, 2)], own_ids, sems.at[parts])
+    ids_copy.start()
     for copy in copies:
         copy.start()
     total[...] = jnp.zeros_like(total)
+    ids_copy.wait()
     for part, copy in enumerate(copies):
         copy.wait()
         for block in range(part * chunk, (part + 1) * chunk):
-            total[slots[0, block], rows[0, block]] += held[block].astype(FULL)
+            total[own_ids[1, 0, block], own_ids[0, 0, block]] += held[block].astype(FULL)
     for slot in range(total.shape[0]):
         for row in range(total.shape[1]):
             place = (pl.ds(slot * quarter, quarter), pl.ds(row * width, width))
@@ -124,7 +136,7 @@
             for part in dense
         )
         product[...] = summed.T.reshape(product.shape)
-        for turn, partial in zip((0, *range(quarters - 1, 0, -1)), partials):
+        for turn, partial in zip((0, 1, *range(quarters - 1, 1, -1)), partials):
             partial[row] = product[partner("edge", turn)].astype(partial.dtype)
 
 
@@ -191,12 +203,12 @@
     teleport = teleport.reshape(shape)
     cotangent = cotangent.reshape(shape)
 
-    def call(kernel, operands, places, outs, scratch, mebibytes=8, cost=None):
+    def call(kernel, operands, places, outs, scratch, mebibytes=8, cost=None, places_out=None):
         return pl.pallas_call(
             kernel,
             out_shape=[jax.ShapeDtypeStruct(*out) for out in outs],
             in_specs=places,
-            out_specs=[VMEM] * len(outs),
+            out_specs=places_out or [VMEM] * len(outs),
             scratch_shapes=scratch,
             compiler_params=params(mebibytes),
             cost_estimate=cost,
@@ -224,30 +236,33 @@
             for turn, array in zip(turns, arrays[1:])
         ]
 
-    kept, away, rounded = call(
+    kept, away, rounded, ids = call(
         start_kernel,
-        (fetch_table, teleport, cotangent),
-        [HBM] * 3,
-        [(half_shape, LOW)] * 2 + [(shape, LOW)],
+        (fetch_table, teleport, cotangent, block_row, block_slot),
+        [HBM] * 5,
+        [(half_shape, LOW)] * 2
+        + [(shape, LOW), ((IDS_ROOM, *block_row.shape), block_row.dtype)],
         [
             pltpu.SMEM(fetch_table.shape, fetch_table.dtype),
             pltpu.VMEM(shape, FULL),
             pltpu.VMEM(shape, FULL),
-            pltpu.SemaphoreType.DMA((3,)),
+            pltpu.SemaphoreType.DMA((5,)),
         ],
         START_MEBIBYTES,
+        places_out=[VMEM] * 3 + [HBM],
     )
     dense_shape = (slot_total * quarter, count * width)
     parts = next(size for size in (12, 8, 4, 2, 1) if block_count % size == 0)
     high, low = call(
         build_kernel,
-        (block_row, block_slot, values),
-        [SMEM, SMEM, HBM],
+        (ids, values),
+        [HBM] * 2,
         [(dense_shape, LOW)] * 2,
         [
             pltpu.VMEM((block_count, quarter, width), LOW),
             pltpu.VMEM((slot_total, count, quarter, width), FULL),
-            pltpu.SemaphoreType.DMA((parts,)),
+            pltpu.SMEM((2, *block_row.shape), block_row.dtype),
+            pltpu.SemaphoreType.DMA((parts + 1,)),
         ],
         BUILD_MEBIBYTES,
         pl.CostEstimate(flops=0, bytes_accessed=values.size * 2, transcendentals=0),
@@ -292,7 +307,7 @@
         )
         (got_sums,) = after((got_sums,), partials[1:])
         transposed = over_node(kept_sums, got_sums)
-        partials = over_edge(partials, range(quarters - 1, 0, -1))
+        partials = over_edge(partials, (1, *range(quarters - 1, 1, -1)))
         total = [pltpu.VMEM(shape, FULL)]
         if not last:
             kept, away = call(

time: 62.6 us -> 60.1 us (0.960)
  waiting for transfers between devices: 15.2 us -> 13.1 us
  starting transfers between devices: 28.5 us -> 29.9 us
  local copies, waits for them, and re-layouts: 1.39 us -> 0.03 us
    ppermute x16, waiting for transfers between devices: 9.24 us -> 7.47 us  [to_node(): lax.ppermute(array, 'node', [(place, place ^ turn) for place in range(own...]
    unnamed x14 -> x10, local copies, waits for them, and re-layouts: 1.39 us -> 0.03 us
    ppermute x16, starting transfers between devices: 20.8 us -> 21.7 us  [to_node(): lax.ppermute(array, 'node', [(place, place ^ turn) for place in range(own...]
  transfers between devices with their start and end apart: 28 -> 28, of which waited for: 16 -> 11; matrix products, arithmetic and copies ran while one was open for 0% -> 0% of each run, Pallas kernels for 21% -> 21%
where the time goes in v8:
time: 60.1 us; the launch traced here: 60 us
  starting transfers between devices  29.9 us (50%)
  Pallas kernels  16.1 us (27%)
  waiting for transfers between devices  13.1 us (22%)
  between operations  0.8 us (1%)
    ppermute x16, starting transfers between devices, to_node(): lax.ppermute(array, 'node', [(place, place ^ turn) for place in range(own...  21.7 us
    pallas_call x14, Pallas kernels, call(): pl.pallas_call(kernel, out_shape=[jax.ShapeDtypeStruct(*out) for out in o...  16.1 us
    ppermute x12, starting transfers between devices, over_edge(): lax.ppermute(array, 'edge', [(place, place ^ turn) for place in range(qua...  8.21 us
    ppermute x16, waiting for transfers between devices, to_node(): lax.ppermute(array, 'node', [(place, place ^ turn) for place in range(own...  7.47 us
    ppermute x12, waiting for transfers between devices, over_edge(): lax.ppermute(array, 'edge', [(place, place ^ turn) for place in range(qua...  5.66 us
  transfers between devices with their start and end apart: 28, of which 11 were waited for; matrix products, arithmetic and copies ran while one was open for 0% of the time, Pallas kernels for 21%

profile of v8, /device:TPU:0, one launch (start us, length us, event | category | flops | bytes accessed | tf_op | source)
XLA Modules:
  0.0 60.0 jit_solution(13960195316263871264)
XLA Ops:
  0.6 2.0 %shard_map.77 = (bf16[4,2,64,128]{3,2,1,0:T(8,128)(2,1)}, bf16[4,2,64,128]{3,2,1,0:T(8,128)(2,1)}, bf16[8,64,128]{2,1,0:T(8,128)(2,1)}, s32[24576,1,192]{2,1,0:T(1,128)}) custom-call(s32[8,16]{1,0:T(8,128)} %table.7, f32[8,64,128]{2,1,0:T(8,128)} %bitcast.4, f32[8,64,128]{2,1,0:T(8,128)} %bitcast.7, s32[1,192]{1,0:T(1,128)} %rows.1, s32[1,192]{1,0:T(1,128)} %slots.1), custom_call_target="tpu_custom_call" | custom-call | tf_op jit(solution)/shard_map/pallas_call | solution.py:207
  2.6 3.0 %collective-permute-start = (bf16[4,2,64,128]{3,2,1,0:T(8,128)(2,1)}, bf16[4,2,64,128]{3,2,1,0:T(8,128)(2,1)S(1)}, u32[]{:S(2)}, u32[]{:S(2)}) collective-permute-start(bf16[4,2,64,128]{3,2,1,0:T(8,128)(2,1)} %get-tuple-element.64), channel_id=1, source_target_pairs={{0,4},{4,0},{8,12},{12,8},{16,20},{20,16},{24,28},{28,24},{1,5},{5... | collective-permute-start | bytes 393224 | tf_op jit(solution)/shard_map/ppermute | solution.py:221
  7.5 4.2 %shard_map.78 = (bf16[1024,2048]{1,0:T(8,128)(2,1)S(1)}, bf16[1024,2048]{1,0:T(8,128)(2,1)S(1)}) custom-call(s32[24576,1,192]{2,1,0:T(1,128)} %get-tuple-element.60.ids, bf16[1,192,64,256]{3,2,1,0:T(8,128)(2,1)} %weights.1), custom_call_target="tpu_custom_call" | custom-call | bytes 6291456 | tf_op jit(solution)/shard_map/pallas_call | solution.py:207
  11.7 3.7 %collective-permute-start.1 = (bf16[2,2,64,128]{3,2,1,0:T(8,128)(2,1)S(1)}, bf16[2,2,64,128]{3,2,1,0:T(8,128)(2,1)S(1)}, u32[]{:S(2)}, u32[]{:S(2)}) collective-permute-start(bf16[2,2,64,128]{3,2,1,0:T(8,128)(2,1)S(1)} %get-tuple-element.66), channel_id=1, source_target_pairs={{0,24},{4,28},{8,16},{12,20},{16,8},{20,12},{24,0},{28,4},{1,25},{... | collective-permute-start | bytes 196616 | tf_op jit(solution)/shard_map/ppermute | solution.py:221
  16.2 2.4 %shard_map.80 = (bf16[4,2,64,128]{3,2,1,0:T(8,128)(2,1)S(1)}, bf16[4,2,64,128]{3,2,1,0:T(8,128)(2,1)S(1)}) custom-call(bf16[1024,2048]{1,0:T(8,128)(2,1)S(1)} %get-tuple-element.61.refs_0_, bf16[1024,2048]{1,0:T(8,128)(2,1)S(1)} %get-tuple-element.62.refs_1_, bf16[8,64,128]{2,1,0:T(8,128)(2,1)S(1)} %copy-done.3, ...), custom_call_target="tpu_custom_call" | custom-call | flops 1073741824 | bytes 8388608 | tf_op jit(solution)/shard_map/pallas_call | solution.py:207
  19.1 2.2 %collective-permute-done.2.refs_5_ = bf16[2,2,64,128]{3,2,1,0:T(8,128)(2,1)S(1)} collective-permute-done((bf16[2,2,64,128]{3,2,1,0:T(8,128)(2,1)S(1)}, bf16[2,2,64,128]{3,2,1,0:T(8,128)(2,1)S(1)}, u32[]{:S(2)}, u32[]{:S(2)}) %collective-permute-start.2) | collective-permute-done | bytes 65568 | tf_op jit(solution)/shard_map/ppermute | solution.py:221
  21.3 1.5 %shard_map.81 = (f32[8,64,128]{2,1,0:T(8,128)S(1)}, bf16[8,64,128]{2,1,0:T(8,128)(2,1)S(1)}, bf16[8,64,128]{2,1,0:T(8,128)(2,1)S(1)}, bf16[8,64,128]{2,1,0:T(8,128)(2,1)S(1)}) custom-call(bf16[1024,2048]{1,0:T(8,128)(2,1)S(1)} %get-tuple-element.61.refs_0_, bf16[1024,2048]{1,0:T(8,128)(2,1)S(1)} %get-tuple-element.62.refs_1_, ...), custom_call_target="tpu_custom_call" | custom-call | flops 1073741824 | bytes 8388608 | tf_op jit(solution)/shard_map/pallas_call | solution.py:207
  22.9 1.5 %collective-permute-start.8 = (bf16[8,64,128]{2,1,0:T(8,128)(2,1)S(1)}, bf16[8,64,128]{2,1,0:T(8,128)(2,1)S(1)}, u32[]{:S(2)}, u32[]{:S(2)}) collective-permute-start(bf16[8,64,128]{2,1,0:T(8,128)(2,1)S(1)} %get-tuple-element.78), channel_id=1, source_target_pairs={{0,3},{1,2},{2,1},{3,0},{4,7},{5,6},{6,5},{7,4},{8,11},{9,10},{10,... | collective-permute-start | bytes 393224 | tf_op jit(solution)/shard_map/ppermute | solution.py:235
  25.0 2.5 %collective-permute-start.12 = (bf16[2,2,64,128]{3,2,1,0:T(8,128)(2,1)S(1)}, bf16[2,2,64,128]{3,2,1,0:T(8,128)(2,1)S(1)}, u32[]{:S(2)}, u32[]{:S(2)}) collective-permute-start(bf16[2,2,64,128]{3,2,1,0:T(8,128)(2,1)S(1)} %get-tuple-element.84), channel_id=1, source_target_pairs={{0,24},{4,28},{8,16},{12,20},{16,8},{20,12},{24,0},{28,4},{1,25},{... | collective-permute-start | bytes 196616 | tf_op jit(solution)/shard_map/ppermute | solution.py:221
  27.7 1.8 %collective-permute-start.14 = (bf16[2,2,64,128]{3,2,1,0:T(8,128)(2,1)S(1)}, bf16[2,2,64,128]{3,2,1,0:T(8,128)(2,1)S(1)}, u32[]{:S(2)}, u32[]{:S(2)}) collective-permute-start(bf16[2,2,64,128]{3,2,1,0:T(8,128)(2,1)S(1)} %get-tuple-element.86), channel_id=1, source_target_pairs={{0,8},{4,12},{8,0},{12,4},{16,24},{20,28},{24,16},{28,20},{1,9},{5... | collective-permute-start | bytes 196616 | tf_op jit(solution)/shard_map/ppermute | solution.py:221
  29.5 2.0 %collective-permute-done.9.refs_3_ = bf16[8,64,128]{2,1,0:T(8,128)(2,1)S(1)} collective-permute-done((bf16[8,64,128]{2,1,0:T(8,128)(2,1)S(1)}, bf16[8,64,128]{2,1,0:T(8,128)(2,1)S(1)}, u32[]{:S(2)}, u32[]{:S(2)}) %collective-permute-start.9) | collective-permute-done | bytes 131104 | tf_op jit(solution)/shard_map/ppermute | solution.py:235
  32.9 1.3 %collective-permute-done.13.refs_3_ = bf16[2,2,64,128]{3,2,1,0:T(8,128)(2,1)S(1)} collective-permute-done((bf16[2,2,64,128]{3,2,1,0:T(8,128)(2,1)S(1)}, bf16[2,2,64,128]{3,2,1,0:T(8,128)(2,1)S(1)}, u32[]{:S(2)}, u32[]{:S(2)}) %collective-permute-start.13) | collective-permute-done | bytes 65568 | tf_op jit(solution)/shard_map/ppermute | solution.py:221
  37.3 2.5 %collective-permute-start.15 = (bf16[2,2,64,128]{3,2,1,0:T(8,128)(2,1)S(1)}, bf16[2,2,64,128]{3,2,1,0:T(8,128)(2,1)S(1)}, u32[]{:S(2)}, u32[]{:S(2)}) collective-permute-start(bf16[2,2,64,128]{3,2,1,0:T(8,128)(2,1)S(1)} %get-tuple-element.94), channel_id=1, source_target_pairs={{0,24},{4,28},{8,16},{12,20},{16,8},{20,12},{24,0},{28,4},{1,25},{... | collective-permute-start | bytes 196616 | tf_op jit(solution)/shard_map/ppermute | solution.py:221
  40.8 1.0 %collective-permute-start.17 = (bf16[2,2,64,128]{3,2,1,0:T(8,128)(2,1)S(1)}, bf16[2,2,64,128]{3,2,1,0:T(8,128)(2,1)S(1)}, u32[]{:S(2)}, u32[]{:S(2)}) collective-permute-start(bf16[2,2,64,128]{3,2,1,0:T(8,128)(2,1)S(1)} %get-tuple-element.96), channel_id=1, source_target_pairs={{0,8},{4,12},{8,0},{12,4},{16,24},{20,28},{24,16},{28,20},{1,9},{5... | collective-permute-start | bytes 196616 | tf_op jit(solution)/shard_map/ppermute | solution.py:221
  41.8 1.6 %collective-permute-done.19.refs_3_ = bf16[8,64,128]{2,1,0:T(8,128)(2,1)S(1)} collective-permute-done((bf16[8,64,128]{2,1,0:T(8,128)(2,1)S(1)}, bf16[8,64,128]{2,1,0:T(8,128)(2,1)S(1)}, u32[]{:S(2)}, u32[]{:S(2)}) %collective-permute-start.19) | collective-permute-done | bytes 131104 | tf_op jit(solution)/shard_map/ppermute | solution.py:235
  43.4 1.3 %shard_map.86 = (bf16[4,2,64,128]{3,2,1,0:T(8,128)(2,1)S(1)}, bf16[4,2,64,128]{3,2,1,0:T(8,128)(2,1)S(1)}) custom-call(bf16[1024,2048]{1,0:T(8,128)(2,1)S(1)} %get-tuple-element.61.refs_0_, bf16[8,64,128]{2,1,0:T(8,128)(2,1)S(1)} %get-tuple-element.92.refs_1_, bf16[8,64,128]{2,1,0:T(8,128)(2,1)S(1)} %collective-permute-done.18.refs_2_, ...), custom_call_target="tpu_custom_call" | custom-call | flops 536870912 | bytes 4194304 | tf_op jit(solution)/shard_map/pallas_call | solution.py:207
  45.3 1.1 %collective-permute-done.16.refs_4_ = bf16[2,2,64,128]{3,2,1,0:T(8,128)(2,1)S(1)} collective-permute-done((bf16[2,2,64,128]{3,2,1,0:T(8,128)(2,1)S(1)}, bf16[2,2,64,128]{3,2,1,0:T(8,128)(2,1)S(1)}, u32[]{:S(2)}, u32[]{:S(2)}) %collective-permute-start.16) | collective-permute-done | bytes 65568 | tf_op jit(solution)/shard_map/ppermute | solution.py:221
  46.4 0.9 %shard_map.87 = (f32[8,64,128]{2,1,0:T(8,128)S(1)}, bf16[8,64,128]{2,1,0:T(8,128)(2,1)S(1)}, bf16[8,64,128]{2,1,0:T(8,128)(2,1)S(1)}, bf16[8,64,128]{2,1,0:T(8,128)(2,1)S(1)}) custom-call(bf16[1024,2048]{1,0:T(8,128)(2,1)S(1)} %get-tuple-element.61.refs_0_, bf16[4,2,64,128]{3,2,1,0:T(8,128)(2,1)S(1)} %get-tuple-element.98.kept.refs_1_, ...), custom_call_target="tpu_custom_call" | custom-call | flops 536870912 | bytes 4194304 | tf_op jit(solution)/shard_map/pallas_call | solution.py:207
  47.4 1.4 %collective-permute-start.22 = (bf16[8,64,128]{2,1,0:T(8,128)(2,1)S(1)}, bf16[8,64,128]{2,1,0:T(8,128)(2,1)S(1)}, u32[]{:S(2)}, u32[]{:S(2)}) collective-permute-start(bf16[8,64,128]{2,1,0:T(8,128)(2,1)S(1)} %get-tuple-element.105), channel_id=1, source_target_pairs={{0,3},{1,2},{2,1},{3,0},{4,7},{5,6},{6,5},{7,4},{8,11},{9,10},{10,... | collective-permute-start | bytes 393224 | tf_op jit(solution)/shard_map/ppermute | solution.py:235
  50.4 1.8 %collective-permute-start.25 = (bf16[2,2,64,128]{3,2,1,0:T(8,128)(2,1)S(1)}, bf16[2,2,64,128]{3,2,1,0:T(8,128)(2,1)S(1)}, u32[]{:S(2)}, u32[]{:S(2)}) collective-permute-start(bf16[2,2,64,128]{3,2,1,0:T(8,128)(2,1)S(1)} %get-tuple-element.110), channel_id=1, source_target_pairs={{0,24},{4,28},{8,16},{12,20},{16,8},{20,12},{24,0},{28,4},{1,25},{... | collective-permute-start | bytes 196616 | tf_op jit(solution)/shard_map/ppermute | solution.py:221
  52.2 2.7 %collective-permute-start.27 = (bf16[2,2,64,128]{3,2,1,0:T(8,128)(2,1)S(1)}, bf16[2,2,64,128]{3,2,1,0:T(8,128)(2,1)S(1)}, u32[]{:S(2)}, u32[]{:S(2)}) collective-permute-start(bf16[2,2,64,128]{3,2,1,0:T(8,128)(2,1)S(1)} %get-tuple-element.112), channel_id=1, source_target_pairs={{0,8},{4,12},{8,0},{12,4},{16,24},{20,28},{24,16},{28,20},{1,9},{5... | collective-permute-start | bytes 196616 | tf_op jit(solution)/shard_map/ppermute | solution.py:221
  54.9 1.2 %collective-permute-done.23.refs_3_ = bf16[8,64,128]{2,1,0:T(8,128)(2,1)S(1)} collective-permute-done((bf16[8,64,128]{2,1,0:T(8,128)(2,1)S(1)}, bf16[8,64,128]{2,1,0:T(8,128)(2,1)S(1)}, u32[]{:S(2)}, u32[]{:S(2)}) %collective-permute-start.23) | collective-permute-done | bytes 131104 | tf_op jit(solution)/shard_map/ppermute | solution.py:235
  57.1 1.4 %collective-permute-done.26.refs_3_ = bf16[2,2,64,128]{3,2,1,0:T(8,128)(2,1)S(1)} collective-permute-done((bf16[2,2,64,128]{3,2,1,0:T(8,128)(2,1)S(1)}, bf16[2,2,64,128]{3,2,1,0:T(8,128)(2,1)S(1)}, u32[]{:S(2)}, u32[]{:S(2)}) %collective-permute-start.26) | collective-permute-done | bytes 65568 | tf_op jit(solution)/shard_map/ppermute | solution.py:221
  58.5 1.4 %shard_map.90 = f32[8,64,128]{2,1,0:T(8,128)} custom-call(s32[8,16]{1,0:T(8,128)S(1)} %copy-done.4, f32[8,64,128]{2,1,0:T(8,128)S(1)} %get-tuple-element.107.gradient_in, bf16[4,2,64,128]{3,2,1,0:T(8,128)(2,1)S(1)} %get-tuple-element.113.kept.refs_0_, bf16[4,2,64,128]{3,2,1,0:T(8,128)(2,1)S(1)} %collective-permute-done.24.got.refs_1_, ...), custom_call_target="tpu_custom_call" | custom-call | tf_op jit(solution)/shard_map/pallas_call | solution.py:207
  (56 shorter events, 12.8 us)
Async XLA Ops:
  2.6 9.1 %collective-permute-start = (bf16[4,2,64,128]{3,2,1,0:T(8,128)(2,1)}, bf16[4,2,64,128]{3,2,1,0:T(8,128)(2,1)S(1)}, u32[]{:S(2)}, u32[]{:S(2)}) collective-permute-start(bf16[4,2,64,128]{3,2,1,0:T(8,128)(2,1)} %get-tuple-element.64), channel_id=1, source_target_pairs={{0,4},{4,0},{8,12},{12,8},{16,20},{20,16},{24,28},{28,24},{1,5},{5... | collective-permute-start | bytes 393224 | tf_op jit(solution)/shard_map/ppermute | solution.py:221
  5.6 9.8 %collective-permute-start.6 = (bf16[8,64,128]{2,1,0:T(8,128)(2,1)}, bf16[8,64,128]{2,1,0:T(8,128)(2,1)S(1)}, u32[]{:S(2)}, u32[]{:S(2)}) collective-permute-start(bf16[8,64,128]{2,1,0:T(8,128)(2,1)} %get-tuple-element.69.refs_2_), channel_id=1, source_target_pairs={{0,3},{1,2},{2,1},{3,0},{4,7},{5,6},{6,5},{7,4},{8,11},{9,10},{10,... | collective-permute-start | bytes 393224 | tf_op jit(solution)/shard_map/ppermute | solution.py:235
  6.3 9.9 %collective-permute-start.5 = (bf16[8,64,128]{2,1,0:T(8,128)(2,1)}, bf16[8,64,128]{2,1,0:T(8,128)(2,1)S(1)}, u32[]{:S(2)}, u32[]{:S(2)}) collective-permute-start(bf16[8,64,128]{2,1,0:T(8,128)(2,1)} %get-tuple-element.69.refs_2_), channel_id=1, source_target_pairs={{0,2},{1,3},{2,0},{3,1},{4,6},{5,7},{6,4},{7,5},{8,10},{9,11},{10,... | collective-permute-start | bytes 393224 | tf_op jit(solution)/shard_map/ppermute | solution.py:235
  7.1 9.0 %collective-permute-start.4 = (bf16[8,64,128]{2,1,0:T(8,128)(2,1)}, bf16[8,64,128]{2,1,0:T(8,128)(2,1)S(1)}, u32[]{:S(2)}, u32[]{:S(2)}) collective-permute-start(bf16[8,64,128]{2,1,0:T(8,128)(2,1)} %get-tuple-element.69.refs_2_), channel_id=1, source_target_pairs={{0,1},{1,0},{2,3},{3,2},{4,5},{5,4},{6,7},{7,6},{8,9},{9,8},{10,11... | collective-permute-start | bytes 393224 | tf_op jit(solution)/shard_map/ppermute | solution.py:235
  11.7 7.4 %collective-permute-start.1 = (bf16[2,2,64,128]{3,2,1,0:T(8,128)(2,1)S(1)}, bf16[2,2,64,128]{3,2,1,0:T(8,128)(2,1)S(1)}, u32[]{:S(2)}, u32[]{:S(2)}) collective-permute-start(bf16[2,2,64,128]{3,2,1,0:T(8,128)(2,1)S(1)} %get-tuple-element.66), channel_id=1, source_target_pairs={{0,24},{4,28},{8,16},{12,20},{16,8},{20,12},{24,0},{28,4},{1,25},{... | collective-permute-start | bytes 196616 | tf_op jit(solution)/shard_map/ppermute | solution.py:221
  15.4 5.9 %collective-permute-start.2 = (bf16[2,2,64,128]{3,2,1,0:T(8,128)(2,1)S(1)}, bf16[2,2,64,128]{3,2,1,0:T(8,128)(2,1)S(1)}, u32[]{:S(2)}, u32[]{:S(2)}) collective-permute-start(bf16[2,2,64,128]{3,2,1,0:T(8,128)(2,1)S(1)} %get-tuple-element.67), channel_id=1, source_target_pairs={{0,16},{4,20},{8,24},{12,28},{16,0},{20,4},{24,8},{28,12},{1,17},{... | collective-permute-start | bytes 196616 | tf_op jit(solution)/shard_map/ppermute | solution.py:221
  15.4 5.9 %collective-permute-start.3 = (bf16[2,2,64,128]{3,2,1,0:T(8,128)(2,1)S(1)}, bf16[2,2,64,128]{3,2,1,0:T(8,128)(2,1)S(1)}, u32[]{:S(2)}, u32[]{:S(2)}) collective-permute-start(bf16[2,2,64,128]{3,2,1,0:T(8,128)(2,1)S(1)} %get-tuple-element.68), channel_id=1, source_target_pairs={{0,8},{4,12},{8,0},{12,4},{16,24},{20,28},{24,16},{28,20},{1,9},{5... | collective-permute-start | bytes 196616 | tf_op jit(solution)/shard_map/ppermute | solution.py:221
  18.6 6.4 %collective-permute-start.11 = (bf16[4,2,64,128]{3,2,1,0:T(8,128)(2,1)S(1)}, bf16[4,2,64,128]{3,2,1,0:T(8,128)(2,1)S(1)}, u32[]{:S(2)}, u32[]{:S(2)}) collective-permute-start(bf16[4,2,64,128]{3,2,1,0:T(8,128)(2,1)S(1)} %get-tuple-element.70), channel_id=1, source_target_pairs={{0,4},{4,0},{8,12},{12,8},{16,20},{20,16},{24,28},{28,24},{1,5},{5... | collective-permute-start | bytes 393224 | tf_op jit(solution)/shard_map/ppermute | solution.py:221
  22.9 6.6 %collective-permute-start.8 = (bf16[8,64,128]{2,1,0:T(8,128)(2,1)S(1)}, bf16[8,64,128]{2,1,0:T(8,128)(2,1)S(1)}, u32[]{:S(2)}, u32[]{:S(2)}) collective-permute-start(bf16[8,64,128]{2,1,0:T(8,128)(2,1)S(1)} %get-tuple-element.78), channel_id=1, source_target_pairs={{0,3},{1,2},{2,1},{3,0},{4,7},{5,6},{6,5},{7,4},{8,11},{9,10},{10,... | collective-permute-start | bytes 393224 | tf_op jit(solution)/shard_map/ppermute | solution.py:235
  24.4 7.2 %collective-permute-start.9 = (bf16[8,64,128]{2,1,0:T(8,128)(2,1)S(1)}, bf16[8,64,128]{2,1,0:T(8,128)(2,1)S(1)}, u32[]{:S(2)}, u32[]{:S(2)}) collective-permute-start(bf16[8,64,128]{2,1,0:T(8,128)(2,1)S(1)} %get-tuple-element.79), channel_id=1, source_target_pairs={{0,2},{1,3},{2,0},{3,1},{4,6},{5,7},{6,4},{7,5},{8,10},{9,11},{10,... | collective-permute-start | bytes 393224 | tf_op jit(solution)/shard_map/ppermute | solution.py:235
  25.0 7.9 %collective-permute-start.12 = (bf16[2,2,64,128]{3,2,1,0:T(8,128)(2,1)S(1)}, bf16[2,2,64,128]{3,2,1,0:T(8,128)(2,1)S(1)}, u32[]{:S(2)}, u32[]{:S(2)}) collective-permute-start(bf16[2,2,64,128]{3,2,1,0:T(8,128)(2,1)S(1)} %get-tuple-element.84), channel_id=1, source_target_pairs={{0,24},{4,28},{8,16},{12,20},{16,8},{20,12},{24,0},{28,4},{1,25},{... | collective-permute-start | bytes 196616 | tf_op jit(solution)/shard_map/ppermute | solution.py:221
  27.6 6.6 %collective-permute-start.13 = (bf16[2,2,64,128]{3,2,1,0:T(8,128)(2,1)S(1)}, bf16[2,2,64,128]{3,2,1,0:T(8,128)(2,1)S(1)}, u32[]{:S(2)}, u32[]{:S(2)}) collective-permute-start(bf16[2,2,64,128]{3,2,1,0:T(8,128)(2,1)S(1)} %get-tuple-element.85), channel_id=1, source_target_pairs={{0,16},{4,20},{8,24},{12,28},{16,0},{20,4},{24,8},{28,12},{1,17},{... | collective-permute-start | bytes 196616 | tf_op jit(solution)/shard_map/ppermute | solution.py:221
  27.7 6.5 %collective-permute-start.14 = (bf16[2,2,64,128]{3,2,1,0:T(8,128)(2,1)S(1)}, bf16[2,2,64,128]{3,2,1,0:T(8,128)(2,1)S(1)}, u32[]{:S(2)}, u32[]{:S(2)}) collective-permute-start(bf16[2,2,64,128]{3,2,1,0:T(8,128)(2,1)S(1)} %get-tuple-element.86), channel_id=1, source_target_pairs={{0,8},{4,12},{8,0},{12,4},{16,24},{20,28},{24,16},{28,20},{1,9},{5... | collective-permute-start | bytes 196616 | tf_op jit(solution)/shard_map/ppermute | solution.py:221
  35.0 5.9 %collective-permute-start.20 = (bf16[8,64,128]{2,1,0:T(8,128)(2,1)S(1)}, bf16[8,64,128]{2,1,0:T(8,128)(2,1)S(1)}, u32[]{:S(2)}, u32[]{:S(2)}) collective-permute-start(bf16[8,64,128]{2,1,0:T(8,128)(2,1)S(1)} %get-tuple-element.92.refs_1_), channel_id=1, source_target_pairs={{0,3},{1,2},{2,1},{3,0},{4,7},{5,6},{6,5},{7,4},{8,11},{9,10},{10,... | collective-permute-start | bytes 393224 | tf_op jit(solution)/shard_map/ppermute | solution.py:235
  35.6 7.8 %collective-permute-start.19 = (bf16[8,64,128]{2,1,0:T(8,128)(2,1)S(1)}, bf16[8,64,128]{2,1,0:T(8,128)(2,1)S(1)}, u32[]{:S(2)}, u32[]{:S(2)}) collective-permute-start(bf16[8,64,128]{2,1,0:T(8,128)(2,1)S(1)} %get-tuple-element.92.refs_1_), channel_id=1, source_target_pairs={{0,2},{1,3},{2,0},{3,1},{4,6},{5,7},{6,4},{7,5},{8,10},{9,11},{10,... | collective-permute-start | bytes 393224 | tf_op jit(solution)/shard_map/ppermute | solution.py:235
  36.4 7.0 %collective-permute-start.18 = (bf16[8,64,128]{2,1,0:T(8,128)(2,1)S(1)}, bf16[8,64,128]{2,1,0:T(8,128)(2,1)S(1)}, u32[]{:S(2)}, u32[]{:S(2)}) collective-permute-start(bf16[8,64,128]{2,1,0:T(8,128)(2,1)S(1)} %get-tuple-element.92.refs_1_), channel_id=1, source_target_pairs={{0,1},{1,0},{2,3},{3,2},{4,5},{5,4},{6,7},{7,6},{8,9},{9,8},{10,11... | collective-permute-start | bytes 393224 | tf_op jit(solution)/shard_map/ppermute | solution.py:235
  37.3 8.0 %collective-permute-start.15 = (bf16[2,2,64,128]{3,2,1,0:T(8,128)(2,1)S(1)}, bf16[2,2,64,128]{3,2,1,0:T(8,128)(2,1)S(1)}, u32[]{:S(2)}, u32[]{:S(2)}) collective-permute-start(bf16[2,2,64,128]{3,2,1,0:T(8,128)(2,1)S(1)} %get-tuple-element.94), channel_id=1, source_target_pairs={{0,24},{4,28},{8,16},{12,20},{16,8},{20,12},{24,0},{28,4},{1,25},{... | collective-permute-start | bytes 196616 | tf_op jit(solution)/shard_map/ppermute | solution.py:221
  39.9 6.5 %collective-permute-start.16 = (bf16[2,2,64,128]{3,2,1,0:T(8,128)(2,1)S(1)}, bf16[2,2,64,128]{3,2,1,0:T(8,128)(2,1)S(1)}, u32[]{:S(2)}, u32[]{:S(2)}) collective-permute-start(bf16[2,2,64,128]{3,2,1,0:T(8,128)(2,1)S(1)} %get-tuple-element.95), channel_id=1, source_target_pairs={{0,16},{4,20},{8,24},{12,28},{16,0},{20,4},{24,8},{28,12},{1,17},{... | collective-permute-start | bytes 196616 | tf_op jit(solution)/shard_map/ppermute | solution.py:221
  44.7 5.7 %collective-permute-start.24 = (bf16[4,2,64,128]{3,2,1,0:T(8,128)(2,1)S(1)}, bf16[4,2,64,128]{3,2,1,0:T(8,128)(2,1)S(1)}, u32[]{:S(2)}, u32[]{:S(2)}) collective-permute-start(bf16[4,2,64,128]{3,2,1,0:T(8,128)(2,1)S(1)} %get-tuple-element.97), channel_id=1, source_target_pairs={{0,4},{4,0},{8,12},{12,8},{16,20},{20,16},{24,28},{28,24},{1,5},{5... | collective-permute-start | bytes 393224 | tf_op jit(solution)/shard_map/ppermute | solution.py:221
  47.4 7.5 %collective-permute-start.22 = (bf16[8,64,128]{2,1,0:T(8,128)(2,1)S(1)}, bf16[8,64,128]{2,1,0:T(8,128)(2,1)S(1)}, u32[]{:S(2)}, u32[]{:S(2)}) collective-permute-start(bf16[8,64,128]{2,1,0:T(8,128)(2,1)S(1)} %get-tuple-element.105), channel_id=1, source_target_pairs={{0,3},{1,2},{2,1},{3,0},{4,7},{5,6},{6,5},{7,4},{8,11},{9,10},{10,... | collective-permute-start | bytes 393224 | tf_op jit(solution)/shard_map/ppermute | solution.py:235
  48.8 7.3 %collective-permute-start.23 = (bf16[8,64,128]{2,1,0:T(8,128)(2,1)S(1)}, bf16[8,64,128]{2,1,0:T(8,128)(2,1)S(1)}, u32[]{:S(2)}, u32[]{:S(2)}) collective-permute-start(bf16[8,64,128]{2,1,0:T(8,128)(2,1)S(1)} %get-tuple-element.106), channel_id=1, source_target_pairs={{0,2},{1,3},{2,0},{3,1},{4,6},{5,7},{6,4},{7,5},{8,10},{9,11},{10,... | collective-permute-start | bytes 393224 | tf_op jit(solution)/shard_map/ppermute | solution.py:235
  50.4 6.7 %collective-permute-start.25 = (bf16[2,2,64,128]{3,2,1,0:T(8,128)(2,1)S(1)}, bf16[2,2,64,128]{3,2,1,0:T(8,128)(2,1)S(1)}, u32[]{:S(2)}, u32[]{:S(2)}) collective-permute-start(bf16[2,2,64,128]{3,2,1,0:T(8,128)(2,1)S(1)} %get-tuple-element.110), channel_id=1, source_target_pairs={{0,24},{4,28},{8,16},{12,20},{16,8},{20,12},{24,0},{28,4},{1,25},{... | collective-permute-start | bytes 196616 | tf_op jit(solution)/shard_map/ppermute | solution.py:221
  52.2 6.3 %collective-permute-start.26 = (bf16[2,2,64,128]{3,2,1,0:T(8,128)(2,1)S(1)}, bf16[2,2,64,128]{3,2,1,0:T(8,128)(2,1)S(1)}, u32[]{:S(2)}, u32[]{:S(2)}) collective-permute-start(bf16[2,2,64,128]{3,2,1,0:T(8,128)(2,1)S(1)} %get-tuple-element.111), channel_id=1, source_target_pairs={{0,16},{4,20},{8,24},{12,28},{16,0},{20,4},{24,8},{28,12},{1,17},{... | collective-permute-start | bytes 196616 | tf_op jit(solution)/shard_map/ppermute | solution.py:221
  52.2 6.3 %collective-permute-start.27 = (bf16[2,2,64,128]{3,2,1,0:T(8,128)(2,1)S(1)}, bf16[2,2,64,128]{3,2,1,0:T(8,128)(2,1)S(1)}, u32[]{:S(2)}, u32[]{:S(2)}) collective-permute-start(bf16[2,2,64,128]{3,2,1,0:T(8,128)(2,1)S(1)} %get-tuple-element.112), channel_id=1, source_target_pairs={{0,8},{4,12},{8,0},{12,4},{16,24},{20,28},{24,16},{28,20},{1,9},{5... | collective-permute-start | bytes 196616 | tf_op jit(solution)/shard_map/ppermute | solution.py:221
  (9 other events, 74.8 us)

commit v9 on v8

--- a/solution.py
+++ b/solution.py
@@ -144,10 +144,12 @@
     *arrived, kept, away, source, product = refs[operators:]
     for turn, part in enumerate(arrived):
         source[:, partner("edge", turn)] = part[...]
-    vectors = source[...].reshape(-1, source.shape[-1])
-    product[...] = sum(
-        jnp.dot(part[...], vectors, preferred_element_type=FULL) for part in refs[:operators]
-    ).reshape(product.shape)
+    vectors = source[...].reshape(-1, source.shape[-1]).T
+    summed = sum(
+        lax.dot_general(vectors, part[...], (((1,), (1,)), ((), ())), preferred_element_type=FULL)
+        for part in refs[:operators]
+    )
+    product[...] = summed.T.reshape(product.shape)
     fill((kept, away), lambda turn, slot: product[partner("node", turn), slot])
 
 

time: 60.1 us -> 60.5 us (level)
  Pallas kernels: 16.1 us -> 17.1 us
    pallas_call x14, Pallas kernels: 16.1 us -> 17.1 us  [call(): pl.pallas_call(kernel, out_shape=[jax.ShapeDtypeStruct(*out) for out in o...]
  transfers between devices with their start and end apart: 28 -> 28, of which waited for: 11 -> 11; matrix products, arithmetic and copies ran while one was open for 0% -> 0% of each run, Pallas kernels for 21% -> 23%
where the time goes in v9:
time: 60.5 us; the launch traced here: 60.3 us
  starting transfers between devices  29.9 us (49%)
  Pallas kernels  17.1 us (28%)
  waiting for transfers between devices  12.5 us (21%)
  between operations  0.8 us (1%)
    ppermute x16, starting transfers between devices, to_node(): lax.ppermute(array, 'node', [(place, place ^ turn) for place in range(own...  21.7 us
    pallas_call x14, Pallas kernels, call(): pl.pallas_call(kernel, out_shape=[jax.ShapeDtypeStruct(*out) for out in o...  17.1 us
    ppermute x12, starting transfers between devices, over_edge(): lax.ppermute(array, 'edge', [(place, place ^ turn) for place in range(qua...  8.21 us
    ppermute x16, waiting for transfers between devices, to_node(): lax.ppermute(array, 'node', [(place, place ^ turn) for place in range(own...  7.18 us
    ppermute x12, waiting for transfers between devices, over_edge(): lax.ppermute(array, 'edge', [(place, place ^ turn) for place in range(qua...  5.32 us
  transfers between devices with their start and end apart: 28, of which 11 were waited for; matrix products, arithmetic and copies ran while one was open for 0% of the time, Pallas kernels for 23%

profile of v9, /device:TPU:0, one launch (start us, length us, event | category | flops | bytes accessed | tf_op | source)
XLA Modules:
  0.0 60.3 jit_solution(8521354182413965001)
XLA Ops:
  0.6 2.0 %shard_map.77 = (bf16[4,2,64,128]{3,2,1,0:T(8,128)(2,1)}, bf16[4,2,64,128]{3,2,1,0:T(8,128)(2,1)}, bf16[8,64,128]{2,1,0:T(8,128)(2,1)}, s32[24576,1,192]{2,1,0:T(1,128)}) custom-call(s32[8,16]{1,0:T(8,128)} %table.7, f32[8,64,128]{2,1,0:T(8,128)} %bitcast.4, f32[8,64,128]{2,1,0:T(8,128)} %bitcast.7, s32[1,192]{1,0:T(1,128)} %rows.1, s32[1,192]{1,0:T(1,128)} %slots.1), custom_call_target="tpu_custom_call" | custom-call | tf_op jit(solution)/shard_map/pallas_call | solution.py:209
  2.6 3.0 %collective-permute-start = (bf16[4,2,64,128]{3,2,1,0:T(8,128)(2,1)}, bf16[4,2,64,128]{3,2,1,0:T(8,128)(2,1)S(1)}, u32[]{:S(2)}, u32[]{:S(2)}) collective-permute-start(bf16[4,2,64,128]{3,2,1,0:T(8,128)(2,1)} %get-tuple-element.64), channel_id=1, source_target_pairs={{0,4},{4,0},{8,12},{12,8},{16,20},{20,16},{24,28},{28,24},{1,5},{5... | collective-permute-start | bytes 393224 | tf_op jit(solution)/shard_map/ppermute | solution.py:223
  6.3 0.9 %collective-permute-start.5 = (bf16[8,64,128]{2,1,0:T(8,128)(2,1)}, bf16[8,64,128]{2,1,0:T(8,128)(2,1)S(1)}, u32[]{:S(2)}, u32[]{:S(2)}) collective-permute-start(bf16[8,64,128]{2,1,0:T(8,128)(2,1)} %get-tuple-element.69.refs_2_), channel_id=1, source_target_pairs={{0,2},{1,3},{2,0},{3,1},{4,6},{5,7},{6,4},{7,5},{8,10},{9,11},{10,... | collective-permute-start | bytes 393224 | tf_op jit(solution)/shard_map/ppermute | solution.py:237
  7.5 4.2 %shard_map.78 = (bf16[1024,2048]{1,0:T(8,128)(2,1)S(1)}, bf16[1024,2048]{1,0:T(8,128)(2,1)S(1)}) custom-call(s32[24576,1,192]{2,1,0:T(1,128)} %get-tuple-element.60.ids, bf16[1,192,64,256]{3,2,1,0:T(8,128)(2,1)} %weights.1), custom_call_target="tpu_custom_call" | custom-call | bytes 6291456 | tf_op jit(solution)/shard_map/pallas_call | solution.py:209
  11.7 3.7 %collective-permute-start.1 = (bf16[2,2,64,128]{3,2,1,0:T(8,128)(2,1)S(1)}, bf16[2,2,64,128]{3,2,1,0:T(8,128)(2,1)S(1)}, u32[]{:S(2)}, u32[]{:S(2)}) collective-permute-start(bf16[2,2,64,128]{3,2,1,0:T(8,128)(2,1)S(1)} %get-tuple-element.66), channel_id=1, source_target_pairs={{0,24},{4,28},{8,16},{12,20},{16,8},{20,12},{24,0},{28,4},{1,25},{... | collective-permute-start | bytes 196616 | tf_op jit(solution)/shard_map/ppermute | solution.py:223
  16.2 3.0 %shard_map.80 = (bf16[4,2,64,128]{3,2,1,0:T(8,128)(2,1)S(1)}, bf16[4,2,64,128]{3,2,1,0:T(8,128)(2,1)S(1)}) custom-call(bf16[1024,2048]{1,0:T(8,128)(2,1)S(1)} %get-tuple-element.61.refs_0_, bf16[1024,2048]{1,0:T(8,128)(2,1)S(1)} %get-tuple-element.62.refs_1_, bf16[8,64,128]{2,1,0:T(8,128)(2,1)S(1)} %copy-done.3, ...), custom_call_target="tpu_custom_call" | custom-call | flops 1073741824 | bytes 8388608 | tf_op jit(solution)/shard_map/pallas_call | solution.py:209
  19.7 1.6 %collective-permute-done.2.refs_5_ = bf16[2,2,64,128]{3,2,1,0:T(8,128)(2,1)S(1)} collective-permute-done((bf16[2,2,64,128]{3,2,1,0:T(8,128)(2,1)S(1)}, bf16[2,2,64,128]{3,2,1,0:T(8,128)(2,1)S(1)}, u32[]{:S(2)}, u32[]{:S(2)}) %collective-permute-start.2) | collective-permute-done | bytes 65568 | tf_op jit(solution)/shard_map/ppermute | solution.py:223
  21.3 1.5 %shard_map.81 = (f32[8,64,128]{2,1,0:T(8,128)S(1)}, bf16[8,64,128]{2,1,0:T(8,128)(2,1)S(1)}, bf16[8,64,128]{2,1,0:T(8,128)(2,1)S(1)}, bf16[8,64,128]{2,1,0:T(8,128)(2,1)S(1)}) custom-call(bf16[1024,2048]{1,0:T(8,128)(2,1)S(1)} %get-tuple-element.61.refs_0_, bf16[1024,2048]{1,0:T(8,128)(2,1)S(1)} %get-tuple-element.62.refs_1_, ...), custom_call_target="tpu_custom_call" | custom-call | flops 1073741824 | bytes 8388608 | tf_op jit(solution)/shard_map/pallas_call | solution.py:209
  22.9 1.5 %collective-permute-start.8 = (bf16[8,64,128]{2,1,0:T(8,128)(2,1)S(1)}, bf16[8,64,128]{2,1,0:T(8,128)(2,1)S(1)}, u32[]{:S(2)}, u32[]{:S(2)}) collective-permute-start(bf16[8,64,128]{2,1,0:T(8,128)(2,1)S(1)} %get-tuple-element.78), channel_id=1, source_target_pairs={{0,3},{1,2},{2,1},{3,0},{4,7},{5,6},{6,5},{7,4},{8,11},{9,10},{10,... | collective-permute-start | bytes 393224 | tf_op jit(solution)/shard_map/ppermute | solution.py:237
  25.0 2.9 %collective-permute-start.12 = (bf16[2,2,64,128]{3,2,1,0:T(8,128)(2,1)S(1)}, bf16[2,2,64,128]{3,2,1,0:T(8,128)(2,1)S(1)}, u32[]{:S(2)}, u32[]{:S(2)}) collective-permute-start(bf16[2,2,64,128]{3,2,1,0:T(8,128)(2,1)S(1)} %get-tuple-element.84), channel_id=1, source_target_pairs={{0,24},{4,28},{8,16},{12,20},{16,8},{20,12},{24,0},{28,4},{1,25},{... | collective-permute-start | bytes 196616 | tf_op jit(solution)/shard_map/ppermute | solution.py:223
  28.0 1.5 %collective-permute-start.14 = (bf16[2,2,64,128]{3,2,1,0:T(8,128)(2,1)S(1)}, bf16[2,2,64,128]{3,2,1,0:T(8,128)(2,1)S(1)}, u32[]{:S(2)}, u32[]{:S(2)}) collective-permute-start(bf16[2,2,64,128]{3,2,1,0:T(8,128)(2,1)S(1)} %get-tuple-element.86), channel_id=1, source_target_pairs={{0,8},{4,12},{8,0},{12,4},{16,24},{20,28},{24,16},{28,20},{1,9},{5... | collective-permute-start | bytes 196616 | tf_op jit(solution)/shard_map/ppermute | solution.py:223
  29.5 2.0 %collective-permute-done.9.refs_3_ = bf16[8,64,128]{2,1,0:T(8,128)(2,1)S(1)} collective-permute-done((bf16[8,64,128]{2,1,0:T(8,128)(2,1)S(1)}, bf16[8,64,128]{2,1,0:T(8,128)(2,1)S(1)}, u32[]{:S(2)}, u32[]{:S(2)}) %collective-permute-start.9) | collective-permute-done | bytes 131104 | tf_op jit(solution)/shard_map/ppermute | solution.py:237
  32.9 1.3 %collective-permute-done.13.refs_3_ = bf16[2,2,64,128]{3,2,1,0:T(8,128)(2,1)S(1)} collective-permute-done((bf16[2,2,64,128]{3,2,1,0:T(8,128)(2,1)S(1)}, bf16[2,2,64,128]{3,2,1,0:T(8,128)(2,1)S(1)}, u32[]{:S(2)}, u32[]{:S(2)}) %collective-permute-start.13) | collective-permute-done | bytes 65568 | tf_op jit(solution)/shard_map/ppermute | solution.py:223
  37.3 2.5 %collective-permute-start.15 = (bf16[2,2,64,128]{3,2,1,0:T(8,128)(2,1)S(1)}, bf16[2,2,64,128]{3,2,1,0:T(8,128)(2,1)S(1)}, u32[]{:S(2)}, u32[]{:S(2)}) collective-permute-start(bf16[2,2,64,128]{3,2,1,0:T(8,128)(2,1)S(1)} %get-tuple-element.94), channel_id=1, source_target_pairs={{0,24},{4,28},{8,16},{12,20},{16,8},{20,12},{24,0},{28,4},{1,25},{... | collective-permute-start | bytes 196616 | tf_op jit(solution)/shard_map/ppermute | solution.py:223
  40.8 1.0 %collective-permute-start.17 = (bf16[2,2,64,128]{3,2,1,0:T(8,128)(2,1)S(1)}, bf16[2,2,64,128]{3,2,1,0:T(8,128)(2,1)S(1)}, u32[]{:S(2)}, u32[]{:S(2)}) collective-permute-start(bf16[2,2,64,128]{3,2,1,0:T(8,128)(2,1)S(1)} %get-tuple-element.96), channel_id=1, source_target_pairs={{0,8},{4,12},{8,0},{12,4},{16,24},{20,28},{24,16},{28,20},{1,9},{5... | collective-permute-start | bytes 196616 | tf_op jit(solution)/shard_map/ppermute | solution.py:223
  41.8 1.6 %collective-permute-done.19.refs_3_ = bf16[8,64,128]{2,1,0:T(8,128)(2,1)S(1)} collective-permute-done((bf16[8,64,128]{2,1,0:T(8,128)(2,1)S(1)}, bf16[8,64,128]{2,1,0:T(8,128)(2,1)S(1)}, u32[]{:S(2)}, u32[]{:S(2)}) %collective-permute-start.19) | collective-permute-done | bytes 131104 | tf_op jit(solution)/shard_map/ppermute | solution.py:237
  43.4 1.7 %shard_map.86 = (bf16[4,2,64,128]{3,2,1,0:T(8,128)(2,1)S(1)}, bf16[4,2,64,128]{3,2,1,0:T(8,128)(2,1)S(1)}) custom-call(bf16[1024,2048]{1,0:T(8,128)(2,1)S(1)} %get-tuple-element.61.refs_0_, bf16[8,64,128]{2,1,0:T(8,128)(2,1)S(1)} %get-tuple-element.92.refs_1_, bf16[8,64,128]{2,1,0:T(8,128)(2,1)S(1)} %collective-permute-done.18.refs_2_, ...), custom_call_target="tpu_custom_call" | custom-call | flops 536870912 | bytes 4194304 | tf_op jit(solution)/shard_map/pallas_call | solution.py:209
  46.4 0.9 %shard_map.87 = (f32[8,64,128]{2,1,0:T(8,128)S(1)}, bf16[8,64,128]{2,1,0:T(8,128)(2,1)S(1)}, bf16[8,64,128]{2,1,0:T(8,128)(2,1)S(1)}, bf16[8,64,128]{2,1,0:T(8,128)(2,1)S(1)}) custom-call(bf16[1024,2048]{1,0:T(8,128)(2,1)S(1)} %get-tuple-element.61.refs_0_, bf16[4,2,64,128]{3,2,1,0:T(8,128)(2,1)S(1)} %get-tuple-element.98.kept.refs_1_, ...), custom_call_target="tpu_custom_call" | custom-call | flops 536870912 | bytes 4194304 | tf_op jit(solution)/shard_map/pallas_call | solution.py:209
  47.4 1.4 %collective-permute-start.22 = (bf16[8,64,128]{2,1,0:T(8,128)(2,1)S(1)}, bf16[8,64,128]{2,1,0:T(8,128)(2,1)S(1)}, u32[]{:S(2)}, u32[]{:S(2)}) collective-permute-start(bf16[8,64,128]{2,1,0:T(8,128)(2,1)S(1)} %get-tuple-element.105), channel_id=1, source_target_pairs={{0,3},{1,2},{2,1},{3,0},{4,7},{5,6},{6,5},{7,4},{8,11},{9,10},{10,... | collective-permute-start | bytes 393224 | tf_op jit(solution)/shard_map/ppermute | solution.py:237
  49.6 1.2 %collective-permute-done.24.got.refs_1_ = bf16[4,2,64,128]{3,2,1,0:T(8,128)(2,1)S(1)} collective-permute-done((bf16[4,2,64,128]{3,2,1,0:T(8,128)(2,1)S(1)}, bf16[4,2,64,128]{3,2,1,0:T(8,128)(2,1)S(1)}, u32[]{:S(2)}, u32[]{:S(2)}) %collective-permute-start.24) | collective-permute-done | bytes 131104 | tf_op jit(solution)/shard_map/ppermute | solution.py:223
  50.8 2.0 %collective-permute-start.25 = (bf16[2,2,64,128]{3,2,1,0:T(8,128)(2,1)S(1)}, bf16[2,2,64,128]{3,2,1,0:T(8,128)(2,1)S(1)}, u32[]{:S(2)}, u32[]{:S(2)}) collective-permute-start(bf16[2,2,64,128]{3,2,1,0:T(8,128)(2,1)S(1)} %get-tuple-element.110), channel_id=1, source_target_pairs={{0,24},{4,28},{8,16},{12,20},{16,8},{20,12},{24,0},{28,4},{1,25},{... | collective-permute-start | bytes 196616 | tf_op jit(solution)/shard_map/ppermute | solution.py:223
  52.8 2.5 %collective-permute-start.27 = (bf16[2,2,64,128]{3,2,1,0:T(8,128)(2,1)S(1)}, bf16[2,2,64,128]{3,2,1,0:T(8,128)(2,1)S(1)}, u32[]{:S(2)}, u32[]{:S(2)}) collective-permute-start(bf16[2,2,64,128]{3,2,1,0:T(8,128)(2,1)S(1)} %get-tuple-element.112), channel_id=1, source_target_pairs={{0,8},{4,12},{8,0},{12,4},{16,24},{20,28},{24,16},{28,20},{1,9},{5... | collective-permute-start | bytes 196616 | tf_op jit(solution)/shard_map/ppermute | solution.py:223
  57.5 1.4 %collective-permute-done.26.refs_3_ = bf16[2,2,64,128]{3,2,1,0:T(8,128)(2,1)S(1)} collective-permute-done((bf16[2,2,64,128]{3,2,1,0:T(8,128)(2,1)S(1)}, bf16[2,2,64,128]{3,2,1,0:T(8,128)(2,1)S(1)}, u32[]{:S(2)}, u32[]{:S(2)}) %collective-permute-start.26) | collective-permute-done | bytes 65568 | tf_op jit(solution)/shard_map/ppermute | solution.py:223
  58.9 1.4 %shard_map.90 = f32[8,64,128]{2,1,0:T(8,128)} custom-call(s32[8,16]{1,0:T(8,128)S(1)} %copy-done.4, f32[8,64,128]{2,1,0:T(8,128)S(1)} %get-tuple-element.107.gradient_in, bf16[4,2,64,128]{3,2,1,0:T(8,128)(2,1)S(1)} %get-tuple-element.113.kept.refs_0_, bf16[4,2,64,128]{3,2,1,0:T(8,128)(2,1)S(1)} %collective-permute-done.24.got.refs_1_, ...), custom_call_target="tpu_custom_call" | custom-call | tf_op jit(solution)/shard_map/pallas_call | solution.py:209
  (56 shorter events, 12.9 us)
Async XLA Ops:
  2.6 9.1 %collective-permute-start = (bf16[4,2,64,128]{3,2,1,0:T(8,128)(2,1)}, bf16[4,2,64,128]{3,2,1,0:T(8,128)(2,1)S(1)}, u32[]{:S(2)}, u32[]{:S(2)}) collective-permute-start(bf16[4,2,64,128]{3,2,1,0:T(8,128)(2,1)} %get-tuple-element.64), channel_id=1, source_target_pairs={{0,4},{4,0},{8,12},{12,8},{16,20},{20,16},{24,28},{28,24},{1,5},{5... | collective-permute-start | bytes 393224 | tf_op jit(solution)/shard_map/ppermute | solution.py:223
  5.6 9.8 %collective-permute-start.6 = (bf16[8,64,128]{2,1,0:T(8,128)(2,1)}, bf16[8,64,128]{2,1,0:T(8,128)(2,1)S(1)}, u32[]{:S(2)}, u32[]{:S(2)}) collective-permute-start(bf16[8,64,128]{2,1,0:T(8,128)(2,1)} %get-tuple-element.69.refs_2_), channel_id=1, source_target_pairs={{0,3},{1,2},{2,1},{3,0},{4,7},{5,6},{6,5},{7,4},{8,11},{9,10},{10,... | collective-permute-start | bytes 393224 | tf_op jit(solution)/shard_map/ppermute | solution.py:237
  6.3 9.9 %collective-permute-start.5 = (bf16[8,64,128]{2,1,0:T(8,128)(2,1)}, bf16[8,64,128]{2,1,0:T(8,128)(2,1)S(1)}, u32[]{:S(2)}, u32[]{:S(2)}) collective-permute-start(bf16[8,64,128]{2,1,0:T(8,128)(2,1)} %get-tuple-element.69.refs_2_), channel_id=1, source_target_pairs={{0,2},{1,3},{2,0},{3,1},{4,6},{5,7},{6,4},{7,5},{8,10},{9,11},{10,... | collective-permute-start | bytes 393224 | tf_op jit(solution)/shard_map/ppermute | solution.py:237
  7.1 9.0 %collective-permute-start.4 = (bf16[8,64,128]{2,1,0:T(8,128)(2,1)}, bf16[8,64,128]{2,1,0:T(8,128)(2,1)S(1)}, u32[]{:S(2)}, u32[]{:S(2)}) collective-permute-start(bf16[8,64,128]{2,1,0:T(8,128)(2,1)} %get-tuple-element.69.refs_2_), channel_id=1, source_target_pairs={{0,1},{1,0},{2,3},{3,2},{4,5},{5,4},{6,7},{7,6},{8,9},{9,8},{10,11... | collective-permute-start | bytes 393224 | tf_op jit(solution)/shard_map/ppermute | solution.py:237
  11.7 8.0 %collective-permute-start.1 = (bf16[2,2,64,128]{3,2,1,0:T(8,128)(2,1)S(1)}, bf16[2,2,64,128]{3,2,1,0:T(8,128)(2,1)S(1)}, u32[]{:S(2)}, u32[]{:S(2)}) collective-permute-start(bf16[2,2,64,128]{3,2,1,0:T(8,128)(2,1)S(1)} %get-tuple-element.66), channel_id=1, source_target_pairs={{0,24},{4,28},{8,16},{12,20},{16,8},{20,12},{24,0},{28,4},{1,25},{... | collective-permute-start | bytes 196616 | tf_op jit(solution)/shard_map/ppermute | solution.py:223
  15.4 5.9 %collective-permute-start.2 = (bf16[2,2,64,128]{3,2,1,0:T(8,128)(2,1)S(1)}, bf16[2,2,64,128]{3,2,1,0:T(8,128)(2,1)S(1)}, u32[]{:S(2)}, u32[]{:S(2)}) collective-permute-start(bf16[2,2,64,128]{3,2,1,0:T(8,128)(2,1)S(1)} %get-tuple-element.67), channel_id=1, source_target_pairs={{0,16},{4,20},{8,24},{12,28},{16,0},{20,4},{24,8},{28,12},{1,17},{... | collective-permute-start | bytes 196616 | tf_op jit(solution)/shard_map/ppermute | solution.py:223
  15.4 5.9 %collective-permute-start.3 = (bf16[2,2,64,128]{3,2,1,0:T(8,128)(2,1)S(1)}, bf16[2,2,64,128]{3,2,1,0:T(8,128)(2,1)S(1)}, u32[]{:S(2)}, u32[]{:S(2)}) collective-permute-start(bf16[2,2,64,128]{3,2,1,0:T(8,128)(2,1)S(1)} %get-tuple-element.68), channel_id=1, source_target_pairs={{0,8},{4,12},{8,0},{12,4},{16,24},{20,28},{24,16},{28,20},{1,9},{5... | collective-permute-start | bytes 196616 | tf_op jit(solution)/shard_map/ppermute | solution.py:223
  19.2 5.8 %collective-permute-start.11 = (bf16[4,2,64,128]{3,2,1,0:T(8,128)(2,1)S(1)}, bf16[4,2,64,128]{3,2,1,0:T(8,128)(2,1)S(1)}, u32[]{:S(2)}, u32[]{:S(2)}) collective-permute-start(bf16[4,2,64,128]{3,2,1,0:T(8,128)(2,1)S(1)} %get-tuple-element.70), channel_id=1, source_target_pairs={{0,4},{4,0},{8,12},{12,8},{16,20},{20,16},{24,28},{28,24},{1,5},{5... | collective-permute-start | bytes 393224 | tf_op jit(solution)/shard_map/ppermute | solution.py:223
  22.9 6.6 %collective-permute-start.8 = (bf16[8,64,128]{2,1,0:T(8,128)(2,1)S(1)}, bf16[8,64,128]{2,1,0:T(8,128)(2,1)S(1)}, u32[]{:S(2)}, u32[]{:S(2)}) collective-permute-start(bf16[8,64,128]{2,1,0:T(8,128)(2,1)S(1)} %get-tuple-element.78), channel_id=1, source_target_pairs={{0,3},{1,2},{2,1},{3,0},{4,7},{5,6},{6,5},{7,4},{8,11},{9,10},{10,... | collective-permute-start | bytes 393224 | tf_op jit(solution)/shard_map/ppermute | solution.py:237
  24.4 7.2 %collective-permute-start.9 = (bf16[8,64,128]{2,1,0:T(8,128)(2,1)S(1)}, bf16[8,64,128]{2,1,0:T(8,128)(2,1)S(1)}, u32[]{:S(2)}, u32[]{:S(2)}) collective-permute-start(bf16[8,64,128]{2,1,0:T(8,128)(2,1)S(1)} %get-tuple-element.79), channel_id=1, source_target_pairs={{0,2},{1,3},{2,0},{3,1},{4,6},{5,7},{6,4},{7,5},{8,10},{9,11},{10,... | collective-permute-start | bytes 393224 | tf_op jit(solution)/shard_map/ppermute | solution.py:237
  25.0 7.9 %collective-permute-start.12 = (bf16[2,2,64,128]{3,2,1,0:T(8,128)(2,1)S(1)}, bf16[2,2,64,128]{3,2,1,0:T(8,128)(2,1)S(1)}, u32[]{:S(2)}, u32[]{:S(2)}) collective-permute-start(bf16[2,2,64,128]{3,2,1,0:T(8,128)(2,1)S(1)} %get-tuple-element.84), channel_id=1, source_target_pairs={{0,24},{4,28},{8,16},{12,20},{16,8},{20,12},{24,0},{28,4},{1,25},{... | collective-permute-start | bytes 196616 | tf_op jit(solution)/shard_map/ppermute | solution.py:223
  28.0 6.2 %collective-permute-start.13 = (bf16[2,2,64,128]{3,2,1,0:T(8,128)(2,1)S(1)}, bf16[2,2,64,128]{3,2,1,0:T(8,128)(2,1)S(1)}, u32[]{:S(2)}, u32[]{:S(2)}) collective-permute-start(bf16[2,2,64,128]{3,2,1,0:T(8,128)(2,1)S(1)} %get-tuple-element.85), channel_id=1, source_target_pairs={{0,16},{4,20},{8,24},{12,28},{16,0},{20,4},{24,8},{28,12},{1,17},{... | collective-permute-start | bytes 196616 | tf_op jit(solution)/shard_map/ppermute | solution.py:223
  28.0 6.2 %collective-permute-start.14 = (bf16[2,2,64,128]{3,2,1,0:T(8,128)(2,1)S(1)}, bf16[2,2,64,128]{3,2,1,0:T(8,128)(2,1)S(1)}, u32[]{:S(2)}, u32[]{:S(2)}) collective-permute-start(bf16[2,2,64,128]{3,2,1,0:T(8,128)(2,1)S(1)} %get-tuple-element.86), channel_id=1, source_target_pairs={{0,8},{4,12},{8,0},{12,4},{16,24},{20,28},{24,16},{28,20},{1,9},{5... | collective-permute-start | bytes 196616 | tf_op jit(solution)/shard_map/ppermute | solution.py:223
  35.0 5.9 %collective-permute-start.20 = (bf16[8,64,128]{2,1,0:T(8,128)(2,1)S(1)}, bf16[8,64,128]{2,1,0:T(8,128)(2,1)S(1)}, u32[]{:S(2)}, u32[]{:S(2)}) collective-permute-start(bf16[8,64,128]{2,1,0:T(8,128)(2,1)S(1)} %get-tuple-element.92.refs_1_), channel_id=1, source_target_pairs={{0,3},{1,2},{2,1},{3,0},{4,7},{5,6},{6,5},{7,4},{8,11},{9,10},{10,... | collective-permute-start | bytes 393224 | tf_op jit(solution)/shard_map/ppermute | solution.py:237
  35.6 7.8 %collective-permute-start.19 = (bf16[8,64,128]{2,1,0:T(8,128)(2,1)S(1)}, bf16[8,64,128]{2,1,0:T(8,128)(2,1)S(1)}, u32[]{:S(2)}, u32[]{:S(2)}) collective-permute-start(bf16[8,64,128]{2,1,0:T(8,128)(2,1)S(1)} %get-tuple-element.92.refs_1_), channel_id=1, source_target_pairs={{0,2},{1,3},{2,0},{3,1},{4,6},{5,7},{6,4},{7,5},{8,10},{9,11},{10,... | collective-permute-start | bytes 393224 | tf_op jit(solution)/shard_map/ppermute | solution.py:237
  36.4 7.0 %collective-permute-start.18 = (bf16[8,64,128]{2,1,0:T(8,128)(2,1)S(1)}, bf16[8,64,128]{2,1,0:T(8,128)(2,1)S(1)}, u32[]{:S(2)}, u32[]{:S(2)}) collective-permute-start(bf16[8,64,128]{2,1,0:T(8,128)(2,1)S(1)} %get-tuple-element.92.refs_1_), channel_id=1, source_target_pairs={{0,1},{1,0},{2,3},{3,2},{4,5},{5,4},{6,7},{7,6},{8,9},{9,8},{10,11... | collective-permute-start | bytes 393224 | tf_op jit(solution)/shard_map/ppermute | solution.py:237
  37.3 8.3 %collective-permute-start.15 = (bf16[2,2,64,128]{3,2,1,0:T(8,128)(2,1)S(1)}, bf16[2,2,64,128]{3,2,1,0:T(8,128)(2,1)S(1)}, u32[]{:S(2)}, u32[]{:S(2)}) collective-permute-start(bf16[2,2,64,128]{3,2,1,0:T(8,128)(2,1)S(1)} %get-tuple-element.94), channel_id=1, source_target_pairs={{0,24},{4,28},{8,16},{12,20},{16,8},{20,12},{24,0},{28,4},{1,25},{... | collective-permute-start | bytes 196616 | tf_op jit(solution)/shard_map/ppermute | solution.py:223
  39.9 6.5 %collective-permute-start.16 = (bf16[2,2,64,128]{3,2,1,0:T(8,128)(2,1)S(1)}, bf16[2,2,64,128]{3,2,1,0:T(8,128)(2,1)S(1)}, u32[]{:S(2)}, u32[]{:S(2)}) collective-permute-start(bf16[2,2,64,128]{3,2,1,0:T(8,128)(2,1)S(1)} %get-tuple-element.95), channel_id=1, source_target_pairs={{0,16},{4,20},{8,24},{12,28},{16,0},{20,4},{24,8},{28,12},{1,17},{... | collective-permute-start | bytes 196616 | tf_op jit(solution)/shard_map/ppermute | solution.py:223
  45.0 5.7 %collective-permute-start.24 = (bf16[4,2,64,128]{3,2,1,0:T(8,128)(2,1)S(1)}, bf16[4,2,64,128]{3,2,1,0:T(8,128)(2,1)S(1)}, u32[]{:S(2)}, u32[]{:S(2)}) collective-permute-start(bf16[4,2,64,128]{3,2,1,0:T(8,128)(2,1)S(1)} %get-tuple-element.97), channel_id=1, source_target_pairs={{0,4},{4,0},{8,12},{12,8},{16,20},{20,16},{24,28},{28,24},{1,5},{5... | collective-permute-start | bytes 393224 | tf_op jit(solution)/shard_map/ppermute | solution.py:223
  47.4 7.8 %collective-permute-start.22 = (bf16[8,64,128]{2,1,0:T(8,128)(2,1)S(1)}, bf16[8,64,128]{2,1,0:T(8,128)(2,1)S(1)}, u32[]{:S(2)}, u32[]{:S(2)}) collective-permute-start(bf16[8,64,128]{2,1,0:T(8,128)(2,1)S(1)} %get-tuple-element.105), channel_id=1, source_target_pairs={{0,3},{1,2},{2,1},{3,0},{4,7},{5,6},{6,5},{7,4},{8,11},{9,10},{10,... | collective-permute-start | bytes 393224 | tf_op jit(solution)/shard_map/ppermute | solution.py:237
  48.8 7.3 %collective-permute-start.23 = (bf16[8,64,128]{2,1,0:T(8,128)(2,1)S(1)}, bf16[8,64,128]{2,1,0:T(8,128)(2,1)S(1)}, u32[]{:S(2)}, u32[]{:S(2)}) collective-permute-start(bf16[8,64,128]{2,1,0:T(8,128)(2,1)S(1)} %get-tuple-element.106), channel_id=1, source_target_pairs={{0,2},{1,3},{2,0},{3,1},{4,6},{5,7},{6,4},{7,5},{8,10},{9,11},{10,... | collective-permute-start | bytes 393224 | tf_op jit(solution)/shard_map/ppermute | solution.py:237
  50.8 6.7 %collective-permute-start.25 = (bf16[2,2,64,128]{3,2,1,0:T(8,128)(2,1)S(1)}, bf16[2,2,64,128]{3,2,1,0:T(8,128)(2,1)S(1)}, u32[]{:S(2)}, u32[]{:S(2)}) collective-permute-start(bf16[2,2,64,128]{3,2,1,0:T(8,128)(2,1)S(1)} %get-tuple-element.110), channel_id=1, source_target_pairs={{0,24},{4,28},{8,16},{12,20},{16,8},{20,12},{24,0},{28,4},{1,25},{... | collective-permute-start | bytes 196616 | tf_op jit(solution)/shard_map/ppermute | solution.py:223
  52.8 6.1 %collective-permute-start.26 = (bf16[2,2,64,128]{3,2,1,0:T(8,128)(2,1)S(1)}, bf16[2,2,64,128]{3,2,1,0:T(8,128)(2,1)S(1)}, u32[]{:S(2)}, u32[]{:S(2)}) collective-permute-start(bf16[2,2,64,128]{3,2,1,0:T(8,128)(2,1)S(1)} %get-tuple-element.111), channel_id=1, source_target_pairs={{0,16},{4,20},{8,24},{12,28},{16,0},{20,4},{24,8},{28,12},{1,17},{... | collective-permute-start | bytes 196616 | tf_op jit(solution)/shard_map/ppermute | solution.py:223
  52.8 6.1 %collective-permute-start.27 = (bf16[2,2,64,128]{3,2,1,0:T(8,128)(2,1)S(1)}, bf16[2,2,64,128]{3,2,1,0:T(8,128)(2,1)S(1)}, u32[]{:S(2)}, u32[]{:S(2)}) collective-permute-start(bf16[2,2,64,128]{3,2,1,0:T(8,128)(2,1)S(1)} %get-tuple-element.112), channel_id=1, source_target_pairs={{0,8},{4,12},{8,0},{12,4},{16,24},{20,28},{24,16},{28,20},{1,9},{5... | collective-permute-start | bytes 196616 | tf_op jit(solution)/shard_map/ppermute | solution.py:223
  (9 other events, 73.8 us)

commit v10 on v9

--- a/solution.py
+++ b/solution.py
@@ -66,10 +66,15 @@
     copies[4].wait()
 
 
+def place_of(turn, owners):
+    return turn % 2 * (owners // 2) + turn // 2
+
+
 def build_kernel(ids, weights, high, low, held, total, own_ids, sems):
     parts = sems.shape[0] - 1
     block_count, quarter, width = held.shape
     chunk = block_count // parts
+    owners = total.shape[0] // CAP
     copies = [
         pltpu.make_async_copy(
             weights.at[0, pl.ds(part * chunk, chunk)],
@@ -87,7 +92,9 @@
     for part, copy in enumerate(copies):
         copy.wait()
         for block in range(part * chunk, (part + 1) * chunk):
-            total[own_ids[1, 0, block], own_ids[0, 0, block]] += held[block].astype(FULL)
+            slot = own_ids[1, 0, block]
+            place = place_of(partner("node", slot // CAP), owners) * CAP + slot % CAP
+            total[place, own_ids[0, 0, block]] += held[block].astype(FULL)
     for slot in range(total.shape[0]):
         for row in range(total.shape[1]):
             place = (pl.ds(slot * quarter, quarter), pl.ds(row * width, width))
@@ -123,7 +130,7 @@
     quarters, quarter, hidden = product.shape
     width = quarters * quarter
     for turn, part in by_turn(parts):
-        source[partner("node", turn)] = part[...]
+        source[place_of(turn, source.shape[0])] = part[...]
     vectors = source[...].reshape(-1, hidden)
     for row in range(partials[0].shape[0]):
         summed = sum(
@@ -140,17 +147,17 @@
             partial[row] = product[partner("edge", turn)].astype(partial.dtype)
 
 
-def adjoint_kernel(operators, *refs):
-    *arrived, kept, away, source, product = refs[operators:]
+def adjoint_kernel(operators, low, *refs):
+    *arrived, send, source = refs[operators:]
     for turn, part in enumerate(arrived):
         source[:, partner("edge", turn)] = part[...]
-    vectors = source[...].reshape(-1, source.shape[-1]).T
-    summed = sum(
-        lax.dot_general(vectors, part[...], (((1,), (1,)), ((), ())), preferred_element_type=FULL)
+    vectors = source[...].reshape(-1, source.shape[-1])
+    half = refs[0].shape[0] // 2
+    product = sum(
+        jnp.dot(part[low * half : (low + 1) * half], vectors, preferred_element_type=FULL)
         for part in refs[:operators]
     )
-    product[...] = summed.T.reshape(product.shape)
-    fill((kept, away), lambda turn, slot: product[partner("node", turn), slot])
+    send[...] = product.reshape(send.shape).astype(LOW)
 
 
 def state_of(arrived, teleport):
@@ -274,28 +281,31 @@
     for step in range(STEPS):
         last = step + 1 == STEPS
         dense = (high,) if last else (high, low)
-        cost = pl.CostEstimate(
-            flops=2 * len(dense) * high.size * hidden,
-            bytes_accessed=len(dense) * high.size * 2,
-            transcendentals=0,
+        cells = len(dense) * high.size
+        half_cost, cost = (
+            pl.CostEstimate(
+                flops=2 * part * hidden, bytes_accessed=2 * part, transcendentals=0
+            )
+            for part in (cells // 2, cells)
         )
         arrived = over_edge([rounded] * quarters, range(1, quarters))
         got = to_node(away, 1)
         (got,) = after((got,), (rounded, high) if step else (high,))
         columns = over_node(kept, got)
-        kept_sums, away_sums = call(
-            functools.partial(adjoint_kernel, len(dense)),
-            (*dense, *arrived),
-            [VMEM] * (quarters + len(dense)),
-            [(half_shape, LOW)] * 2,
-            [
-                pltpu.VMEM((count, quarters, quarter, hidden), LOW),
-                pltpu.VMEM((owners, CAP, quarter, hidden), FULL),
-            ],
-            cost=cost,
-        )
+        def adjoint_half(low, rows):
+            return call(
+                functools.partial(adjoint_kernel, len(dense), low),
+                (*dense, *rows),
+                [VMEM] * (quarters + len(dense)),
+                [(half_shape, LOW)],
+                [pltpu.VMEM((count, quarters, quarter, hidden), LOW)],
+                cost=half_cost,
+            )[0]
+
+        away_sums = adjoint_half(1, arrived)
+        kept_sums = adjoint_half(0, after(arrived, (away_sums,)))
         got_sums = to_node(away_sums, 1)
-        columns = after(columns, (away_sums,))
+        columns = after(columns, (kept_sums,))
         partials = call(
             functools.partial(forward_kernel, len(dense)),
             (*dense, *columns),

time: 60.5 us -> 60.4 us (level)
    ppermute x16, waiting for transfers between devices: 7.18 us -> 6.04 us  [to_node(): lax.ppermute(array, 'node', [(place, place ^ turn) for place in range(own...]
    ppermute x12, waiting for transfers between devices: 5.32 us -> 6.21 us  [over_edge(): lax.ppermute(array, 'edge', [(place, place ^ turn) for place in range(qua...]
    pallas_call x14 -> x16, Pallas kernels: 17.1 us -> 17.3 us  [call(): pl.pallas_call(kernel, out_shape=[jax.ShapeDtypeStruct(*out) for out in o...]
  transfers between devices with their start and end apart: 28 -> 28, of which waited for: 11 -> 10; matrix products, arithmetic and copies ran while one was open for 0% -> 0% of each run, Pallas kernels for 23% -> 23%
where the time goes in v10:
time: 60.4 us; the launch traced here: 60.3 us
  starting transfers between devices  29.9 us (50%)
  Pallas kernels  17.3 us (29%)
  waiting for transfers between devices  12.3 us (20%)
  between operations  0.81 us (1%)
    ppermute x16, starting transfers between devices, to_node(): lax.ppermute(array, 'node', [(place, place ^ turn) for place in range(own...  21.7 us
    pallas_call x16, Pallas kernels, call(): pl.pallas_call(kernel, out_shape=[jax.ShapeDtypeStruct(*out) for out in o...  17.3 us
    ppermute x12, starting transfers between devices, over_edge(): lax.ppermute(array, 'edge', [(place, place ^ turn) for place in range(qua...  8.21 us
    ppermute x12, waiting for transfers between devices, over_edge(): lax.ppermute(array, 'edge', [(place, place ^ turn) for place in range(qua...  6.21 us
    ppermute x16, waiting for transfers between devices, to_node(): lax.ppermute(array, 'node', [(place, place ^ turn) for place in range(own...  6.04 us
  transfers between devices with their start and end apart: 28, of which 10 were waited for; matrix products, arithmetic and copies ran while one was open for 0% of the time, Pallas kernels for 23%

profile of v10, /device:TPU:0, one launch (start us, length us, event | category | flops | bytes accessed | tf_op | source)
XLA Modules:
  0.0 60.3 jit_solution(14480451816668518035)
XLA Ops:
  0.6 2.0 %shard_map.77 = (bf16[4,2,64,128]{3,2,1,0:T(8,128)(2,1)}, bf16[4,2,64,128]{3,2,1,0:T(8,128)(2,1)}, bf16[8,64,128]{2,1,0:T(8,128)(2,1)}, s32[24576,1,192]{2,1,0:T(1,128)}) custom-call(s32[8,16]{1,0:T(8,128)} %table.7, f32[8,64,128]{2,1,0:T(8,128)} %bitcast.4, f32[8,64,128]{2,1,0:T(8,128)} %bitcast.7, s32[1,192]{1,0:T(1,128)} %rows.1, s32[1,192]{1,0:T(1,128)} %slots.1), custom_call_target="tpu_custom_call" | custom-call | tf_op jit(solution)/shard_map/pallas_call | solution.py:216
  2.6 3.0 %collective-permute-start = (bf16[4,2,64,128]{3,2,1,0:T(8,128)(2,1)}, bf16[4,2,64,128]{3,2,1,0:T(8,128)(2,1)S(1)}, u32[]{:S(2)}, u32[]{:S(2)}) collective-permute-start(bf16[4,2,64,128]{3,2,1,0:T(8,128)(2,1)} %get-tuple-element.68), channel_id=1, source_target_pairs={{0,4},{4,0},{8,12},{12,8},{16,20},{20,16},{24,28},{28,24},{1,5},{5... | collective-permute-start | bytes 393224 | tf_op jit(solution)/shard_map/ppermute | solution.py:230
  6.3 0.9 %collective-permute-start.5 = (bf16[8,64,128]{2,1,0:T(8,128)(2,1)}, bf16[8,64,128]{2,1,0:T(8,128)(2,1)S(1)}, u32[]{:S(2)}, u32[]{:S(2)}) collective-permute-start(bf16[8,64,128]{2,1,0:T(8,128)(2,1)} %get-tuple-element.74.refs_2_), channel_id=1, source_target_pairs={{0,2},{1,3},{2,0},{3,1},{4,6},{5,7},{6,4},{7,5},{8,10},{9,11},{10,... | collective-permute-start | bytes 393224 | tf_op jit(solution)/shard_map/ppermute | solution.py:244
  7.5 5.0 %shard_map.78 = (bf16[1024,2048]{1,0:T(8,128)(2,1)S(1)}, bf16[1024,2048]{1,0:T(8,128)(2,1)S(1)}) custom-call(s32[24576,1,192]{2,1,0:T(1,128)} %get-tuple-element.64.ids, bf16[1,192,64,256]{3,2,1,0:T(8,128)(2,1)} %weights.1), custom_call_target="tpu_custom_call" | custom-call | bytes 6291456 | tf_op jit(solution)/shard_map/pallas_call | solution.py:216
  12.5 3.7 %collective-permute-start.1 = (bf16[2,2,64,128]{3,2,1,0:T(8,128)(2,1)S(1)}, bf16[2,2,64,128]{3,2,1,0:T(8,128)(2,1)S(1)}, u32[]{:S(2)}, u32[]{:S(2)}) collective-permute-start(bf16[2,2,64,128]{3,2,1,0:T(8,128)(2,1)S(1)} %get-tuple-element.70), channel_id=1, source_target_pairs={{0,24},{4,28},{8,16},{12,20},{16,8},{20,12},{24,0},{28,4},{1,25},{... | collective-permute-start | bytes 196616 | tf_op jit(solution)/shard_map/ppermute | solution.py:230
  17.0 1.3 %shard_map.80 = bf16[4,2,64,128]{3,2,1,0:T(8,128)(2,1)S(1)} custom-call(bf16[1024,2048]{1,0:T(8,128)(2,1)S(1)} %get-tuple-element.65.refs_0_, bf16[1024,2048]{1,0:T(8,128)(2,1)S(1)} %get-tuple-element.66.refs_1_, bf16[8,64,128]{2,1,0:T(8,128)(2,1)S(1)} %copy-done.2, bf16[8,64,128]{2,1,0:T(8,128)(2,1)S(1)} %collective-permute-done.4.refs_3_, ...), custom_call_target="tpu_custom_call" | custom-call | flops 536870912 | bytes 4194304 | tf_op jit(solution)/shard_map/pallas_call | solution.py:216
  18.8 1.3 %shard_map.81.kept.refs_0_ = bf16[4,2,64,128]{3,2,1,0:T(8,128)(2,1)S(1)} custom-call(bf16[1024,2048]{1,0:T(8,128)(2,1)S(1)} %get-tuple-element.65.refs_0_, bf16[1024,2048]{1,0:T(8,128)(2,1)S(1)} %get-tuple-element.66.refs_1_, bf16[8,64,128]{2,1,0:T(8,128)(2,1)S(1)} %copy-done.2, bf16[8,64,128]{2,1,0:T(8,128)(2,1)S(1)} %collective-permute-done.4.refs_3_, ...), custom_call_target="tpu_custom_call" | custom-call | flops 536870912 | bytes 4194304 | tf_op jit(solution)/shard_map/pallas_call | solution.py:216
  20.1 2.0 %collective-permute-done.2.refs_5_ = bf16[2,2,64,128]{3,2,1,0:T(8,128)(2,1)S(1)} collective-permute-done((bf16[2,2,64,128]{3,2,1,0:T(8,128)(2,1)S(1)}, bf16[2,2,64,128]{3,2,1,0:T(8,128)(2,1)S(1)}, u32[]{:S(2)}, u32[]{:S(2)}) %collective-permute-start.2) | collective-permute-done | bytes 65568 | tf_op jit(solution)/shard_map/ppermute | solution.py:230
  22.1 1.5 %shard_map.82 = (f32[8,64,128]{2,1,0:T(8,128)S(1)}, bf16[8,64,128]{2,1,0:T(8,128)(2,1)S(1)}, bf16[8,64,128]{2,1,0:T(8,128)(2,1)S(1)}, bf16[8,64,128]{2,1,0:T(8,128)(2,1)S(1)}) custom-call(bf16[1024,2048]{1,0:T(8,128)(2,1)S(1)} %get-tuple-element.65.refs_0_, bf16[1024,2048]{1,0:T(8,128)(2,1)S(1)} %get-tuple-element.66.refs_1_, ...), custom_call_target="tpu_custom_call" | custom-call | flops 1073741824 | bytes 8388608 | tf_op jit(solution)/shard_map/pallas_call | solution.py:216
  23.6 1.5 %collective-permute-start.8 = (bf16[8,64,128]{2,1,0:T(8,128)(2,1)S(1)}, bf16[8,64,128]{2,1,0:T(8,128)(2,1)S(1)}, u32[]{:S(2)}, u32[]{:S(2)}) collective-permute-start(bf16[8,64,128]{2,1,0:T(8,128)(2,1)S(1)} %get-tuple-element.85), channel_id=1, source_target_pairs={{0,3},{1,2},{2,1},{3,0},{4,7},{5,6},{6,5},{7,4},{8,11},{9,10},{10,... | collective-permute-start | bytes 393224 | tf_op jit(solution)/shard_map/ppermute | solution.py:244
  25.8 2.5 %collective-permute-start.12 = (bf16[2,2,64,128]{3,2,1,0:T(8,128)(2,1)S(1)}, bf16[2,2,64,128]{3,2,1,0:T(8,128)(2,1)S(1)}, u32[]{:S(2)}, u32[]{:S(2)}) collective-permute-start(bf16[2,2,64,128]{3,2,1,0:T(8,128)(2,1)S(1)} %get-tuple-element.90), channel_id=1, source_target_pairs={{0,24},{4,28},{8,16},{12,20},{16,8},{20,12},{24,0},{28,4},{1,25},{... | collective-permute-start | bytes 196616 | tf_op jit(solution)/shard_map/ppermute | solution.py:230
  28.5 1.8 %collective-permute-start.14 = (bf16[2,2,64,128]{3,2,1,0:T(8,128)(2,1)S(1)}, bf16[2,2,64,128]{3,2,1,0:T(8,128)(2,1)S(1)}, u32[]{:S(2)}, u32[]{:S(2)}) collective-permute-start(bf16[2,2,64,128]{3,2,1,0:T(8,128)(2,1)S(1)} %get-tuple-element.92), channel_id=1, source_target_pairs={{0,8},{4,12},{8,0},{12,4},{16,24},{20,28},{24,16},{28,20},{1,9},{5... | collective-permute-start | bytes 196616 | tf_op jit(solution)/shard_map/ppermute | solution.py:230
  30.3 2.0 %collective-permute-done.9.refs_3_ = bf16[8,64,128]{2,1,0:T(8,128)(2,1)S(1)} collective-permute-done((bf16[8,64,128]{2,1,0:T(8,128)(2,1)S(1)}, bf16[8,64,128]{2,1,0:T(8,128)(2,1)S(1)}, u32[]{:S(2)}, u32[]{:S(2)}) %collective-permute-start.9) | collective-permute-done | bytes 131104 | tf_op jit(solution)/shard_map/ppermute | solution.py:244
  33.7 1.3 %collective-permute-done.13.refs_3_ = bf16[2,2,64,128]{3,2,1,0:T(8,128)(2,1)S(1)} collective-permute-done((bf16[2,2,64,128]{3,2,1,0:T(8,128)(2,1)S(1)}, bf16[2,2,64,128]{3,2,1,0:T(8,128)(2,1)S(1)}, u32[]{:S(2)}, u32[]{:S(2)}) %collective-permute-start.13) | collective-permute-done | bytes 65568 | tf_op jit(solution)/shard_map/ppermute | solution.py:230
  38.1 2.5 %collective-permute-start.15 = (bf16[2,2,64,128]{3,2,1,0:T(8,128)(2,1)S(1)}, bf16[2,2,64,128]{3,2,1,0:T(8,128)(2,1)S(1)}, u32[]{:S(2)}, u32[]{:S(2)}) collective-permute-start(bf16[2,2,64,128]{3,2,1,0:T(8,128)(2,1)S(1)} %get-tuple-element.100), channel_id=1, source_target_pairs={{0,24},{4,28},{8,16},{12,20},{16,8},{20,12},{24,0},{28,4},{1,25},{... | collective-permute-start | bytes 196616 | tf_op jit(solution)/shard_map/ppermute | solution.py:230
  41.6 1.0 %collective-permute-start.17 = (bf16[2,2,64,128]{3,2,1,0:T(8,128)(2,1)S(1)}, bf16[2,2,64,128]{3,2,1,0:T(8,128)(2,1)S(1)}, u32[]{:S(2)}, u32[]{:S(2)}) collective-permute-start(bf16[2,2,64,128]{3,2,1,0:T(8,128)(2,1)S(1)} %get-tuple-element.102), channel_id=1, source_target_pairs={{0,8},{4,12},{8,0},{12,4},{16,24},{20,28},{24,16},{28,20},{1,9},{5... | collective-permute-start | bytes 196616 | tf_op jit(solution)/shard_map/ppermute | solution.py:230
  42.6 1.6 %collective-permute-done.19.refs_3_ = bf16[8,64,128]{2,1,0:T(8,128)(2,1)S(1)} collective-permute-done((bf16[8,64,128]{2,1,0:T(8,128)(2,1)S(1)}, bf16[8,64,128]{2,1,0:T(8,128)(2,1)S(1)}, u32[]{:S(2)}, u32[]{:S(2)}) %collective-permute-start.19) | collective-permute-done | bytes 131104 | tf_op jit(solution)/shard_map/ppermute | solution.py:244
  47.2 0.9 %shard_map.89 = (f32[8,64,128]{2,1,0:T(8,128)S(1)}, bf16[8,64,128]{2,1,0:T(8,128)(2,1)S(1)}, bf16[8,64,128]{2,1,0:T(8,128)(2,1)S(1)}, bf16[8,64,128]{2,1,0:T(8,128)(2,1)S(1)}) custom-call(bf16[1024,2048]{1,0:T(8,128)(2,1)S(1)} %get-tuple-element.65.refs_0_, bf16[4,2,64,128]{3,2,1,0:T(8,128)(2,1)S(1)} %get-tuple-element.107.kept.refs_1_, ...), custom_call_target="tpu_custom_call" | custom-call | flops 536870912 | bytes 4194304 | tf_op jit(solution)/shard_map/pallas_call | solution.py:216
  48.2 1.4 %collective-permute-start.22 = (bf16[8,64,128]{2,1,0:T(8,128)(2,1)S(1)}, bf16[8,64,128]{2,1,0:T(8,128)(2,1)S(1)}, u32[]{:S(2)}, u32[]{:S(2)}) collective-permute-start(bf16[8,64,128]{2,1,0:T(8,128)(2,1)S(1)} %get-tuple-element.114), channel_id=1, source_target_pairs={{0,3},{1,2},{2,1},{3,0},{4,7},{5,6},{6,5},{7,4},{8,11},{9,10},{10,... | collective-permute-start | bytes 393224 | tf_op jit(solution)/shard_map/ppermute | solution.py:244
  50.6 2.0 %collective-permute-start.25 = (bf16[2,2,64,128]{3,2,1,0:T(8,128)(2,1)S(1)}, bf16[2,2,64,128]{3,2,1,0:T(8,128)(2,1)S(1)}, u32[]{:S(2)}, u32[]{:S(2)}) collective-permute-start(bf16[2,2,64,128]{3,2,1,0:T(8,128)(2,1)S(1)} %get-tuple-element.118), channel_id=1, source_target_pairs={{0,24},{4,28},{8,16},{12,20},{16,8},{20,12},{24,0},{28,4},{1,25},{... | collective-permute-start | bytes 196616 | tf_op jit(solution)/shard_map/ppermute | solution.py:230
  52.6 2.5 %collective-permute-start.27 = (bf16[2,2,64,128]{3,2,1,0:T(8,128)(2,1)S(1)}, bf16[2,2,64,128]{3,2,1,0:T(8,128)(2,1)S(1)}, u32[]{:S(2)}, u32[]{:S(2)}) collective-permute-start(bf16[2,2,64,128]{3,2,1,0:T(8,128)(2,1)S(1)} %get-tuple-element.120), channel_id=1, source_target_pairs={{0,8},{4,12},{8,0},{12,4},{16,24},{20,28},{24,16},{28,20},{1,9},{5... | collective-permute-start | bytes 196616 | tf_op jit(solution)/shard_map/ppermute | solution.py:230
  55.1 1.8 %collective-permute-done.23.refs_3_ = bf16[8,64,128]{2,1,0:T(8,128)(2,1)S(1)} collective-permute-done((bf16[8,64,128]{2,1,0:T(8,128)(2,1)S(1)}, bf16[8,64,128]{2,1,0:T(8,128)(2,1)S(1)}, u32[]{:S(2)}, u32[]{:S(2)}) %collective-permute-start.23) | collective-permute-done | bytes 131104 | tf_op jit(solution)/shard_map/ppermute | solution.py:244
  57.7 1.1 %collective-permute-done.26.refs_3_ = bf16[2,2,64,128]{3,2,1,0:T(8,128)(2,1)S(1)} collective-permute-done((bf16[2,2,64,128]{3,2,1,0:T(8,128)(2,1)S(1)}, bf16[2,2,64,128]{3,2,1,0:T(8,128)(2,1)S(1)}, u32[]{:S(2)}, u32[]{:S(2)}) %collective-permute-start.26) | collective-permute-done | bytes 65568 | tf_op jit(solution)/shard_map/ppermute | solution.py:230
  58.8 1.4 %shard_map.92 = f32[8,64,128]{2,1,0:T(8,128)} custom-call(s32[8,16]{1,0:T(8,128)S(1)} %copy-done.4, f32[8,64,128]{2,1,0:T(8,128)S(1)} %get-tuple-element.116.gradient_in, bf16[4,2,64,128]{3,2,1,0:T(8,128)(2,1)S(1)} %shard_map.88.kept.refs_0_, bf16[4,2,64,128]{3,2,1,0:T(8,128)(2,1)S(1)} %collective-permute-done.24.got.refs_1_, ...), custom_call_target="tpu_custom_call" | custom-call | tf_op jit(solution)/shard_map/pallas_call | solution.py:216
  (58 shorter events, 13.5 us)
Async XLA Ops:
  2.6 9.9 %collective-permute-start = (bf16[4,2,64,128]{3,2,1,0:T(8,128)(2,1)}, bf16[4,2,64,128]{3,2,1,0:T(8,128)(2,1)S(1)}, u32[]{:S(2)}, u32[]{:S(2)}) collective-permute-start(bf16[4,2,64,128]{3,2,1,0:T(8,128)(2,1)} %get-tuple-element.68), channel_id=1, source_target_pairs={{0,4},{4,0},{8,12},{12,8},{16,20},{20,16},{24,28},{28,24},{1,5},{5... | collective-permute-start | bytes 393224 | tf_op jit(solution)/shard_map/ppermute | solution.py:230
  5.6 10.6 %collective-permute-start.6 = (bf16[8,64,128]{2,1,0:T(8,128)(2,1)}, bf16[8,64,128]{2,1,0:T(8,128)(2,1)S(1)}, u32[]{:S(2)}, u32[]{:S(2)}) collective-permute-start(bf16[8,64,128]{2,1,0:T(8,128)(2,1)} %get-tuple-element.74.refs_2_), channel_id=1, source_target_pairs={{0,3},{1,2},{2,1},{3,0},{4,7},{5,6},{6,5},{7,4},{8,11},{9,10},{10,... | collective-permute-start | bytes 393224 | tf_op jit(solution)/shard_map/ppermute | solution.py:244
  6.3 10.7 %collective-permute-start.5 = (bf16[8,64,128]{2,1,0:T(8,128)(2,1)}, bf16[8,64,128]{2,1,0:T(8,128)(2,1)S(1)}, u32[]{:S(2)}, u32[]{:S(2)}) collective-permute-start(bf16[8,64,128]{2,1,0:T(8,128)(2,1)} %get-tuple-element.74.refs_2_), channel_id=1, source_target_pairs={{0,2},{1,3},{2,0},{3,1},{4,6},{5,7},{6,4},{7,5},{8,10},{9,11},{10,... | collective-permute-start | bytes 393224 | tf_op jit(solution)/shard_map/ppermute | solution.py:244
  7.2 9.8 %collective-permute-start.4 = (bf16[8,64,128]{2,1,0:T(8,128)(2,1)}, bf16[8,64,128]{2,1,0:T(8,128)(2,1)S(1)}, u32[]{:S(2)}, u32[]{:S(2)}) collective-permute-start(bf16[8,64,128]{2,1,0:T(8,128)(2,1)} %get-tuple-element.74.refs_2_), channel_id=1, source_target_pairs={{0,1},{1,0},{2,3},{3,2},{4,5},{5,4},{6,7},{7,6},{8,9},{9,8},{10,11... | collective-permute-start | bytes 393224 | tf_op jit(solution)/shard_map/ppermute | solution.py:244
  12.5 7.6 %collective-permute-start.1 = (bf16[2,2,64,128]{3,2,1,0:T(8,128)(2,1)S(1)}, bf16[2,2,64,128]{3,2,1,0:T(8,128)(2,1)S(1)}, u32[]{:S(2)}, u32[]{:S(2)}) collective-permute-start(bf16[2,2,64,128]{3,2,1,0:T(8,128)(2,1)S(1)} %get-tuple-element.70), channel_id=1, source_target_pairs={{0,24},{4,28},{8,16},{12,20},{16,8},{20,12},{24,0},{28,4},{1,25},{... | collective-permute-start | bytes 196616 | tf_op jit(solution)/shard_map/ppermute | solution.py:230
  16.2 5.9 %collective-permute-start.2 = (bf16[2,2,64,128]{3,2,1,0:T(8,128)(2,1)S(1)}, bf16[2,2,64,128]{3,2,1,0:T(8,128)(2,1)S(1)}, u32[]{:S(2)}, u32[]{:S(2)}) collective-permute-start(bf16[2,2,64,128]{3,2,1,0:T(8,128)(2,1)S(1)} %get-tuple-element.71), channel_id=1, source_target_pairs={{0,16},{4,20},{8,24},{12,28},{16,0},{20,4},{24,8},{28,12},{1,17},{... | collective-permute-start | bytes 196616 | tf_op jit(solution)/shard_map/ppermute | solution.py:230
  16.2 5.9 %collective-permute-start.3 = (bf16[2,2,64,128]{3,2,1,0:T(8,128)(2,1)S(1)}, bf16[2,2,64,128]{3,2,1,0:T(8,128)(2,1)S(1)}, u32[]{:S(2)}, u32[]{:S(2)}) collective-permute-start(bf16[2,2,64,128]{3,2,1,0:T(8,128)(2,1)S(1)} %get-tuple-element.72), channel_id=1, source_target_pairs={{0,8},{4,12},{8,0},{12,4},{16,24},{20,28},{24,16},{28,20},{1,9},{5... | collective-permute-start | bytes 196616 | tf_op jit(solution)/shard_map/ppermute | solution.py:230
  18.3 7.5 %collective-permute-start.11 = (bf16[4,2,64,128]{3,2,1,0:T(8,128)(2,1)S(1)}, bf16[4,2,64,128]{3,2,1,0:T(8,128)(2,1)S(1)}, u32[]{:S(2)}, u32[]{:S(2)}) collective-permute-start(bf16[4,2,64,128]{3,2,1,0:T(8,128)(2,1)S(1)} %shard_map.80), channel_id=1, source_target_pairs={{0,4},{4,0},{8,12},{12,8},{16,20},{20,16},{24,28},{28,24},{1,5},{5... | collective-permute-start | bytes 393224 | tf_op jit(solution)/shard_map/ppermute | solution.py:230
  23.6 6.6 %collective-permute-start.8 = (bf16[8,64,128]{2,1,0:T(8,128)(2,1)S(1)}, bf16[8,64,128]{2,1,0:T(8,128)(2,1)S(1)}, u32[]{:S(2)}, u32[]{:S(2)}) collective-permute-start(bf16[8,64,128]{2,1,0:T(8,128)(2,1)S(1)} %get-tuple-element.85), channel_id=1, source_target_pairs={{0,3},{1,2},{2,1},{3,0},{4,7},{5,6},{6,5},{7,4},{8,11},{9,10},{10,... | collective-permute-start | bytes 393224 | tf_op jit(solution)/shard_map/ppermute | solution.py:244
  25.2 7.1 %collective-permute-start.9 = (bf16[8,64,128]{2,1,0:T(8,128)(2,1)S(1)}, bf16[8,64,128]{2,1,0:T(8,128)(2,1)S(1)}, u32[]{:S(2)}, u32[]{:S(2)}) collective-permute-start(bf16[8,64,128]{2,1,0:T(8,128)(2,1)S(1)} %get-tuple-element.86), channel_id=1, source_target_pairs={{0,2},{1,3},{2,0},{3,1},{4,6},{5,7},{6,4},{7,5},{8,10},{9,11},{10,... | collective-permute-start | bytes 393224 | tf_op jit(solution)/shard_map/ppermute | solution.py:244
  25.8 7.9 %collective-permute-start.12 = (bf16[2,2,64,128]{3,2,1,0:T(8,128)(2,1)S(1)}, bf16[2,2,64,128]{3,2,1,0:T(8,128)(2,1)S(1)}, u32[]{:S(2)}, u32[]{:S(2)}) collective-permute-start(bf16[2,2,64,128]{3,2,1,0:T(8,128)(2,1)S(1)} %get-tuple-element.90), channel_id=1, source_target_pairs={{0,24},{4,28},{8,16},{12,20},{16,8},{20,12},{24,0},{28,4},{1,25},{... | collective-permute-start | bytes 196616 | tf_op jit(solution)/shard_map/ppermute | solution.py:230
  28.3 6.6 %collective-permute-start.13 = (bf16[2,2,64,128]{3,2,1,0:T(8,128)(2,1)S(1)}, bf16[2,2,64,128]{3,2,1,0:T(8,128)(2,1)S(1)}, u32[]{:S(2)}, u32[]{:S(2)}) collective-permute-start(bf16[2,2,64,128]{3,2,1,0:T(8,128)(2,1)S(1)} %get-tuple-element.91), channel_id=1, source_target_pairs={{0,16},{4,20},{8,24},{12,28},{16,0},{20,4},{24,8},{28,12},{1,17},{... | collective-permute-start | bytes 196616 | tf_op jit(solution)/shard_map/ppermute | solution.py:230
  28.5 6.5 %collective-permute-start.14 = (bf16[2,2,64,128]{3,2,1,0:T(8,128)(2,1)S(1)}, bf16[2,2,64,128]{3,2,1,0:T(8,128)(2,1)S(1)}, u32[]{:S(2)}, u32[]{:S(2)}) collective-permute-start(bf16[2,2,64,128]{3,2,1,0:T(8,128)(2,1)S(1)} %get-tuple-element.92), channel_id=1, source_target_pairs={{0,8},{4,12},{8,0},{12,4},{16,24},{20,28},{24,16},{28,20},{1,9},{5... | collective-permute-start | bytes 196616 | tf_op jit(solution)/shard_map/ppermute | solution.py:230
  35.7 5.9 %collective-permute-start.20 = (bf16[8,64,128]{2,1,0:T(8,128)(2,1)S(1)}, bf16[8,64,128]{2,1,0:T(8,128)(2,1)S(1)}, u32[]{:S(2)}, u32[]{:S(2)}) collective-permute-start(bf16[8,64,128]{2,1,0:T(8,128)(2,1)S(1)} %get-tuple-element.103.refs_1_), channel_id=1, source_target_pairs={{0,3},{1,2},{2,1},{3,0},{4,7},{5,6},{6,5},{7,4},{8,11},{9,10},{10,... | collective-permute-start | bytes 393224 | tf_op jit(solution)/shard_map/ppermute | solution.py:244
  36.3 7.8 %collective-permute-start.19 = (bf16[8,64,128]{2,1,0:T(8,128)(2,1)S(1)}, bf16[8,64,128]{2,1,0:T(8,128)(2,1)S(1)}, u32[]{:S(2)}, u32[]{:S(2)}) collective-permute-start(bf16[8,64,128]{2,1,0:T(8,128)(2,1)S(1)} %get-tuple-element.103.refs_1_), channel_id=1, source_target_pairs={{0,2},{1,3},{2,0},{3,1},{4,6},{5,7},{6,4},{7,5},{8,10},{9,11},{10,... | collective-permute-start | bytes 393224 | tf_op jit(solution)/shard_map/ppermute | solution.py:244
  37.2 7.0 %collective-permute-start.18 = (bf16[8,64,128]{2,1,0:T(8,128)(2,1)S(1)}, bf16[8,64,128]{2,1,0:T(8,128)(2,1)S(1)}, u32[]{:S(2)}, u32[]{:S(2)}) collective-permute-start(bf16[8,64,128]{2,1,0:T(8,128)(2,1)S(1)} %get-tuple-element.103.refs_1_), channel_id=1, source_target_pairs={{0,1},{1,0},{2,3},{3,2},{4,5},{5,4},{6,7},{7,6},{8,9},{9,8},{10,11... | collective-permute-start | bytes 393224 | tf_op jit(solution)/shard_map/ppermute | solution.py:244
  38.1 8.2 %collective-permute-start.15 = (bf16[2,2,64,128]{3,2,1,0:T(8,128)(2,1)S(1)}, bf16[2,2,64,128]{3,2,1,0:T(8,128)(2,1)S(1)}, u32[]{:S(2)}, u32[]{:S(2)}) collective-permute-start(bf16[2,2,64,128]{3,2,1,0:T(8,128)(2,1)S(1)} %get-tuple-element.100), channel_id=1, source_target_pairs={{0,24},{4,28},{8,16},{12,20},{16,8},{20,12},{24,0},{28,4},{1,25},{... | collective-permute-start | bytes 196616 | tf_op jit(solution)/shard_map/ppermute | solution.py:230
  40.6 6.5 %collective-permute-start.16 = (bf16[2,2,64,128]{3,2,1,0:T(8,128)(2,1)S(1)}, bf16[2,2,64,128]{3,2,1,0:T(8,128)(2,1)S(1)}, u32[]{:S(2)}, u32[]{:S(2)}) collective-permute-start(bf16[2,2,64,128]{3,2,1,0:T(8,128)(2,1)S(1)} %get-tuple-element.101), channel_id=1, source_target_pairs={{0,16},{4,20},{8,24},{12,28},{16,0},{20,4},{24,8},{28,12},{1,17},{... | collective-permute-start | bytes 196616 | tf_op jit(solution)/shard_map/ppermute | solution.py:230
  44.9 5.7 %collective-permute-start.24 = (bf16[4,2,64,128]{3,2,1,0:T(8,128)(2,1)S(1)}, bf16[4,2,64,128]{3,2,1,0:T(8,128)(2,1)S(1)}, u32[]{:S(2)}, u32[]{:S(2)}) collective-permute-start(bf16[4,2,64,128]{3,2,1,0:T(8,128)(2,1)S(1)} %shard_map.87), channel_id=1, source_target_pairs={{0,4},{4,0},{8,12},{12,8},{16,20},{20,16},{24,28},{28,24},{1,5},{5... | collective-permute-start | bytes 393224 | tf_op jit(solution)/shard_map/ppermute | solution.py:230
  48.2 6.9 %collective-permute-start.22 = (bf16[8,64,128]{2,1,0:T(8,128)(2,1)S(1)}, bf16[8,64,128]{2,1,0:T(8,128)(2,1)S(1)}, u32[]{:S(2)}, u32[]{:S(2)}) collective-permute-start(bf16[8,64,128]{2,1,0:T(8,128)(2,1)S(1)} %get-tuple-element.114), channel_id=1, source_target_pairs={{0,3},{1,2},{2,1},{3,0},{4,7},{5,6},{6,5},{7,4},{8,11},{9,10},{10,... | collective-permute-start | bytes 393224 | tf_op jit(solution)/shard_map/ppermute | solution.py:244
  49.6 7.3 %collective-permute-start.23 = (bf16[8,64,128]{2,1,0:T(8,128)(2,1)S(1)}, bf16[8,64,128]{2,1,0:T(8,128)(2,1)S(1)}, u32[]{:S(2)}, u32[]{:S(2)}) collective-permute-start(bf16[8,64,128]{2,1,0:T(8,128)(2,1)S(1)} %get-tuple-element.115), channel_id=1, source_target_pairs={{0,2},{1,3},{2,0},{3,1},{4,6},{5,7},{6,4},{7,5},{8,10},{9,11},{10,... | collective-permute-start | bytes 393224 | tf_op jit(solution)/shard_map/ppermute | solution.py:244
  50.6 7.0 %collective-permute-start.25 = (bf16[2,2,64,128]{3,2,1,0:T(8,128)(2,1)S(1)}, bf16[2,2,64,128]{3,2,1,0:T(8,128)(2,1)S(1)}, u32[]{:S(2)}, u32[]{:S(2)}) collective-permute-start(bf16[2,2,64,128]{3,2,1,0:T(8,128)(2,1)S(1)} %get-tuple-element.118), channel_id=1, source_target_pairs={{0,24},{4,28},{8,16},{12,20},{16,8},{20,12},{24,0},{28,4},{1,25},{... | collective-permute-start | bytes 196616 | tf_op jit(solution)/shard_map/ppermute | solution.py:230
  52.6 6.2 %collective-permute-start.26 = (bf16[2,2,64,128]{3,2,1,0:T(8,128)(2,1)S(1)}, bf16[2,2,64,128]{3,2,1,0:T(8,128)(2,1)S(1)}, u32[]{:S(2)}, u32[]{:S(2)}) collective-permute-start(bf16[2,2,64,128]{3,2,1,0:T(8,128)(2,1)S(1)} %get-tuple-element.119), channel_id=1, source_target_pairs={{0,16},{4,20},{8,24},{12,28},{16,0},{20,4},{24,8},{28,12},{1,17},{... | collective-permute-start | bytes 196616 | tf_op jit(solution)/shard_map/ppermute | solution.py:230
  52.6 6.2 %collective-permute-start.27 = (bf16[2,2,64,128]{3,2,1,0:T(8,128)(2,1)S(1)}, bf16[2,2,64,128]{3,2,1,0:T(8,128)(2,1)S(1)}, u32[]{:S(2)}, u32[]{:S(2)}) collective-permute-start(bf16[2,2,64,128]{3,2,1,0:T(8,128)(2,1)S(1)} %get-tuple-element.120), channel_id=1, source_target_pairs={{0,8},{4,12},{8,0},{12,4},{16,24},{20,28},{24,16},{28,20},{1,9},{5... | collective-permute-start | bytes 196616 | tf_op jit(solution)/shard_map/ppermute | solution.py:230
  (9 other events, 74.0 us)

commit v11 on v10

--- a/solution.py
+++ b/solution.py
@@ -67,10 +67,10 @@
 
 
 def place_of(turn, owners):
-    return turn % 2 * (owners // 2) + turn // 2
-
-
-def build_kernel(ids, weights, high, low, held, total, own_ids, sems):
+    return (turn & 1) * (owners // 2) + (turn >> 1)
+
+
+def build_kernel(ids, weights, high, low, held, total, own_ids, places, sems):
     parts = sems.shape[0] - 1
     block_count, quarter, width = held.shape
     chunk = block_count // parts
@@ -87,14 +87,14 @@
     ids_copy.start()
     for copy in copies:
         copy.start()
+    for slot in range(total.shape[0]):
+        places[slot] = place_of(partner("node", slot // CAP), owners) * CAP + slot % CAP
     total[...] = jnp.zeros_like(total)
     ids_copy.wait()
     for part, copy in enumerate(copies):
         copy.wait()
         for block in range(part * chunk, (part + 1) * chunk):
-            slot = own_ids[1, 0, block]
-            place = place_of(partner("node", slot // CAP), owners) * CAP + slot % CAP
-            total[place, own_ids[0, 0, block]] += held[block].astype(FULL)
+            total[places[own_ids[1, 0, block]], own_ids[0, 0, block]] += held[block].astype(FULL)
     for slot in range(total.shape[0]):
         for row in range(total.shape[1]):
             place = (pl.ds(slot * quarter, quarter), pl.ds(row * width, width))
@@ -271,6 +271,7 @@
             pltpu.VMEM((block_count, quarter, width), LOW),
             pltpu.VMEM((slot_total, count, quarter, width), FULL),
             pltpu.SMEM((2, *block_row.shape), block_row.dtype),
+            pltpu.SMEM((slot_total,), block_row.dtype),
             pltpu.SemaphoreType.DMA((parts + 1,)),
         ],
         BUILD_MEBIBYTES,

time: 60.4 us -> 59.7 us (0.988)
  Pallas kernels: 17.3 us -> 16.5 us
    pallas_call x16, Pallas kernels: 17.3 us -> 16.5 us  [call(): pl.pallas_call(kernel, out_shape=[jax.ShapeDtypeStruct(*out) for out in o...]
  transfers between devices with their start and end apart: 28 -> 28, of which waited for: 10 -> 10; matrix products, arithmetic and copies ran while one was open for 0% -> 0% of each run, Pallas kernels for 23% -> 22%
where the time goes in v11:
time: 59.7 us; the launch traced here: 59.5 us
  starting transfers between devices  29.9 us (50%)
  Pallas kernels  16.5 us (28%)
  waiting for transfers between devices  12.3 us (21%)
  between operations  0.81 us (1%)
    ppermute x16, starting transfers between devices, to_node(): lax.ppermute(array, 'node', [(place, place ^ turn) for place in range(own...  21.7 us
    pallas_call x16, Pallas kernels, call(): pl.pallas_call(kernel, out_shape=[jax.ShapeDtypeStruct(*out) for out in o...  16.5 us
    ppermute x12, starting transfers between devices, over_edge(): lax.ppermute(array, 'edge', [(place, place ^ turn) for place in range(qua...  8.21 us
    ppermute x12, waiting for transfers between devices, over_edge(): lax.ppermute(array, 'edge', [(place, place ^ turn) for place in range(qua...  6.25 us
    ppermute x16, waiting for transfers between devices, to_node(): lax.ppermute(array, 'node', [(place, place ^ turn) for place in range(own...  6.04 us
  transfers between devices with their start and end apart: 28, of which 10 were waited for; matrix products, arithmetic and copies ran while one was open for 0% of the time, Pallas kernels for 22%

profile of v11, /device:TPU:0, one launch (start us, length us, event | category | flops | bytes accessed | tf_op | source)
XLA Modules:
  0.0 59.5 jit_solution(8762404487097604938)
XLA Ops:
  0.6 2.0 %shard_map.77 = (bf16[4,2,64,128]{3,2,1,0:T(8,128)(2,1)}, bf16[4,2,64,128]{3,2,1,0:T(8,128)(2,1)}, bf16[8,64,128]{2,1,0:T(8,128)(2,1)}, s32[24576,1,192]{2,1,0:T(1,128)}) custom-call(s32[8,16]{1,0:T(8,128)} %table.7, f32[8,64,128]{2,1,0:T(8,128)} %bitcast.4, f32[8,64,128]{2,1,0:T(8,128)} %bitcast.7, s32[1,192]{1,0:T(1,128)} %rows.1, s32[1,192]{1,0:T(1,128)} %slots.1), custom_call_target="tpu_custom_call" | custom-call | tf_op jit(solution)/shard_map/pallas_call | solution.py:216
  2.6 3.0 %collective-permute-start = (bf16[4,2,64,128]{3,2,1,0:T(8,128)(2,1)}, bf16[4,2,64,128]{3,2,1,0:T(8,128)(2,1)S(1)}, u32[]{:S(2)}, u32[]{:S(2)}) collective-permute-start(bf16[4,2,64,128]{3,2,1,0:T(8,128)(2,1)} %get-tuple-element.68), channel_id=1, source_target_pairs={{0,4},{4,0},{8,12},{12,8},{16,20},{20,16},{24,28},{28,24},{1,5},{5... | collective-permute-start | bytes 393224 | tf_op jit(solution)/shard_map/ppermute | solution.py:230
  7.5 4.2 %shard_map.78 = (bf16[1024,2048]{1,0:T(8,128)(2,1)S(1)}, bf16[1024,2048]{1,0:T(8,128)(2,1)S(1)}) custom-call(s32[24576,1,192]{2,1,0:T(1,128)} %get-tuple-element.64.ids, bf16[1,192,64,256]{3,2,1,0:T(8,128)(2,1)} %weights.1), custom_call_target="tpu_custom_call" | custom-call | bytes 6291456 | tf_op jit(solution)/shard_map/pallas_call | solution.py:216
  11.7 3.7 %collective-permute-start.1 = (bf16[2,2,64,128]{3,2,1,0:T(8,128)(2,1)S(1)}, bf16[2,2,64,128]{3,2,1,0:T(8,128)(2,1)S(1)}, u32[]{:S(2)}, u32[]{:S(2)}) collective-permute-start(bf16[2,2,64,128]{3,2,1,0:T(8,128)(2,1)S(1)} %get-tuple-element.70), channel_id=1, source_target_pairs={{0,24},{4,28},{8,16},{12,20},{16,8},{20,12},{24,0},{28,4},{1,25},{... | collective-permute-start | bytes 196616 | tf_op jit(solution)/shard_map/ppermute | solution.py:230
  16.2 1.3 %shard_map.80 = bf16[4,2,64,128]{3,2,1,0:T(8,128)(2,1)S(1)} custom-call(bf16[1024,2048]{1,0:T(8,128)(2,1)S(1)} %get-tuple-element.65.refs_0_, bf16[1024,2048]{1,0:T(8,128)(2,1)S(1)} %get-tuple-element.66.refs_1_, bf16[8,64,128]{2,1,0:T(8,128)(2,1)S(1)} %copy-done.2, bf16[8,64,128]{2,1,0:T(8,128)(2,1)S(1)} %collective-permute-done.4.refs_3_, ...), custom_call_target="tpu_custom_call" | custom-call | flops 536870912 | bytes 4194304 | tf_op jit(solution)/shard_map/pallas_call | solution.py:216
  18.0 1.3 %shard_map.81.kept.refs_0_ = bf16[4,2,64,128]{3,2,1,0:T(8,128)(2,1)S(1)} custom-call(bf16[1024,2048]{1,0:T(8,128)(2,1)S(1)} %get-tuple-element.65.refs_0_, bf16[1024,2048]{1,0:T(8,128)(2,1)S(1)} %get-tuple-element.66.refs_1_, bf16[8,64,128]{2,1,0:T(8,128)(2,1)S(1)} %copy-done.2, bf16[8,64,128]{2,1,0:T(8,128)(2,1)S(1)} %collective-permute-done.4.refs_3_, ...), custom_call_target="tpu_custom_call" | custom-call | flops 536870912 | bytes 4194304 | tf_op jit(solution)/shard_map/pallas_call | solution.py:216
  19.3 2.0 %collective-permute-done.2.refs_5_ = bf16[2,2,64,128]{3,2,1,0:T(8,128)(2,1)S(1)} collective-permute-done((bf16[2,2,64,128]{3,2,1,0:T(8,128)(2,1)S(1)}, bf16[2,2,64,128]{3,2,1,0:T(8,128)(2,1)S(1)}, u32[]{:S(2)}, u32[]{:S(2)}) %collective-permute-start.2) | collective-permute-done | bytes 65568 | tf_op jit(solution)/shard_map/ppermute | solution.py:230
  21.3 1.5 %shard_map.82 = (f32[8,64,128]{2,1,0:T(8,128)S(1)}, bf16[8,64,128]{2,1,0:T(8,128)(2,1)S(1)}, bf16[8,64,128]{2,1,0:T(8,128)(2,1)S(1)}, bf16[8,64,128]{2,1,0:T(8,128)(2,1)S(1)}) custom-call(bf16[1024,2048]{1,0:T(8,128)(2,1)S(1)} %get-tuple-element.65.refs_0_, bf16[1024,2048]{1,0:T(8,128)(2,1)S(1)} %get-tuple-element.66.refs_1_, ...), custom_call_target="tpu_custom_call" | custom-call | flops 1073741824 | bytes 8388608 | tf_op jit(solution)/shard_map/pallas_call | solution.py:216
  22.8 1.5 %collective-permute-start.8 = (bf16[8,64,128]{2,1,0:T(8,128)(2,1)S(1)}, bf16[8,64,128]{2,1,0:T(8,128)(2,1)S(1)}, u32[]{:S(2)}, u32[]{:S(2)}) collective-permute-start(bf16[8,64,128]{2,1,0:T(8,128)(2,1)S(1)} %get-tuple-element.85), channel_id=1, source_target_pairs={{0,3},{1,2},{2,1},{3,0},{4,7},{5,6},{6,5},{7,4},{8,11},{9,10},{10,... | collective-permute-start | bytes 393224 | tf_op jit(solution)/shard_map/ppermute | solution.py:244
  25.0 2.5 %collective-permute-start.12 = (bf16[2,2,64,128]{3,2,1,0:T(8,128)(2,1)S(1)}, bf16[2,2,64,128]{3,2,1,0:T(8,128)(2,1)S(1)}, u32[]{:S(2)}, u32[]{:S(2)}) collective-permute-start(bf16[2,2,64,128]{3,2,1,0:T(8,128)(2,1)S(1)} %get-tuple-element.90), channel_id=1, source_target_pairs={{0,24},{4,28},{8,16},{12,20},{16,8},{20,12},{24,0},{28,4},{1,25},{... | collective-permute-start | bytes 196616 | tf_op jit(solution)/shard_map/ppermute | solution.py:230
  27.7 1.8 %collective-permute-start.14 = (bf16[2,2,64,128]{3,2,1,0:T(8,128)(2,1)S(1)}, bf16[2,2,64,128]{3,2,1,0:T(8,128)(2,1)S(1)}, u32[]{:S(2)}, u32[]{:S(2)}) collective-permute-start(bf16[2,2,64,128]{3,2,1,0:T(8,128)(2,1)S(1)} %get-tuple-element.92), channel_id=1, source_target_pairs={{0,8},{4,12},{8,0},{12,4},{16,24},{20,28},{24,16},{28,20},{1,9},{5... | collective-permute-start | bytes 196616 | tf_op jit(solution)/shard_map/ppermute | solution.py:230
  29.5 2.0 %collective-permute-done.9.refs_3_ = bf16[8,64,128]{2,1,0:T(8,128)(2,1)S(1)} collective-permute-done((bf16[8,64,128]{2,1,0:T(8,128)(2,1)S(1)}, bf16[8,64,128]{2,1,0:T(8,128)(2,1)S(1)}, u32[]{:S(2)}, u32[]{:S(2)}) %collective-permute-start.9) | collective-permute-done | bytes 131104 | tf_op jit(solution)/shard_map/ppermute | solution.py:244
  32.9 1.3 %collective-permute-done.13.refs_3_ = bf16[2,2,64,128]{3,2,1,0:T(8,128)(2,1)S(1)} collective-permute-done((bf16[2,2,64,128]{3,2,1,0:T(8,128)(2,1)S(1)}, bf16[2,2,64,128]{3,2,1,0:T(8,128)(2,1)S(1)}, u32[]{:S(2)}, u32[]{:S(2)}) %collective-permute-start.13) | collective-permute-done | bytes 65568 | tf_op jit(solution)/shard_map/ppermute | solution.py:230
  37.3 2.5 %collective-permute-start.15 = (bf16[2,2,64,128]{3,2,1,0:T(8,128)(2,1)S(1)}, bf16[2,2,64,128]{3,2,1,0:T(8,128)(2,1)S(1)}, u32[]{:S(2)}, u32[]{:S(2)}) collective-permute-start(bf16[2,2,64,128]{3,2,1,0:T(8,128)(2,1)S(1)} %get-tuple-element.100), channel_id=1, source_target_pairs={{0,24},{4,28},{8,16},{12,20},{16,8},{20,12},{24,0},{28,4},{1,25},{... | collective-permute-start | bytes 196616 | tf_op jit(solution)/shard_map/ppermute | solution.py:230
  40.8 1.0 %collective-permute-start.17 = (bf16[2,2,64,128]{3,2,1,0:T(8,128)(2,1)S(1)}, bf16[2,2,64,128]{3,2,1,0:T(8,128)(2,1)S(1)}, u32[]{:S(2)}, u32[]{:S(2)}) collective-permute-start(bf16[2,2,64,128]{3,2,1,0:T(8,128)(2,1)S(1)} %get-tuple-element.102), channel_id=1, source_target_pairs={{0,8},{4,12},{8,0},{12,4},{16,24},{20,28},{24,16},{28,20},{1,9},{5... | collective-permute-start | bytes 196616 | tf_op jit(solution)/shard_map/ppermute | solution.py:230
  41.8 1.6 %collective-permute-done.19.refs_3_ = bf16[8,64,128]{2,1,0:T(8,128)(2,1)S(1)} collective-permute-done((bf16[8,64,128]{2,1,0:T(8,128)(2,1)S(1)}, bf16[8,64,128]{2,1,0:T(8,128)(2,1)S(1)}, u32[]{:S(2)}, u32[]{:S(2)}) %collective-permute-start.19) | collective-permute-done | bytes 131104 | tf_op jit(solution)/shard_map/ppermute | solution.py:244
  45.5 0.9 %collective-permute-done.16.refs_4_ = bf16[2,2,64,128]{3,2,1,0:T(8,128)(2,1)S(1)} collective-permute-done((bf16[2,2,64,128]{3,2,1,0:T(8,128)(2,1)S(1)}, bf16[2,2,64,128]{3,2,1,0:T(8,128)(2,1)S(1)}, u32[]{:S(2)}, u32[]{:S(2)}) %collective-permute-start.16) | collective-permute-done | bytes 65568 | tf_op jit(solution)/shard_map/ppermute | solution.py:230
  46.4 0.9 %shard_map.89 = (f32[8,64,128]{2,1,0:T(8,128)S(1)}, bf16[8,64,128]{2,1,0:T(8,128)(2,1)S(1)}, bf16[8,64,128]{2,1,0:T(8,128)(2,1)S(1)}, bf16[8,64,128]{2,1,0:T(8,128)(2,1)S(1)}) custom-call(bf16[1024,2048]{1,0:T(8,128)(2,1)S(1)} %get-tuple-element.65.refs_0_, bf16[4,2,64,128]{3,2,1,0:T(8,128)(2,1)S(1)} %get-tuple-element.107.kept.refs_1_, ...), custom_call_target="tpu_custom_call" | custom-call | flops 536870912 | bytes 4194304 | tf_op jit(solution)/shard_map/pallas_call | solution.py:216
  47.4 1.4 %collective-permute-start.22 = (bf16[8,64,128]{2,1,0:T(8,128)(2,1)S(1)}, bf16[8,64,128]{2,1,0:T(8,128)(2,1)S(1)}, u32[]{:S(2)}, u32[]{:S(2)}) collective-permute-start(bf16[8,64,128]{2,1,0:T(8,128)(2,1)S(1)} %get-tuple-element.114), channel_id=1, source_target_pairs={{0,3},{1,2},{2,1},{3,0},{4,7},{5,6},{6,5},{7,4},{8,11},{9,10},{10,... | collective-permute-start | bytes 393224 | tf_op jit(solution)/shard_map/ppermute | solution.py:244
  49.9 1.9 %collective-permute-start.25 = (bf16[2,2,64,128]{3,2,1,0:T(8,128)(2,1)S(1)}, bf16[2,2,64,128]{3,2,1,0:T(8,128)(2,1)S(1)}, u32[]{:S(2)}, u32[]{:S(2)}) collective-permute-start(bf16[2,2,64,128]{3,2,1,0:T(8,128)(2,1)S(1)} %get-tuple-element.118), channel_id=1, source_target_pairs={{0,24},{4,28},{8,16},{12,20},{16,8},{20,12},{24,0},{28,4},{1,25},{... | collective-permute-start | bytes 196616 | tf_op jit(solution)/shard_map/ppermute | solution.py:230
  51.8 2.5 %collective-permute-start.27 = (bf16[2,2,64,128]{3,2,1,0:T(8,128)(2,1)S(1)}, bf16[2,2,64,128]{3,2,1,0:T(8,128)(2,1)S(1)}, u32[]{:S(2)}, u32[]{:S(2)}) collective-permute-start(bf16[2,2,64,128]{3,2,1,0:T(8,128)(2,1)S(1)} %get-tuple-element.120), channel_id=1, source_target_pairs={{0,8},{4,12},{8,0},{12,4},{16,24},{20,28},{24,16},{28,20},{1,9},{5... | collective-permute-start | bytes 196616 | tf_op jit(solution)/shard_map/ppermute | solution.py:230
  54.3 1.8 %collective-permute-done.23.refs_3_ = bf16[8,64,128]{2,1,0:T(8,128)(2,1)S(1)} collective-permute-done((bf16[8,64,128]{2,1,0:T(8,128)(2,1)S(1)}, bf16[8,64,128]{2,1,0:T(8,128)(2,1)S(1)}, u32[]{:S(2)}, u32[]{:S(2)}) %collective-permute-start.23) | collective-permute-done | bytes 131104 | tf_op jit(solution)/shard_map/ppermute | solution.py:244
  56.9 1.1 %collective-permute-done.26.refs_3_ = bf16[2,2,64,128]{3,2,1,0:T(8,128)(2,1)S(1)} collective-permute-done((bf16[2,2,64,128]{3,2,1,0:T(8,128)(2,1)S(1)}, bf16[2,2,64,128]{3,2,1,0:T(8,128)(2,1)S(1)}, u32[]{:S(2)}, u32[]{:S(2)}) %collective-permute-start.26) | collective-permute-done | bytes 65568 | tf_op jit(solution)/shard_map/ppermute | solution.py:230
  58.0 1.5 %shard_map.92 = f32[8,64,128]{2,1,0:T(8,128)} custom-call(s32[8,16]{1,0:T(8,128)S(1)} %copy-done.4, f32[8,64,128]{2,1,0:T(8,128)S(1)} %get-tuple-element.116.gradient_in, bf16[4,2,64,128]{3,2,1,0:T(8,128)(2,1)S(1)} %shard_map.88.kept.refs_0_, bf16[4,2,64,128]{3,2,1,0:T(8,128)(2,1)S(1)} %collective-permute-done.24.got.refs_1_, ...), custom_call_target="tpu_custom_call" | custom-call | tf_op jit(solution)/shard_map/pallas_call | solution.py:216
  (58 shorter events, 13.5 us)
Async XLA Ops:
  2.6 9.1 %collective-permute-start = (bf16[4,2,64,128]{3,2,1,0:T(8,128)(2,1)}, bf16[4,2,64,128]{3,2,1,0:T(8,128)(2,1)S(1)}, u32[]{:S(2)}, u32[]{:S(2)}) collective-permute-start(bf16[4,2,64,128]{3,2,1,0:T(8,128)(2,1)} %get-tuple-element.68), channel_id=1, source_target_pairs={{0,4},{4,0},{8,12},{12,8},{16,20},{20,16},{24,28},{28,24},{1,5},{5... | collective-permute-start | bytes 393224 | tf_op jit(solution)/shard_map/ppermute | solution.py:230
  5.6 9.8 %collective-permute-start.6 = (bf16[8,64,128]{2,1,0:T(8,128)(2,1)}, bf16[8,64,128]{2,1,0:T(8,128)(2,1)S(1)}, u32[]{:S(2)}, u32[]{:S(2)}) collective-permute-start(bf16[8,64,128]{2,1,0:T(8,128)(2,1)} %get-tuple-element.74.refs_2_), channel_id=1, source_target_pairs={{0,3},{1,2},{2,1},{3,0},{4,7},{5,6},{6,5},{7,4},{8,11},{9,10},{10,... | collective-permute-start | bytes 393224 | tf_op jit(solution)/shard_map/ppermute | solution.py:244
  6.3 9.9 %collective-permute-start.5 = (bf16[8,64,128]{2,1,0:T(8,128)(2,1)}, bf16[8,64,128]{2,1,0:T(8,128)(2,1)S(1)}, u32[]{:S(2)}, u32[]{:S(2)}) collective-permute-start(bf16[8,64,128]{2,1,0:T(8,128)(2,1)} %get-tuple-element.74.refs_2_), channel_id=1, source_target_pairs={{0,2},{1,3},{2,0},{3,1},{4,6},{5,7},{6,4},{7,5},{8,10},{9,11},{10,... | collective-permute-start | bytes 393224 | tf_op jit(solution)/shard_map/ppermute | solution.py:244
  7.2 9.0 %collective-permute-start.4 = (bf16[8,64,128]{2,1,0:T(8,128)(2,1)}, bf16[8,64,128]{2,1,0:T(8,128)(2,1)S(1)}, u32[]{:S(2)}, u32[]{:S(2)}) collective-permute-start(bf16[8,64,128]{2,1,0:T(8,128)(2,1)} %get-tuple-element.74.refs_2_), channel_id=1, source_target_pairs={{0,1},{1,0},{2,3},{3,2},{4,5},{5,4},{6,7},{7,6},{8,9},{9,8},{10,11... | collective-permute-start | bytes 393224 | tf_op jit(solution)/shard_map/ppermute | solution.py:244
  11.7 7.6 %collective-permute-start.1 = (bf16[2,2,64,128]{3,2,1,0:T(8,128)(2,1)S(1)}, bf16[2,2,64,128]{3,2,1,0:T(8,128)(2,1)S(1)}, u32[]{:S(2)}, u32[]{:S(2)}) collective-permute-start(bf16[2,2,64,128]{3,2,1,0:T(8,128)(2,1)S(1)} %get-tuple-element.70), channel_id=1, source_target_pairs={{0,24},{4,28},{8,16},{12,20},{16,8},{20,12},{24,0},{28,4},{1,25},{... | collective-permute-start | bytes 196616 | tf_op jit(solution)/shard_map/ppermute | solution.py:230
  15.4 5.9 %collective-permute-start.2 = (bf16[2,2,64,128]{3,2,1,0:T(8,128)(2,1)S(1)}, bf16[2,2,64,128]{3,2,1,0:T(8,128)(2,1)S(1)}, u32[]{:S(2)}, u32[]{:S(2)}) collective-permute-start(bf16[2,2,64,128]{3,2,1,0:T(8,128)(2,1)S(1)} %get-tuple-element.71), channel_id=1, source_target_pairs={{0,16},{4,20},{8,24},{12,28},{16,0},{20,4},{24,8},{28,12},{1,17},{... | collective-permute-start | bytes 196616 | tf_op jit(solution)/shard_map/ppermute | solution.py:230
  15.4 5.9 %collective-permute-start.3 = (bf16[2,2,64,128]{3,2,1,0:T(8,128)(2,1)S(1)}, bf16[2,2,64,128]{3,2,1,0:T(8,128)(2,1)S(1)}, u32[]{:S(2)}, u32[]{:S(2)}) collective-permute-start(bf16[2,2,64,128]{3,2,1,0:T(8,128)(2,1)S(1)} %get-tuple-element.72), channel_id=1, source_target_pairs={{0,8},{4,12},{8,0},{12,4},{16,24},{20,28},{24,16},{28,20},{1,9},{5... | collective-permute-start | bytes 196616 | tf_op jit(solution)/shard_map/ppermute | solution.py:230
  17.5 7.5 %collective-permute-start.11 = (bf16[4,2,64,128]{3,2,1,0:T(8,128)(2,1)S(1)}, bf16[4,2,64,128]{3,2,1,0:T(8,128)(2,1)S(1)}, u32[]{:S(2)}, u32[]{:S(2)}) collective-permute-start(bf16[4,2,64,128]{3,2,1,0:T(8,128)(2,1)S(1)} %shard_map.80), channel_id=1, source_target_pairs={{0,4},{4,0},{8,12},{12,8},{16,20},{20,16},{24,28},{28,24},{1,5},{5... | collective-permute-start | bytes 393224 | tf_op jit(solution)/shard_map/ppermute | solution.py:230
  22.8 6.6 %collective-permute-start.8 = (bf16[8,64,128]{2,1,0:T(8,128)(2,1)S(1)}, bf16[8,64,128]{2,1,0:T(8,128)(2,1)S(1)}, u32[]{:S(2)}, u32[]{:S(2)}) collective-permute-start(bf16[8,64,128]{2,1,0:T(8,128)(2,1)S(1)} %get-tuple-element.85), channel_id=1, source_target_pairs={{0,3},{1,2},{2,1},{3,0},{4,7},{5,6},{6,5},{7,4},{8,11},{9,10},{10,... | collective-permute-start | bytes 393224 | tf_op jit(solution)/shard_map/ppermute | solution.py:244
  24.4 7.2 %collective-permute-start.9 = (bf16[8,64,128]{2,1,0:T(8,128)(2,1)S(1)}, bf16[8,64,128]{2,1,0:T(8,128)(2,1)S(1)}, u32[]{:S(2)}, u32[]{:S(2)}) collective-permute-start(bf16[8,64,128]{2,1,0:T(8,128)(2,1)S(1)} %get-tuple-element.86), channel_id=1, source_target_pairs={{0,2},{1,3},{2,0},{3,1},{4,6},{5,7},{6,4},{7,5},{8,10},{9,11},{10,... | collective-permute-start | bytes 393224 | tf_op jit(solution)/shard_map/ppermute | solution.py:244
  25.0 7.9 %collective-permute-start.12 = (bf16[2,2,64,128]{3,2,1,0:T(8,128)(2,1)S(1)}, bf16[2,2,64,128]{3,2,1,0:T(8,128)(2,1)S(1)}, u32[]{:S(2)}, u32[]{:S(2)}) collective-permute-start(bf16[2,2,64,128]{3,2,1,0:T(8,128)(2,1)S(1)} %get-tuple-element.90), channel_id=1, source_target_pairs={{0,24},{4,28},{8,16},{12,20},{16,8},{20,12},{24,0},{28,4},{1,25},{... | collective-permute-start | bytes 196616 | tf_op jit(solution)/shard_map/ppermute | solution.py:230
  27.5 6.6 %collective-permute-start.13 = (bf16[2,2,64,128]{3,2,1,0:T(8,128)(2,1)S(1)}, bf16[2,2,64,128]{3,2,1,0:T(8,128)(2,1)S(1)}, u32[]{:S(2)}, u32[]{:S(2)}) collective-permute-start(bf16[2,2,64,128]{3,2,1,0:T(8,128)(2,1)S(1)} %get-tuple-element.91), channel_id=1, source_target_pairs={{0,16},{4,20},{8,24},{12,28},{16,0},{20,4},{24,8},{28,12},{1,17},{... | collective-permute-start | bytes 196616 | tf_op jit(solution)/shard_map/ppermute | solution.py:230
  27.7 6.5 %collective-permute-start.14 = (bf16[2,2,64,128]{3,2,1,0:T(8,128)(2,1)S(1)}, bf16[2,2,64,128]{3,2,1,0:T(8,128)(2,1)S(1)}, u32[]{:S(2)}, u32[]{:S(2)}) collective-permute-start(bf16[2,2,64,128]{3,2,1,0:T(8,128)(2,1)S(1)} %get-tuple-element.92), channel_id=1, source_target_pairs={{0,8},{4,12},{8,0},{12,4},{16,24},{20,28},{24,16},{28,20},{1,9},{5... | collective-permute-start | bytes 196616 | tf_op jit(solution)/shard_map/ppermute | solution.py:230
  35.0 5.9 %collective-permute-start.20 = (bf16[8,64,128]{2,1,0:T(8,128)(2,1)S(1)}, bf16[8,64,128]{2,1,0:T(8,128)(2,1)S(1)}, u32[]{:S(2)}, u32[]{:S(2)}) collective-permute-start(bf16[8,64,128]{2,1,0:T(8,128)(2,1)S(1)} %get-tuple-element.103.refs_1_), channel_id=1, source_target_pairs={{0,3},{1,2},{2,1},{3,0},{4,7},{5,6},{6,5},{7,4},{8,11},{9,10},{10,... | collective-permute-start | bytes 393224 | tf_op jit(solution)/shard_map/ppermute | solution.py:244
  35.6 7.8 %collective-permute-start.19 = (bf16[8,64,128]{2,1,0:T(8,128)(2,1)S(1)}, bf16[8,64,128]{2,1,0:T(8,128)(2,1)S(1)}, u32[]{:S(2)}, u32[]{:S(2)}) collective-permute-start(bf16[8,64,128]{2,1,0:T(8,128)(2,1)S(1)} %get-tuple-element.103.refs_1_), channel_id=1, source_target_pairs={{0,2},{1,3},{2,0},{3,1},{4,6},{5,7},{6,4},{7,5},{8,10},{9,11},{10,... | collective-permute-start | bytes 393224 | tf_op jit(solution)/shard_map/ppermute | solution.py:244
  36.4 7.0 %collective-permute-start.18 = (bf16[8,64,128]{2,1,0:T(8,128)(2,1)S(1)}, bf16[8,64,128]{2,1,0:T(8,128)(2,1)S(1)}, u32[]{:S(2)}, u32[]{:S(2)}) collective-permute-start(bf16[8,64,128]{2,1,0:T(8,128)(2,1)S(1)} %get-tuple-element.103.refs_1_), channel_id=1, source_target_pairs={{0,1},{1,0},{2,3},{3,2},{4,5},{5,4},{6,7},{7,6},{8,9},{9,8},{10,11... | collective-permute-start | bytes 393224 | tf_op jit(solution)/shard_map/ppermute | solution.py:244
  37.3 8.2 %collective-permute-start.15 = (bf16[2,2,64,128]{3,2,1,0:T(8,128)(2,1)S(1)}, bf16[2,2,64,128]{3,2,1,0:T(8,128)(2,1)S(1)}, u32[]{:S(2)}, u32[]{:S(2)}) collective-permute-start(bf16[2,2,64,128]{3,2,1,0:T(8,128)(2,1)S(1)} %get-tuple-element.100), channel_id=1, source_target_pairs={{0,24},{4,28},{8,16},{12,20},{16,8},{20,12},{24,0},{28,4},{1,25},{... | collective-permute-start | bytes 196616 | tf_op jit(solution)/shard_map/ppermute | solution.py:230
  39.9 6.5 %collective-permute-start.16 = (bf16[2,2,64,128]{3,2,1,0:T(8,128)(2,1)S(1)}, bf16[2,2,64,128]{3,2,1,0:T(8,128)(2,1)S(1)}, u32[]{:S(2)}, u32[]{:S(2)}) collective-permute-start(bf16[2,2,64,128]{3,2,1,0:T(8,128)(2,1)S(1)} %get-tuple-element.101), channel_id=1, source_target_pairs={{0,16},{4,20},{8,24},{12,28},{16,0},{20,4},{24,8},{28,12},{1,17},{... | collective-permute-start | bytes 196616 | tf_op jit(solution)/shard_map/ppermute | solution.py:230
  44.1 5.7 %collective-permute-start.24 = (bf16[4,2,64,128]{3,2,1,0:T(8,128)(2,1)S(1)}, bf16[4,2,64,128]{3,2,1,0:T(8,128)(2,1)S(1)}, u32[]{:S(2)}, u32[]{:S(2)}) collective-permute-start(bf16[4,2,64,128]{3,2,1,0:T(8,128)(2,1)S(1)} %shard_map.87), channel_id=1, source_target_pairs={{0,4},{4,0},{8,12},{12,8},{16,20},{20,16},{24,28},{28,24},{1,5},{5... | collective-permute-start | bytes 393224 | tf_op jit(solution)/shard_map/ppermute | solution.py:230
  47.4 6.9 %collective-permute-start.22 = (bf16[8,64,128]{2,1,0:T(8,128)(2,1)S(1)}, bf16[8,64,128]{2,1,0:T(8,128)(2,1)S(1)}, u32[]{:S(2)}, u32[]{:S(2)}) collective-permute-start(bf16[8,64,128]{2,1,0:T(8,128)(2,1)S(1)} %get-tuple-element.114), channel_id=1, source_target_pairs={{0,3},{1,2},{2,1},{3,0},{4,7},{5,6},{6,5},{7,4},{8,11},{9,10},{10,... | collective-permute-start | bytes 393224 | tf_op jit(solution)/shard_map/ppermute | solution.py:244
  48.8 7.3 %collective-permute-start.23 = (bf16[8,64,128]{2,1,0:T(8,128)(2,1)S(1)}, bf16[8,64,128]{2,1,0:T(8,128)(2,1)S(1)}, u32[]{:S(2)}, u32[]{:S(2)}) collective-permute-start(bf16[8,64,128]{2,1,0:T(8,128)(2,1)S(1)} %get-tuple-element.115), channel_id=1, source_target_pairs={{0,2},{1,3},{2,0},{3,1},{4,6},{5,7},{6,4},{7,5},{8,10},{9,11},{10,... | collective-permute-start | bytes 393224 | tf_op jit(solution)/shard_map/ppermute | solution.py:244
  49.9 7.0 %collective-permute-start.25 = (bf16[2,2,64,128]{3,2,1,0:T(8,128)(2,1)S(1)}, bf16[2,2,64,128]{3,2,1,0:T(8,128)(2,1)S(1)}, u32[]{:S(2)}, u32[]{:S(2)}) collective-permute-start(bf16[2,2,64,128]{3,2,1,0:T(8,128)(2,1)S(1)} %get-tuple-element.118), channel_id=1, source_target_pairs={{0,24},{4,28},{8,16},{12,20},{16,8},{20,12},{24,0},{28,4},{1,25},{... | collective-permute-start | bytes 196616 | tf_op jit(solution)/shard_map/ppermute | solution.py:230
  51.8 6.2 %collective-permute-start.26 = (bf16[2,2,64,128]{3,2,1,0:T(8,128)(2,1)S(1)}, bf16[2,2,64,128]{3,2,1,0:T(8,128)(2,1)S(1)}, u32[]{:S(2)}, u32[]{:S(2)}) collective-permute-start(bf16[2,2,64,128]{3,2,1,0:T(8,128)(2,1)S(1)} %get-tuple-element.119), channel_id=1, source_target_pairs={{0,16},{4,20},{8,24},{12,28},{16,0},{20,4},{24,8},{28,12},{1,17},{... | collective-permute-start | bytes 196616 | tf_op jit(solution)/shard_map/ppermute | solution.py:230
  51.8 6.2 %collective-permute-start.27 = (bf16[2,2,64,128]{3,2,1,0:T(8,128)(2,1)S(1)}, bf16[2,2,64,128]{3,2,1,0:T(8,128)(2,1)S(1)}, u32[]{:S(2)}, u32[]{:S(2)}) collective-permute-start(bf16[2,2,64,128]{3,2,1,0:T(8,128)(2,1)S(1)} %get-tuple-element.120), channel_id=1, source_target_pairs={{0,8},{4,12},{8,0},{12,4},{16,24},{20,28},{24,16},{28,20},{1,9},{5... | collective-permute-start | bytes 196616 | tf_op jit(solution)/shard_map/ppermute | solution.py:230
  (9 other events, 72.4 us)

commit v12 on v11

--- a/solution.py
+++ b/solution.py
@@ -261,7 +261,7 @@
         places_out=[VMEM] * 3 + [HBM],
     )
     dense_shape = (slot_total * quarter, count * width)
-    parts = next(size for size in (12, 8, 4, 2, 1) if block_count % size == 0)
+    parts = next(size for size in (6, 4, 2, 1) if block_count % size == 0)
     high, low = call(
         build_kernel,
         (ids, values),

time: 59.7 us -> 59.8 us (level)
  no operation moved by 1% of the time
where the time goes in v12:
time: 59.8 us; the launch traced here: 59.6 us
  starting transfers between devices  29.9 us (50%)
  Pallas kernels  16.6 us (28%)
  waiting for transfers between devices  12.3 us (21%)
  between operations  0.82 us (1%)
    ppermute x16, starting transfers between devices, to_node(): lax.ppermute(array, 'node', [(place, place ^ turn) for place in range(own...  21.7 us
    pallas_call x16, Pallas kernels, call(): pl.pallas_call(kernel, out_shape=[jax.ShapeDtypeStruct(*out) for out in o...  16.6 us
    ppermute x12, starting transfers between devices, over_edge(): lax.ppermute(array, 'edge', [(place, place ^ turn) for place in range(qua...  8.21 us
    ppermute x12, waiting for transfers between devices, over_edge(): lax.ppermute(array, 'edge', [(place, place ^ turn) for place in range(qua...  6.24 us
    ppermute x16, waiting for transfers between devices, to_node(): lax.ppermute(array, 'node', [(place, place ^ turn) for place in range(own...  6.06 us
  transfers between devices with their start and end apart: 28, of which 10 were waited for; matrix products, arithmetic and copies ran while one was open for 0% of the time, Pallas kernels for 22%

profile of v12, /device:TPU:0, one launch (start us, length us, event | category | flops | bytes accessed | tf_op | source)
XLA Modules:
  0.0 59.6 jit_solution(2083798069984089107)
XLA Ops:
  0.6 2.0 %shard_map.77 = (bf16[4,2,64,128]{3,2,1,0:T(8,128)(2,1)}, bf16[4,2,64,128]{3,2,1,0:T(8,128)(2,1)}, bf16[8,64,128]{2,1,0:T(8,128)(2,1)}, s32[24576,1,192]{2,1,0:T(1,128)}) custom-call(s32[8,16]{1,0:T(8,128)} %table.7, f32[8,64,128]{2,1,0:T(8,128)} %bitcast.4, f32[8,64,128]{2,1,0:T(8,128)} %bitcast.7, s32[1,192]{1,0:T(1,128)} %rows.1, s32[1,192]{1,0:T(1,128)} %slots.1), custom_call_target="tpu_custom_call" | custom-call | tf_op jit(solution)/shard_map/pallas_call | solution.py:216
  2.6 3.0 %collective-permute-start = (bf16[4,2,64,128]{3,2,1,0:T(8,128)(2,1)}, bf16[4,2,64,128]{3,2,1,0:T(8,128)(2,1)S(1)}, u32[]{:S(2)}, u32[]{:S(2)}) collective-permute-start(bf16[4,2,64,128]{3,2,1,0:T(8,128)(2,1)} %get-tuple-element.68), channel_id=1, source_target_pairs={{0,4},{4,0},{8,12},{12,8},{16,20},{20,16},{24,28},{28,24},{1,5},{5... | collective-permute-start | bytes 393224 | tf_op jit(solution)/shard_map/ppermute | solution.py:230
  7.5 4.3 %shard_map.78 = (bf16[1024,2048]{1,0:T(8,128)(2,1)S(1)}, bf16[1024,2048]{1,0:T(8,128)(2,1)S(1)}) custom-call(s32[24576,1,192]{2,1,0:T(1,128)} %get-tuple-element.64.ids, bf16[1,192,64,256]{3,2,1,0:T(8,128)(2,1)} %weights.1), custom_call_target="tpu_custom_call" | custom-call | bytes 6291456 | tf_op jit(solution)/shard_map/pallas_call | solution.py:216
  11.9 3.7 %collective-permute-start.1 = (bf16[2,2,64,128]{3,2,1,0:T(8,128)(2,1)S(1)}, bf16[2,2,64,128]{3,2,1,0:T(8,128)(2,1)S(1)}, u32[]{:S(2)}, u32[]{:S(2)}) collective-permute-start(bf16[2,2,64,128]{3,2,1,0:T(8,128)(2,1)S(1)} %get-tuple-element.70), channel_id=1, source_target_pairs={{0,24},{4,28},{8,16},{12,20},{16,8},{20,12},{24,0},{28,4},{1,25},{... | collective-permute-start | bytes 196616 | tf_op jit(solution)/shard_map/ppermute | solution.py:230
  16.3 1.3 %shard_map.80 = bf16[4,2,64,128]{3,2,1,0:T(8,128)(2,1)S(1)} custom-call(bf16[1024,2048]{1,0:T(8,128)(2,1)S(1)} %get-tuple-element.65.refs_0_, bf16[1024,2048]{1,0:T(8,128)(2,1)S(1)} %get-tuple-element.66.refs_1_, bf16[8,64,128]{2,1,0:T(8,128)(2,1)S(1)} %copy-done.2, bf16[8,64,128]{2,1,0:T(8,128)(2,1)S(1)} %collective-permute-done.4.refs_3_, ...), custom_call_target="tpu_custom_call" | custom-call | flops 536870912 | bytes 4194304 | tf_op jit(solution)/shard_map/pallas_call | solution.py:216
  18.1 1.3 %shard_map.81.kept.refs_0_ = bf16[4,2,64,128]{3,2,1,0:T(8,128)(2,1)S(1)} custom-call(bf16[1024,2048]{1,0:T(8,128)(2,1)S(1)} %get-tuple-element.65.refs_0_, bf16[1024,2048]{1,0:T(8,128)(2,1)S(1)} %get-tuple-element.66.refs_1_, bf16[8,64,128]{2,1,0:T(8,128)(2,1)S(1)} %copy-done.2, bf16[8,64,128]{2,1,0:T(8,128)(2,1)S(1)} %collective-permute-done.4.refs_3_, ...), custom_call_target="tpu_custom_call" | custom-call | flops 536870912 | bytes 4194304 | tf_op jit(solution)/shard_map/pallas_call | solution.py:216
  19.4 2.0 %collective-permute-done.2.refs_5_ = bf16[2,2,64,128]{3,2,1,0:T(8,128)(2,1)S(1)} collective-permute-done((bf16[2,2,64,128]{3,2,1,0:T(8,128)(2,1)S(1)}, bf16[2,2,64,128]{3,2,1,0:T(8,128)(2,1)S(1)}, u32[]{:S(2)}, u32[]{:S(2)}) %collective-permute-start.2) | collective-permute-done | bytes 65568 | tf_op jit(solution)/shard_map/ppermute | solution.py:230
  21.4 1.5 %shard_map.82 = (f32[8,64,128]{2,1,0:T(8,128)S(1)}, bf16[8,64,128]{2,1,0:T(8,128)(2,1)S(1)}, bf16[8,64,128]{2,1,0:T(8,128)(2,1)S(1)}, bf16[8,64,128]{2,1,0:T(8,128)(2,1)S(1)}) custom-call(bf16[1024,2048]{1,0:T(8,128)(2,1)S(1)} %get-tuple-element.65.refs_0_, bf16[1024,2048]{1,0:T(8,128)(2,1)S(1)} %get-tuple-element.66.refs_1_, ...), custom_call_target="tpu_custom_call" | custom-call | flops 1073741824 | bytes 8388608 | tf_op jit(solution)/shard_map/pallas_call | solution.py:216
  23.0 1.5 %collective-permute-start.8 = (bf16[8,64,128]{2,1,0:T(8,128)(2,1)S(1)}, bf16[8,64,128]{2,1,0:T(8,128)(2,1)S(1)}, u32[]{:S(2)}, u32[]{:S(2)}) collective-permute-start(bf16[8,64,128]{2,1,0:T(8,128)(2,1)S(1)} %get-tuple-element.85), channel_id=1, source_target_pairs={{0,3},{1,2},{2,1},{3,0},{4,7},{5,6},{6,5},{7,4},{8,11},{9,10},{10,... | collective-permute-start | bytes 393224 | tf_op jit(solution)/shard_map/ppermute | solution.py:244
  25.1 2.5 %collective-permute-start.12 = (bf16[2,2,64,128]{3,2,1,0:T(8,128)(2,1)S(1)}, bf16[2,2,64,128]{3,2,1,0:T(8,128)(2,1)S(1)}, u32[]{:S(2)}, u32[]{:S(2)}) collective-permute-start(bf16[2,2,64,128]{3,2,1,0:T(8,128)(2,1)S(1)} %get-tuple-element.90), channel_id=1, source_target_pairs={{0,24},{4,28},{8,16},{12,20},{16,8},{20,12},{24,0},{28,4},{1,25},{... | collective-permute-start | bytes 196616 | tf_op jit(solution)/shard_map/ppermute | solution.py:230
  27.8 1.8 %collective-permute-start.14 = (bf16[2,2,64,128]{3,2,1,0:T(8,128)(2,1)S(1)}, bf16[2,2,64,128]{3,2,1,0:T(8,128)(2,1)S(1)}, u32[]{:S(2)}, u32[]{:S(2)}) collective-permute-start(bf16[2,2,64,128]{3,2,1,0:T(8,128)(2,1)S(1)} %get-tuple-element.92), channel_id=1, source_target_pairs={{0,8},{4,12},{8,0},{12,4},{16,24},{20,28},{24,16},{28,20},{1,9},{5... | collective-permute-start | bytes 196616 | tf_op jit(solution)/shard_map/ppermute | solution.py:230
  29.6 2.0 %collective-permute-done.9.refs_3_ = bf16[8,64,128]{2,1,0:T(8,128)(2,1)S(1)} collective-permute-done((bf16[8,64,128]{2,1,0:T(8,128)(2,1)S(1)}, bf16[8,64,128]{2,1,0:T(8,128)(2,1)S(1)}, u32[]{:S(2)}, u32[]{:S(2)}) %collective-permute-start.9) | collective-permute-done | bytes 131104 | tf_op jit(solution)/shard_map/ppermute | solution.py:244
  33.0 1.3 %collective-permute-done.13.refs_3_ = bf16[2,2,64,128]{3,2,1,0:T(8,128)(2,1)S(1)} collective-permute-done((bf16[2,2,64,128]{3,2,1,0:T(8,128)(2,1)S(1)}, bf16[2,2,64,128]{3,2,1,0:T(8,128)(2,1)S(1)}, u32[]{:S(2)}, u32[]{:S(2)}) %collective-permute-start.13) | collective-permute-done | bytes 65568 | tf_op jit(solution)/shard_map/ppermute | solution.py:230
  37.4 2.5 %collective-permute-start.15 = (bf16[2,2,64,128]{3,2,1,0:T(8,128)(2,1)S(1)}, bf16[2,2,64,128]{3,2,1,0:T(8,128)(2,1)S(1)}, u32[]{:S(2)}, u32[]{:S(2)}) collective-permute-start(bf16[2,2,64,128]{3,2,1,0:T(8,128)(2,1)S(1)} %get-tuple-element.100), channel_id=1, source_target_pairs={{0,24},{4,28},{8,16},{12,20},{16,8},{20,12},{24,0},{28,4},{1,25},{... | collective-permute-start | bytes 196616 | tf_op jit(solution)/shard_map/ppermute | solution.py:230
  40.9 1.0 %collective-permute-start.17 = (bf16[2,2,64,128]{3,2,1,0:T(8,128)(2,1)S(1)}, bf16[2,2,64,128]{3,2,1,0:T(8,128)(2,1)S(1)}, u32[]{:S(2)}, u32[]{:S(2)}) collective-permute-start(bf16[2,2,64,128]{3,2,1,0:T(8,128)(2,1)S(1)} %get-tuple-element.102), channel_id=1, source_target_pairs={{0,8},{4,12},{8,0},{12,4},{16,24},{20,28},{24,16},{28,20},{1,9},{5... | collective-permute-start | bytes 196616 | tf_op jit(solution)/shard_map/ppermute | solution.py:230
  41.9 1.6 %collective-permute-done.19.refs_3_ = bf16[8,64,128]{2,1,0:T(8,128)(2,1)S(1)} collective-permute-done((bf16[8,64,128]{2,1,0:T(8,128)(2,1)S(1)}, bf16[8,64,128]{2,1,0:T(8,128)(2,1)S(1)}, u32[]{:S(2)}, u32[]{:S(2)}) %collective-permute-start.19) | collective-permute-done | bytes 131104 | tf_op jit(solution)/shard_map/ppermute | solution.py:244
  45.6 0.9 %collective-permute-done.16.refs_4_ = bf16[2,2,64,128]{3,2,1,0:T(8,128)(2,1)S(1)} collective-permute-done((bf16[2,2,64,128]{3,2,1,0:T(8,128)(2,1)S(1)}, bf16[2,2,64,128]{3,2,1,0:T(8,128)(2,1)S(1)}, u32[]{:S(2)}, u32[]{:S(2)}) %collective-permute-start.16) | collective-permute-done | bytes 65568 | tf_op jit(solution)/shard_map/ppermute | solution.py:230
  46.5 0.9 %shard_map.89 = (f32[8,64,128]{2,1,0:T(8,128)S(1)}, bf16[8,64,128]{2,1,0:T(8,128)(2,1)S(1)}, bf16[8,64,128]{2,1,0:T(8,128)(2,1)S(1)}, bf16[8,64,128]{2,1,0:T(8,128)(2,1)S(1)}) custom-call(bf16[1024,2048]{1,0:T(8,128)(2,1)S(1)} %get-tuple-element.65.refs_0_, bf16[4,2,64,128]{3,2,1,0:T(8,128)(2,1)S(1)} %get-tuple-element.107.kept.refs_1_, ...), custom_call_target="tpu_custom_call" | custom-call | flops 536870912 | bytes 4194304 | tf_op jit(solution)/shard_map/pallas_call | solution.py:216
  47.5 1.4 %collective-permute-start.22 = (bf16[8,64,128]{2,1,0:T(8,128)(2,1)S(1)}, bf16[8,64,128]{2,1,0:T(8,128)(2,1)S(1)}, u32[]{:S(2)}, u32[]{:S(2)}) collective-permute-start(bf16[8,64,128]{2,1,0:T(8,128)(2,1)S(1)} %get-tuple-element.114), channel_id=1, source_target_pairs={{0,3},{1,2},{2,1},{3,0},{4,7},{5,6},{6,5},{7,4},{8,11},{9,10},{10,... | collective-permute-start | bytes 393224 | tf_op jit(solution)/shard_map/ppermute | solution.py:244
  50.0 1.9 %collective-permute-start.25 = (bf16[2,2,64,128]{3,2,1,0:T(8,128)(2,1)S(1)}, bf16[2,2,64,128]{3,2,1,0:T(8,128)(2,1)S(1)}, u32[]{:S(2)}, u32[]{:S(2)}) collective-permute-start(bf16[2,2,64,128]{3,2,1,0:T(8,128)(2,1)S(1)} %get-tuple-element.118), channel_id=1, source_target_pairs={{0,24},{4,28},{8,16},{12,20},{16,8},{20,12},{24,0},{28,4},{1,25},{... | collective-permute-start | bytes 196616 | tf_op jit(solution)/shard_map/ppermute | solution.py:230
  51.9 2.5 %collective-permute-start.27 = (bf16[2,2,64,128]{3,2,1,0:T(8,128)(2,1)S(1)}, bf16[2,2,64,128]{3,2,1,0:T(8,128)(2,1)S(1)}, u32[]{:S(2)}, u32[]{:S(2)}) collective-permute-start(bf16[2,2,64,128]{3,2,1,0:T(8,128)(2,1)S(1)} %get-tuple-element.120), channel_id=1, source_target_pairs={{0,8},{4,12},{8,0},{12,4},{16,24},{20,28},{24,16},{28,20},{1,9},{5... | collective-permute-start | bytes 196616 | tf_op jit(solution)/shard_map/ppermute | solution.py:230
  54.4 1.8 %collective-permute-done.23.refs_3_ = bf16[8,64,128]{2,1,0:T(8,128)(2,1)S(1)} collective-permute-done((bf16[8,64,128]{2,1,0:T(8,128)(2,1)S(1)}, bf16[8,64,128]{2,1,0:T(8,128)(2,1)S(1)}, u32[]{:S(2)}, u32[]{:S(2)}) %collective-permute-start.23) | collective-permute-done | bytes 131104 | tf_op jit(solution)/shard_map/ppermute | solution.py:244
  57.0 1.1 %collective-permute-done.26.refs_3_ = bf16[2,2,64,128]{3,2,1,0:T(8,128)(2,1)S(1)} collective-permute-done((bf16[2,2,64,128]{3,2,1,0:T(8,128)(2,1)S(1)}, bf16[2,2,64,128]{3,2,1,0:T(8,128)(2,1)S(1)}, u32[]{:S(2)}, u32[]{:S(2)}) %collective-permute-start.26) | collective-permute-done | bytes 65568 | tf_op jit(solution)/shard_map/ppermute | solution.py:230
  58.2 1.4 %shard_map.92 = f32[8,64,128]{2,1,0:T(8,128)} custom-call(s32[8,16]{1,0:T(8,128)S(1)} %copy-done.4, f32[8,64,128]{2,1,0:T(8,128)S(1)} %get-tuple-element.116.gradient_in, bf16[4,2,64,128]{3,2,1,0:T(8,128)(2,1)S(1)} %shard_map.88.kept.refs_0_, bf16[4,2,64,128]{3,2,1,0:T(8,128)(2,1)S(1)} %collective-permute-done.24.got.refs_1_, ...), custom_call_target="tpu_custom_call" | custom-call | tf_op jit(solution)/shard_map/pallas_call | solution.py:216
  (58 shorter events, 13.5 us)
Async XLA Ops:
  2.6 9.2 %collective-permute-start = (bf16[4,2,64,128]{3,2,1,0:T(8,128)(2,1)}, bf16[4,2,64,128]{3,2,1,0:T(8,128)(2,1)S(1)}, u32[]{:S(2)}, u32[]{:S(2)}) collective-permute-start(bf16[4,2,64,128]{3,2,1,0:T(8,128)(2,1)} %get-tuple-element.68), channel_id=1, source_target_pairs={{0,4},{4,0},{8,12},{12,8},{16,20},{20,16},{24,28},{28,24},{1,5},{5... | collective-permute-start | bytes 393224 | tf_op jit(solution)/shard_map/ppermute | solution.py:230
  5.6 9.9 %collective-permute-start.6 = (bf16[8,64,128]{2,1,0:T(8,128)(2,1)}, bf16[8,64,128]{2,1,0:T(8,128)(2,1)S(1)}, u32[]{:S(2)}, u32[]{:S(2)}) collective-permute-start(bf16[8,64,128]{2,1,0:T(8,128)(2,1)} %get-tuple-element.74.refs_2_), channel_id=1, source_target_pairs={{0,3},{1,2},{2,1},{3,0},{4,7},{5,6},{6,5},{7,4},{8,11},{9,10},{10,... | collective-permute-start | bytes 393224 | tf_op jit(solution)/shard_map/ppermute | solution.py:244
  6.3 10.0 %collective-permute-start.5 = (bf16[8,64,128]{2,1,0:T(8,128)(2,1)}, bf16[8,64,128]{2,1,0:T(8,128)(2,1)S(1)}, u32[]{:S(2)}, u32[]{:S(2)}) collective-permute-start(bf16[8,64,128]{2,1,0:T(8,128)(2,1)} %get-tuple-element.74.refs_2_), channel_id=1, source_target_pairs={{0,2},{1,3},{2,0},{3,1},{4,6},{5,7},{6,4},{7,5},{8,10},{9,11},{10,... | collective-permute-start | bytes 393224 | tf_op jit(solution)/shard_map/ppermute | solution.py:244
  7.2 9.2 %collective-permute-start.4 = (bf16[8,64,128]{2,1,0:T(8,128)(2,1)}, bf16[8,64,128]{2,1,0:T(8,128)(2,1)S(1)}, u32[]{:S(2)}, u32[]{:S(2)}) collective-permute-start(bf16[8,64,128]{2,1,0:T(8,128)(2,1)} %get-tuple-element.74.refs_2_), channel_id=1, source_target_pairs={{0,1},{1,0},{2,3},{3,2},{4,5},{5,4},{6,7},{7,6},{8,9},{9,8},{10,11... | collective-permute-start | bytes 393224 | tf_op jit(solution)/shard_map/ppermute | solution.py:244
  11.9 7.6 %collective-permute-start.1 = (bf16[2,2,64,128]{3,2,1,0:T(8,128)(2,1)S(1)}, bf16[2,2,64,128]{3,2,1,0:T(8,128)(2,1)S(1)}, u32[]{:S(2)}, u32[]{:S(2)}) collective-permute-start(bf16[2,2,64,128]{3,2,1,0:T(8,128)(2,1)S(1)} %get-tuple-element.70), channel_id=1, source_target_pairs={{0,24},{4,28},{8,16},{12,20},{16,8},{20,12},{24,0},{28,4},{1,25},{... | collective-permute-start | bytes 196616 | tf_op jit(solution)/shard_map/ppermute | solution.py:230
  15.5 5.9 %collective-permute-start.2 = (bf16[2,2,64,128]{3,2,1,0:T(8,128)(2,1)S(1)}, bf16[2,2,64,128]{3,2,1,0:T(8,128)(2,1)S(1)}, u32[]{:S(2)}, u32[]{:S(2)}) collective-permute-start(bf16[2,2,64,128]{3,2,1,0:T(8,128)(2,1)S(1)} %get-tuple-element.71), channel_id=1, source_target_pairs={{0,16},{4,20},{8,24},{12,28},{16,0},{20,4},{24,8},{28,12},{1,17},{... | collective-permute-start | bytes 196616 | tf_op jit(solution)/shard_map/ppermute | solution.py:230
  15.5 5.9 %collective-permute-start.3 = (bf16[2,2,64,128]{3,2,1,0:T(8,128)(2,1)S(1)}, bf16[2,2,64,128]{3,2,1,0:T(8,128)(2,1)S(1)}, u32[]{:S(2)}, u32[]{:S(2)}) collective-permute-start(bf16[2,2,64,128]{3,2,1,0:T(8,128)(2,1)S(1)} %get-tuple-element.72), channel_id=1, source_target_pairs={{0,8},{4,12},{8,0},{12,4},{16,24},{20,28},{24,16},{28,20},{1,9},{5... | collective-permute-start | bytes 196616 | tf_op jit(solution)/shard_map/ppermute | solution.py:230
  17.6 7.5 %collective-permute-start.11 = (bf16[4,2,64,128]{3,2,1,0:T(8,128)(2,1)S(1)}, bf16[4,2,64,128]{3,2,1,0:T(8,128)(2,1)S(1)}, u32[]{:S(2)}, u32[]{:S(2)}) collective-permute-start(bf16[4,2,64,128]{3,2,1,0:T(8,128)(2,1)S(1)} %shard_map.80), channel_id=1, source_target_pairs={{0,4},{4,0},{8,12},{12,8},{16,20},{20,16},{24,28},{28,24},{1,5},{5... | collective-permute-start | bytes 393224 | tf_op jit(solution)/shard_map/ppermute | solution.py:230
  23.0 6.6 %collective-permute-start.8 = (bf16[8,64,128]{2,1,0:T(8,128)(2,1)S(1)}, bf16[8,64,128]{2,1,0:T(8,128)(2,1)S(1)}, u32[]{:S(2)}, u32[]{:S(2)}) collective-permute-start(bf16[8,64,128]{2,1,0:T(8,128)(2,1)S(1)} %get-tuple-element.85), channel_id=1, source_target_pairs={{0,3},{1,2},{2,1},{3,0},{4,7},{5,6},{6,5},{7,4},{8,11},{9,10},{10,... | collective-permute-start | bytes 393224 | tf_op jit(solution)/shard_map/ppermute | solution.py:244
  24.5 7.2 %collective-permute-start.9 = (bf16[8,64,128]{2,1,0:T(8,128)(2,1)S(1)}, bf16[8,64,128]{2,1,0:T(8,128)(2,1)S(1)}, u32[]{:S(2)}, u32[]{:S(2)}) collective-permute-start(bf16[8,64,128]{2,1,0:T(8,128)(2,1)S(1)} %get-tuple-element.86), channel_id=1, source_target_pairs={{0,2},{1,3},{2,0},{3,1},{4,6},{5,7},{6,4},{7,5},{8,10},{9,11},{10,... | collective-permute-start | bytes 393224 | tf_op jit(solution)/shard_map/ppermute | solution.py:244
  25.1 7.9 %collective-permute-start.12 = (bf16[2,2,64,128]{3,2,1,0:T(8,128)(2,1)S(1)}, bf16[2,2,64,128]{3,2,1,0:T(8,128)(2,1)S(1)}, u32[]{:S(2)}, u32[]{:S(2)}) collective-permute-start(bf16[2,2,64,128]{3,2,1,0:T(8,128)(2,1)S(1)} %get-tuple-element.90), channel_id=1, source_target_pairs={{0,24},{4,28},{8,16},{12,20},{16,8},{20,12},{24,0},{28,4},{1,25},{... | collective-permute-start | bytes 196616 | tf_op jit(solution)/shard_map/ppermute | solution.py:230
  27.7 6.6 %collective-permute-start.13 = (bf16[2,2,64,128]{3,2,1,0:T(8,128)(2,1)S(1)}, bf16[2,2,64,128]{3,2,1,0:T(8,128)(2,1)S(1)}, u32[]{:S(2)}, u32[]{:S(2)}) collective-permute-start(bf16[2,2,64,128]{3,2,1,0:T(8,128)(2,1)S(1)} %get-tuple-element.91), channel_id=1, source_target_pairs={{0,16},{4,20},{8,24},{12,28},{16,0},{20,4},{24,8},{28,12},{1,17},{... | collective-permute-start | bytes 196616 | tf_op jit(solution)/shard_map/ppermute | solution.py:230
  27.8 6.5 %collective-permute-start.14 = (bf16[2,2,64,128]{3,2,1,0:T(8,128)(2,1)S(1)}, bf16[2,2,64,128]{3,2,1,0:T(8,128)(2,1)S(1)}, u32[]{:S(2)}, u32[]{:S(2)}) collective-permute-start(bf16[2,2,64,128]{3,2,1,0:T(8,128)(2,1)S(1)} %get-tuple-element.92), channel_id=1, source_target_pairs={{0,8},{4,12},{8,0},{12,4},{16,24},{20,28},{24,16},{28,20},{1,9},{5... | collective-permute-start | bytes 196616 | tf_op jit(solution)/shard_map/ppermute | solution.py:230
  35.1 5.9 %collective-permute-start.20 = (bf16[8,64,128]{2,1,0:T(8,128)(2,1)S(1)}, bf16[8,64,128]{2,1,0:T(8,128)(2,1)S(1)}, u32[]{:S(2)}, u32[]{:S(2)}) collective-permute-start(bf16[8,64,128]{2,1,0:T(8,128)(2,1)S(1)} %get-tuple-element.103.refs_1_), channel_id=1, source_target_pairs={{0,3},{1,2},{2,1},{3,0},{4,7},{5,6},{6,5},{7,4},{8,11},{9,10},{10,... | collective-permute-start | bytes 393224 | tf_op jit(solution)/shard_map/ppermute | solution.py:244
  35.7 7.8 %collective-permute-start.19 = (bf16[8,64,128]{2,1,0:T(8,128)(2,1)S(1)}, bf16[8,64,128]{2,1,0:T(8,128)(2,1)S(1)}, u32[]{:S(2)}, u32[]{:S(2)}) collective-permute-start(bf16[8,64,128]{2,1,0:T(8,128)(2,1)S(1)} %get-tuple-element.103.refs_1_), channel_id=1, source_target_pairs={{0,2},{1,3},{2,0},{3,1},{4,6},{5,7},{6,4},{7,5},{8,10},{9,11},{10,... | collective-permute-start | bytes 393224 | tf_op jit(solution)/shard_map/ppermute | solution.py:244
  36.5 7.0 %collective-permute-start.18 = (bf16[8,64,128]{2,1,0:T(8,128)(2,1)S(1)}, bf16[8,64,128]{2,1,0:T(8,128)(2,1)S(1)}, u32[]{:S(2)}, u32[]{:S(2)}) collective-permute-start(bf16[8,64,128]{2,1,0:T(8,128)(2,1)S(1)} %get-tuple-element.103.refs_1_), channel_id=1, source_target_pairs={{0,1},{1,0},{2,3},{3,2},{4,5},{5,4},{6,7},{7,6},{8,9},{9,8},{10,11... | collective-permute-start | bytes 393224 | tf_op jit(solution)/shard_map/ppermute | solution.py:244
  37.4 8.2 %collective-permute-start.15 = (bf16[2,2,64,128]{3,2,1,0:T(8,128)(2,1)S(1)}, bf16[2,2,64,128]{3,2,1,0:T(8,128)(2,1)S(1)}, u32[]{:S(2)}, u32[]{:S(2)}) collective-permute-start(bf16[2,2,64,128]{3,2,1,0:T(8,128)(2,1)S(1)} %get-tuple-element.100), channel_id=1, source_target_pairs={{0,24},{4,28},{8,16},{12,20},{16,8},{20,12},{24,0},{28,4},{1,25},{... | collective-permute-start | bytes 196616 | tf_op jit(solution)/shard_map/ppermute | solution.py:230
  40.0 6.5 %collective-permute-start.16 = (bf16[2,2,64,128]{3,2,1,0:T(8,128)(2,1)S(1)}, bf16[2,2,64,128]{3,2,1,0:T(8,128)(2,1)S(1)}, u32[]{:S(2)}, u32[]{:S(2)}) collective-permute-start(bf16[2,2,64,128]{3,2,1,0:T(8,128)(2,1)S(1)} %get-tuple-element.101), channel_id=1, source_target_pairs={{0,16},{4,20},{8,24},{12,28},{16,0},{20,4},{24,8},{28,12},{1,17},{... | collective-permute-start | bytes 196616 | tf_op jit(solution)/shard_map/ppermute | solution.py:230
  44.3 5.7 %collective-permute-start.24 = (bf16[4,2,64,128]{3,2,1,0:T(8,128)(2,1)S(1)}, bf16[4,2,64,128]{3,2,1,0:T(8,128)(2,1)S(1)}, u32[]{:S(2)}, u32[]{:S(2)}) collective-permute-start(bf16[4,2,64,128]{3,2,1,0:T(8,128)(2,1)S(1)} %shard_map.87), channel_id=1, source_target_pairs={{0,4},{4,0},{8,12},{12,8},{16,20},{20,16},{24,28},{28,24},{1,5},{5... | collective-permute-start | bytes 393224 | tf_op jit(solution)/shard_map/ppermute | solution.py:230
  47.5 6.9 %collective-permute-start.22 = (bf16[8,64,128]{2,1,0:T(8,128)(2,1)S(1)}, bf16[8,64,128]{2,1,0:T(8,128)(2,1)S(1)}, u32[]{:S(2)}, u32[]{:S(2)}) collective-permute-start(bf16[8,64,128]{2,1,0:T(8,128)(2,1)S(1)} %get-tuple-element.114), channel_id=1, source_target_pairs={{0,3},{1,2},{2,1},{3,0},{4,7},{5,6},{6,5},{7,4},{8,11},{9,10},{10,... | collective-permute-start | bytes 393224 | tf_op jit(solution)/shard_map/ppermute | solution.py:244
  48.9 7.3 %collective-permute-start.23 = (bf16[8,64,128]{2,1,0:T(8,128)(2,1)S(1)}, bf16[8,64,128]{2,1,0:T(8,128)(2,1)S(1)}, u32[]{:S(2)}, u32[]{:S(2)}) collective-permute-start(bf16[8,64,128]{2,1,0:T(8,128)(2,1)S(1)} %get-tuple-element.115), channel_id=1, source_target_pairs={{0,2},{1,3},{2,0},{3,1},{4,6},{5,7},{6,4},{7,5},{8,10},{9,11},{10,... | collective-permute-start | bytes 393224 | tf_op jit(solution)/shard_map/ppermute | solution.py:244
  50.0 7.0 %collective-permute-start.25 = (bf16[2,2,64,128]{3,2,1,0:T(8,128)(2,1)S(1)}, bf16[2,2,64,128]{3,2,1,0:T(8,128)(2,1)S(1)}, u32[]{:S(2)}, u32[]{:S(2)}) collective-permute-start(bf16[2,2,64,128]{3,2,1,0:T(8,128)(2,1)S(1)} %get-tuple-element.118), channel_id=1, source_target_pairs={{0,24},{4,28},{8,16},{12,20},{16,8},{20,12},{24,0},{28,4},{1,25},{... | collective-permute-start | bytes 196616 | tf_op jit(solution)/shard_map/ppermute | solution.py:230
  51.9 6.2 %collective-permute-start.26 = (bf16[2,2,64,128]{3,2,1,0:T(8,128)(2,1)S(1)}, bf16[2,2,64,128]{3,2,1,0:T(8,128)(2,1)S(1)}, u32[]{:S(2)}, u32[]{:S(2)}) collective-permute-start(bf16[2,2,64,128]{3,2,1,0:T(8,128)(2,1)S(1)} %get-tuple-element.119), channel_id=1, source_target_pairs={{0,16},{4,20},{8,24},{12,28},{16,0},{20,4},{24,8},{28,12},{1,17},{... | collective-permute-start | bytes 196616 | tf_op jit(solution)/shard_map/ppermute | solution.py:230
  51.9 6.2 %collective-permute-start.27 = (bf16[2,2,64,128]{3,2,1,0:T(8,128)(2,1)S(1)}, bf16[2,2,64,128]{3,2,1,0:T(8,128)(2,1)S(1)}, u32[]{:S(2)}, u32[]{:S(2)}) collective-permute-start(bf16[2,2,64,128]{3,2,1,0:T(8,128)(2,1)S(1)} %get-tuple-element.120), channel_id=1, source_target_pairs={{0,8},{4,12},{8,0},{12,4},{16,24},{20,28},{24,16},{28,20},{1,9},{5... | collective-permute-start | bytes 196616 | tf_op jit(solution)/shard_map/ppermute | solution.py:230
  (9 other events, 72.6 us)
